TPU v7x, 32 devices: a whole 2x2x4 slice. The times are simulated.
32 devices in a mesh: dp: 8 (over z, x), tensor: 4 (over y, core).
Axes of the slice: x: 2, y: 2, z: 4, core: 2. Of those that a mesh axis runs over, the one named last changes fastest.
Arguments:
- tokens: bfloat16 [32768, 768], P(('dp', 'tensor')), may hold values from -6 to 6
- out_grad: bfloat16 [32768, 768], P(('dp', 'tensor')), may hold values from -6 to 6
- slot_kind: int32 [256, 128], P(('dp', 'tensor')), may hold values from 0 to 1, as said below
- slot_valid: int32 [256, 128], P(('dp', 'tensor')), may hold values from 0 to 1, as said below
- qkv_weight: float32 [2, 768, 2304], P(None, 'dp', 'tensor'), may hold values from -0.21875 to 0.21875
- qkv_first: float32 [2, 768, 2304], P(None, 'dp', 'tensor'), may hold values from -0.0002 to 0.0002
- qkv_second: float32 [2, 768, 2304], P(None, 'dp', 'tensor'), may hold values from 1e-10 to 1e-08
- out_weight: float32 [2, 768, 768], P(None, 'dp', 'tensor'), may hold values from -0.875 to 0.875
- out_first: float32 [2, 768, 768], P(None, 'dp', 'tensor'), may hold values from -0.0002 to 0.0002
- out_second: float32 [2, 768, 768], P(None, 'dp', 'tensor'), may hold values from 1e-10 to 1e-08
- up_weight: float32 [2, 768, 3072], P(None, 'dp', 'tensor'), may hold values from -0.21875 to 0.21875
- up_first: float32 [2, 768, 3072], P(None, 'dp', 'tensor'), may hold values from -0.0002 to 0.0002
- up_second: float32 [2, 768, 3072], P(None, 'dp', 'tensor'), may hold values from 1e-10 to 1e-08
- down_weight: float32 [2, 3072, 768], P(None, 'tensor', 'dp'), may hold values from -0.109375 to 0.109375
- down_first: float32 [2, 3072, 768], P(None, 'tensor', 'dp'), may hold values from -0.0002 to 0.0002
- down_second: float32 [2, 3072, 768], P(None, 'tensor', 'dp'), may hold values from 1e-10 to 1e-08
- gain_weight: float32 [2, 2, 768], P(None, None, 'tensor'), may hold values from 0.5 to 1.5
- gain_first: float32 [2, 2, 768], P(None, None, 'tensor'), may hold values from -0.0002 to 0.0002
- gain_second: float32 [2, 2, 768], P(None, None, 'tensor'), may hold values from 1e-10 to 1e-08
- bias_weight: float32 [2, 6, 768], P(None, None, 'tensor'), may hold values from -3 to 3
- bias_first: float32 [2, 6, 768], P(None, None, 'tensor'), may hold values from -0.0002 to 0.0002
- bias_second: float32 [2, 6, 768], P(None, None, 'tensor'), may hold values from 1e-10 to 1e-08
- hidden_weight: float32 [2, 3072], P(None, 'tensor'), may hold values from -3 to 3
- hidden_first: float32 [2, 3072], P(None, 'tensor'), may hold values from -0.0002 to 0.0002
- hidden_second: float32 [2, 3072], P(None, 'tensor'), may hold values from 3e-12 to 3e-10
Outputs:
- block_output: float32 [32768, 768], P(('dp', 'tensor'))
- input_grad: float32 [32768, 768], P(('dp', 'tensor'))
- grad_norm: float32 [], replicated
- qkv_grad: float32 [2, 768, 2304], P(None, 'dp', 'tensor')
- qkv_update: float32 [2, 768, 2304], P(None, 'dp', 'tensor')
- qkv_first_new: float32 [2, 768, 2304], P(None, 'dp', 'tensor')
- qkv_second_new: float32 [2, 768, 2304], P(None, 'dp', 'tensor')
- out_grad_weight: float32 [2, 768, 768], P(None, 'dp', 'tensor')
- out_update: float32 [2, 768, 768], P(None, 'dp', 'tensor')
- out_first_new: float32 [2, 768, 768], P(None, 'dp', 'tensor')
- out_second_new: float32 [2, 768, 768], P(None, 'dp', 'tensor')
- up_grad: float32 [2, 768, 3072], P(None, 'dp', 'tensor')
- up_update: float32 [2, 768, 3072], P(None, 'dp', 'tensor')
- up_first_new: float32 [2, 768, 3072], P(None, 'dp', 'tensor')
- up_second_new: float32 [2, 768, 3072], P(None, 'dp', 'tensor')
- down_grad: float32 [2, 3072, 768], P(None, 'tensor', 'dp')
- down_update: float32 [2, 3072, 768], P(None, 'tensor', 'dp')
- down_first_new: float32 [2, 3072, 768], P(None, 'tensor', 'dp')
- down_second_new: float32 [2, 3072, 768], P(None, 'tensor', 'dp')
- gain_grad: float32 [2, 2, 768], P(None, None, 'tensor')
- gain_update: float32 [2, 2, 768], P(None, None, 'tensor')
- gain_first_new: float32 [2, 2, 768], P(None, None, 'tensor')
- gain_second_new: float32 [2, 2, 768], P(None, None, 'tensor')
- bias_grad: float32 [2, 6, 768], P(None, None, 'tensor')
- bias_update: float32 [2, 6, 768], P(None, None, 'tensor')
- bias_first_new: float32 [2, 6, 768], P(None, None, 'tensor')
- bias_second_new: float32 [2, 6, 768], P(None, None, 'tensor')
- hidden_grad: float32 [2, 3072], P(None, 'tensor')
- hidden_update: float32 [2, 3072], P(None, 'tensor')
- hidden_first_new: float32 [2, 3072], P(None, 'tensor')
- hidden_second_new: float32 [2, 3072], P(None, 'tensor')
Inputs may be any that keep to these rules, and one draw needn't show every extreme that they name: `slot_kind`: every page has exactly 96 slots of kind 0 and 32 of kind 1, in any order. `slot_valid`: every text slot is valid; every page has 1 to 32 valid visual slots; some page has all 32 valid and some page exactly one.
All inputs are finite; a program needn't handle non-finite values.
Results may differ from a plain program's by a relative error of at most 0.01225.
Values may be sent and summed in bfloat16 or wider, within the bound.
No kernel may reach another device: no remote copies, remote signals or barrier semaphores. Data moves between devices by JAX's collectives and lax.ppermute only.
A program may use at most 320 MiB of HBM per device.

v0:
```python
import jax
import jax.numpy as jnp
from jax import lax
from jax.sharding import PartitionSpec as P

HEADS = 12


beta_one = 0.9
beta_two = 0.99
learn_rate = 0.01
weight_decay = 0.01
epsilon = 1e-08
clip_norm = 1.0
bias_one = 1.0 - beta_one**10
bias_two = 1.0 - beta_two**10


def norm_rows(stream, gains_row, shift_row):
    average = jnp.mean(stream, axis=-1, keepdims=True)
    centered = stream - average
    spread = jnp.mean(centered * centered, axis=-1, keepdims=True)
    return centered * lax.rsqrt(spread + 1e-05) * gains_row + shift_row


def pair_mask(slot_kind, slot_valid, across):
    same_kind = slot_kind[:, :, None] == slot_kind[:, None, :]
    partner = jnp.logical_not(same_kind) if across else same_kind
    return jnp.logical_and(partner, slot_valid[:, None, :] > 0)[:, None]


def ffn_forward(normed_ffn, up_w, down_w, up_b):
    rows_all = lax.all_gather(normed_ffn, "tensor", axis=0, tiled=True)
    upper = jnp.dot(rows_all, up_w, preferred_element_type=jnp.float32) + up_b
    active, gelu_back = jax.vjp(jax.nn.gelu, upper)
    active_b = active.astype(jnp.bfloat16)
    lower = lax.psum_scatter(
        jnp.dot(active_b, down_w, preferred_element_type=jnp.float32),
        "tensor",
        scatter_dimension=0,
        tiled=True,
    )
    return (lower, (rows_all, gelu_back, active_b))


def ffn_backward(lower_b, ffn_kept, up_w, down_w):
    rows_all, gelu_back, active_b = ffn_kept
    lower_all = lax.all_gather(lower_b, "tensor", axis=0, tiled=True)
    grad_down = jnp.dot(active_b.T, lower_all, preferred_element_type=jnp.float32)
    grad_active = jnp.dot(lower_all, down_w.T, preferred_element_type=jnp.float32)
    grad_upper = gelu_back(grad_active)[0]
    upper_b = grad_upper.astype(jnp.bfloat16)
    grad_hidden = jnp.sum(upper_b, axis=0, dtype=jnp.float32)
    grad_up = jnp.dot(rows_all.T, upper_b, preferred_element_type=jnp.float32)
    grad_normed = lax.psum_scatter(
        jnp.dot(upper_b, up_w.T, preferred_element_type=jnp.float32),
        "tensor",
        scatter_dimension=0,
        tiled=True,
    )
    return (grad_normed, grad_up, grad_down, grad_hidden)


def scores_of(queries, keys_in, allowed, scale):
    scores = (
        jnp.einsum("pihd,pjhd->phij", queries, keys_in, preferred_element_type=jnp.float32) * scale
    )
    return jnp.where(allowed, scores, -1e30)


def layer_forward(stream, allowed, qkv_w, out_w, gains_v, biases_v, up_w, down_w, up_b):
    pages = allowed.shape[0]
    slots = allowed.shape[2]
    width = stream.shape[1]
    head_dim = width // HEADS
    scale = head_dim ** (-0.5)
    normed, norm_back = jax.vjp(norm_rows, stream, gains_v[0], biases_v[0])
    normed_b = normed.astype(jnp.bfloat16)
    projected = jnp.dot(normed_b, qkv_w, preferred_element_type=jnp.float32)
    shape_four = (pages, slots, HEADS, head_dim)
    queries = (projected[:, :width] + biases_v[1]).astype(jnp.bfloat16).reshape(shape_four)
    keys_in = projected[:, width : 2 * width].astype(jnp.bfloat16).reshape(shape_four)
    values = (projected[:, 2 * width :] + biases_v[2]).astype(jnp.bfloat16).reshape(shape_four)
    masked = scores_of(queries, keys_in, allowed, scale)
    peak = jnp.max(masked, axis=-1, keepdims=True)
    exponent = jnp.exp(masked - peak)
    total = jnp.sum(exponent, axis=-1, keepdims=True)
    soft_weights = (exponent / total).astype(jnp.bfloat16)
    log_total = peak + jnp.log(total)
    mixed = jnp.einsum("phij,pjhd->pihd", soft_weights, values, preferred_element_type=jnp.float32)
    mixed = mixed.reshape(stream.shape).astype(jnp.bfloat16)
    middle = stream + jnp.dot(mixed, out_w, preferred_element_type=jnp.float32) + biases_v[3]
    normed_ffn, ffn_norm_back = jax.vjp(norm_rows, middle, gains_v[1], biases_v[4])
    lower, ffn_kept = ffn_forward(normed_ffn.astype(jnp.bfloat16), up_w, down_w, up_b)
    result = middle + lower + biases_v[5]
    kept = (
        norm_back,
        normed_b,
        queries,
        keys_in,
        values,
        log_total,
        mixed,
        ffn_norm_back,
        ffn_kept,
    )
    return (result, kept)


def layer_backward(grad_stream, kept, allowed, qkv_w, out_w, up_w, down_w):
    norm_back, normed_b, queries, keys_in, values, log_total, mixed, ffn_norm_back, ffn_kept = kept
    rows = grad_stream.shape[0]
    width = grad_stream.shape[1]
    scale = (width // HEADS) ** (-0.5)
    lower_b = grad_stream.astype(jnp.bfloat16)
    grad_bdown = jnp.sum(lower_b, axis=0, dtype=jnp.float32)
    grad_normed_ffn, grad_up, grad_down, grad_hidden = ffn_backward(lower_b, ffn_kept, up_w, down_w)
    grad_middle_norm, grad_gain_two, grad_shift_two = ffn_norm_back(grad_normed_ffn)
    grad_middle = grad_stream + grad_middle_norm
    branch_b = grad_middle.astype(jnp.bfloat16)
    grad_bout = jnp.sum(branch_b, axis=0, dtype=jnp.float32)
    grad_out = jnp.dot(mixed.T, branch_b, preferred_element_type=jnp.float32)
    grad_mixed = (
        jnp.dot(branch_b, out_w.T, preferred_element_type=jnp.float32)
        .astype(jnp.bfloat16)
        .reshape(queries.shape)
    )
    masked = scores_of(queries, keys_in, allowed, scale)
    soft = jnp.exp(masked - log_total)
    grad_soft = jnp.einsum(
        "pihd,pjhd->phij", grad_mixed, values, preferred_element_type=jnp.float32
    )
    grad_values = jnp.einsum(
        "phij,pihd->pjhd", soft.astype(jnp.bfloat16), grad_mixed, preferred_element_type=jnp.float32
    )
    inner = jnp.sum(soft * grad_soft, axis=-1, keepdims=True)
    grad_scores = (soft * (grad_soft - inner)).astype(jnp.bfloat16)
    grad_queries = (
        (
            jnp.einsum("phij,pjhd->pihd", grad_scores, keys_in, preferred_element_type=jnp.float32)
            * scale
        )
        .astype(jnp.bfloat16)
        .reshape(rows, width)
    )
    grad_keys = (
        (
            jnp.einsum("phij,pihd->pjhd", grad_scores, queries, preferred_element_type=jnp.float32)
            * scale
        )
        .astype(jnp.bfloat16)
        .reshape(rows, width)
    )
    grad_values_b = grad_values.astype(jnp.bfloat16).reshape(rows, width)
    grad_project = jnp.concatenate([grad_queries, grad_keys, grad_values_b], axis=1)
    grad_bquery = jnp.sum(grad_queries, axis=0, dtype=jnp.float32)
    grad_bvalue = jnp.sum(grad_values_b, axis=0, dtype=jnp.float32)
    grad_qkv = jnp.dot(normed_b.T, grad_project, preferred_element_type=jnp.float32)
    grad_normed = jnp.dot(grad_project, qkv_w.T, preferred_element_type=jnp.float32)
    grad_in_norm, grad_gain_one, grad_shift_one = norm_back(grad_normed)
    grad_in = grad_middle + grad_in_norm
    gains_grad = jnp.stack([grad_gain_one, grad_gain_two])
    biases_grad = jnp.stack(
        [grad_shift_one, grad_bquery, grad_bvalue, grad_bout, grad_shift_two, grad_bdown]
    )
    return (grad_in, (grad_qkv, grad_out, grad_up, grad_down, gains_grad, biases_grad, grad_hidden))


def adam_step(master, grad, moment_one, moment_two, factor, decayed):
    clipped = grad * factor
    first_new = beta_one * moment_one + (1.0 - beta_one) * clipped
    second_new = beta_two * moment_two + (1.0 - beta_two) * clipped * clipped
    change = first_new / bias_one / (jnp.sqrt(second_new / bias_two) + epsilon)
    if decayed:
        change = change + weight_decay * master
    return (-learn_rate * change, first_new, second_new)


def shards(
    tokens,
    out_grad,
    slot_kind,
    slot_valid,
    qkv_weight,
    qkv_first,
    qkv_second,
    out_weight,
    out_first,
    out_second,
    up_weight,
    up_first,
    up_second,
    down_weight,
    down_first,
    down_second,
    gain_weight,
    gain_first,
    gain_second,
    bias_weight,
    bias_first,
    bias_second,
    hidden_weight,
    hidden_first,
    hidden_second,
):
    qkv_cols, out_cols, gain_full, bias_full = (
        lax.all_gather(qkv_weight.astype(jnp.bfloat16), "tensor", axis=2, tiled=True),
        lax.all_gather(out_weight.astype(jnp.bfloat16), "tensor", axis=2, tiled=True),
        lax.all_gather(gain_weight.astype(jnp.bfloat16), "tensor", axis=2, tiled=True),
        lax.all_gather(bias_weight.astype(jnp.bfloat16), "tensor", axis=2, tiled=True),
    )
    up_cols = up_weight.astype(jnp.bfloat16)
    down_cols = down_weight.astype(jnp.bfloat16)
    hidden_cols = hidden_weight.astype(jnp.bfloat16)
    qkv_full, out_full, up_full, down_full = (
        lax.all_gather(qkv_cols, "dp", axis=1, tiled=True),
        lax.all_gather(out_cols, "dp", axis=1, tiled=True),
        lax.all_gather(up_cols, "dp", axis=1, tiled=True),
        lax.all_gather(down_cols, "dp", axis=2, tiled=True),
    )
    gains_f = gain_full.astype(jnp.float32)
    biases_f = bias_full.astype(jnp.float32)
    hidden_f = hidden_cols.astype(jnp.float32)
    stream = tokens.astype(jnp.float32)
    saved = []
    masks = []
    for index in range(2):
        allowed = pair_mask(slot_kind, slot_valid, index == 0)
        stream, kept = layer_forward(
            stream,
            allowed,
            qkv_full[index],
            out_full[index],
            gains_f[index],
            biases_f[index],
            up_full[index],
            down_full[index],
            hidden_f[index],
        )
        saved.append(kept)
        masks.append(allowed)
    grad_stream = out_grad.astype(jnp.float32)
    layer_grads = [None, None]
    for index in (1, 0):
        grad_stream, layer_grads[index] = layer_backward(
            grad_stream,
            saved[index],
            masks[index],
            qkv_full[index],
            out_full[index],
            up_full[index],
            down_full[index],
        )
    stacked = [jnp.stack([layer_grads[0][member], layer_grads[1][member]]) for member in range(7)]
    grad_qkv, grad_out, grad_up, grad_down = (
        lax.psum_scatter(stacked[0], "dp", scatter_dimension=1, tiled=True),
        lax.psum_scatter(stacked[1], "dp", scatter_dimension=1, tiled=True),
        lax.psum_scatter(stacked[2], "dp", scatter_dimension=1, tiled=True),
        lax.psum_scatter(stacked[3], "dp", scatter_dimension=2, tiled=True),
    )
    grad_gain, grad_bias, grad_hidden = lax.psum((stacked[4], stacked[5], stacked[6]), "dp")
    grad_qkv, grad_out, grad_gain, grad_bias = (
        lax.psum_scatter(grad_qkv, "tensor", scatter_dimension=2, tiled=True),
        lax.psum_scatter(grad_out, "tensor", scatter_dimension=2, tiled=True),
        lax.psum_scatter(grad_gain, "tensor", scatter_dimension=2, tiled=True),
        lax.psum_scatter(grad_bias, "tensor", scatter_dimension=2, tiled=True),
    )
    owner = (lax.axis_index("dp") == 0).astype(jnp.float32)
    local_squares = (
        jnp.sum(grad_qkv * grad_qkv)
        + jnp.sum(grad_out * grad_out)
        + jnp.sum(grad_up * grad_up)
        + jnp.sum(grad_down * grad_down)
    )
    shared_squares = (
        jnp.sum(grad_gain * grad_gain)
        + jnp.sum(grad_bias * grad_bias)
        + jnp.sum(grad_hidden * grad_hidden)
    )
    total_squares = lax.psum(local_squares + owner * shared_squares, ("dp", "tensor"))
    grad_norm = jnp.sqrt(total_squares)
    factor = clip_norm / jnp.maximum(grad_norm, clip_norm)
    masters = (
        qkv_weight,
        out_weight,
        up_weight,
        down_weight,
        gain_weight,
        bias_weight,
        hidden_weight,
    )
    firsts = (qkv_first, out_first, up_first, down_first, gain_first, bias_first, hidden_first)
    seconds = (
        qkv_second,
        out_second,
        up_second,
        down_second,
        gain_second,
        bias_second,
        hidden_second,
    )
    gradients = (grad_qkv, grad_out, grad_up, grad_down, grad_gain, grad_bias, grad_hidden)
    results = [stream, grad_stream, grad_norm]
    for member in range(7):
        update, first_new, second_new = adam_step(
            masters[member], gradients[member], firsts[member], seconds[member], factor, member < 4
        )
        results = results + [gradients[member], update, first_new, second_new]
    return tuple(results)


def solution(mesh):
    return jax.shard_map(
        shards,
        mesh=mesh,
        in_specs=(
            P(("dp", "tensor"), None),
            P(("dp", "tensor"), None),
            P(("dp", "tensor"), None),
            P(("dp", "tensor"), None),
            P(None, "dp", "tensor"),
            P(None, "dp", "tensor"),
            P(None, "dp", "tensor"),
            P(None, "dp", "tensor"),
            P(None, "dp", "tensor"),
            P(None, "dp", "tensor"),
            P(None, "dp", "tensor"),
            P(None, "dp", "tensor"),
            P(None, "dp", "tensor"),
            P(None, "tensor", "dp"),
            P(None, "tensor", "dp"),
            P(None, "tensor", "dp"),
            P(None, None, "tensor"),
            P(None, None, "tensor"),
            P(None, None, "tensor"),
            P(None, None, "tensor"),
            P(None, None, "tensor"),
            P(None, None, "tensor"),
            P(None, "tensor"),
            P(None, "tensor"),
            P(None, "tensor"),
        ),
        out_specs=(
            P(("dp", "tensor"), None),
            P(("dp", "tensor"), None),
            P(),
            P(None, "dp", "tensor"),
            P(None, "dp", "tensor"),
            P(None, "dp", "tensor"),
            P(None, "dp", "tensor"),
            P(None, "dp", "tensor"),
            P(None, "dp", "tensor"),
            P(None, "dp", "tensor"),
            P(None, "dp", "tensor"),
            P(None, "dp", "tensor"),
            P(None, "dp", "tensor"),
            P(None, "dp", "tensor"),
            P(None, "dp", "tensor"),
            P(None, "tensor", "dp"),
            P(None, "tensor", "dp"),
            P(None, "tensor", "dp"),
            P(None, "tensor", "dp"),
            P(None, None, "tensor"),
            P(None, None, "tensor"),
            P(None, None, "tensor"),
            P(None, None, "tensor"),
            P(None, None, "tensor"),
            P(None, None, "tensor"),
            P(None, None, "tensor"),
            P(None, None, "tensor"),
            P(None, "tensor"),
            P(None, "tensor"),
            P(None, "tensor"),
            P(None, "tensor"),
        ),
        check_vma=False,
    )
```

profile of v0, /device:TPU:0, one launch (start us, length us, event | category | flops | bytes accessed | tf_op | source)
XLA Modules:
  0.0 1820.1 jit_solution(11792696394630484389)
XLA Ops:
  45.9 33.8 %slice_reduce_fusion = (f32[768]{0:T(1024)}, f32[768]{0:T(1024)S(1)}, f32[768]{0:T(1024)S(1)}, f32[768]{0:T(1024)S(1)}, f32[768]{0:T(1024)S(1)}, /*index=5*/f32[...) fusion(f32[2,6,768]{1,0,2:T(2,128)S(1)} %convert_element_type.203), kind=kLoop, calls=%fused_computation.203 | loop fusion | bytes 73728 | tf_op jit(solution)/shard_map/slice | solution.py:95
  91.9 41.3 %all-gather.9.cloned.1.call-done = bf16[2,768,2304]{2,1,0:T(8,128)(2,1)} async-done(((bf16[2,96,2304]{2,1,0:T(8,128)(2,1)}), bf16[2,768,2304]{2,1,0:T(8,128)(2,1)}) %all-gather.9.cloned.1.call-update) | async-done | bytes 7077904 | tf_op jit(solution)/shard_map/all_gather | solution.py:216
  157.6 28.4 %all-gather.11.cloned.1.call-done = bf16[2,768,768]{2,1,0:T(8,128)(2,1)} async-done(((bf16[2,96,768]{2,1,0:T(8,128)(2,1)}), bf16[2,768,768]{2,1,0:T(8,128)(2,1)}) %all-gather.11.cloned.1.call-update) | async-done | bytes 2359312 | tf_op jit(solution)/shard_map/all_gather | solution.py:217
  194.2 45.2 %all-gather.15.cloned.1.call-done = bf16[2,768,768]{2,1,0:T(8,128)(2,1)} async-done(((bf16[2,96,768]{2,1,0:T(8,128)(2,1)}), bf16[2,768,768]{2,1,0:T(8,128)(2,1)}) %all-gather.15.cloned.1.call-update) | async-done | bytes 2359312 | tf_op jit(solution)/shard_map/all_gather | solution.py:218
  239.4 46.9 %all-gather.13.cloned.1.call-done = bf16[4096,768]{0,1:T(8,128)(2,1)} async-done(((bf16[1024,768]{0,1:T(8,128)(2,1)}), bf16[4096,768]{0,1:T(8,128)(2,1)}) %all-gather.13.cloned.1.call-update) | async-done | bytes 6291472 | tf_op jit(solution)/shard_map/all_gather | solution.py:33
  296.7 44.2 %all-gather.17.cloned.1.call-done = bf16[2,768,768]{1,2,0:T(8,128)(2,1)} async-done(((bf16[2,768,96]{1,2,0:T(8,128)(2,1)}), bf16[2,768,768]{1,2,0:T(8,128)(2,1)}) %all-gather.17.cloned.1.call-update) | async-done | bytes 2359312 | tf_op jit(solution)/shard_map/all_gather | solution.py:219
  352.3 97.7 %reduce-scatter.20.cloned.1.call-done = f32[1024,768]{0,1:T(8,128)} async-done(((f32[4096,768]{0,1:T(8,128)}), f32[1024,768]{0,1:T(8,128)}) %reduce-scatter.20.cloned.1.call-update) | async-done | bytes 3145744 | tf_op jit(solution)/shard_map/reduce_scatter | solution.py:37
  482.4 45.7 %all-gather.19.cloned.1.call-done = bf16[4096,768]{0,1:T(8,128)(2,1)} async-done(((bf16[1024,768]{0,1:T(8,128)(2,1)}), bf16[4096,768]{0,1:T(8,128)(2,1)}) %all-gather.19.cloned.1.call-update) | async-done | bytes 6291472 | tf_op jit(solution)/shard_map/all_gather | solution.py:33
  539.1 37.0 %all-gather.21.cloned.1.call-done = bf16[4096,768]{1,0:T(8,128)(2,1)} async-done(((bf16[1024,768]{1,0:T(8,128)(2,1)}), bf16[4096,768]{1,0:T(8,128)(2,1)}) %all-gather.21.cloned.1.call-update) | async-done | bytes 6291472 | tf_op jit(solution)/shard_map/all_gather | solution.py:48
  576.1 17.2 convert_reduce_fusion
  603.9 12.8 fusion.101
  619.7 83.4 %reduce-scatter.24.cloned.1.call-done = f32[1024,768]{0,1:T(8,128)} async-done(((f32[4096,768]{0,1:T(8,128)}), f32[1024,768]{0,1:T(8,128)}) %reduce-scatter.24.cloned.1.call-update) | async-done | bytes 3145744 | tf_op jit(solution)/shard_map/reduce_scatter | solution.py:55
  706.6 98.0 %reduce-scatter.22.cloned.1.call-done = f32[1024,768]{0,1:T(8,128)} async-done(((f32[4096,768]{0,1:T(8,128)}), f32[1024,768]{0,1:T(8,128)}) %reduce-scatter.22.cloned.1.call-update) | async-done | bytes 3145744 | tf_op jit(solution)/shard_map/reduce_scatter | solution.py:37
  861.3 46.5 %all-gather.23.cloned.1.call-done = bf16[4096,768]{0,1:T(8,128)(2,1)} async-done(((bf16[1024,768]{0,1:T(8,128)(2,1)}), bf16[4096,768]{0,1:T(8,128)(2,1)}) %all-gather.23.cloned.1.call-update) | async-done | bytes 6291472 | tf_op jit(solution)/shard_map/all_gather | solution.py:48
  907.8 17.9 convert_reduce_fusion.1
  941.4 94.0 %reduce-scatter.26.cloned.1.call-done = f32[1024,768]{0,1:T(8,128)} async-done(((f32[4096,768]{0,1:T(8,128)}), f32[1024,768]{0,1:T(8,128)}) %reduce-scatter.26.cloned.1.call-update) | async-done | bytes 3145744 | tf_op jit(solution)/shard_map/reduce_scatter | solution.py:55
  1110.1 13.7 convolution_bitcast_fusion.5
  1180.0 193.9 %reduce-scatter.28.cloned.1.call-done = f32[2,96,2304]{2,1,0:T(8,128)} async-done(((f32[2,768,2304]{2,1,0:T(8,128)}), f32[2,96,2304]{2,1,0:T(8,128)}) %reduce-scatter.28.cloned.1.call-update) | async-done | bytes 1769488 | tf_op jit(solution)/shard_map/reduce_scatter | solution.py:256
  1386.9 159.3 %all-reduce.4.cloned.1.call-done = f32[2,768,768]{1,0,2:T(2,128)} async-done(((f32[2,768,768]{1,0,2:T(2,128)}), f32[2,768,768]{1,0,2:T(2,128)}) %all-reduce.4.cloned.1.call-update) | async-done | bytes 4718608
  1548.5 96.1 %reduce-scatter.32.cloned.1.call-done = f32[2,96,768]{2,1,0:T(8,128)} async-done(((f32[2,768,768]{2,1,0:T(8,128)}), f32[2,96,768]{2,1,0:T(8,128)}) %reduce-scatter.32.cloned.1.call-update) | async-done | bytes 589840 | tf_op jit(solution)/shard_map/reduce_scatter | solution.py:258
  1669.3 22.6 %reduce-scatter.40.cloned.1.call-done = f32[192,12]{1,0:T(8,128)} async-done(((f32[768,12]{1,0:T(8,128)}), f32[192,12]{1,0:T(8,128)}) %reduce-scatter.40.cloned.1.call-update) | async-done | bytes 9232
  1693.1 37.1 %all-reduce.1 = (f32[2,2,192]{2,1,0:T(2,128)S(1)}, f32[2,6,192]{2,1,0:T(8,128)S(1)}, f32[2,768]{1,0:T(2,128)S(1)}) all-reduce(f32[2,2,192]{2,1,0:T(2,128)S(1)} %copy.396, f32[2,6,192]{2,1,0:T(8,128)S(1)} %copy.398, f32[2,768]{1,0:T(2,128)S(1)} %pad_maximum_fusion.6), channel_id=1, replica_groups=mesh['dp'=8,'tensor'=4] {'dp'}, use_global_device_ids=true, to_apply=%region_40.41 | all-reduce | flops 4608 | bytes 36864 | tf_op jit(solution)/shard_map/psum | solution.py:261
  1735.9 17.4 reduce-scatter.34.cloned.1.call-done
  1759.0 39.3 %psum.31 = f32[]{:T(128)} all-reduce(f32[]{:T(128)S(6)} %add.445), channel_id=1, replica_groups=mesh['dp'=8,'tensor'=4] {'dp','tensor'}, use_global_device_ids=true, to_apply=%region_62.63 | all-reduce | flops 1 | bytes 8 | tf_op jit(solution)/shard_map/psum | solution.py:280
  (480 shorter events, 426.9 us)
Async XLA Ops:
  7.2 126.0 %all-gather.9.cloned.1.call-start = ((), (), s32[]{:S(2)}) async-start(), calls=%async_computation.11 | async-start | bytes 7962624 | tf_op jit(solution)/shard_map/all_gather | solution.py:216
  23.4 162.7 %all-gather.11.cloned.1.call-start = ((), (), s32[]{:S(2)}) async-start(), calls=%async_computation.12 | async-start | bytes 2654208 | tf_op jit(solution)/shard_map/all_gather | solution.py:217
  31.2 208.1 %all-gather.15.cloned.1.call-start = ((), (), s32[]{:S(2)}) async-start(), calls=%async_computation.14 | async-start | bytes 2654208 | tf_op jit(solution)/shard_map/all_gather | solution.py:218
  32.0 254.3 %all-gather.13.cloned.1.call-start = ((), (), s32[]{:S(2)}) async-start(), calls=%async_computation.13 | async-start | bytes 7864320 | tf_op jit(solution)/shard_map/all_gather | solution.py:33
  79.7 373.0 %copy-start.92 = (f32[768]{0:T(1024)}, f32[768]{0:T(1024)S(1)}, u32[]{:S(2)}) copy-start(f32[768]{0:T(1024)S(1)} %get-tuple-element.201) | copy-start | bytes 9220
  189.9 260.0 %copy-start.2 = (f32[1024,768]{0,1:T(8,128)}, f32[1024,768]{0,1:T(8,128)S(1)}, u32[]{:S(2)}) copy-start(f32[1024,768]{0,1:T(8,128)S(1)} %get-tuple-element.269) | copy-start | bytes 9437188
  192.2 148.7 %all-gather.17.cloned.1.call-start = ((), (), s32[]{:S(2)}) async-start(), calls=%async_computation.15 | async-start | bytes 2654208 | tf_op jit(solution)/shard_map/all_gather | solution.py:219
  194.0 255.9 %reduce-scatter.20.cloned.1.call-start = ((), (), s32[]{:S(2)}) async-start(), calls=%async_computation.16 | async-start | bytes 15728640 | tf_op jit(solution)/shard_map/reduce_scatter | solution.py:37
  194.2 409.7 %copy-start.96 = (f32[768]{0:T(1024)}, f32[768]{0:T(1024)S(1)}, u32[]{:S(2)}) copy-start(f32[768]{0:T(1024)S(1)} %get-tuple-element.212) | copy-start | bytes 9220
  352.2 175.9 %all-gather.19.cloned.1.call-start = ((), (), s32[]{:S(2)}) async-start(), calls=%async_computation.17 | async-start | bytes 7864320 | tf_op jit(solution)/shard_map/all_gather | solution.py:33
  481.6 94.5 %all-gather.21.cloned.1.call-start = ((), (), s32[]{:S(2)}) async-start(), calls=%async_computation.19 | async-start | bytes 7864320 | tf_op jit(solution)/shard_map/all_gather | solution.py:48
  482.4 220.7 %reduce-scatter.24.cloned.1.call-start = ((), (), s32[]{:S(2)}) async-start(), calls=%async_computation.20 | async-start | bytes 15728640 | tf_op jit(solution)/shard_map/reduce_scatter | solution.py:55
  603.8 200.8 %reduce-scatter.22.cloned.1.call-start = ((), (), s32[]{:S(2)}) async-start(), calls=%async_computation.18 | async-start | bytes 15728640 | tf_op jit(solution)/shard_map/reduce_scatter | solution.py:37
  616.7 291.1 %all-gather.23.cloned.1.call-start = ((), (), s32[]{:S(2)}) async-start(), calls=%async_computation.21 | async-start | bytes 7864320 | tf_op jit(solution)/shard_map/all_gather | solution.py:48
  619.7 184.9 %copy-start.85 = (f32[768]{0:T(1024)S(1)}, f32[768]{0:T(1024)}, u32[]{:S(2)}) copy-start(f32[768]{0:T(1024)} %get-tuple-element.196) | copy-start | bytes 9220
  861.3 174.1 %reduce-scatter.26.cloned.1.call-start = ((), (), s32[]{:S(2)}) async-start(), calls=%async_computation.22 | async-start | bytes 15728640 | tf_op jit(solution)/shard_map/reduce_scatter | solution.py:55
  936.2 240.9 %reduce-scatter.30.cloned.1.call-start = ((), (), s32[]{:S(2)}) async-start(), calls=%async_computation.24 | async-start | bytes 5308416 | tf_op jit(solution)/shard_map/reduce_scatter | solution.py:257
  1046.1 327.9 %reduce-scatter.28.cloned.1.call-start = ((), (), s32[]{:S(2)}) async-start(), calls=%async_computation.23 | async-start | bytes 15925248 | tf_op jit(solution)/shard_map/reduce_scatter | solution.py:256
  1098.6 447.6 %all-reduce.4.cloned.1.call-start = ((), (), s32[]{:S(2)}) async-start(), calls=%async_computation.30 | async-start | bytes 9437184
  1134.6 510.0 %reduce-scatter.32.cloned.1.call-start = ((), (), s32[]{:S(2)}) async-start(), calls=%async_computation.25 | async-start | bytes 5308416 | tf_op jit(solution)/shard_map/reduce_scatter | solution.py:258
  1155.3 512.8 %reduce-scatter.38.cloned.1.call-start = ((), (), s32[]{:S(2)}) async-start(), calls=%async_computation.28 | async-start | bytes 491520
  1175.0 516.9 %reduce-scatter.40.cloned.1.call-start = ((), (), s32[]{:S(2)}) async-start(), calls=%async_computation.29 | async-start | bytes 491520
  1176.8 557.1 %reduce-scatter.36.cloned.1.call-start = ((), (), s32[]{:S(2)}) async-start(), calls=%async_computation.27 | async-start | bytes 983040
  1180.0 573.3 %reduce-scatter.34.cloned.1.call-start = ((), (), s32[]{:S(2)}) async-start(), calls=%async_computation.26 | async-start | bytes 2949120
  (113 other events, 2328.1 us)
Sparse Core Ops, SparseCore 0:
  23.5 109.6 all-gather.8
  135.9 50.1 all-gather.10
  188.9 50.4 all-gather.14
  241.4 44.9 all-gather.12
  288.9 51.9 all-gather.16
  352.3 97.5 reduce-scatter.19
  481.7 46.3 all-gather.18
  529.7 46.3 all-gather.20
  603.9 99.0 reduce-scatter.23
  705.5 99.0 reduce-scatter.21
  861.4 46.3 all-gather.22
  936.3 99.0 reduce-scatter.25
  1046.2 95.2 reduce-scatter.29
  1145.0 228.9 reduce-scatter.27
  1377.4 168.7 all-reduce.3
  1550.3 94.2 reduce-scatter.31
  1647.5 20.5 reduce-scatter.37
  1671.0 20.8 reduce-scatter.39
  1694.4 23.2 reduce-scatter.35
  1720.3 33.0 reduce-scatter.33
where the time goes:
time: 1830 us; the launch traced here: 1820 us
  waiting for transfers between devices  1210 us (66%)
  matrix products  230 us (13%)
  local copies, waits for them, and re-layouts  154 us (8%)
  blocking collectives  108 us (6%)
  other arithmetic  93.1 us (5%)
  between operations  23.7 us (1%)
    unnamed x25, waiting for transfers between devices  211 us
    reduce_scatter x2, waiting for transfers between devices, ffn_forward(): lax.psum_scatter(jnp.dot(active_b, down_w, preferred_element_type=jnp.flo...  196 us
    reduce_scatter x1, waiting for transfers between devices, shards(): lax.psum_scatter(stacked[0], 'dp', scatter_dimension=1, tiled=True)  194 us
    reduce_scatter x2, waiting for transfers between devices, ffn_backward(): lax.psum_scatter(jnp.dot(upper_b, up_w.T, preferred_element_type=jnp.floa...  177 us
    reduce_scatter x1, waiting for transfers between devices, shards(): lax.psum_scatter(stacked[2], 'dp', scatter_dimension=1, tiled=True)  96.1 us
    all_gather x2, waiting for transfers between devices, ffn_forward(): rows_all = lax.all_gather(normed_ffn, 'tensor', axis=0, tiled=True)  92.7 us
    all_gather x2, waiting for transfers between devices, ffn_backward(): lower_all = lax.all_gather(lower_b, 'tensor', axis=0, tiled=True)  83.5 us
    unnamed x272, local copies, waits for them, and re-layouts  64.4 us
  transfers between devices with their start and end apart: 20, of which 18 were waited for; matrix products, arithmetic and copies ran while one was open for 16% of the time, Pallas kernels for 0%

commit v1 on v0

v1 whole, which is shorter than its diff:
```python
import functools

import jax
import jax.numpy as jnp
from jax import lax
from jax.experimental import pallas as pl
from jax.experimental.pallas import tpu as pltpu
from jax.sharding import PartitionSpec as P

HEADS = 12
PAIRS = HEADS // 2

beta_one = 0.9
beta_two = 0.99
learn_rate = 0.01
weight_decay = 0.01
epsilon = 1e-08
clip_norm = 1.0
bias_one = 1.0 - beta_one**10
bias_two = 1.0 - beta_two**10

BF = jnp.bfloat16
F32 = jnp.float32
VMEM_LIMIT = 56 * 1024 * 1024


def dot_nn(a, b):
    return lax.dot_general(a, b, (((1,), (0,)), ((), ())), preferred_element_type=F32)


def dot_nt(a, b):
    return lax.dot_general(a, b, (((1,), (1,)), ((), ())), preferred_element_type=F32)


def dot_tn(a, b):
    return lax.dot_general(a, b, (((0,), (0,)), ((), ())), preferred_element_type=F32)


def normalize(stream):
    average = jnp.mean(stream, axis=-1, keepdims=True)
    centered = stream - average
    spread = jnp.mean(centered * centered, axis=-1, keepdims=True)
    root = lax.rsqrt(spread + 1e-05)
    return centered * root, root


def norm_backward(grad, unit, root, gain):
    scaled = grad * gain
    first = jnp.mean(scaled, axis=-1, keepdims=True)
    second = jnp.mean(scaled * unit, axis=-1, keepdims=True)
    return root * (scaled - first - unit * second)


def column_sum(value):
    return jnp.sum(value, axis=0, keepdims=True)


def split_heads(pair):
    lane = lax.broadcasted_iota(jnp.int32, pair.shape, 1)
    zero = jnp.zeros_like(pair)
    half = pair.shape[1] // 2
    return jnp.concatenate([jnp.where(lane < half, pair, zero), jnp.where(lane >= half, pair, zero)], axis=0)


def weight_copies(plan, refs, me_ref, full, sems):
    copies = []

    def add(source, target):
        copies.append(pltpu.make_async_copy(source, target, sems.at[len(copies)]))

    if plan[0] == "whole":
        add(refs[0], full)
    elif plan[0] == "rows":
        parts, width, _ = full.shape
        high = width * parts // refs[0].shape[0]
        for index in range(refs[0].shape[0]):
            stripe, part = divmod(index, parts)
            add(refs[0].at[index, pl.ds(plan[1], high), :], full.at[part, pl.ds(stripe * high, high), :])
    else:
        for ref, (row, positions) in zip(refs, plan[1]):
            _, depth, high, width = ref.shape
            for place, (x, y, core) in enumerate(positions):
                part = jnp.bitwise_xor(me_ref[1], 2 * y + core)
                for z in range(depth):
                    stripe = jnp.bitwise_xor(me_ref[0], 2 * z + x)
                    start = pl.multiple_of(stripe * (width // (2 * depth)) + row, 16)
                    add(ref.at[place, z], full.at[part, pl.ds(start, high), :])
    return copies


def load_weights(groups):
    copies = [copy for group in groups for copy in weight_copies(*group)]
    for copy in copies:
        copy.start()
    for copy in copies:
        copy.wait()


def copy_count(plan, refs):
    if plan[0] == "whole":
        return 1
    if plan[0] == "rows":
        return refs[0].shape[0]
    return sum(ref.shape[0] * ref.shape[1] for ref in refs)


def split_attention(raw, qkv_s, out_s):
    parts = raw.shape[0]
    cut = qkv_s.shape[1] // parts
    step = 96

    def relay(index, _):
        rows = pl.ds(pl.multiple_of(index * step, step), step)
        pieces = [raw[part, rows, :] for part in range(parts)]
        qkv_s[rows, :] = jnp.concatenate([piece[:, :cut] for piece in pieces], axis=1)
        out_s[rows, :] = jnp.concatenate([piece[:, cut:] for piece in pieces], axis=1)
        return 0

    lax.fori_loop(0, raw.shape[1] // step, relay, 0)


def attention_forward_kernel(plan, me_ref, stream_ref, mask_ref, vec_ref, *refs):
    weight_refs = refs[:-10]
    middle_ref, nffn_ref, normed_ref, proj_ref, probs_ref, mixed_ref, qkv_s, out_s, raw, sems = refs[-10:]

    @pl.when(pl.program_id(0) == 0)
    def _():
        load_weights([(plan, weight_refs, me_ref, raw, sems)])
        split_attention(raw, qkv_s, out_s)

    width = stream_ref.shape[1]
    slots = mask_ref.shape[1]
    scale = (width // HEADS) ** (-0.5)
    stream = stream_ref[...].astype(F32)
    unit, _ = normalize(stream)
    normed = (unit * vec_ref[0:1, :] + vec_ref[2:3, :]).astype(BF)
    normed_ref[...] = normed
    projected = dot_nn(normed, qkv_s[...])
    proj_ref[:, :width] = (projected[:, :width] + vec_ref[3:4, :]).astype(BF)
    proj_ref[:, width : 2 * width] = projected[:, width : 2 * width].astype(BF)
    proj_ref[:, 2 * width :] = (projected[:, 2 * width :] + vec_ref[4:5, :]).astype(BF)
    lanes = 2 * (width // HEADS)
    for page in range(mask_ref.shape[0]):
        rows = slice(page * slots, (page + 1) * slots)
        bias = mask_ref[page]
        for pair in range(PAIRS):
            at = pair * lanes
            queries = proj_ref[rows, at : at + lanes] * jnp.asarray(scale, BF)
            keys_in = split_heads(proj_ref[rows, width + at : width + at + lanes])
            values = split_heads(proj_ref[rows, 2 * width + at : 2 * width + at + lanes])
            scores = dot_nt(queries, keys_in)
            soft = []
            for head in range(2):
                masked = scores[:, head * slots : (head + 1) * slots] + bias
                peak = jnp.max(masked, axis=-1, keepdims=True)
                exponent = jnp.exp(masked - peak)
                total = jnp.sum(exponent, axis=-1, keepdims=True)
                soft.append((exponent * (1.0 / total)).astype(BF))
            probs = jnp.concatenate(soft, axis=1)
            probs_ref[page, pair] = probs
            mixed_ref[rows, at : at + lanes] = dot_nn(probs, values).astype(BF)
    middle = stream + dot_nn(mixed_ref[...], out_s[...]) + vec_ref[5:6, :]
    middle_ref[...] = middle
    unit, _ = normalize(middle)
    nffn_ref[...] = (unit * vec_ref[1:2, :] + vec_ref[6:7, :]).astype(BF)


def attention_forward(me, stream, mask, vec, weight, block_pages, parts):
    plan, arrays = weight
    rows, width = stream.shape
    pages, slots, _ = mask.shape
    block = block_pages * slots
    row_spec = lambda cols: pl.BlockSpec((block, cols), lambda i: (i, 0))
    return pl.pallas_call(
        functools.partial(attention_forward_kernel, plan),
        grid=(pages // block_pages,),
        in_specs=[
            pl.BlockSpec(memory_space=pltpu.SMEM),
            row_spec(width),
            pl.BlockSpec((block_pages, slots, slots), lambda i: (i, 0, 0)),
            pl.BlockSpec(vec.shape, lambda i: (0, 0)),
        ]
        + [pl.BlockSpec(memory_space=pl.ANY)] * len(arrays),
        out_specs=[
            row_spec(width),
            row_spec(width),
            row_spec(width),
            row_spec(3 * width),
            pl.BlockSpec((block_pages, PAIRS, slots, 2 * slots), lambda i: (i, 0, 0, 0)),
            row_spec(width),
            pl.BlockSpec((width, 3 * width), lambda i: (0, 0)),
            pl.BlockSpec((width, width), lambda i: (0, 0)),
        ],
        out_shape=[
            jax.ShapeDtypeStruct((rows, width), F32),
            jax.ShapeDtypeStruct((rows, width), BF),
            jax.ShapeDtypeStruct((rows, width), BF),
            jax.ShapeDtypeStruct((rows, 3 * width), BF),
            jax.ShapeDtypeStruct((pages, PAIRS, slots, 2 * slots), BF),
            jax.ShapeDtypeStruct((rows, width), BF),
            jax.ShapeDtypeStruct((width, 3 * width), BF),
            jax.ShapeDtypeStruct((width, width), BF),
        ],
        scratch_shapes=[
            pltpu.VMEM((parts, width, width), BF),
            pltpu.SemaphoreType.DMA((copy_count(plan, arrays),)),
        ],
        compiler_params=pltpu.CompilerParams(vmem_limit_bytes=VMEM_LIMIT),
        cost_estimate=pl.CostEstimate(flops=20 * 10**9, bytes_accessed=30 * 10**6, transcendentals=0),
        name="attention_forward",
    )(me, stream, mask, vec, *arrays)


def ffn_forward_kernel(plans, me_ref, nffn_ref, middle_ref, vec_ref, hidden_ref, *refs):
    result_ref, active_ref, slope_ref, up_s, down_s, up_sems, down_sems = refs[-7:]
    up_refs = refs[: (len(refs) - 7) // 2]
    down_refs = refs[len(up_refs) : -7]

    @pl.when(pl.program_id(0) == 0)
    def _():
        load_weights([(plans[0], up_refs, me_ref, up_s, up_sems), (plans[1], down_refs, me_ref, down_s, down_sems)])

    nffn = nffn_ref[...]
    parts, _, chunk = up_s.shape
    total = middle_ref[...] + vec_ref[7:8, :]
    curve = 0.7978845608028654
    for part in range(parts):
        cols = slice(part * chunk, (part + 1) * chunk)
        upper = dot_nn(nffn, up_s[part]) + hidden_ref[:, cols]
        square = upper * upper
        angle = jnp.tanh(upper * (curve + (curve * 0.044715) * square))
        half = 0.5 * upper
        lift = 1.0 + angle
        active = (half * lift).astype(BF)
        slope = 0.5 * lift + half * (1.0 - angle * angle) * (curve + (3.0 * curve * 0.044715) * square)
        active_ref[:, cols] = active
        slope_ref[:, cols] = slope.astype(BF)
        total = total + dot_nt(active, down_s[part])
    result_ref[...] = total


def ffn_forward(me, nffn, middle, vec, hidden, up_w, down_w, block, parts):
    rows, width = nffn.shape
    ffn = hidden.shape[1]
    arrays = up_w[1] + down_w[1]
    row_spec = lambda cols: pl.BlockSpec((block, cols), lambda i: (i, 0))
    return pl.pallas_call(
        functools.partial(ffn_forward_kernel, (up_w[0], down_w[0])),
        grid=(rows // block,),
        in_specs=[
            pl.BlockSpec(memory_space=pltpu.SMEM),
            row_spec(width),
            row_spec(width),
            pl.BlockSpec(vec.shape, lambda i: (0, 0)),
            pl.BlockSpec(hidden.shape, lambda i: (0, 0)),
        ]
        + [pl.BlockSpec(memory_space=pl.ANY)] * len(arrays),
        out_specs=[row_spec(width), row_spec(ffn), row_spec(ffn)],
        out_shape=[
            jax.ShapeDtypeStruct((rows, width), F32),
            jax.ShapeDtypeStruct((rows, ffn), BF),
            jax.ShapeDtypeStruct((rows, ffn), BF),
        ],
        scratch_shapes=[
            pltpu.VMEM((parts, width, ffn // parts), BF),
            pltpu.VMEM((parts, width, ffn // parts), BF),
            pltpu.SemaphoreType.DMA((copy_count(*up_w),)),
            pltpu.SemaphoreType.DMA((copy_count(*down_w),)),
        ],
        compiler_params=pltpu.CompilerParams(vmem_limit_bytes=VMEM_LIMIT),
        cost_estimate=pl.CostEstimate(flops=15 * 10**9, bytes_accessed=30 * 10**6, transcendentals=0),
        name="ffn_forward",
    )(me, nffn, middle, vec, hidden, *arrays)


def ffn_backward_kernel(plans, me_ref, grad_ref, slope_ref, middle_ref, vec_ref, *refs):
    gupper_ref, gmiddle_ref, small_ref, ghidden_ref, up_s, down_s, up_sems, down_sems = refs[-8:]
    up_refs = refs[: (len(refs) - 8) // 2]
    down_refs = refs[len(up_refs) : -8]

    @pl.when(pl.program_id(0) == 0)
    def _():
        small_ref[...] = jnp.zeros_like(small_ref)
        ghidden_ref[...] = jnp.zeros_like(ghidden_ref)
        load_weights([(plans[0], up_refs, me_ref, up_s, up_sems), (plans[1], down_refs, me_ref, down_s, down_sems)])

    grad = grad_ref[...].astype(F32)
    lower = grad.astype(BF)
    parts, _, chunk = up_s.shape
    gnormed = jnp.zeros(grad.shape, F32)
    for part in range(parts):
        cols = slice(part * chunk, (part + 1) * chunk)
        gupper = (dot_nn(lower, down_s[part]) * slope_ref[:, cols].astype(F32)).astype(BF)
        gupper_ref[:, cols] = gupper
        ghidden_ref[:, cols] += column_sum(gupper.astype(F32))
        gnormed = gnormed + dot_nt(gupper, up_s[part])
    unit, root = normalize(middle_ref[...])
    gmiddle = grad + norm_backward(gnormed, unit, root, vec_ref[1:2, :])
    gmiddle_ref[...] = gmiddle
    small_ref[0:1, :] += column_sum(gnormed * unit)
    small_ref[1:2, :] += column_sum(gnormed)
    small_ref[2:3, :] += column_sum(lower.astype(F32))
    small_ref[3:4, :] += column_sum(gmiddle.astype(BF).astype(F32))


def ffn_backward(me, grad, slope, middle, vec, up_w, down_w, block, parts):
    rows, width = grad.shape
    ffn = slope.shape[1]
    arrays = up_w[1] + down_w[1]
    row_spec = lambda cols: pl.BlockSpec((block, cols), lambda i: (i, 0))
    return pl.pallas_call(
        functools.partial(ffn_backward_kernel, (up_w[0], down_w[0])),
        grid=(rows // block,),
        in_specs=[
            pl.BlockSpec(memory_space=pltpu.SMEM),
            row_spec(width),
            row_spec(ffn),
            row_spec(width),
            pl.BlockSpec(vec.shape, lambda i: (0, 0)),
        ]
        + [pl.BlockSpec(memory_space=pl.ANY)] * len(arrays),
        out_specs=[
            row_spec(ffn),
            row_spec(width),
            pl.BlockSpec((8, width), lambda i: (0, 0)),
            pl.BlockSpec((1, ffn), lambda i: (0, 0)),
        ],
        out_shape=[
            jax.ShapeDtypeStruct((rows, ffn), BF),
            jax.ShapeDtypeStruct((rows, width), F32),
            jax.ShapeDtypeStruct((8, width), F32),
            jax.ShapeDtypeStruct((1, ffn), F32),
        ],
        scratch_shapes=[
            pltpu.VMEM((parts, width, ffn // parts), BF),
            pltpu.VMEM((parts, width, ffn // parts), BF),
            pltpu.SemaphoreType.DMA((copy_count(*up_w),)),
            pltpu.SemaphoreType.DMA((copy_count(*down_w),)),
        ],
        compiler_params=pltpu.CompilerParams(vmem_limit_bytes=VMEM_LIMIT),
        cost_estimate=pl.CostEstimate(flops=15 * 10**9, bytes_accessed=30 * 10**6, transcendentals=0),
        name="ffn_backward",
    )(me, grad, slope, middle, vec, *arrays)


def ffn_weight_kernel(nffn_ref, grad_ref, gupper_ref, active_ref, out_ref, nffn_t, grad_t):
    @pl.when(pl.program_id(0) == 0)
    def _():
        nffn_t[...] = nffn_ref[...].T
        grad_t[...] = grad_ref[...].astype(BF).T

    shape = (out_ref.shape[0],) + out_ref.shape[3:]
    out_ref[:, 0, 0] = dot_nn(nffn_t[...], gupper_ref[...]).astype(BF).reshape(shape)
    out_ref[:, 0, 1] = dot_nn(grad_t[...], active_ref[...]).astype(BF).reshape(shape)


def ffn_weight(nffn, grad, gupper, active, stripes, parts):
    rows, width = nffn.shape
    piece = gupper.shape[1] // parts
    high = width // stripes
    whole = pl.BlockSpec((rows, width), lambda i: (0, 0))
    return pl.pallas_call(
        ffn_weight_kernel,
        grid=(parts,),
        in_specs=[
            whole,
            whole,
            pl.BlockSpec((rows, piece), lambda i: (0, i)),
            pl.BlockSpec((rows, piece), lambda i: (0, i)),
        ],
        out_specs=pl.BlockSpec((stripes, 1, 2, high, piece), lambda i: (0, i, 0, 0, 0)),
        out_shape=jax.ShapeDtypeStruct((stripes, parts, 3, high, piece), BF),
        scratch_shapes=[pltpu.VMEM((width, rows), BF), pltpu.VMEM((width, rows), BF)],
        compiler_params=pltpu.CompilerParams(vmem_limit_bytes=VMEM_LIMIT),
        cost_estimate=pl.CostEstimate(flops=15 * 10**9, bytes_accessed=30 * 10**6, transcendentals=0),
        name="ffn_weight",
    )(nffn, grad, gupper, active)


def attention_backward_kernel(gmiddle_ref, stream_ref, proj_ref, probs_ref, vec_ref, qkv_s, out_s, *refs):
    gstream_ref, gproj_ref, small_ref, gmixed_s = refs[-4:]

    @pl.when(pl.program_id(0) == 0)
    def _():
        small_ref[...] = jnp.zeros_like(small_ref)

    width = stream_ref.shape[1]
    block_pages, _, slots, _ = probs_ref.shape
    scale = (width // HEADS) ** (-0.5)
    gmiddle = gmiddle_ref[...]
    gmixed_s[...] = dot_nt(gmiddle.astype(BF), out_s[...]).astype(BF)
    lanes = 2 * (width // HEADS)
    for page in range(block_pages):
        rows = slice(page * slots, (page + 1) * slots)
        for pair in range(PAIRS):
            at = pair * lanes
            gmixed = gmixed_s[rows, at : at + lanes]
            queries = split_heads(proj_ref[rows, at : at + lanes])
            keys_in = split_heads(proj_ref[rows, width + at : width + at + lanes])
            values = split_heads(proj_ref[rows, 2 * width + at : 2 * width + at + lanes])
            probs = probs_ref[page, pair]
            gsoft = dot_nt(gmixed, values)
            gscore = []
            for head in range(2):
                cols = slice(head * slots, (head + 1) * slots)
                soft = probs[:, cols].astype(F32)
                grad = gsoft[:, cols]
                inner = jnp.sum(soft * grad, axis=-1, keepdims=True)
                gscore.append((soft * (grad - inner)).astype(BF))
            stacked = jnp.concatenate([probs[:, :slots], probs[:, slots:]], axis=0)
            gvalues = dot_tn(stacked, split_heads(gmixed))
            gqueries = dot_nn(jnp.concatenate(gscore, axis=1), keys_in) * scale
            gkeys = dot_tn(jnp.concatenate(gscore, axis=0), queries) * scale
            gproj_ref[rows, at : at + lanes] = gqueries.astype(BF)
            gproj_ref[rows, width + at : width + at + lanes] = gkeys.astype(BF)
            gproj_ref[rows, 2 * width + at : 2 * width + at + lanes] = gvalues.astype(BF)
    gnormed = dot_nt(gproj_ref[...], qkv_s[...])
    unit, root = normalize(stream_ref[...].astype(F32))
    gstream_ref[...] = gmiddle + norm_backward(gnormed, unit, root, vec_ref[0:1, :])
    small_ref[0:1, :] += column_sum(gnormed * unit)
    small_ref[1:2, :] += column_sum(gnormed)
    small_ref[2:3, :] += column_sum(gproj_ref[:, :width].astype(F32))
    small_ref[3:4, :] += column_sum(gproj_ref[:, 2 * width :].astype(F32))


def attention_backward(gmiddle, stream, proj, probs, vec, weight, block_pages, begin, end, before):
    rows, width = stream.shape
    _, _, slots, _ = probs.shape
    block = block_pages * slots
    first = begin // block_pages
    row_spec = lambda cols: pl.BlockSpec((block, cols), lambda i: (i + first, 0))
    whole = lambda array: pl.BlockSpec(array.shape, lambda i: (0, 0))
    before = [] if before is None else list(before)
    operands = [gmiddle, stream, proj, probs, vec, weight[0], weight[1]]
    return pl.pallas_call(
        attention_backward_kernel,
        grid=((end - begin) // block_pages,),
        in_specs=[
            row_spec(width),
            row_spec(width),
            row_spec(3 * width),
            pl.BlockSpec((block_pages, PAIRS, slots, 2 * slots), lambda i: (i + first, 0, 0, 0)),
            whole(vec),
            whole(weight[0]),
            whole(weight[1]),
        ]
        + [pl.BlockSpec(memory_space=pl.ANY)] * len(before),
        out_specs=[row_spec(width), row_spec(3 * width), pl.BlockSpec((8, width), lambda i: (0, 0))],
        out_shape=[
            jax.ShapeDtypeStruct((rows, width), F32),
            jax.ShapeDtypeStruct((rows, 3 * width), BF),
            jax.ShapeDtypeStruct((8, width), F32),
        ],
        scratch_shapes=[pltpu.VMEM((block, width), BF)],
        input_output_aliases={len(operands) + index: index for index in range(len(before))},
        compiler_params=pltpu.CompilerParams(vmem_limit_bytes=VMEM_LIMIT),
        cost_estimate=pl.CostEstimate(flops=15 * 10**9, bytes_accessed=20 * 10**6, transcendentals=0),
        name="attention_backward",
    )(*operands, *before)


def attention_weight_kernel(normed_ref, mixed_ref, gproj_ref, gmiddle_ref, _, grad_ref):
    gqkv = dot_tn(normed_ref[...], gproj_ref[...])
    gout = dot_tn(mixed_ref[...], gmiddle_ref[...].astype(BF))
    parts = grad_ref.shape[1]
    cut = gqkv.shape[1] // parts
    rest = gout.shape[1] // parts
    shape = (grad_ref.shape[0],) + grad_ref.shape[3:]
    for part in range(parts):
        qkv_part = gqkv[:, part * cut : (part + 1) * cut].astype(BF)
        out_part = gout[:, part * rest : (part + 1) * rest].astype(BF)
        grad_ref[:, part, 0] = jnp.concatenate([qkv_part, out_part], axis=1).reshape(shape)


def attention_weight(normed, mixed, gproj, gmiddle, before):
    rows, width = normed.shape
    block = width // 2
    stripes, parts, _, high, _ = before.shape
    return pl.pallas_call(
        attention_weight_kernel,
        grid=(2,),
        in_specs=[
            pl.BlockSpec((rows, block), lambda i: (0, i)),
            pl.BlockSpec((rows, block), lambda i: (0, i)),
            pl.BlockSpec((rows, 3 * width), lambda i: (0, 0)),
            pl.BlockSpec((rows, width), lambda i: (0, 0)),
            pl.BlockSpec(memory_space=pl.ANY),
        ],
        out_specs=pl.BlockSpec((stripes // 2, parts, 1, high, width), lambda i: (i, 0, 2, 0, 0)),
        out_shape=jax.ShapeDtypeStruct(before.shape, BF),
        input_output_aliases={4: 0},
        compiler_params=pltpu.CompilerParams(vmem_limit_bytes=VMEM_LIMIT),
        cost_estimate=pl.CostEstimate(flops=10 * 10**9, bytes_accessed=20 * 10**6, transcendentals=0),
        name="attention_weight",
    )(normed, mixed, gproj, gmiddle, before)


def relative_rows(order, source, target, me, high, offset):
    stripe = source.shape[0] // len(order)
    for place, relative in enumerate(order):
        start = pl.multiple_of(jnp.bitwise_xor(me, relative) * stripe + offset, 16)
        target[place * high : (place + 1) * high, :] = source[pl.ds(start, high), :]


def plane_order(depth):
    return [2 * z + x for x in range(2) for z in range(depth)]


def ffn_weight_split_kernel(
    me_ref, nffn_ref, grad_ref, gupper_ref, active_ref, up_one, up_zero, down_one, down_zero, turned, nffn_t, grad_t
):
    step = pl.program_id(0)
    depth, high = up_one.shape[2:4]

    @pl.when(step == 0)
    def _():
        turned[...] = nffn_ref[...].T
        relative_rows(plane_order(depth), turned, nffn_t, me_ref[0], high, 0)
        turned[...] = grad_ref[...].astype(BF).T
        relative_rows(plane_order(depth), turned, grad_t, me_ref[0], high, 0)

    gup = dot_nn(nffn_t[...], gupper_ref[...]).astype(BF)
    gdown = dot_nn(grad_t[...], active_ref[...]).astype(BF)

    @pl.when(step < 2)
    def _():
        up_one[...] = gup.reshape(up_one.shape)
        down_one[...] = gdown.reshape(down_one.shape)

    @pl.when(step >= 2)
    def _():
        up_zero[...] = gup.reshape(up_zero.shape)
        down_zero[...] = gdown.reshape(down_zero.shape)


def ffn_weight_split(me, nffn, grad, gupper, active, depth):
    rows, width = nffn.shape
    piece = gupper.shape[1] // 4
    high = width // (2 * depth)

    def column(step, me):
        return (0, jnp.bitwise_xor(me[1], 2 * jnp.bitwise_and(step, 1) + 1 - step // 2))

    whole = pl.BlockSpec((rows, width), lambda i, me: (0, 0))
    up_block, down_block = (1, 2, depth, high, piece), (2, 1, depth, high, piece)
    return pl.pallas_call(
        ffn_weight_split_kernel,
        grid_spec=pltpu.PrefetchScalarGridSpec(
            num_scalar_prefetch=1,
            grid=(4,),
            in_specs=[whole, whole, pl.BlockSpec((rows, piece), column), pl.BlockSpec((rows, piece), column)],
            out_specs=[
                pl.BlockSpec(up_block, lambda i, me: (jnp.minimum(i, 1), 0, 0, 0, 0)),
                pl.BlockSpec(up_block, lambda i, me: (jnp.maximum(i - 2, 0), 0, 0, 0, 0)),
                pl.BlockSpec(down_block, lambda i, me: (0, jnp.minimum(i, 1), 0, 0, 0)),
                pl.BlockSpec(down_block, lambda i, me: (0, jnp.maximum(i - 2, 0), 0, 0, 0)),
            ],
            scratch_shapes=[pltpu.VMEM((width, rows), BF)] * 3,
        ),
        out_shape=[jax.ShapeDtypeStruct((2, 2, depth, high, piece), BF)] * 4,
        compiler_params=pltpu.CompilerParams(vmem_limit_bytes=VMEM_LIMIT),
        cost_estimate=pl.CostEstimate(flops=15 * 10**9, bytes_accessed=30 * 10**6, transcendentals=0),
        name="ffn_weight",
    )(me, nffn, grad, gupper, active)


def attention_weight_split_kernel(
    me_ref, normed_ref, mixed_ref, gproj_ref, gmiddle_ref,
    a_one, a_zero, b_one, b_zero, normed_t, mixed_t, normed_r, mixed_r, joined,
):
    half = pl.program_id(0)
    depth, high, width = a_one.shape[2:]

    @pl.when(half == 0)
    def _():
        normed_t[...] = normed_ref[...].T
        mixed_t[...] = mixed_ref[...].T

    relative_rows(plane_order(depth), normed_t, normed_r, me_ref[0], high, half * high)
    relative_rows(plane_order(depth), mixed_t, mixed_r, me_ref[0], high, half * high)
    gqkv = dot_nn(normed_r[...], gproj_ref[...])
    gout = dot_nn(mixed_r[...], gmiddle_ref[...].astype(BF))
    cut = gqkv.shape[1] // 4
    rest = gout.shape[1] // 4
    for part in range(4):
        qkv_part = gqkv[:, part * cut : (part + 1) * cut].astype(BF)
        out_part = gout[:, part * rest : (part + 1) * rest].astype(BF)
        joined[jnp.bitwise_xor(me_ref[1], part)] = jnp.concatenate([qkv_part, out_part], axis=1)

    @pl.when(half == 0)
    def _():
        for y in range(2):
            a_zero[y] = joined[2 * y].reshape(2, depth, high, width)
            a_one[y] = joined[2 * y + 1].reshape(2, depth, high, width)

    @pl.when(half == 1)
    def _():
        for y in range(2):
            b_zero[:, y] = joined[2 * y].reshape(2, depth, high, width)
            b_one[:, y] = joined[2 * y + 1].reshape(2, depth, high, width)


def attention_weight_split(me, normed, mixed, gproj, gmiddle, depth):
    rows, width = normed.shape
    high = width // (4 * depth)
    whole = lambda array: pl.BlockSpec(array.shape, lambda i: (0, 0))
    shape = (2, 2, depth, high, width)
    return pl.pallas_call(
        attention_weight_split_kernel,
        grid=(2,),
        in_specs=[pl.BlockSpec(memory_space=pltpu.SMEM), whole(normed), whole(mixed), whole(gproj), whole(gmiddle)],
        out_specs=[pl.BlockSpec(shape, lambda i: (0, 0, 0, 0, 0))] * 4,
        out_shape=[jax.ShapeDtypeStruct(shape, BF)] * 4,
        scratch_shapes=[
            pltpu.VMEM((width, rows), BF),
            pltpu.VMEM((width, rows), BF),
            pltpu.VMEM((width // 2, rows), BF),
            pltpu.VMEM((width // 2, rows), BF),
            pltpu.VMEM((4, width // 2, width), BF),
        ],
        compiler_params=pltpu.CompilerParams(vmem_limit_bytes=VMEM_LIMIT),
        cost_estimate=pl.CostEstimate(flops=10 * 10**9, bytes_accessed=20 * 10**6, transcendentals=0),
        name="attention_weight",
    )(me, normed, mixed, gproj, gmiddle)


def pair_bias(slot_kind, slot_valid, across):
    same_kind = slot_kind[:, :, None] == slot_kind[:, None, :]
    partner = jnp.logical_not(same_kind) if across else same_kind
    allowed = jnp.logical_and(partner, slot_valid[:, None, :] > 0)
    return jnp.where(allowed, 0.0, -1e30).astype(F32)


def adam_step(master, grad, moment_one, moment_two, factor, decayed):
    clipped = grad * factor
    first_new = beta_one * moment_one + (1.0 - beta_one) * clipped
    second_new = beta_two * moment_two + (1.0 - beta_two) * clipped * clipped
    change = first_new / bias_one / (jnp.sqrt(second_new / bias_two) + epsilon)
    if decayed:
        change = change + weight_decay * master
    return (-learn_rate * change, first_new, second_new)


def gather_rows(pieces, sizes):
    high, width = pieces.shape[1:]
    rows = lax.all_gather(pieces.reshape(-1, width), ("dp", "tensor"), axis=0, tiled=False)
    if high % 16 == 0:
        return [(("rows", offset * high), [rows]) for offset in (2, 0, 1)]
    split = rows.reshape(sizes["dp"], sizes["tensor"], 3, high, width)
    return [(("whole",), [jnp.swapaxes(split[:, :, kind], 0, 1).reshape(-1, width, width)]) for kind in (2, 0, 1)]


def scatter_rows(grad, sizes):
    stripes, parts, kinds, high, width = grad.shape
    inner = sizes["dp"] // stripes
    if inner > 1:
        grad = jnp.moveaxis(grad.reshape(stripes, parts, kinds, inner, high // inner, width), 3, 1)
    mine = lax.psum_scatter(grad.reshape(-1, width), ("dp", "tensor"), scatter_dimension=0, tiled=True)
    return mine.reshape(kinds, -1, width).astype(F32)


class Exchange:
    def __init__(self, sizes):
        self.sizes = sizes
        self.depth = sizes["dp"] // 2

    def swap(self, axis, bits, value):
        return lax.ppermute(value, axis, [(index, index ^ bits) for index in range(self.sizes[axis])])

    def core(self, value):
        return self.swap("tensor", 1, value)

    def along(self, name, value):
        return self.swap("dp", 1, value) if name == "x" else self.swap("tensor", 2, value)

    def depths(self, values):
        return [self.swap("dp", 2 * z, values[z]) for z in range(1, self.depth)]

    def diagonal(self, value):
        dp, tensor = self.sizes["dp"], self.sizes["tensor"]
        pairs = [(i * tensor + j, (i ^ 1) * tensor + (j ^ 2)) for i in range(dp) for j in range(tensor)]
        return lax.ppermute(value, ("dp", "tensor"), pairs)

    def rounds(self):
        along_z = [functools.partial(self.swap, "dp", 2 * z) for z in range(1, self.depth)]
        plane = [functools.partial(self.along, "x"), functools.partial(self.along, "y"), self.diagonal]
        return along_z, plane, [self.core]

    def total(self, value):
        for moves in self.rounds():
            value = tree_sum([value] + [move(value) for move in moves])
        return value


def tree_sum(values):
    while len(values) > 1:
        values = [values[at] + values[at + 1] for at in range(0, len(values), 2)]
    return values[0]


def tie(values, after):
    return lax.optimization_barrier((values, after))[0]


class Spread:
    def __init__(self, exchange, first, second, row, pieces):
        self.exchange, self.first, self.second, self.row = exchange, first, second, row
        self.quad = jnp.stack(pieces)

    def go_first(self, after=None):
        quad = self.quad if after is None else tie(self.quad, after)
        self.one = self.exchange.along(self.first, quad)
        self.pair = jnp.stack([quad, self.one])
        return self.one

    def go_second(self):
        self.two = self.exchange.along(self.second, self.pair)
        return self.two

    def go_core(self, after=None):
        two = self.two if after is None else tie(self.two, after)
        self.far = [self.exchange.core(self.pair), self.exchange.core(two)]

    def units(self):
        spot = lambda near, side, core: (near, side, core) if self.first == "x" else (side, near, core)
        plan, arrays = [], []
        for core, (pair, two) in enumerate(((self.pair, self.two), self.far)):
            for side, value in enumerate((pair, two)):
                plan.append((self.row, [spot(0, side, core), spot(1, side, core)]))
                arrays.append(value)
        return plan, arrays


def near_weight(spreads):
    units = [spread.units() for spread in spreads]
    return (("near", sum([unit[0] for unit in units], [])), sum([unit[1] for unit in units], []))


class Reduce:
    def __init__(self, exchange, first, second, other, own):
        self.exchange, self.first, self.second, self.other, self.own = exchange, first, second, other, own

    def go_core(self):
        return [(self.exchange.core, self.other)]

    def took_core(self, came):
        self.came = came[0]

    def wide(self, value):
        return value.astype(F32)

    def go_second(self):
        value = (self.wide(self.own[1]) + self.wide(self.came[1])).astype(BF)
        return [(functools.partial(self.exchange.along, self.second), value)]

    def took_second(self, came):
        self.beside = came[0]

    def near(self, at):
        return self.wide(self.own[0, at]) + self.wide(self.came[0, at]) + self.wide(self.beside[at])

    def go_first(self):
        return [(functools.partial(self.exchange.along, self.first), self.near(1).astype(BF))]

    def took_first(self, came):
        self.ahead = came[0]
        self.layers = [
            self.wide(self.own[0, 0, z])
            + self.wide(self.came[0, 0, z])
            + self.wide(self.beside[0, z])
            + self.wide(self.ahead[z])
            for z in range(self.exchange.depth)
        ]


def depth_sends(exchange, reduces):
    return [
        (
            functools.partial(exchange.swap, "dp", 2 * z),
            jnp.concatenate([reduce.layers[z].astype(BF) for reduce in reduces], axis=0),
        )
        for z in range(1, exchange.depth)
    ]


def depth_total(reduces, came):
    total = jnp.concatenate([reduce.layers[0] for reduce in reduces], axis=0)
    for value in came:
        total = total + value.astype(F32)
    return total


class Lane:
    def __init__(self):
        self.last = None
        self.flying = []

    def send(self, sends):
        values = [value for _, value in sends]
        if self.last is not None:
            values = tie(values, self.last)
        came = [move(value) for (move, _), value in zip(sends, values)]
        return came

    def run(self, kernel, arrays, landed=()):
        if self.last is not None:
            arrays = tie(list(arrays), (self.last, list(landed)))
        result = kernel(*arrays)
        self.last = result[-1]
        return result


def shards(
    sizes,
    tokens, out_grad, slot_kind, slot_valid,
    qkv_weight, qkv_first, qkv_second,
    out_weight, out_first, out_second,
    up_weight, up_first, up_second,
    down_weight, down_first, down_second,
    gain_weight, gain_first, gain_second,
    bias_weight, bias_first, bias_second,
    hidden_weight, hidden_first, hidden_second,
):
    parts = sizes["tensor"]
    width = tokens.shape[1]
    cut = qkv_weight.shape[2]
    high = qkv_weight.shape[1]
    split = parts == 4 and high % 32 == 0 and sizes["dp"] in (4, 8, 16)
    exchange = Exchange(sizes)
    stripes = sizes["dp"] if high % 16 == 0 else 2
    me = jnp.stack([lax.axis_index("dp"), lax.axis_index("tensor")]).astype(jnp.int32)
    attn_pieces = jnp.concatenate([qkv_weight.astype(BF), out_weight.astype(BF)], axis=2)
    up_pieces = up_weight.astype(BF)
    down_pieces = jnp.swapaxes(down_weight.astype(BF), 1, 2)
    pages = slot_kind.shape[0]
    block_pages = 2 if pages % 2 == 0 else 1
    block = block_pages * slot_kind.shape[1]
    middle_page = block_pages
    masks = [pair_bias(slot_kind, slot_valid, index == 0) for index in range(2)]
    lane = Lane()
    gathered = lambda index: gather_rows(
        jnp.stack([up_pieces[index], down_pieces[index], attn_pieces[index]]), sizes
    )
    attn_w, up_w, down_w = ([None, None] for _ in range(3))
    attn_w[1], up_w[1], down_w[1] = gathered(1)
    if split:
        piece = attn_pieces[0]
        depth_attn = [piece] + exchange.depths([piece] * exchange.depth)
        own_small = jnp.concatenate(
            [gain_weight, bias_weight, hidden_weight.reshape(2, -1, gain_weight.shape[2])], axis=1
        )
        own_small = lax.reduce_precision(own_small, 8, 7)
        others = [exchange.swap("tensor", bits, own_small) for bits in range(1, 4)]
        mine = lax.axis_index("tensor")
        every = jnp.zeros((4,) + own_small.shape, F32)
        for bits, value in enumerate([own_small] + others):
            every = lax.dynamic_update_slice_in_dim(every, value[None], jnp.bitwise_xor(mine, bits), 0)
        small = jnp.moveaxis(every[:, :, :8], 0, 2).reshape(2, 8, width)
        hidden = jnp.moveaxis(every[:, :, 8:], 0, 1).reshape(2, -1)

        piece = jnp.concatenate([up_pieces[0], down_pieces[0]], axis=0)
        piece = tie(piece, depth_attn[1:])
        depth_ffn = [piece] + exchange.depths([piece] * exchange.depth)
        attn_a = Spread(exchange, "x", "y", 0, [part[: high // 2] for part in depth_attn])
        attn_b = Spread(exchange, "y", "x", high // 2, [part[high // 2 :] for part in depth_attn])
        up_a = Spread(exchange, "x", "y", 0, [part[:high] for part in depth_ffn])
        down_b = Spread(exchange, "y", "x", 0, [part[high:] for part in depth_ffn])
        attn_a.go_first(others), attn_b.go_first(others)
        second = [attn_a.go_second(), attn_b.go_second()]
        attn_a.go_core(), attn_b.go_core()
        ready = [up_a.go_first(second), down_b.go_first(second)]
        attn_w[0] = near_weight([attn_a, attn_b])
        tokens_in = tie(tokens, ready)
        up_a.go_second(), down_b.go_second()
    else:
        small = jnp.concatenate([gain_weight, bias_weight], axis=1).astype(BF)
        small = lax.all_gather(small, "tensor", axis=2, tiled=True).astype(F32)
        hidden = lax.all_gather(hidden_weight.astype(BF), "tensor", axis=1, tiled=True).astype(F32)
        attn_w[0], up_w[0], down_w[0] = gathered(0)
        tokens_in = tokens

    stream = tokens_in
    saved = []
    for index in range(2):
        middle, nffn, normed, proj, probs, mixed, qkv_w, out_w = attention_forward(
            me, stream, masks[index], small[index], attn_w[index], block_pages, parts
        )
        if split and index == 0:
            up_a.go_core(nffn), down_b.go_core(nffn)
            up_w[0] = near_weight([up_a])
            down_w[0] = near_weight([down_b])
        result, active, slope = ffn_forward(
            me, nffn, middle, small[index], hidden[index : index + 1], up_w[index], down_w[index], block, parts
        )
        saved.append((stream, middle, nffn, normed, proj, probs, mixed, active, slope, (qkv_w, out_w)))
        stream = result
    block_output = stream

    def run_ffn_backward(index, grad, landed=()):
        _, middle, _, _, _, _, _, _, slope, _ = saved[index]
        kernel = lambda grad: ffn_backward(
            me, grad, slope, middle, small[index], up_w[index], down_w[index], block, parts
        )
        return lane.run(kernel, [grad], landed)

    def run_ffn_weight(index, grad, gupper, landed=()):
        _, _, nffn, _, _, _, _, active, _, _ = saved[index]
        if split and index == 0:
            kernel = lambda gupper: ffn_weight_split(me, nffn, grad, gupper, active, exchange.depth)
        else:
            kernel = lambda gupper: (ffn_weight(nffn, grad, gupper, active, stripes, parts),)
        return lane.run(kernel, [gupper], landed)

    def run_attention_backward(index, gmiddle, begin, end, before, landed=()):
        stream, _, _, _, proj, probs, _, _, _, weight = saved[index]
        kernel = lambda gmiddle: attention_backward(
            gmiddle, stream, proj, probs, small[index], weight, block_pages, begin, end, before
        )
        return lane.run(kernel, [gmiddle], landed)

    def run_attention_weight(index, gproj, gmiddle, before=None, landed=()):
        _, _, _, normed, _, _, mixed, _, _, _ = saved[index]
        if split and index == 0:
            kernel = lambda gproj: attention_weight_split(me, normed, mixed, gproj, gmiddle, exchange.depth)
        else:
            kernel = lambda gproj: (attention_weight(normed, mixed, gproj, gmiddle, before),)
        return lane.run(kernel, [gproj], landed)

    attn_g, up_g, down_g, small_g, hidden_g = ([None, None] for _ in range(5))
    grad = out_grad
    for index in (1, 0):
        gupper, gmiddle, small_two, ghidden = run_ffn_backward(index, grad)
        if split and index == 0:
            up_one, up_zero, down_one, down_zero = run_ffn_weight(index, grad, gupper)
            ffn = [Reduce(exchange, "x", "y", up_one, up_zero), Reduce(exchange, "y", "x", down_one, down_zero)]
            came = lane.send(ffn[0].go_core() + ffn[1].go_core())
            before = run_attention_backward(index, gmiddle, 0, middle_page, None)
            ffn[0].took_core(came[:1]), ffn[1].took_core(came[1:])
            landed = came
            came = lane.send(ffn[0].go_second() + ffn[1].go_second())
            after = run_attention_backward(index, gmiddle, middle_page, pages, before[:2], landed)
            ffn[0].took_second(came[:1]), ffn[1].took_second(came[1:])
            next_grad, gproj = after[:2]
            small_one = before[2] + after[2]
            landed = came
            came = lane.send(ffn[0].go_first() + ffn[1].go_first())
            a_one, a_zero, b_one, b_zero = run_attention_weight(index, gproj, gmiddle, None, landed)
            ffn[0].took_first(came[:1]), ffn[1].took_first(came[1:2])
            attn = [Reduce(exchange, "x", "y", a_one, a_zero), Reduce(exchange, "y", "x", b_one, b_zero)]
        else:
            (gffn,) = run_ffn_weight(index, grad, gupper)
            next_grad, gproj, small_one = run_attention_backward(index, gmiddle, 0, pages, None)
            (both,) = run_attention_weight(index, gproj, gmiddle, gffn)
            up_g[index], down_g[index], attn_g[index] = scatter_rows(both, sizes)
        grad = next_grad
        small_g[index] = jnp.concatenate([small_one, small_two], axis=0)
        hidden_g[index] = ghidden
    input_grad = grad

    if split:
        whole = jnp.concatenate(small_g + [value.reshape(-1, width) for value in hidden_g], axis=0)
        along_z, plane, across = exchange.rounds()
        count = exchange.depth - 1
        came = lane.send(attn[0].go_core() + attn[1].go_core() + depth_sends(exchange, ffn) + [(move, whole) for move in along_z])
        attn[0].took_core(came[:1]), attn[1].took_core(came[1:2])
        total = depth_total(ffn, came[2 : 2 + count])
        up_g[0], down_g[0] = total[:high], total[high:]
        whole = tree_sum([whole] + came[2 + count :])
        came = lane.send(attn[0].go_second() + attn[1].go_second() + [(move, whole) for move in plane])
        attn[0].took_second(came[:1]), attn[1].took_second(came[1:2])
        whole = tree_sum([whole] + came[2:])
        came = lane.send(attn[0].go_first() + attn[1].go_first() + [(move, whole) for move in across])
        attn[0].took_first(came[:1]), attn[1].took_first(came[1:2])
        whole = tree_sum([whole] + came[2:])
        attn_g[0] = depth_total(attn, lane.send(depth_sends(exchange, attn)))
        vectors = whole[:32].reshape(2, 16, width)
        grad_hidden = whole[32:].reshape(2, -1)
    else:
        vectors, grad_hidden = lax.psum((jnp.stack(small_g), jnp.concatenate(hidden_g, axis=0)), ("dp", "tensor"))
    grad_gain = jnp.stack([vectors[:, 0], vectors[:, 8]], axis=1)
    grad_bias = jnp.stack([vectors[:, row] for row in (1, 2, 3, 11, 9, 10)], axis=1)
    shared_squares = (
        jnp.sum(grad_gain * grad_gain) + jnp.sum(grad_bias * grad_bias) + jnp.sum(grad_hidden * grad_hidden)
    )
    at = lax.axis_index("tensor")
    slice_of = lambda whole, axis: lax.dynamic_slice_in_dim(
        whole, at * (whole.shape[axis] // parts), whole.shape[axis] // parts, axis
    )
    grad_gain = slice_of(grad_gain, 2)
    grad_bias = slice_of(grad_bias, 2)
    grad_hidden = slice_of(grad_hidden, 1)
    grad_attn = jnp.stack(attn_g)
    grad_up = jnp.stack(up_g)
    grad_down = jnp.stack(down_g)
    local_squares = (
        jnp.sum(grad_attn * grad_attn) + jnp.sum(grad_up * grad_up) + jnp.sum(grad_down * grad_down)
    )
    grad_down = jnp.swapaxes(grad_down, 1, 2)
    if split:
        local_squares = exchange.total(local_squares.reshape(1, 1))[0, 0]
    else:
        local_squares = lax.psum(local_squares, ("dp", "tensor"))
    total_squares = local_squares + shared_squares
    grad_norm = jnp.sqrt(total_squares)
    factor = clip_norm / jnp.maximum(grad_norm, clip_norm)
    masters = (qkv_weight, out_weight, up_weight, down_weight, gain_weight, bias_weight, hidden_weight)
    firsts = (qkv_first, out_first, up_first, down_first, gain_first, bias_first, hidden_first)
    seconds = (qkv_second, out_second, up_second, down_second, gain_second, bias_second, hidden_second)
    gradients = (
        grad_attn[:, :, :cut], grad_attn[:, :, cut:], grad_up, grad_down, grad_gain, grad_bias, grad_hidden,
    )
    results = [block_output, input_grad, grad_norm]
    for member in range(7):
        update, first_new, second_new = adam_step(
            masters[member], gradients[member], firsts[member], seconds[member], factor, member < 4
        )
        results = results + [gradients[member], update, first_new, second_new]
    return tuple(results)


def solution(mesh):
    rows = P(("dp", "tensor"), None)
    matrix = P(None, "dp", "tensor")
    turned = P(None, "tensor", "dp")
    vectors = P(None, None, "tensor")
    hidden = P(None, "tensor")
    return jax.shard_map(
        functools.partial(shards, dict(mesh.shape)),
        mesh=mesh,
        in_specs=(rows,) * 4 + (matrix,) * 9 + (turned,) * 3 + (vectors,) * 6 + (hidden,) * 3,
        out_specs=(rows, rows, P()) + (matrix,) * 12 + (turned,) * 4 + (vectors,) * 8 + (hidden,) * 4,
        check_vma=False,
    )
```

time: 1830 us -> 577 us (0.32)
  waiting for transfers between devices: 1210 us -> 167 us
  Pallas kernels: 0 us -> 242 us
  matrix products: 230 us -> 0 us
  local copies, waits for them, and re-layouts: 154 us -> 16.1 us
  blocking collectives: 108 us -> 0 us
  starting transfers between devices: 1.29 us -> 78.2 us
  other arithmetic: 93.1 us -> 44.6 us
    reduce_scatter x7 -> x1, waiting for transfers between devices: 663 us -> 0.02 us  [scatter_rows(): lax.psum_scatter(grad.reshape(-1, width), ('dp', 'tensor'), scatter_dimen...]
    all_gather x8 -> x1, waiting for transfers between devices: 335 us -> 0.02 us  [gather_rows(): lax.all_gather(pieces.reshape(-1, width), ('dp', 'tensor'), axis=0, tiled...]
    pallas_call x0 -> x13, Pallas kernels: none -> 242 us  [the longest x3 54.9 us: attention_backward(): pl.pallas_call(attention_backward_kernel, grid=((end - begin) // block_pa...]
    dot_general x36 -> x0, matrix products: 230 us -> none  [the longest x2 35.1 us: ffn_backward(): jnp.dot(lower_all, down_w.T, preferred_element_type=jnp.float32)]
    unnamed x25 -> x2, waiting for transfers between devices: 211 us -> 0.03 us
    ppermute x0 -> x57, waiting for transfers between devices: none -> 167 us  [the longest x55 165 us: swap(): lax.ppermute(value, axis, [(index, index ^ bits) for index in range(self....]
    ppermute x0 -> x57, starting transfers between devices: none -> 78.1 us  [the longest x55 73.4 us: swap(): lax.ppermute(value, axis, [(index, index ^ bits) for index in range(self....]
    psum x2 -> x0, blocking collectives: 76.4 us -> none  [the longest x1 39.3 us: shards(): lax.psum(local_squares + owner * shared_squares, ('dp', 'tensor'))]
  transfers between devices with their start and end apart: 20 -> 59, of which waited for: 18 -> 23; matrix products, arithmetic and copies ran while one was open for 16% -> 8% of each run, Pallas kernels for 0% -> 22%
where the time goes in v1:
time: 577 us; the launch traced here: 573 us
  Pallas kernels  242 us (42%)
  waiting for transfers between devices  167 us (29%)
  starting transfers between devices  78.2 us (14%)
  other arithmetic  44.6 us (8%)
  between operations  24.8 us (4%)
  local copies, waits for them, and re-layouts  16.1 us (3%)
    ppermute x55, waiting for transfers between devices, swap(): lax.ppermute(value, axis, [(index, index ^ bits) for index in range(self....  165 us
    ppermute x55, starting transfers between devices, swap(): lax.ppermute(value, axis, [(index, index ^ bits) for index in range(self....  73.4 us
    pallas_call x3, Pallas kernels, attention_backward(): pl.pallas_call(attention_backward_kernel, grid=((end - begin) // block_pa...  54.9 us
    pallas_call x2, Pallas kernels, ffn_forward(): pl.pallas_call(functools.partial(ffn_forward_kernel, (up_w[0], down_w[0])...  44 us
    pallas_call x2, Pallas kernels, attention_forward(): pl.pallas_call(functools.partial(attention_forward_kernel, plan), grid=(p...  42.3 us
    pallas_call x2, Pallas kernels, ffn_backward(): pl.pallas_call(functools.partial(ffn_backward_kernel, (up_w[0], down_w[0]...  41.1 us
    pallas_call x1, Pallas kernels, ffn_weight_split(): pl.pallas_call(ffn_weight_split_kernel, grid_spec=pltpu.PrefetchScalarGri...  19.8 us
    pallas_call x1, Pallas kernels, ffn_weight(): pl.pallas_call(ffn_weight_kernel, grid=(parts,), in_specs=[whole, whole,...  15.8 us
  transfers between devices with their start and end apart: 59, of which 23 were waited for; matrix products, arithmetic and copies ran while one was open for 8% of the time, Pallas kernels for 22%

profile of v1, /device:TPU:0, one launch (start us, length us, event | category | flops | bytes accessed | tf_op | source)
XLA Modules:
  0.0 572.6 jit_solution(14799891426614666111)
XLA Ops:
  19.5 9.5 %collective-permute-done.1 = bf16[96,768]{1,0:T(8,128)(2,1)S(1)} collective-permute-done((bf16[96,768]{1,0:T(8,128)(2,1)S(1)}, bf16[96,768]{1,0:T(8,128)(2,1)S(1)}, u32[]{:S(2)}, u32[]{:S(2)}) %collective-permute-start.1) | collective-permute-done | bytes 147488 | tf_op jit(solution)/shard_map/ppermute | solution.py:668
  31.1 8.7 %collective-permute-start.3 = (bf16[192,768]{1,0:T(8,128)(2,1)S(1)}, bf16[192,768]{1,0:T(8,128)(2,1)S(1)}, u32[]{:S(2)}, u32[]{:S(2)}) collective-permute-start(bf16[192,768]{1,0:T(8,128)(2,1)S(1)} %pad_maximum_fusion.9), channel_id=1, source_target_pairs={{0,8},{4,12},{8,0},{12,4},{16,24},{20,28},{24,16},{28,20},{1,9},{5... | collective-permute-start | bytes 884744 | tf_op jit(solution)/shard_map/ppermute | solution.py:668
  46.5 12.3 %collective-permute-done.9 = bf16[4,48,768]{2,1,0:T(8,128)(2,1)S(1)} collective-permute-done((bf16[4,48,768]{2,1,0:T(8,128)(2,1)S(1)}, bf16[4,48,768]{2,1,0:T(8,128)(2,1)S(1)}, u32[]{:S(2)}, u32[]{:S(2)}) %collective-permute-start.9) | collective-permute-done | bytes 294944 | tf_op jit(solution)/shard_map/ppermute | solution.py:668
  59.9 12.3 %collective-permute-done.4 = bf16[192,768]{1,0:T(8,128)(2,1)S(1)} collective-permute-done((bf16[192,768]{1,0:T(8,128)(2,1)S(1)}, bf16[192,768]{1,0:T(8,128)(2,1)S(1)}, u32[]{:S(2)}, u32[]{:S(2)}) %collective-permute-start.4) | collective-permute-done | bytes 294944 | tf_op jit(solution)/shard_map/ppermute | solution.py:668
  93.3 21.1 %attention_forward.2 = (f32[1024,768]{1,0:T(8,128)}, bf16[1024,768]{1,0:T(8,128)(2,1)}, bf16[1024,768]{1,0:T(8,128)(2,1)}, bf16[1024,2304]{1,0:T(8,128)(2,1)}, b...) custom-call(s32[2]{0:T(128)} %pad_add_fusion.me_ref, ...), custom_call_target="tpu_custom_call" | custom-call | flops 20000000000 | bytes 30000000 | tf_op jit(solution)/shard_map/attention_forward/pallas_call | solution.py:174
  114.4 26.6 %collective-permute-done.22.refs_5_ = bf16[2,4,96,768]{3,2,1,0:T(8,128)(2,1)} collective-permute-done((bf16[2,4,96,768]{3,2,1,0:T(8,128)(2,1)S(1)}, bf16[2,4,96,768]{3,2,1,0:T(8,128)(2,1)}, u32[]{:S(2)}, u32[]{:S(2)}) %collective-permute-start.22) | collective-permute-done | bytes 1179680 | tf_op jit(solution)/shard_map/ppermute | solution.py:668
  146.3 22.3 %ffn_forward.2 = (f32[1024,768]{1,0:T(8,128)}, bf16[1024,3072]{1,0:T(8,128)(2,1)}, bf16[1024,3072]{1,0:T(8,128)(2,1)}) custom-call(s32[2]{0:T(128)} %pad_add_fusion.me_ref, bf16[1024,768]{1,0:T(8,128)(2,1)} %get-tuple-element.125.nffn_ref, f32[1024,768]{1,0:T(8,128)} %get-tuple-element.126.middle_ref, f32[8,768]{1,0:T(8,128)} %squeeze.15.vec_ref, ...), custom_call_target="tpu_custom_call" | custom-call | flops 15000000512 | bytes 30000000 | tf_op jit(solution)/shard_map/ffn_forward/pallas_call | solution.py:247
  168.6 21.2 %attention_forward.3 = (f32[1024,768]{1,0:T(8,128)}, bf16[1024,768]{1,0:T(8,128)(2,1)}, bf16[1024,768]{1,0:T(8,128)(2,1)}, bf16[1024,2304]{1,0:T(8,128)(2,1)}, b...) custom-call(s32[2]{0:T(128)} %pad_add_fusion.me_ref, ...), custom_call_target="tpu_custom_call" | custom-call | flops 20000000000 | bytes 30000000 | tf_op jit(solution)/shard_map/attention_forward/pallas_call | solution.py:174
  189.8 21.8 %ffn_forward.3 = (f32[1024,768]{1,0:T(8,128)}, bf16[1024,3072]{1,0:T(8,128)(2,1)}, bf16[1024,3072]{1,0:T(8,128)(2,1)}) custom-call(s32[2]{0:T(128)} %pad_add_fusion.me_ref, bf16[1024,768]{1,0:T(8,128)(2,1)} %get-tuple-element.130.nffn_ref, f32[1024,768]{1,0:T(8,128)} %get-tuple-element.131.middle_ref, f32[8,768]{1,0:T(8,128)} %squeeze.16.vec_ref, ...), custom_call_target="tpu_custom_call" | custom-call | flops 15000000512 | bytes 30000000 | tf_op jit(solution)/shard_map/ffn_forward/pallas_call | solution.py:247
  211.6 20.5 %ffn_backward.2 = (bf16[1024,3072]{1,0:T(8,128)(2,1)}, f32[1024,768]{1,0:T(8,128)}, f32[8,768]{1,0:T(8,128)}, f32[1,3072]{1,0:T(1,128)}) custom-call(s32[2]{0:T(128)} %pad_add_fusion.me_ref, bf16[1024,768]{1,0:T(8,128)(2,1)} %grad_ref.3, bf16[1024,3072]{1,0:T(8,128)(2,1)} %get-tuple-element.133.slope_ref, f32[1024,768]{1,0:T(8,128)} %get-tuple-element.131.middle_ref, ...), custom_call_target="tpu_custom_call" | custom-call | flops 15000000512 | bytes 30000000 | tf_op jit(solution)/shard_map/ffn_backward/pallas_call | solution.py:311
  232.0 15.8 %ffn_weight.2._ = bf16[8,4,3,96,768]{4,3,2,1,0:T(8,128)(2,1)} custom-call(bf16[1024,768]{1,0:T(8,128)(2,1)} %get-tuple-element.130.nffn_ref, bf16[1024,768]{1,0:T(8,128)(2,1)} %grad_ref.3, bf16[1024,3072]{1,0:T(8,128)(2,1)} %get-tuple-element.137.gupper_ref, bf16[1024,3072]{1,0:T(8,128)(2,1)} %get-tuple-element.138.active_ref), custom_call_target="tpu_custom_call" | custom-call | flops 15000000512 | bytes 30000000 | tf_op jit(solution)/shard_map/ffn_weight/pallas_call | solution.py:362
  247.9 25.5 %attention_backward.3 = (f32[1024,768]{1,0:T(8,128)}, bf16[1024,2304]{1,0:T(8,128)(2,1)}, f32[8,768]{1,0:T(8,128)}) custom-call(f32[1024,768]{1,0:T(8,128)} %get-tuple-element.139.gmiddle_ref, f32[1024,768]{1,0:T(8,128)} %get-tuple-element.129.stream_ref, bf16[1024,2304]{1,0:T(8,128)(2,1)} %get-tuple-element.140.proj_ref, ...), custom_call_target="tpu_custom_call" | custom-call | flops 15000000512 | bytes 20000000 | tf_op jit(solution)/shard_map/attention_backward/pallas_call | solution.py:435
  273.4 10.7 %attention_weight.2 = bf16[8,4,3,96,768]{4,3,2,1,0:T(8,128)(2,1)} custom-call(bf16[1024,768]{1,0:T(8,128)(2,1)} %get-tuple-element.145.normed_ref, bf16[1024,768]{1,0:T(8,128)(2,1)} %get-tuple-element.146.mixed_ref, bf16[1024,2304]{1,0:T(8,128)(2,1)} %get-tuple-element.149.gproj_ref, ...), custom_call_target="tpu_custom_call", output_to_operand_aliasing={{}: (4, {})} | custom-call | flops 10000000000 | bytes 20000000 | tf_op jit(solution)/shard_map/attention_weight/pallas_call | solution.py:479
  284.1 20.7 %ffn_backward.3 = (bf16[1024,3072]{1,0:T(8,128)(2,1)}, f32[1024,768]{1,0:T(8,128)}, f32[8,768]{1,0:T(8,128)}, f32[1,3072]{1,0:T(1,128)}) custom-call(s32[2]{0:T(128)} %pad_add_fusion.me_ref, f32[1024,768]{1,0:T(8,128)} %get-tuple-element.150.grad_ref, bf16[1024,3072]{1,0:T(8,128)(2,1)} %get-tuple-element.151.slope_ref, ...), custom_call_target="tpu_custom_call" | custom-call | flops 15000000512 | bytes 30000000 | tf_op jit(solution)/shard_map/ffn_backward/pallas_call | solution.py:311
  304.8 19.8 %ffn_weight.3 = (bf16[2,2,4,96,768]{4,3,2,1,0:T(8,128)(2,1)}, bf16[2,2,4,96,768]{4,3,2,1,0:T(8,128)(2,1)}, bf16[2,2,4,96,768]{4,3,2,1,0:T(8,128)(2,1)}, bf16[2,2,4,96,768]{4,3,2,1,0:T(8,128)(2,1)}) custom-call(s32[2]{0:T(128)} %pad_add_fusion.me_ref, bf16[1024,768]{1,0:T(8,128)(2,1)} %get-tuple-element.125.nffn_ref, ...), custom_call_target="tpu_custom_call" | custom-call | flops 15000000512 | bytes 30000000 | tf_op jit(solution)/shard_map/ffn_weight/pallas_call | solution.py:546
  327.7 9.4 %attention_backward.4 = (f32[1024,768]{1,0:T(8,128)}, bf16[1024,2304]{1,0:T(8,128)(2,1)}, f32[8,768]{1,0:T(8,128)}) custom-call(f32[1024,768]{1,0:T(8,128)} %get-tuple-element.168.gmiddle_ref, bf16[1024,768]{1,0:T(8,128)(2,1)} %stream_ref.2, bf16[1024,2304]{1,0:T(8,128)(2,1)} %get-tuple-element.159.proj_ref, ...), custom_call_target="tpu_custom_call" | custom-call | flops 15000000512 | bytes 20000000 | tf_op jit(solution)/shard_map/attention_backward/pallas_call | solution.py:435
  343.2 19.9 %attention_backward.5 = (f32[1024,768]{1,0:T(8,128)}, bf16[1024,2304]{1,0:T(8,128)(2,1)}, f32[8,768]{1,0:T(8,128)}) custom-call(f32[1024,768]{1,0:T(8,128)} %get-tuple-element.168.gmiddle_ref, bf16[1024,768]{1,0:T(8,128)(2,1)} %stream_ref.2, bf16[1024,2304]{1,0:T(8,128)(2,1)} %get-tuple-element.159.proj_ref, ...), custom_call_target="tpu_custom_call", output_to_operand_aliasing={{0}: (7, {}), {1}: (8, {})} | custom-call | flops 15000000512 | bytes 20000000 | tf_op jit(solution)/shard_map/attention_backward/pallas_call | solution.py:435
  371.2 11.8 %collective-permute-done.28 = bf16[2,4,96,768]{3,2,1,0:T(8,128)(2,1)} collective-permute-done((bf16[2,4,96,768]{3,2,1,0:T(8,128)(2,1)}, bf16[2,4,96,768]{3,2,1,0:T(8,128)(2,1)}, u32[]{:S(2)}, u32[]{:S(2)}) %collective-permute-start.28) | collective-permute-done | bytes 1179680 | tf_op jit(solution)/shard_map/ppermute | solution.py:668
  387.3 13.5 %attention_weight.3 = (bf16[2,2,4,48,768]{4,3,2,1,0:T(8,128)(2,1)}, bf16[2,2,4,48,768]{4,3,2,1,0:T(8,128)(2,1)}, bf16[2,2,4,48,768]{4,3,2,1,0:T(8,128)(2,1)}, bf16[2,2,4,48,768]{4,3,2,1,0:T(8,128)(2,1)}) custom-call(s32[2]{0:T(128)} %pad_add_fusion.me_ref, bf16[1024,768]{1,0:T(8,128)(2,1)} %get-tuple-element.172.normed_ref, ...), custom_call_target="tpu_custom_call" | custom-call | flops 10000000000 | bytes 20000000 | tf_op jit(solution)/shard_map/attention_weight/pallas_call | solution.py:608
  400.8 12.3 %collective-permute-done.29 = bf16[4,96,768]{2,1,0:T(8,128)(2,1)S(1)} collective-permute-done((bf16[4,96,768]{2,1,0:T(8,128)(2,1)S(1)}, bf16[4,96,768]{2,1,0:T(8,128)(2,1)S(1)}, u32[]{:S(2)}, u32[]{:S(2)}) %collective-permute-start.29) | collective-permute-done | bytes 589856 | tf_op jit(solution)/shard_map/ppermute | solution.py:668
  446.5 8.2 %collective-permute-done.46 = bf16[192,768]{1,0:T(8,128)(2,1)} collective-permute-done((bf16[192,768]{1,0:T(8,128)(2,1)}, bf16[192,768]{1,0:T(8,128)(2,1)}, u32[]{:S(2)}, u32[]{:S(2)}) %collective-permute-start.46) | collective-permute-done | bytes 294944 | tf_op jit(solution)/shard_map/ppermute | solution.py:668
  454.7 19.0 %collective-permute-done.47 = bf16[192,768]{1,0:T(8,128)(2,1)} collective-permute-done((bf16[192,768]{1,0:T(8,128)(2,1)}, bf16[192,768]{1,0:T(8,128)(2,1)}, u32[]{:S(2)}, u32[]{:S(2)}) %collective-permute-start.47) | collective-permute-done | bytes 294944 | tf_op jit(solution)/shard_map/ppermute | solution.py:668
  480.9 9.1 %collective-permute-done.36 = bf16[2,4,48,768]{3,2,1,0:T(8,128)(2,1)S(1)} collective-permute-done((bf16[2,4,48,768]{3,2,1,0:T(8,128)(2,1)}, bf16[2,4,48,768]{3,2,1,0:T(8,128)(2,1)S(1)}, u32[]{:S(2)}, u32[]{:S(2)}) %collective-permute-start.36) | collective-permute-done | bytes 589856 | tf_op jit(solution)/shard_map/ppermute | solution.py:668
  515.2 8.3 %collective-permute-done.44 = bf16[96,768]{1,0:T(8,128)(2,1)S(1)} collective-permute-done((bf16[96,768]{1,0:T(8,128)(2,1)S(1)}, bf16[96,768]{1,0:T(8,128)(2,1)S(1)}, u32[]{:S(2)}, u32[]{:S(2)}) %collective-permute-start.44) | collective-permute-done | bytes 147488 | tf_op jit(solution)/shard_map/ppermute | solution.py:668
  (307 shorter events, 167.4 us)
Async XLA Ops:
  7.2 161.4 %all-gather.2.cloned.1.call-start = ((), (), s32[]{:S(2)}) async-start(), calls=%async_computation.1 | async-start | bytes 14598144 | tf_op jit(solution)/shard_map/all_gather | solution.py:646
  10.4 513.1 %reduce-scatter.2.cloned.1.call-start = ((), (), s32[]{:S(2)}) async-start(), calls=%async_computation.2 | async-start | bytes 14598144 | tf_op jit(solution)/shard_map/reduce_scatter | solution.py:658
  29.2 16.1 %collective-permute-start.11 = (bf16[4,48,768]{2,1,0:T(8,128)(2,1)S(1)}, bf16[4,48,768]{2,1,0:T(8,128)(2,1)S(1)}, u32[]{:S(2)}, u32[]{:S(2)}) collective-permute-start(bf16[4,48,768]{2,1,0:T(8,128)(2,1)S(1)} %get-tuple-element.121), channel_id=1, source_target_pairs={{0,2},{1,3},{2,0},{3,1},{4,6},{5,7},{6,4},{7,5},{8,10},{9,11},{10,... | collective-permute-start | bytes 884744 | tf_op jit(solution)/shard_map/ppermute | solution.py:668
  31.1 28.7 %collective-permute-start.3 = (bf16[192,768]{1,0:T(8,128)(2,1)S(1)}, bf16[192,768]{1,0:T(8,128)(2,1)S(1)}, u32[]{:S(2)}, u32[]{:S(2)}) collective-permute-start(bf16[192,768]{1,0:T(8,128)(2,1)S(1)} %pad_maximum_fusion.9), channel_id=1, source_target_pairs={{0,8},{4,12},{8,0},{12,4},{16,24},{20,28},{24,16},{28,20},{1,9},{5... | collective-permute-start | bytes 884744 | tf_op jit(solution)/shard_map/ppermute | solution.py:668
  39.8 32.4 %collective-permute-start.4 = (bf16[192,768]{1,0:T(8,128)(2,1)S(1)}, bf16[192,768]{1,0:T(8,128)(2,1)S(1)}, u32[]{:S(2)}, u32[]{:S(2)}) collective-permute-start(bf16[192,768]{1,0:T(8,128)(2,1)S(1)} %pad_maximum_fusion.9), channel_id=1, source_target_pairs={{0,16},{4,20},{8,24},{12,28},{16,0},{20,4},{24,8},{28,12},{1,17},{... | collective-permute-start | bytes 884744 | tf_op jit(solution)/shard_map/ppermute | solution.py:668
  42.2 30.0 %collective-permute-start.5 = (bf16[192,768]{1,0:T(8,128)(2,1)S(1)}, bf16[192,768]{1,0:T(8,128)(2,1)S(1)}, u32[]{:S(2)}, u32[]{:S(2)}) collective-permute-start(bf16[192,768]{1,0:T(8,128)(2,1)S(1)} %pad_maximum_fusion.9), channel_id=1, source_target_pairs={{0,24},{4,28},{8,16},{12,20},{16,8},{20,12},{24,0},{28,4},{1,25},{... | collective-permute-start | bytes 884744 | tf_op jit(solution)/shard_map/ppermute | solution.py:668
  46.2 29.9 %collective-permute-start.12 = (bf16[2,4,48,768]{3,2,1,0:T(8,128)(2,1)}, bf16[2,4,48,768]{3,2,1,0:T(8,128)(2,1)}, u32[]{:S(2)}, u32[]{:S(2)}) collective-permute-start(bf16[2,4,48,768]{3,2,1,0:T(8,128)(2,1)} %pad_maximum_fusion.5.refs_4_), channel_id=1, source_target_pairs={{0,4},{4,0},{8,12},{12,8},{16,20},{20,16},{24,28},{28,24},{1,5},{5... | collective-permute-start | bytes 1769480 | tf_op jit(solution)/shard_map/ppermute | solution.py:668
  59.7 16.5 %collective-permute-start.10 = (bf16[2,4,48,768]{3,2,1,0:T(8,128)(2,1)}, bf16[2,4,48,768]{3,2,1,0:T(8,128)(2,1)}, u32[]{:S(2)}, u32[]{:S(2)}) collective-permute-start(bf16[2,4,48,768]{3,2,1,0:T(8,128)(2,1)} %pad_maximum_fusion.4.refs_0_), channel_id=1, source_target_pairs={{0,2},{1,3},{2,0},{3,1},{4,6},{5,7},{6,4},{7,5},{8,10},{9,11},{10,... | collective-permute-start | bytes 1769480 | tf_op jit(solution)/shard_map/ppermute | solution.py:668
  88.0 53.0 %collective-permute-start.22 = (bf16[2,4,96,768]{3,2,1,0:T(8,128)(2,1)S(1)}, bf16[2,4,96,768]{3,2,1,0:T(8,128)(2,1)}, u32[]{:S(2)}, u32[]{:S(2)}) collective-permute-start(bf16[2,4,96,768]{3,2,1,0:T(8,128)(2,1)S(1)} %pad_maximum_fusion.1.refs_4_), channel_id=1, source_target_pairs={{0,4},{4,0},{8,12},{12,8},{16,20},{20,16},{24,28},{28,24},{1,5},{5... | collective-permute-start | bytes 3538952 | tf_op jit(solution)/shard_map/ppermute | solution.py:668
  91.0 53.3 %collective-permute-start.23 = (bf16[2,4,96,768]{3,2,1,0:T(8,128)(2,1)S(1)}, bf16[2,4,96,768]{3,2,1,0:T(8,128)(2,1)}, u32[]{:S(2)}, u32[]{:S(2)}) collective-permute-start(bf16[2,4,96,768]{3,2,1,0:T(8,128)(2,1)S(1)} %pad_maximum_fusion.1.refs_4_), channel_id=1, source_target_pairs={{0,1},{1,0},{2,3},{3,2},{4,5},{5,4},{6,7},{7,6},{8,9},{9,8},{10,11... | collective-permute-start | bytes 3538952 | tf_op jit(solution)/shard_map/ppermute | solution.py:668
  91.3 49.7 %collective-permute-start.19 = (bf16[2,4,96,768]{3,2,1,0:T(8,128)(2,1)S(1)}, bf16[2,4,96,768]{3,2,1,0:T(8,128)(2,1)}, u32[]{:S(2)}, u32[]{:S(2)}) collective-permute-start(bf16[2,4,96,768]{3,2,1,0:T(8,128)(2,1)S(1)} %pad_maximum_fusion.refs_0_), channel_id=1, source_target_pairs={{0,2},{1,3},{2,0},{3,1},{4,6},{5,7},{6,4},{7,5},{8,10},{9,11},{10,... | collective-permute-start | bytes 3538952 | tf_op jit(solution)/shard_map/ppermute | solution.py:668
  93.1 51.2 %collective-permute-start.20 = (bf16[2,4,96,768]{3,2,1,0:T(8,128)(2,1)S(1)}, bf16[2,4,96,768]{3,2,1,0:T(8,128)(2,1)}, u32[]{:S(2)}, u32[]{:S(2)}) collective-permute-start(bf16[2,4,96,768]{3,2,1,0:T(8,128)(2,1)S(1)} %pad_maximum_fusion.refs_0_), channel_id=1, source_target_pairs={{0,1},{1,0},{2,3},{3,2},{4,5},{5,4},{6,7},{7,6},{8,9},{9,8},{10,11... | collective-permute-start | bytes 3538952 | tf_op jit(solution)/shard_map/ppermute | solution.py:668
  341.5 41.5 %collective-permute-start.28 = (bf16[2,4,96,768]{3,2,1,0:T(8,128)(2,1)}, bf16[2,4,96,768]{3,2,1,0:T(8,128)(2,1)}, u32[]{:S(2)}, u32[]{:S(2)}) collective-permute-start(bf16[2,4,96,768]{3,2,1,0:T(8,128)(2,1)} %fusion.1), channel_id=1, source_target_pairs={{0,4},{4,0},{8,12},{12,8},{16,20},{20,16},{24,28},{28,24},{1,5},{5... | collective-permute-start | bytes 3538952 | tf_op jit(solution)/shard_map/ppermute | solution.py:668
  341.6 42.9 %collective-permute-start.27 = (bf16[2,4,96,768]{3,2,1,0:T(8,128)(2,1)S(1)}, bf16[2,4,96,768]{3,2,1,0:T(8,128)(2,1)}, u32[]{:S(2)}, u32[]{:S(2)}) collective-permute-start(bf16[2,4,96,768]{3,2,1,0:T(8,128)(2,1)S(1)} %fusion), channel_id=1, source_target_pairs={{0,2},{1,3},{2,0},{3,1},{4,6},{5,7},{6,4},{7,5},{8,10},{9,11},{10,... | collective-permute-start | bytes 3538952 | tf_op jit(solution)/shard_map/ppermute | solution.py:668
  386.0 27.1 %collective-permute-start.29 = (bf16[4,96,768]{2,1,0:T(8,128)(2,1)S(1)}, bf16[4,96,768]{2,1,0:T(8,128)(2,1)S(1)}, u32[]{:S(2)}, u32[]{:S(2)}) collective-permute-start(bf16[4,96,768]{2,1,0:T(8,128)(2,1)S(1)} %fusion.3), channel_id=1, source_target_pairs={{0,4},{4,0},{8,12},{12,8},{16,20},{20,16},{24,28},{28,24},{1,5},{5... | collective-permute-start | bytes 1769480 | tf_op jit(solution)/shard_map/ppermute | solution.py:668
  386.4 28.4 %collective-permute-start.30 = (bf16[4,96,768]{2,1,0:T(8,128)(2,1)S(1)}, bf16[4,96,768]{2,1,0:T(8,128)(2,1)S(1)}, u32[]{:S(2)}, u32[]{:S(2)}) collective-permute-start(bf16[4,96,768]{2,1,0:T(8,128)(2,1)S(1)} %fusion.2), channel_id=1, source_target_pairs={{0,2},{1,3},{2,0},{3,1},{4,6},{5,7},{6,4},{7,5},{8,10},{9,11},{10,... | collective-permute-start | bytes 1769480 | tf_op jit(solution)/shard_map/ppermute | solution.py:668
  418.8 23.3 %collective-permute-start.32 = (bf16[2,2,4,48,768]{4,3,2,1,0:T(8,128)(2,1)S(1)}, bf16[2,2,4,48,768]{4,3,2,1,0:T(8,128)(2,1)S(1)}, u32[]{:S(2)}, u32[]{:S(2)}) collective-permute-start(bf16[2,2,4,48,768]{4,3,2,1,0:T(8,128)(2,1)S(1)} %copy-done.45), channel_id=1, source_target_pairs={{0,1},{1,0},{2,3},{3,2},{4,5},{5,4},{6,7},{7,6},{8,9},{9,8},{10,11... | collective-permute-start | bytes 3538952 | tf_op jit(solution)/shard_map/ppermute | solution.py:668
  418.9 23.5 %collective-permute-start.31 = (bf16[2,2,4,48,768]{4,3,2,1,0:T(8,128)(2,1)S(1)}, bf16[2,2,4,48,768]{4,3,2,1,0:T(8,128)(2,1)S(1)}, u32[]{:S(2)}, u32[]{:S(2)}) collective-permute-start(bf16[2,2,4,48,768]{4,3,2,1,0:T(8,128)(2,1)S(1)} %copy-done.44), channel_id=1, source_target_pairs={{0,1},{1,0},{2,3},{3,2},{4,5},{5,4},{6,7},{7,6},{8,9},{9,8},{10,11... | collective-permute-start | bytes 3538952 | tf_op jit(solution)/shard_map/ppermute | solution.py:668
  426.7 28.0 %collective-permute-start.46 = (bf16[192,768]{1,0:T(8,128)(2,1)}, bf16[192,768]{1,0:T(8,128)(2,1)}, u32[]{:S(2)}, u32[]{:S(2)}) collective-permute-start(bf16[192,768]{1,0:T(8,128)(2,1)} %pad_maximum_fusion.12), channel_id=1, source_target_pairs={{0,8},{4,12},{8,0},{12,4},{16,24},{20,28},{24,16},{28,20},{1,9},{5... | collective-permute-start | bytes 884744 | tf_op jit(solution)/shard_map/ppermute | solution.py:668
  432.7 41.0 %collective-permute-start.47 = (bf16[192,768]{1,0:T(8,128)(2,1)}, bf16[192,768]{1,0:T(8,128)(2,1)}, u32[]{:S(2)}, u32[]{:S(2)}) collective-permute-start(bf16[192,768]{1,0:T(8,128)(2,1)} %pad_maximum_fusion.13), channel_id=1, source_target_pairs={{0,16},{4,20},{8,24},{12,28},{16,0},{20,4},{24,8},{28,12},{1,17},{... | collective-permute-start | bytes 884744 | tf_op jit(solution)/shard_map/ppermute | solution.py:668
  437.8 37.3 %collective-permute-start.48 = (bf16[192,768]{1,0:T(8,128)(2,1)}, bf16[192,768]{1,0:T(8,128)(2,1)}, u32[]{:S(2)}, u32[]{:S(2)}) collective-permute-start(bf16[192,768]{1,0:T(8,128)(2,1)} %pad_maximum_fusion.14), channel_id=1, source_target_pairs={{0,24},{4,28},{8,16},{12,20},{16,8},{20,12},{24,0},{28,4},{1,25},{... | collective-permute-start | bytes 884744 | tf_op jit(solution)/shard_map/ppermute | solution.py:668
  444.4 35.4 %collective-permute-start.37 = (bf16[2,4,48,768]{3,2,1,0:T(8,128)(2,1)S(1)}, bf16[2,4,48,768]{3,2,1,0:T(8,128)(2,1)}, u32[]{:S(2)}, u32[]{:S(2)}) collective-permute-start(bf16[2,4,48,768]{3,2,1,0:T(8,128)(2,1)S(1)} %fusion.11), channel_id=1, source_target_pairs={{0,4},{4,0},{8,12},{12,8},{16,20},{20,16},{24,28},{28,24},{1,5},{5... | collective-permute-start | bytes 1769480 | tf_op jit(solution)/shard_map/ppermute | solution.py:668
  444.4 33.6 %collective-permute-start.38 = (f32[40,768]{1,0:T(8,128)}, f32[40,768]{1,0:T(8,128)S(1)}, u32[]{:S(2)}, u32[]{:S(2)}) collective-permute-start(f32[40,768]{1,0:T(8,128)} %add_add_fusion.1), channel_id=1, source_target_pairs={{0,4},{4,0},{8,12},{12,8},{16,20},{20,16},{24,28},{28,24},{1,5},{5... | collective-permute-start | bytes 368648 | tf_op jit(solution)/shard_map/ppermute | solution.py:668
  454.7 23.3 %collective-permute-start.39 = (f32[40,768]{1,0:T(8,128)}, f32[40,768]{1,0:T(8,128)S(1)}, u32[]{:S(2)}, u32[]{:S(2)}) collective-permute-start(f32[40,768]{1,0:T(8,128)} %add_add_fusion.1), channel_id=1, source_target_pairs={{0,2},{1,3},{2,0},{3,1},{4,6},{5,7},{6,4},{7,5},{8,10},{9,11},{10,... | collective-permute-start | bytes 368648 | tf_op jit(solution)/shard_map/ppermute | solution.py:668
  (81 other events, 915.3 us)
Sparse Core Ops, SparseCore 0:
  11.5 142.0 all-gather.1
  284.2 212.0 reduce-scatter.1

commit v2 on v1

--- a/solution.py
+++ b/solution.py
@@ -62,29 +62,36 @@
     return jnp.concatenate([jnp.where(lane < half, pair, zero), jnp.where(lane >= half, pair, zero)], axis=0)
 
 
+def plane(me_ref, first, second, core):
+    turned = jnp.bitwise_xor(jnp.bitwise_and(me_ref[1], 1), core) == 1
+    return jnp.where(turned, second, first), jnp.where(turned, first, second)
+
+
 def weight_copies(plan, refs, me_ref, full, sems):
     copies = []
 
     def add(source, target):
         copies.append(pltpu.make_async_copy(source, target, sems.at[len(copies)]))
 
+    parts, width, _ = full.shape
     if plan[0] == "whole":
         add(refs[0], full)
     elif plan[0] == "rows":
-        parts, width, _ = full.shape
         high = width * parts // refs[0].shape[0]
         for index in range(refs[0].shape[0]):
             stripe, part = divmod(index, parts)
             add(refs[0].at[index, pl.ds(plan[1], high), :], full.at[part, pl.ds(stripe * high, high), :])
     else:
-        for ref, (row, positions) in zip(refs, plan[1]):
-            _, depth, high, width = ref.shape
-            for place, (x, y, core) in enumerate(positions):
+        for ref, positions in zip(refs, plan[2]):
+            depth = ref.shape[1]
+            high = width // (2 * depth)
+            for place, (first, second, core) in enumerate(positions):
+                x, y = plane(me_ref, first, second, core)
                 part = jnp.bitwise_xor(me_ref[1], 2 * y + core)
+                origin = jnp.bitwise_and(me_ref[0], 1) if plan[3] else me_ref[0]
                 for z in range(depth):
-                    stripe = jnp.bitwise_xor(me_ref[0], 2 * z + x)
-                    start = pl.multiple_of(stripe * (width // (2 * depth)) + row, 16)
-                    add(ref.at[place, z], full.at[part, pl.ds(start, high), :])
+                    start = pl.multiple_of(jnp.bitwise_xor(origin, 2 * z + x) * high, 16)
+                    add(ref.at[place, z, pl.ds(plan[1], high), :], full.at[part, pl.ds(start, high), :])
     return copies
 
 
@@ -369,7 +376,7 @@
             pl.BlockSpec((rows, piece), lambda i: (0, i)),
         ],
         out_specs=pl.BlockSpec((stripes, 1, 2, high, piece), lambda i: (0, i, 0, 0, 0)),
-        out_shape=jax.ShapeDtypeStruct((stripes, parts, 3, high, piece), BF),
+        out_shape=jax.ShapeDtypeStruct((stripes, parts, 2, high, piece), BF),
         scratch_shapes=[pltpu.VMEM((width, rows), BF), pltpu.VMEM((width, rows), BF)],
         compiler_params=pltpu.CompilerParams(vmem_limit_bytes=VMEM_LIMIT),
         cost_estimate=pl.CostEstimate(flops=15 * 10**9, bytes_accessed=30 * 10**6, transcendentals=0),
@@ -459,7 +466,7 @@
     )(*operands, *before)
 
 
-def attention_weight_kernel(normed_ref, mixed_ref, gproj_ref, gmiddle_ref, _, grad_ref):
+def attention_weight_kernel(normed_ref, mixed_ref, gproj_ref, gmiddle_ref, grad_ref):
     gqkv = dot_tn(normed_ref[...], gproj_ref[...])
     gout = dot_tn(mixed_ref[...], gmiddle_ref[...].astype(BF))
     parts = grad_ref.shape[1]
@@ -472,10 +479,10 @@
         grad_ref[:, part, 0] = jnp.concatenate([qkv_part, out_part], axis=1).reshape(shape)
 
 
-def attention_weight(normed, mixed, gproj, gmiddle, before):
+def attention_weight(normed, mixed, gproj, gmiddle, stripes, parts):
     rows, width = normed.shape
     block = width // 2
-    stripes, parts, _, high, _ = before.shape
+    high = width // stripes
     return pl.pallas_call(
         attention_weight_kernel,
         grid=(2,),
@@ -484,53 +491,50 @@
             pl.BlockSpec((rows, block), lambda i: (0, i)),
             pl.BlockSpec((rows, 3 * width), lambda i: (0, 0)),
             pl.BlockSpec((rows, width), lambda i: (0, 0)),
-            pl.BlockSpec(memory_space=pl.ANY),
-        ],
-        out_specs=pl.BlockSpec((stripes // 2, parts, 1, high, width), lambda i: (i, 0, 2, 0, 0)),
-        out_shape=jax.ShapeDtypeStruct(before.shape, BF),
-        input_output_aliases={4: 0},
+        ],
+        out_specs=pl.BlockSpec((stripes // 2, parts, 1, high, width), lambda i: (i, 0, 0, 0, 0)),
+        out_shape=jax.ShapeDtypeStruct((stripes, parts, 1, high, width), BF),
         compiler_params=pltpu.CompilerParams(vmem_limit_bytes=VMEM_LIMIT),
         cost_estimate=pl.CostEstimate(flops=10 * 10**9, bytes_accessed=20 * 10**6, transcendentals=0),
         name="attention_weight",
-    )(normed, mixed, gproj, gmiddle, before)
-
-
-def relative_rows(order, source, target, me, high, offset):
-    stripe = source.shape[0] // len(order)
-    for place, relative in enumerate(order):
-        start = pl.multiple_of(jnp.bitwise_xor(me, relative) * stripe + offset, 16)
-        target[place * high : (place + 1) * high, :] = source[pl.ds(start, high), :]
-
-
-def plane_order(depth):
-    return [2 * z + x for x in range(2) for z in range(depth)]
+    )(normed, mixed, gproj, gmiddle)
+
+
+def relative_rows(source, target, me, depth):
+    high = source.shape[0] // (2 * depth)
+    for x in range(2):
+        for z in range(depth):
+            start = pl.multiple_of(jnp.bitwise_xor(me, 2 * z + x) * high, 16)
+            target[x, z * high : (z + 1) * high, :] = source[pl.ds(start, high), :]
 
 
 def ffn_weight_split_kernel(
-    me_ref, nffn_ref, grad_ref, gupper_ref, active_ref, up_one, up_zero, down_one, down_zero, turned, nffn_t, grad_t
+    me_ref, nffn_ref, grad_ref, gupper_ref, active_ref, other_ref, own_ref, turned, nffn_t, grad_t
 ):
     step = pl.program_id(0)
-    depth, high = up_one.shape[2:4]
+    _, _, depth, high, width = own_ref.shape
+    high = high // 2
 
     @pl.when(step == 0)
     def _():
         turned[...] = nffn_ref[...].T
-        relative_rows(plane_order(depth), turned, nffn_t, me_ref[0], high, 0)
+        relative_rows(turned, nffn_t, me_ref[0], depth)
         turned[...] = grad_ref[...].astype(BF).T
-        relative_rows(plane_order(depth), turned, grad_t, me_ref[0], high, 0)
-
-    gup = dot_nn(nffn_t[...], gupper_ref[...]).astype(BF)
-    gdown = dot_nn(grad_t[...], active_ref[...]).astype(BF)
-
-    @pl.when(step < 2)
+        relative_rows(turned, grad_t, me_ref[0], depth)
+
+    x, _ = plane(me_ref, step % 2, step // 2 % 2, 1 - step // 4)
+    gup = dot_nn(nffn_t[x], gupper_ref[...]).astype(BF).reshape(depth, high, width)
+    gdown = dot_nn(grad_t[x], active_ref[...]).astype(BF).reshape(depth, high, width)
+
+    @pl.when(step < 4)
     def _():
-        up_one[...] = gup.reshape(up_one.shape)
-        down_one[...] = gdown.reshape(down_one.shape)
-
-    @pl.when(step >= 2)
+        other_ref[0, 0, :, :high, :] = gup
+        other_ref[0, 0, :, high:, :] = gdown
+
+    @pl.when(step >= 4)
     def _():
-        up_zero[...] = gup.reshape(up_zero.shape)
-        down_zero[...] = gdown.reshape(down_zero.shape)
+        own_ref[0, 0, :, :high, :] = gup
+        own_ref[0, 0, :, high:, :] = gdown
 
 
 def ffn_weight_split(me, nffn, grad, gupper, active, depth):
@@ -539,89 +543,101 @@
     high = width // (2 * depth)
 
     def column(step, me):
-        return (0, jnp.bitwise_xor(me[1], 2 * jnp.bitwise_and(step, 1) + 1 - step // 2))
+        core = 1 - step // 4
+        _, y = plane(me, step % 2, step // 2 % 2, core)
+        return (0, jnp.bitwise_xor(me[1], 2 * y + core))
+
+    def place(begin):
+        def at(step, me):
+            step = jnp.clip(step - begin, 0, 3)
+            return (step // 2, step % 2, 0, 0, 0)
+
+        return at
 
     whole = pl.BlockSpec((rows, width), lambda i, me: (0, 0))
-    up_block, down_block = (1, 2, depth, high, piece), (2, 1, depth, high, piece)
+    block = (1, 1, depth, 2 * high, piece)
     return pl.pallas_call(
         ffn_weight_split_kernel,
         grid_spec=pltpu.PrefetchScalarGridSpec(
             num_scalar_prefetch=1,
-            grid=(4,),
+            grid=(8,),
             in_specs=[whole, whole, pl.BlockSpec((rows, piece), column), pl.BlockSpec((rows, piece), column)],
-            out_specs=[
-                pl.BlockSpec(up_block, lambda i, me: (jnp.minimum(i, 1), 0, 0, 0, 0)),
-                pl.BlockSpec(up_block, lambda i, me: (jnp.maximum(i - 2, 0), 0, 0, 0, 0)),
-                pl.BlockSpec(down_block, lambda i, me: (0, jnp.minimum(i, 1), 0, 0, 0)),
-                pl.BlockSpec(down_block, lambda i, me: (0, jnp.maximum(i - 2, 0), 0, 0, 0)),
-            ],
-            scratch_shapes=[pltpu.VMEM((width, rows), BF)] * 3,
+            out_specs=[pl.BlockSpec(block, place(0)), pl.BlockSpec(block, place(4))],
+            scratch_shapes=[pltpu.VMEM((width, rows), BF)] + [pltpu.VMEM((2, width // 2, rows), BF)] * 2,
         ),
-        out_shape=[jax.ShapeDtypeStruct((2, 2, depth, high, piece), BF)] * 4,
+        out_shape=[jax.ShapeDtypeStruct((2, 2, depth, 2 * high, piece), BF)] * 2,
         compiler_params=pltpu.CompilerParams(vmem_limit_bytes=VMEM_LIMIT),
         cost_estimate=pl.CostEstimate(flops=15 * 10**9, bytes_accessed=30 * 10**6, transcendentals=0),
         name="ffn_weight",
     )(me, nffn, grad, gupper, active)
 
 
-def attention_weight_split_kernel(
-    me_ref, normed_ref, mixed_ref, gproj_ref, gmiddle_ref,
-    a_one, a_zero, b_one, b_zero, normed_t, mixed_t, normed_r, mixed_r, joined,
-):
-    half = pl.program_id(0)
-    depth, high, width = a_one.shape[2:]
-
-    @pl.when(half == 0)
+def attention_weight_split_kernel(me_ref, normed_ref, mixed_ref, gproj_ref, gmiddle_ref, *refs):
+    other_ref, own_ref, turned, normed_t, mixed_t, joined, extra_s = refs[-7:]
+    extra_refs = refs[:-7]
+    x = pl.program_id(0)
+    _, _, depth, rows, width = own_ref.shape
+    high = width // (2 * depth)
+
+    @pl.when(x == 0)
     def _():
-        normed_t[...] = normed_ref[...].T
-        mixed_t[...] = mixed_ref[...].T
-
-    relative_rows(plane_order(depth), normed_t, normed_r, me_ref[0], high, half * high)
-    relative_rows(plane_order(depth), mixed_t, mixed_r, me_ref[0], high, half * high)
-    gqkv = dot_nn(normed_r[...], gproj_ref[...])
-    gout = dot_nn(mixed_r[...], gmiddle_ref[...].astype(BF))
+        turned[...] = normed_ref[...].T
+        relative_rows(turned, normed_t, me_ref[0], depth)
+        turned[...] = mixed_ref[...].T
+        relative_rows(turned, mixed_t, me_ref[0], depth)
+        if extra_refs:
+            share = width // 4
+            extra_s[...] = jnp.zeros_like(extra_s)
+            for index in range(2):
+                one_ref, more_ref, two_ref, hidden_ref = extra_refs[4 * index : 4 * index + 4]
+                sums = jnp.concatenate([one_ref[:4, :] + more_ref[:4, :], two_ref[:4, :]], axis=0)
+                for part in range(4):
+                    at = index * (width // 3)
+                    extra_s[part, :8, at : at + share] = sums[:, part * share : (part + 1) * share]
+                    extra_s[part, 8 + index : 9 + index, :] = hidden_ref[:, part * width : (part + 1) * width]
+
+    gqkv = dot_nn(normed_t[x], gproj_ref[...])
+    gout = dot_nn(mixed_t[x], gmiddle_ref[...].astype(BF))
     cut = gqkv.shape[1] // 4
     rest = gout.shape[1] // 4
     for part in range(4):
         qkv_part = gqkv[:, part * cut : (part + 1) * cut].astype(BF)
         out_part = gout[:, part * rest : (part + 1) * rest].astype(BF)
         joined[jnp.bitwise_xor(me_ref[1], part)] = jnp.concatenate([qkv_part, out_part], axis=1)
-
-    @pl.when(half == 0)
-    def _():
-        for y in range(2):
-            a_zero[y] = joined[2 * y].reshape(2, depth, high, width)
-            a_one[y] = joined[2 * y + 1].reshape(2, depth, high, width)
-
-    @pl.when(half == 1)
-    def _():
-        for y in range(2):
-            b_zero[:, y] = joined[2 * y].reshape(2, depth, high, width)
-            b_one[:, y] = joined[2 * y + 1].reshape(2, depth, high, width)
-
-
-def attention_weight_split(me, normed, mixed, gproj, gmiddle, depth):
+    for near in range(4):
+        y, core = divmod(near, 2)
+        first, second = plane(me_ref, x, y, core)
+        target = own_ref if core == 0 else other_ref
+        target[second, first, :, :high, :] = joined[near].reshape(depth, high, width)
+        if extra_refs:
+            extra = extra_s[jnp.bitwise_xor(me_ref[1], near)].astype(BF)
+            target[second, first, :, high:, :] = jnp.broadcast_to(extra[None], (depth,) + extra.shape)
+
+
+def attention_weight_split(me, normed, mixed, gproj, gmiddle, depth, extra=None):
     rows, width = normed.shape
-    high = width // (4 * depth)
-    whole = lambda array: pl.BlockSpec(array.shape, lambda i: (0, 0))
-    shape = (2, 2, depth, high, width)
+    high = width // (2 * depth)
+    whole = lambda array: pl.BlockSpec(array.shape, lambda i: (0,) * array.ndim)
+    extras = [] if extra is None else list(extra)
+    shape = (2, 2, depth, high + (0 if extra is None else 16), width)
+    operands = [normed, mixed, gproj, gmiddle] + extras
     return pl.pallas_call(
         attention_weight_split_kernel,
         grid=(2,),
-        in_specs=[pl.BlockSpec(memory_space=pltpu.SMEM), whole(normed), whole(mixed), whole(gproj), whole(gmiddle)],
-        out_specs=[pl.BlockSpec(shape, lambda i: (0, 0, 0, 0, 0))] * 4,
-        out_shape=[jax.ShapeDtypeStruct(shape, BF)] * 4,
+        in_specs=[pl.BlockSpec(memory_space=pltpu.SMEM)] + [whole(operand) for operand in operands],
+        out_specs=[pl.BlockSpec(shape, lambda i: (0, 0, 0, 0, 0))] * 2,
+        out_shape=[jax.ShapeDtypeStruct(shape, BF)] * 2,
         scratch_shapes=[
             pltpu.VMEM((width, rows), BF),
-            pltpu.VMEM((width, rows), BF),
-            pltpu.VMEM((width // 2, rows), BF),
-            pltpu.VMEM((width // 2, rows), BF),
+            pltpu.VMEM((2, width // 2, rows), BF),
+            pltpu.VMEM((2, width // 2, rows), BF),
             pltpu.VMEM((4, width // 2, width), BF),
+            pltpu.VMEM((4, 16, width), F32),
         ],
         compiler_params=pltpu.CompilerParams(vmem_limit_bytes=VMEM_LIMIT),
         cost_estimate=pl.CostEstimate(flops=10 * 10**9, bytes_accessed=20 * 10**6, transcendentals=0),
         name="attention_weight",
-    )(me, normed, mixed, gproj, gmiddle)
+    )(me, *operands)
 
 
 def pair_bias(slot_kind, slot_valid, across):
@@ -629,6 +645,12 @@
     partner = jnp.logical_not(same_kind) if across else same_kind
     allowed = jnp.logical_and(partner, slot_valid[:, None, :] > 0)
     return jnp.where(allowed, 0.0, -1e30).astype(F32)
+
+
+def ordered_vectors(small_one, small_two):
+    picked = (small_one, 0), (small_two, 0), (small_one, 1), (small_one, 2)
+    picked += (small_one, 3), (small_two, 3), (small_two, 1), (small_two, 2)
+    return jnp.stack([sums[row] for sums, row in picked])
 
 
 def adam_step(master, grad, moment_one, moment_two, factor, decayed):
@@ -642,12 +664,12 @@
 
 
 def gather_rows(pieces, sizes):
-    high, width = pieces.shape[1:]
+    kinds, high, width = pieces.shape
     rows = lax.all_gather(pieces.reshape(-1, width), ("dp", "tensor"), axis=0, tiled=False)
     if high % 16 == 0:
-        return [(("rows", offset * high), [rows]) for offset in (2, 0, 1)]
-    split = rows.reshape(sizes["dp"], sizes["tensor"], 3, high, width)
-    return [(("whole",), [jnp.swapaxes(split[:, :, kind], 0, 1).reshape(-1, width, width)]) for kind in (2, 0, 1)]
+        return [(("rows", kind * high), [rows]) for kind in range(kinds)]
+    split = rows.reshape(sizes["dp"], sizes["tensor"], kinds, high, width)
+    return [(("whole",), [jnp.swapaxes(split[:, :, kind], 0, 1).reshape(-1, width, width)]) for kind in range(kinds)]
 
 
 def scatter_rows(grad, sizes):
@@ -664,38 +686,55 @@
         self.sizes = sizes
         self.depth = sizes["dp"] // 2
 
-    def swap(self, axis, bits, value):
-        return lax.ppermute(value, axis, [(index, index ^ bits) for index in range(self.sizes[axis])])
+    def swap(self, value, partner):
+        dp, tensor = self.sizes["dp"], self.sizes["tensor"]
+        pairs = []
+        for i in range(dp):
+            for j in range(tensor):
+                far_i, far_j = partner(i, j)
+                pairs.append((i * tensor + j, far_i * tensor + far_j))
+        return lax.ppermute(value, ("dp", "tensor"), pairs)
+
+    def part(self, bits, value):
+        return self.swap(value, lambda i, j: (i, j ^ bits))
 
     def core(self, value):
-        return self.swap("tensor", 1, value)
-
-    def along(self, name, value):
-        return self.swap("dp", 1, value) if name == "x" else self.swap("tensor", 2, value)
-
-    def depths(self, values):
-        return [self.swap("dp", 2 * z, values[z]) for z in range(1, self.depth)]
+        return self.part(1, value)
+
+    def x(self, value):
+        return self.swap(value, lambda i, j: (i ^ 1, j))
+
+    def y(self, value):
+        return self.part(2, value)
 
     def diagonal(self, value):
-        dp, tensor = self.sizes["dp"], self.sizes["tensor"]
-        pairs = [(i * tensor + j, (i ^ 1) * tensor + (j ^ 2)) for i in range(dp) for j in range(tensor)]
-        return lax.ppermute(value, ("dp", "tensor"), pairs)
-
-    def rounds(self):
-        along_z = [functools.partial(self.swap, "dp", 2 * z) for z in range(1, self.depth)]
-        plane = [functools.partial(self.along, "x"), functools.partial(self.along, "y"), self.diagonal]
-        return along_z, plane, [self.core]
+        return self.swap(value, lambda i, j: (i ^ 1, j ^ 2))
+
+    def first(self, value):
+        return self.swap(value, lambda i, j: (i, j ^ 2) if j & 1 else (i ^ 1, j))
+
+    def second(self, value):
+        return self.swap(value, lambda i, j: (i ^ 1, j) if j & 1 else (i, j ^ 2))
+
+    def z(self, distance, value):
+        return self.swap(value, lambda i, j: (i ^ (2 * distance), j))
+
+    def z_sends(self, values):
+        return [(functools.partial(self.z, distance), values[distance]) for distance in range(1, self.depth)]
+
+    def gather_z(self, piece):
+        groups = [[2 * z + x for z in range(self.depth)] for x in range(2)]
+        return lax.all_gather(piece, "dp", axis=0, tiled=False, axis_index_groups=groups)
 
     def total(self, value):
-        for moves in self.rounds():
-            value = tree_sum([value] + [move(value) for move in moves])
+        value = value + self.core(value)
+        value = value + self.y(value)
+        value = value + self.x(value)
+        bit = 1
+        while bit < self.depth:
+            value = value + self.z(bit, value)
+            bit *= 2
         return value
-
-
-def tree_sum(values):
-    while len(values) > 1:
-        values = [values[at] + values[at + 1] for at in range(0, len(values), 2)]
-    return values[0]
 
 
 def tie(values, after):
@@ -703,111 +742,68 @@
 
 
 class Spread:
-    def __init__(self, exchange, first, second, row, pieces):
-        self.exchange, self.first, self.second, self.row = exchange, first, second, row
-        self.quad = jnp.stack(pieces)
-
-    def go_first(self, after=None):
-        quad = self.quad if after is None else tie(self.quad, after)
-        self.one = self.exchange.along(self.first, quad)
-        self.pair = jnp.stack([quad, self.one])
-        return self.one
-
-    def go_second(self):
-        self.two = self.exchange.along(self.second, self.pair)
-        return self.two
-
-    def go_core(self, after=None):
-        two = self.two if after is None else tie(self.two, after)
-        self.far = [self.exchange.core(self.pair), self.exchange.core(two)]
-
-    def units(self):
-        spot = lambda near, side, core: (near, side, core) if self.first == "x" else (side, near, core)
-        plan, arrays = [], []
-        for core, (pair, two) in enumerate(((self.pair, self.two), self.far)):
-            for side, value in enumerate((pair, two)):
-                plan.append((self.row, [spot(0, side, core), spot(1, side, core)]))
-                arrays.append(value)
-        return plan, arrays
-
-
-def near_weight(spreads):
-    units = [spread.units() for spread in spreads]
-    return (("near", sum([unit[0] for unit in units], [])), sum([unit[1] for unit in units], []))
+    def __init__(self, exchange, quad, fixed):
+        self.exchange, self.quad, self.fixed = exchange, quad, fixed
+
+    def go_first(self):
+        return [(self.exchange.first, self.quad)]
+
+    def go_second(self, came):
+        self.pair = jnp.stack([self.quad, came[0]])
+        return [(self.exchange.second, self.pair), (self.exchange.core, self.pair)]
+
+    def go_core(self, came):
+        self.two, self.far_pair = came
+        return [(self.exchange.core, self.two)]
+
+    def weight(self, came, offset=0):
+        positions = [[(0, second, core), (1, second, core)] for core in range(2) for second in range(2)]
+        arrays = [self.pair, self.two, self.far_pair, came[0]]
+        return (("near", offset, positions, self.fixed), arrays)
 
 
 class Reduce:
-    def __init__(self, exchange, first, second, other, own):
-        self.exchange, self.first, self.second, self.other, self.own = exchange, first, second, other, own
+    def __init__(self, exchange, other, own):
+        self.exchange, self.other, self.own = exchange, other, own
+
+    def wide(self, value):
+        return value.astype(F32)
 
     def go_core(self):
         return [(self.exchange.core, self.other)]
 
-    def took_core(self, came):
+    def go_second(self, came):
         self.came = came[0]
-
-    def wide(self, value):
-        return value.astype(F32)
-
-    def go_second(self):
         value = (self.wide(self.own[1]) + self.wide(self.came[1])).astype(BF)
-        return [(functools.partial(self.exchange.along, self.second), value)]
-
-    def took_second(self, came):
+        return [(self.exchange.second, value)]
+
+    def go_first(self, came):
         self.beside = came[0]
-
-    def near(self, at):
-        return self.wide(self.own[0, at]) + self.wide(self.came[0, at]) + self.wide(self.beside[at])
-
-    def go_first(self):
-        return [(functools.partial(self.exchange.along, self.first), self.near(1).astype(BF))]
-
-    def took_first(self, came):
-        self.ahead = came[0]
-        self.layers = [
-            self.wide(self.own[0, 0, z])
-            + self.wide(self.came[0, 0, z])
-            + self.wide(self.beside[0, z])
-            + self.wide(self.ahead[z])
-            for z in range(self.exchange.depth)
-        ]
-
-
-def depth_sends(exchange, reduces):
-    return [
-        (
-            functools.partial(exchange.swap, "dp", 2 * z),
-            jnp.concatenate([reduce.layers[z].astype(BF) for reduce in reduces], axis=0),
-        )
-        for z in range(1, exchange.depth)
-    ]
-
-
-def depth_total(reduces, came):
-    total = jnp.concatenate([reduce.layers[0] for reduce in reduces], axis=0)
-    for value in came:
-        total = total + value.astype(F32)
-    return total
+        value = self.wide(self.own[0, 1]) + self.wide(self.came[0, 1]) + self.wide(self.beside[1])
+        return [(self.exchange.first, value.astype(BF))]
+
+    def depths(self, came):
+        ahead = came[0]
+        return (
+            self.wide(self.own[0, 0]) + self.wide(self.came[0, 0]) + self.wide(self.beside[0]) + self.wide(ahead)
+        )
 
 
 class Lane:
     def __init__(self):
         self.last = None
-        self.flying = []
-
-    def send(self, sends):
+
+    def after_last(self, values):
+        return values if self.last is None else tie(values, self.last)
+
+    def step(self, sends, kernel=None, arrays=()):
         values = [value for _, value in sends]
-        if self.last is not None:
-            values = tie(values, self.last)
+        values, arrays = self.after_last((values, list(arrays)))
         came = [move(value) for (move, _), value in zip(sends, values)]
-        return came
-
-    def run(self, kernel, arrays, landed=()):
-        if self.last is not None:
-            arrays = tie(list(arrays), (self.last, list(landed)))
-        result = kernel(*arrays)
-        self.last = result[-1]
-        return result
+        results = [] if kernel is None else list(kernel(*arrays))
+        came, results = lax.optimization_barrier((came, results))
+        self.last = results[-1] if results else came[-1]
+        return came, results
 
 
 def shards(
@@ -839,168 +835,201 @@
     masks = [pair_bias(slot_kind, slot_valid, index == 0) for index in range(2)]
     lane = Lane()
     gathered = lambda index: gather_rows(
-        jnp.stack([up_pieces[index], down_pieces[index], attn_pieces[index]]), sizes
+        jnp.stack([attn_pieces[index], up_pieces[index], down_pieces[index]]), sizes
     )
-    attn_w, up_w, down_w = ([None, None] for _ in range(3))
-    attn_w[1], up_w[1], down_w[1] = gathered(1)
+    small = hidden = None
+    saved = [None, None]
+
+    def attention_forward_of(index, weight):
+        return lambda stream: attention_forward(
+            me, stream, masks[index], small[index], weight, block_pages, parts
+        )
+
+    def ffn_forward_of(index, up_w, down_w):
+        return lambda nffn, middle: ffn_forward(
+            me, nffn, middle, small[index], hidden[index : index + 1], up_w, down_w, block, parts
+        )
+
+    def ffn_backward_of(index):
+        kept = saved[index]
+        return lambda grad: ffn_backward(
+            me, grad, kept["slope"], kept["middle"], small[index], kept["up_w"], kept["down_w"], block, parts
+        )
+
+    def ffn_weight_of(index, grad):
+        kept = saved[index]
+        if split:
+            return lambda gupper: ffn_weight_split(
+                me, kept["nffn"], grad, gupper, kept["active"], exchange.depth
+            )
+        return lambda gupper: (ffn_weight(kept["nffn"], grad, gupper, kept["active"], stripes, parts),)
+
+    def attention_backward_of(index, begin, end, before=None):
+        kept = saved[index]
+        return lambda gmiddle: attention_backward(
+            gmiddle, kept["stream"], kept["proj"], kept["probs"], small[index], kept["weight"],
+            block_pages, begin, end, before,
+        )
+
+    def attention_weight_of(index, gmiddle, extra=None):
+        kept = saved[index]
+        if split:
+            return lambda gproj: attention_weight_split(
+                me, kept["normed"], kept["mixed"], gproj, gmiddle, exchange.depth, extra
+            )
+        return lambda gproj: (attention_weight(kept["normed"], kept["mixed"], gproj, gmiddle, stripes, parts),)
+
+    def keep(index, stream, attention, ffn, up_w, down_w):
+        middle, nffn, normed, proj, probs, mixed, qkv_w, out_w = attention
+        saved[index] = dict(
+            stream=stream, middle=middle, nffn=nffn, normed=normed, proj=proj, probs=probs, mixed=mixed,
+            weight=(qkv_w, out_w), active=ffn[1], slope=ffn[2], up_w=up_w, down_w=down_w,
+        )
+
     if split:
-        piece = attn_pieces[0]
-        depth_attn = [piece] + exchange.depths([piece] * exchange.depth)
+        depth = exchange.depth
+        late = exchange.gather_z(jnp.concatenate([attn_pieces[1], up_pieces[1], down_pieces[1]], axis=0))
         own_small = jnp.concatenate(
             [gain_weight, bias_weight, hidden_weight.reshape(2, -1, gain_weight.shape[2])], axis=1
         )
         own_small = lax.reduce_precision(own_small, 8, 7)
-        others = [exchange.swap("tensor", bits, own_small) for bits in range(1, 4)]
+        small_sends = [(functools.partial(exchange.part, bits), own_small) for bits in range(1, 4)]
+        came, _ = lane.step(exchange.z_sends([attn_pieces[0]] * depth) + small_sends)
+        attn_zero = Spread(exchange, jnp.stack([attn_pieces[0]] + came[: depth - 1]), False)
         mine = lax.axis_index("tensor")
         every = jnp.zeros((4,) + own_small.shape, F32)
-        for bits, value in enumerate([own_small] + others):
+        for bits, value in enumerate([own_small] + came[depth - 1 :]):
             every = lax.dynamic_update_slice_in_dim(every, value[None], jnp.bitwise_xor(mine, bits), 0)
         small = jnp.moveaxis(every[:, :, :8], 0, 2).reshape(2, 8, width)
         hidden = jnp.moveaxis(every[:, :, 8:], 0, 1).reshape(2, -1)
-
-        piece = jnp.concatenate([up_pieces[0], down_pieces[0]], axis=0)
-        piece = tie(piece, depth_attn[1:])
-        depth_ffn = [piece] + exchange.depths([piece] * exchange.depth)
-        attn_a = Spread(exchange, "x", "y", 0, [part[: high // 2] for part in depth_attn])
-        attn_b = Spread(exchange, "y", "x", high // 2, [part[high // 2 :] for part in depth_attn])
-        up_a = Spread(exchange, "x", "y", 0, [part[:high] for part in depth_ffn])
-        down_b = Spread(exchange, "y", "x", 0, [part[high:] for part in depth_ffn])
-        attn_a.go_first(others), attn_b.go_first(others)
-        second = [attn_a.go_second(), attn_b.go_second()]
-        attn_a.go_core(), attn_b.go_core()
-        ready = [up_a.go_first(second), down_b.go_first(second)]
-        attn_w[0] = near_weight([attn_a, attn_b])
-        tokens_in = tie(tokens, ready)
-        up_a.go_second(), down_b.go_second()
+        ffn_piece = jnp.concatenate([up_pieces[0], down_pieces[0]], axis=0)
+        ffn_sends = exchange.z_sends([ffn_piece] * depth)
+        middle_at = depth // 2 - 1
+        came, _ = lane.step(attn_zero.go_first() + ffn_sends[middle_at : middle_at + 1])
+        ffn_came = came[1:]
+        ffn_sends = ffn_sends[:middle_at] + ffn_sends[middle_at + 1 :]
+        came, _ = lane.step(attn_zero.go_second(came[:1]) + ffn_sends)
+        others = came[2:]
+        others.insert(middle_at, ffn_came[0])
+        ffn_zero = Spread(exchange, jnp.stack([ffn_piece] + others), False)
+        came, _ = lane.step(attn_zero.go_core(came[:2]) + ffn_zero.go_first())
+        attn_w = attn_zero.weight(came[:1])
+        came, attention = lane.step(ffn_zero.go_second(came[1:]), attention_forward_of(0, attn_w), [tokens])
+        attn_one = Spread(exchange, late[:, :high], True)
+        ffn_one = Spread(exchange, late[:, high:], True)
+        came, _ = lane.step(ffn_zero.go_core(came) + attn_one.go_first())
+        up_w, down_w = ffn_zero.weight(came[:1]), ffn_zero.weight(came[:1], high)
+        came, ffn = lane.step(
+            attn_one.go_second(came[1:]) + ffn_one.go_first(), ffn_forward_of(0, up_w, down_w), attention[1::-1]
+        )
+        keep(0, tokens, attention, ffn, up_w, down_w)
+        stream = ffn[0]
+        ffn_came = came[2:]
+        came, _ = lane.step(attn_one.go_core(came[:2]))
+        attn_w = attn_one.weight(came)
+        came, attention = lane.step(ffn_one.go_second(ffn_came), attention_forward_of(1, attn_w), [stream])
+        came, _ = lane.step(ffn_one.go_core(came))
+        up_w, down_w = ffn_one.weight(came), ffn_one.weight(came, high)
+        _, ffn = lane.step([], ffn_forward_of(1, up_w, down_w), attention[1::-1])
+        keep(1, stream, attention, ffn, up_w, down_w)
+        block_output = ffn[0]
+
+        _, (gupper, gmiddle, small_two, hidden_one) = lane.step([], ffn_backward_of(1), [out_grad])
+        _, grads = lane.step([], ffn_weight_of(1, out_grad), [gupper])
+        ffn_one = Reduce(exchange, *grads)
+        came, before = lane.step(ffn_one.go_core(), attention_backward_of(1, 0, middle_page), [gmiddle])
+        came, after = lane.step(
+            ffn_one.go_second(came), attention_backward_of(1, middle_page, pages, before[:2]), [gmiddle]
+        )
+        grad, gproj = after[:2]
+        sums_one = (before[2], after[2], small_two, hidden_one)
+        came, grads = lane.step(ffn_one.go_first(came), attention_weight_of(1, gmiddle), [gproj])
+        layers = ffn_one.depths(came)
+        attn_one = Reduce(exchange, *grads)
+        came, results = lane.step(attn_one.go_core(), ffn_backward_of(0), [grad])
+        gupper, gmiddle, small_two, hidden_zero = results
+        came, grads = lane.step(attn_one.go_second(came), ffn_weight_of(0, grad), [gupper])
+        ffn_zero = Reduce(exchange, *grads)
+        came, before = lane.step(
+            ffn_zero.go_core() + attn_one.go_first(came), attention_backward_of(0, 0, middle_page), [gmiddle]
+        )
+        layers = jnp.concatenate([attn_one.depths(came[1:]), layers], axis=1)
+        late_sends = exchange.z_sends([layers[z].astype(BF) for z in range(depth)])
+        late_sends = late_sends[middle_at : middle_at + 1] + late_sends[:middle_at] + late_sends[middle_at + 1 :]
+        came, after = lane.step(
+            ffn_zero.go_second(came[:1]) + late_sends[:1],
+            attention_backward_of(0, middle_page, pages, before[:2]),
+            [gmiddle],
+        )
+        late_came = came[1:]
+        input_grad, gproj = after[:2]
+        came, grads = lane.step(
+            ffn_zero.go_first(came[:1]) + late_sends[1:],
+            attention_weight_of(0, gmiddle, (before[2], after[2], small_two, hidden_zero) + sums_one),
+            [gproj],
+        )
+        total = layers[0] + sum(value.astype(F32) for value in late_came + came[1:])
+        grad_attn, grad_up, grad_down = ([None, total[at : at + high]] for at in (0, high, 2 * high))
+        layers = ffn_zero.depths(came[:1])
+        ffn_sends = exchange.z_sends([layers[z].astype(BF) for z in range(depth)])
+        ffn_sends = ffn_sends[middle_at : middle_at + 1] + ffn_sends[:middle_at] + ffn_sends[middle_at + 1 :]
+        attn_zero = Reduce(exchange, *grads)
+        came, _ = lane.step(attn_zero.go_core())
+        came, _ = lane.step(attn_zero.go_second(came) + ffn_sends[:1])
+        ffn_came = came[1:]
+        came, _ = lane.step(attn_zero.go_first(came[:1]) + ffn_sends[1:])
+        total = layers[0] + sum(value.astype(F32) for value in ffn_came + came[1:])
+        grad_up[0], grad_down[0] = total[:high], total[high:]
+        layers = attn_zero.depths(came[:1])
+        came, _ = lane.step(exchange.z_sends([layers[z].astype(BF) for z in range(depth)]))
+        total = layers[0] + sum(value.astype(F32) for value in came)
+        grad_attn[0] = total[:high]
+        share = width // parts
+        vectors = []
+        for at in (0, width // 3):
+            sums = total[high : high + 8, at : at + share]
+            vectors.append(ordered_vectors(sums[:4], sums[4:]))
+        vectors = jnp.stack(vectors)
+        grad_hidden = total[high + 8 : high + 10]
     else:
         small = jnp.concatenate([gain_weight, bias_weight], axis=1).astype(BF)
         small = lax.all_gather(small, "tensor", axis=2, tiled=True).astype(F32)
         hidden = lax.all_gather(hidden_weight.astype(BF), "tensor", axis=1, tiled=True).astype(F32)
-        attn_w[0], up_w[0], down_w[0] = gathered(0)
-        tokens_in = tokens
-
-    stream = tokens_in
-    saved = []
-    for index in range(2):
-        middle, nffn, normed, proj, probs, mixed, qkv_w, out_w = attention_forward(
-            me, stream, masks[index], small[index], attn_w[index], block_pages, parts
-        )
-        if split and index == 0:
-            up_a.go_core(nffn), down_b.go_core(nffn)
-            up_w[0] = near_weight([up_a])
-            down_w[0] = near_weight([down_b])
-        result, active, slope = ffn_forward(
-            me, nffn, middle, small[index], hidden[index : index + 1], up_w[index], down_w[index], block, parts
-        )
-        saved.append((stream, middle, nffn, normed, proj, probs, mixed, active, slope, (qkv_w, out_w)))
-        stream = result
-    block_output = stream
-
-    def run_ffn_backward(index, grad, landed=()):
-        _, middle, _, _, _, _, _, _, slope, _ = saved[index]
-        kernel = lambda grad: ffn_backward(
-            me, grad, slope, middle, small[index], up_w[index], down_w[index], block, parts
-        )
-        return lane.run(kernel, [grad], landed)
-
-    def run_ffn_weight(index, grad, gupper, landed=()):
-        _, _, nffn, _, _, _, _, active, _, _ = saved[index]
-        if split and index == 0:
-            kernel = lambda gupper: ffn_weight_split(me, nffn, grad, gupper, active, exchange.depth)
-        else:
-            kernel = lambda gupper: (ffn_weight(nffn, grad, gupper, active, stripes, parts),)
-        return lane.run(kernel, [gupper], landed)
-
-    def run_attention_backward(index, gmiddle, begin, end, before, landed=()):
-        stream, _, _, _, proj, probs, _, _, _, weight = saved[index]
-        kernel = lambda gmiddle: attention_backward(
-            gmiddle, stream, proj, probs, small[index], weight, block_pages, begin, end, before
-        )
-        return lane.run(kernel, [gmiddle], landed)
-
-    def run_attention_weight(index, gproj, gmiddle, before=None, landed=()):
-        _, _, _, normed, _, _, mixed, _, _, _ = saved[index]
-        if split and index == 0:
-            kernel = lambda gproj: attention_weight_split(me, normed, mixed, gproj, gmiddle, exchange.depth)
-        else:
-            kernel = lambda gproj: (attention_weight(normed, mixed, gproj, gmiddle, before),)
-        return lane.run(kernel, [gproj], landed)
-
-    attn_g, up_g, down_g, small_g, hidden_g = ([None, None] for _ in range(5))
-    grad = out_grad
-    for index in (1, 0):
-        gupper, gmiddle, small_two, ghidden = run_ffn_backward(index, grad)
-        if split and index == 0:
-            up_one, up_zero, down_one, down_zero = run_ffn_weight(index, grad, gupper)
-            ffn = [Reduce(exchange, "x", "y", up_one, up_zero), Reduce(exchange, "y", "x", down_one, down_zero)]
-            came = lane.send(ffn[0].go_core() + ffn[1].go_core())
-            before = run_attention_backward(index, gmiddle, 0, middle_page, None)
-            ffn[0].took_core(came[:1]), ffn[1].took_core(came[1:])
-            landed = came
-            came = lane.send(ffn[0].go_second() + ffn[1].go_second())
-            after = run_attention_backward(index, gmiddle, middle_page, pages, before[:2], landed)
-            ffn[0].took_second(came[:1]), ffn[1].took_second(came[1:])
-            next_grad, gproj = after[:2]
-            small_one = before[2] + after[2]
-            landed = came
-            came = lane.send(ffn[0].go_first() + ffn[1].go_first())
-            a_one, a_zero, b_one, b_zero = run_attention_weight(index, gproj, gmiddle, None, landed)
-            ffn[0].took_first(came[:1]), ffn[1].took_first(came[1:2])
-            attn = [Reduce(exchange, "x", "y", a_one, a_zero), Reduce(exchange, "y", "x", b_one, b_zero)]
-        else:
-            (gffn,) = run_ffn_weight(index, grad, gupper)
-            next_grad, gproj, small_one = run_attention_backward(index, gmiddle, 0, pages, None)
-            (both,) = run_attention_weight(index, gproj, gmiddle, gffn)
-            up_g[index], down_g[index], attn_g[index] = scatter_rows(both, sizes)
-        grad = next_grad
-        small_g[index] = jnp.concatenate([small_one, small_two], axis=0)
-        hidden_g[index] = ghidden
-    input_grad = grad
-
-    if split:
-        whole = jnp.concatenate(small_g + [value.reshape(-1, width) for value in hidden_g], axis=0)
-        along_z, plane, across = exchange.rounds()
-        count = exchange.depth - 1
-        came = lane.send(attn[0].go_core() + attn[1].go_core() + depth_sends(exchange, ffn) + [(move, whole) for move in along_z])
-        attn[0].took_core(came[:1]), attn[1].took_core(came[1:2])
-        total = depth_total(ffn, came[2 : 2 + count])
-        up_g[0], down_g[0] = total[:high], total[high:]
-        whole = tree_sum([whole] + came[2 + count :])
-        came = lane.send(attn[0].go_second() + attn[1].go_second() + [(move, whole) for move in plane])
-        attn[0].took_second(came[:1]), attn[1].took_second(came[1:2])
-        whole = tree_sum([whole] + came[2:])
-        came = lane.send(attn[0].go_first() + attn[1].go_first() + [(move, whole) for move in across])
-        attn[0].took_first(came[:1]), attn[1].took_first(came[1:2])
-        whole = tree_sum([whole] + came[2:])
-        attn_g[0] = depth_total(attn, lane.send(depth_sends(exchange, attn)))
-        vectors = whole[:32].reshape(2, 16, width)
-        grad_hidden = whole[32:].reshape(2, -1)
-    else:
-        vectors, grad_hidden = lax.psum((jnp.stack(small_g), jnp.concatenate(hidden_g, axis=0)), ("dp", "tensor"))
-    grad_gain = jnp.stack([vectors[:, 0], vectors[:, 8]], axis=1)
-    grad_bias = jnp.stack([vectors[:, row] for row in (1, 2, 3, 11, 9, 10)], axis=1)
-    shared_squares = (
-        jnp.sum(grad_gain * grad_gain) + jnp.sum(grad_bias * grad_bias) + jnp.sum(grad_hidden * grad_hidden)
-    )
-    at = lax.axis_index("tensor")
-    slice_of = lambda whole, axis: lax.dynamic_slice_in_dim(
-        whole, at * (whole.shape[axis] // parts), whole.shape[axis] // parts, axis
-    )
-    grad_gain = slice_of(grad_gain, 2)
-    grad_bias = slice_of(grad_bias, 2)
-    grad_hidden = slice_of(grad_hidden, 1)
-    grad_attn = jnp.stack(attn_g)
-    grad_up = jnp.stack(up_g)
-    grad_down = jnp.stack(down_g)
+        stream = tokens
+        for index in range(2):
+            attn_w, up_w, down_w = gathered(index)
+            attention = attention_forward_of(index, attn_w)(stream)
+            ffn = ffn_forward_of(index, up_w, down_w)(*attention[1::-1])
+            keep(index, stream, attention, ffn, up_w, down_w)
+            stream = ffn[0]
+        block_output = stream
+        grad = out_grad
+        grad_attn, grad_up, grad_down, vectors, grad_hidden = ([None, None] for _ in range(5))
+        for index in (1, 0):
+            gupper, gmiddle, small_two, grad_hidden[index] = ffn_backward_of(index)(grad)
+            (gffn,) = ffn_weight_of(index, grad)(gupper)
+            grad_up[index], grad_down[index] = scatter_rows(gffn, sizes)
+            grad, gproj, small_one = attention_backward_of(index, 0, pages)(gmiddle)
+            (grad_attn[index],) = scatter_rows(attention_weight_of(index, gmiddle)(gproj)[0], sizes)
+            vectors[index] = ordered_vectors(small_one, small_two)
+        input_grad = grad
+        vectors, grad_hidden = lax.psum((jnp.stack(vectors), jnp.concatenate(grad_hidden, axis=0)), ("dp", "tensor"))
+        at = lax.axis_index("tensor")
+        slice_of = lambda whole: lax.dynamic_slice_in_dim(
+            whole, at * (whole.shape[-1] // parts), whole.shape[-1] // parts, whole.ndim - 1
+        )
+        vectors, grad_hidden = slice_of(vectors), slice_of(grad_hidden)
+    grad_gain, grad_bias = vectors[:, :2], vectors[:, 2:]
+    grad_attn, grad_up, grad_down = jnp.stack(grad_attn), jnp.stack(grad_up), jnp.stack(grad_down)
+    shared_squares = jnp.sum(vectors * vectors) + jnp.sum(grad_hidden * grad_hidden)
     local_squares = (
         jnp.sum(grad_attn * grad_attn) + jnp.sum(grad_up * grad_up) + jnp.sum(grad_down * grad_down)
-    )
+    ) + jnp.where(lax.axis_index("dp") == 0, shared_squares, 0.0)
     grad_down = jnp.swapaxes(grad_down, 1, 2)
     if split:
-        local_squares = exchange.total(local_squares.reshape(1, 1))[0, 0]
+        total_squares = exchange.total(local_squares.reshape(1, 1))[0, 0]
     else:
-        local_squares = lax.psum(local_squares, ("dp", "tensor"))
-    total_squares = local_squares + shared_squares
+        total_squares = lax.psum(local_squares, ("dp", "tensor"))
     grad_norm = jnp.sqrt(total_squares)
     factor = clip_norm / jnp.maximum(grad_norm, clip_norm)
     masters = (qkv_weight, out_weight, up_weight, down_weight, gain_weight, bias_weight, hidden_weight)

time: 577 us -> 554 us (0.960)
  starting transfers between devices: 78.2 us -> 54.9 us
  waiting for transfers between devices: 167 us -> 146 us
  Pallas kernels: 242 us -> 256 us
  other arithmetic: 44.6 us -> 50.7 us
    pallas_call x2 -> x0, Pallas kernels: 26.5 us -> none  [the longest x1 15.8 us: ffn_weight(): pl.pallas_call(ffn_weight_kernel, grid=(parts,), in_specs=[whole, whole,...]
    ppermute x57 -> x51, waiting for transfers between devices: 167 us -> 141 us  [swap(): return lax.ppermute(value, ('dp', 'tensor'), pairs)]
    ppermute x57 -> x51, starting transfers between devices: 78.1 us -> 54.9 us  [swap(): return lax.ppermute(value, ('dp', 'tensor'), pairs)]
    pallas_call x1 -> x2, Pallas kernels: 19.8 us -> 42.3 us  [ffn_weight_split(): pl.pallas_call(ffn_weight_split_kernel, grid_spec=pltpu.PrefetchScalarGri...]
    pallas_call x1 -> x2, Pallas kernels: 13.5 us -> 27.3 us  [attention_weight_split(): pl.pallas_call(attention_weight_split_kernel, grid=(2,), in_specs=[pl.Blo...]
    concatenate x1 -> x0, local copies, waits for them, and re-layouts: 6.71 us -> none  [shards(): jnp.concatenate(small_g + [value.reshape(-1, width) for value in hidden_g...]
    pallas_call x3 -> x4, Pallas kernels: 54.9 us -> 59 us  [attention_backward(): pl.pallas_call(attention_backward_kernel, grid=((end - begin) // block_pa...]
  transfers between devices with their start and end apart: 59 -> 52, of which waited for: 23 -> 31; matrix products, arithmetic and copies ran while one was open for 8% -> 5% of each run, Pallas kernels for 22% -> 35%
where the time goes in v2:
time: 554 us; the launch traced here: 549 us
  Pallas kernels  256 us (46%)
  waiting for transfers between devices  146 us (26%)
  starting transfers between devices  54.9 us (10%)
  other arithmetic  50.7 us (9%)
  between operations  22.6 us (4%)
  local copies, waits for them, and re-layouts  18.8 us (3%)
    ppermute x51, waiting for transfers between devices, swap(): return lax.ppermute(value, ('dp', 'tensor'), pairs)  141 us
    pallas_call x4, Pallas kernels, attention_backward(): pl.pallas_call(attention_backward_kernel, grid=((end - begin) // block_pa...  59 us
    ppermute x51, starting transfers between devices, swap(): return lax.ppermute(value, ('dp', 'tensor'), pairs)  54.9 us
    pallas_call x2, Pallas kernels, ffn_forward(): pl.pallas_call(functools.partial(ffn_forward_kernel, (up_w[0], down_w[0])...  43.6 us
    pallas_call x2, Pallas kernels, ffn_weight_split(): pl.pallas_call(ffn_weight_split_kernel, grid_spec=pltpu.PrefetchScalarGri...  42.3 us
    pallas_call x2, Pallas kernels, attention_forward(): pl.pallas_call(functools.partial(attention_forward_kernel, plan), grid=(p...  42.2 us
    pallas_call x2, Pallas kernels, ffn_backward(): pl.pallas_call(functools.partial(ffn_backward_kernel, (up_w[0], down_w[0]...  41.6 us
    pallas_call x2, Pallas kernels, attention_weight_split(): pl.pallas_call(attention_weight_split_kernel, grid=(2,), in_specs=[pl.Blo...  27.3 us
  transfers between devices with their start and end apart: 52, of which 31 were waited for; matrix products, arithmetic and copies ran while one was open for 5% of the time, Pallas kernels for 35%

profile of v2, /device:TPU:0, one launch (start us, length us, event | category | flops | bytes accessed | tf_op | source)
XLA Modules:
  0.0 549.3 jit_solution(3425400704999868458)
XLA Ops:
  23.4 7.9 %collective-permute-done.1 = bf16[96,768]{1,0:T(8,128)(2,1)S(1)} collective-permute-done((bf16[96,768]{1,0:T(8,128)(2,1)S(1)}, bf16[96,768]{1,0:T(8,128)(2,1)S(1)}, u32[]{:S(2)}, u32[]{:S(2)}) %collective-permute-start.1) | collective-permute-done | bytes 147488 | tf_op jit(solution)/shard_map/ppermute | solution.py:696
  33.0 15.4 %collective-permute-done.7 = bf16[192,768]{1,0:T(8,128)(2,1)S(1)} collective-permute-done((bf16[192,768]{1,0:T(8,128)(2,1)S(1)}, bf16[192,768]{1,0:T(8,128)(2,1)S(1)}, u32[]{:S(2)}, u32[]{:S(2)}) %collective-permute-start.7) | collective-permute-done | bytes 294944 | tf_op jit(solution)/shard_map/ppermute | solution.py:696
  52.1 12.0 %collective-permute-done.10 = bf16[192,768]{1,0:T(8,128)(2,1)S(1)} collective-permute-done((bf16[192,768]{1,0:T(8,128)(2,1)S(1)}, bf16[192,768]{1,0:T(8,128)(2,1)S(1)}, u32[]{:S(2)}, u32[]{:S(2)}) %collective-permute-start.10) | collective-permute-done | bytes 294944 | tf_op jit(solution)/shard_map/ppermute | solution.py:696
  64.1 6.5 %collective-permute-done.11 = bf16[192,768]{1,0:T(8,128)(2,1)S(1)} collective-permute-done((bf16[192,768]{1,0:T(8,128)(2,1)S(1)}, bf16[192,768]{1,0:T(8,128)(2,1)S(1)}, u32[]{:S(2)}, u32[]{:S(2)}) %collective-permute-start.11) | collective-permute-done | bytes 294944 | tf_op jit(solution)/shard_map/ppermute | solution.py:696
  74.1 13.2 %collective-permute-done.13 = bf16[4,192,768]{2,1,0:T(8,128)(2,1)} collective-permute-done((bf16[4,192,768]{2,1,0:T(8,128)(2,1)S(1)}, bf16[4,192,768]{2,1,0:T(8,128)(2,1)}, u32[]{:S(2)}, u32[]{:S(2)}) %collective-permute-start.13) | collective-permute-done | bytes 1179680 | tf_op jit(solution)/shard_map/ppermute | solution.py:696
  97.4 21.2 %attention_forward.2 = (f32[1024,768]{1,0:T(8,128)}, bf16[1024,768]{1,0:T(8,128)(2,1)}, bf16[1024,768]{1,0:T(8,128)(2,1)}, bf16[1024,2304]{1,0:T(8,128)(2,1)}, b...) custom-call(s32[2]{0:T(128)} %pad_add_fusion.me_ref, ...), custom_call_target="tpu_custom_call" | custom-call | flops 20000000000 | bytes 30000000 | tf_op jit(solution)/shard_map/attention_forward/pallas_call | solution.py:181
  122.8 5.8 %collective-permute-done.17 = bf16[4,96,768]{2,1,0:T(8,128)(2,1)S(1)} collective-permute-done((bf16[4,96,768]{2,1,0:T(8,128)(2,1)S(1)}, bf16[4,96,768]{2,1,0:T(8,128)(2,1)S(1)}, u32[]{:S(2)}, u32[]{:S(2)}) %collective-permute-start.17) | collective-permute-done | bytes 589856 | tf_op jit(solution)/shard_map/ppermute | solution.py:696
  131.6 21.6 %ffn_forward.2 = (f32[1024,768]{1,0:T(8,128)}, bf16[1024,3072]{1,0:T(8,128)(2,1)}, bf16[1024,3072]{1,0:T(8,128)(2,1)}) custom-call(s32[2]{0:T(128)} %pad_add_fusion.me_ref, bf16[1024,768]{1,0:T(8,128)(2,1)} %get-tuple-element.264.nffn_ref, f32[1024,768]{1,0:T(8,128)} %get-tuple-element.265.middle_ref, f32[8,768]{1,0:T(8,128)} %squeeze.28.vec_ref, ...), custom_call_target="tpu_custom_call" | custom-call | flops 15000000512 | bytes 30000000 | tf_op jit(solution)/shard_map/ffn_forward/pallas_call | solution.py:254
  163.7 21.0 %attention_forward.3 = (f32[1024,768]{1,0:T(8,128)}, bf16[1024,768]{1,0:T(8,128)(2,1)}, bf16[1024,768]{1,0:T(8,128)(2,1)}, bf16[1024,2304]{1,0:T(8,128)(2,1)}, b...) custom-call(s32[2]{0:T(128)} %pad_add_fusion.me_ref, ...), custom_call_target="tpu_custom_call" | custom-call | flops 20000000000 | bytes 30000000 | tf_op jit(solution)/shard_map/attention_forward/pallas_call | solution.py:181
  196.4 22.1 %ffn_forward.3 = (f32[1024,768]{1,0:T(8,128)}, bf16[1024,3072]{1,0:T(8,128)(2,1)}, bf16[1024,3072]{1,0:T(8,128)(2,1)}) custom-call(s32[2]{0:T(128)} %pad_add_fusion.me_ref, bf16[1024,768]{1,0:T(8,128)(2,1)} %get-tuple-element.293.nffn_ref, f32[1024,768]{1,0:T(8,128)} %get-tuple-element.294.middle_ref, f32[8,768]{1,0:T(8,128)} %squeeze.29.vec_ref, ...), custom_call_target="tpu_custom_call" | custom-call | flops 15000000512 | bytes 30000000 | tf_op jit(solution)/shard_map/ffn_forward/pallas_call | solution.py:254
  218.5 20.5 %ffn_backward.2 = (bf16[1024,3072]{1,0:T(8,128)(2,1)}, f32[1024,768]{1,0:T(8,128)}, f32[8,768]{1,0:T(8,128)}, f32[1,3072]{1,0:T(1,128)}) custom-call(s32[2]{0:T(128)} %pad_add_fusion.me_ref, bf16[1024,768]{1,0:T(8,128)(2,1)} %grad_ref.2, bf16[1024,3072]{1,0:T(8,128)(2,1)} %get-tuple-element.297.slope_ref, f32[1024,768]{1,0:T(8,128)} %get-tuple-element.294.middle_ref, ...), custom_call_target="tpu_custom_call" | custom-call | flops 15000000512 | bytes 30000000 | tf_op jit(solution)/shard_map/ffn_backward/pallas_call | solution.py:318
  239.0 21.0 %ffn_weight.2 = (bf16[2,2,4,192,768]{4,3,2,1,0:T(8,128)(2,1)}, bf16[2,2,4,192,768]{4,3,2,1,0:T(8,128)(2,1)}) custom-call(s32[2]{0:T(128)} %pad_add_fusion.me_ref, bf16[1024,768]{1,0:T(8,128)(2,1)} %get-tuple-element.293.nffn_ref, bf16[1024,768]{1,0:T(8,128)(2,1)} %grad_ref.2, bf16[1024,3072]{1,0:T(8,128)(2,1)} %get-tuple-element.301.gupper_ref, ...), custom_call_target="tpu_custom_call" | custom-call | flops 15000000512 | bytes 30000000 | tf_op jit(solution)/shard_map/ffn_weight/pallas_call | solution.py:559
  260.4 9.6 %attention_backward.4 = (f32[1024,768]{1,0:T(8,128)}, bf16[1024,2304]{1,0:T(8,128)(2,1)}, f32[8,768]{1,0:T(8,128)}) custom-call(f32[1024,768]{1,0:T(8,128)} %get-tuple-element.317.gmiddle_ref, f32[1024,768]{1,0:T(8,128)} %get-tuple-element.278.stream_ref, bf16[1024,2304]{1,0:T(8,128)(2,1)} %get-tuple-element.308.proj_ref, ...), custom_call_target="tpu_custom_call" | custom-call | flops 15000000512 | bytes 20000000 | tf_op jit(solution)/shard_map/attention_backward/pallas_call | solution.py:442
  274.1 20.0 %attention_backward.5 = (f32[1024,768]{1,0:T(8,128)}, bf16[1024,2304]{1,0:T(8,128)(2,1)}, f32[8,768]{1,0:T(8,128)}) custom-call(f32[1024,768]{1,0:T(8,128)} %get-tuple-element.317.gmiddle_ref, f32[1024,768]{1,0:T(8,128)} %get-tuple-element.278.stream_ref, ...), custom_call_target="tpu_custom_call", output_to_operand_aliasing={{0}: (7, {}), {1}: (8, {})} | custom-call | flops 15000000512 | bytes 20000000 | tf_op jit(solution)/shard_map/attention_backward/pallas_call | solution.py:442
  294.1 7.2 %collective-permute-done.26 = bf16[2,4,192,768]{3,2,1,0:T(8,128)(2,1)} collective-permute-done((bf16[2,4,192,768]{3,2,1,0:T(8,128)(2,1)S(1)}, bf16[2,4,192,768]{3,2,1,0:T(8,128)(2,1)}, u32[]{:S(2)}, u32[]{:S(2)}) %collective-permute-start.26) | collective-permute-done | bytes 2359328 | tf_op jit(solution)/shard_map/ppermute | solution.py:696
  304.8 13.4 %attention_weight.2 = (bf16[2,2,4,96,768]{4,3,2,1,0:T(8,128)(2,1)}, bf16[2,2,4,96,768]{4,3,2,1,0:T(8,128)(2,1)}) custom-call(s32[2]{0:T(128)} %pad_add_fusion.me_ref, bf16[1024,768]{1,0:T(8,128)(2,1)} %get-tuple-element.327.normed_ref, bf16[1024,768]{1,0:T(8,128)(2,1)} %get-tuple-element.328.mixed_ref, bf16[1024,2304]{1,0:T(8,128)(2,1)} %get-tuple-element.329.gproj_ref, ...), custom_call_target="tpu_custom_call" | custom-call | flops 10000000000 | bytes 20000000 | tf_op jit(solution)/shard_map/attention_weight/pallas_call | solution.py:624
  319.6 21.0 %ffn_backward.3 = (bf16[1024,3072]{1,0:T(8,128)(2,1)}, f32[1024,768]{1,0:T(8,128)}, f32[8,768]{1,0:T(8,128)}, f32[1,3072]{1,0:T(1,128)}) custom-call(s32[2]{0:T(128)} %pad_add_fusion.me_ref, f32[1024,768]{1,0:T(8,128)} %get-tuple-element.336.grad_ref, bf16[1024,3072]{1,0:T(8,128)(2,1)} %get-tuple-element.274.slope_ref, ...), custom_call_target="tpu_custom_call" | custom-call | flops 15000000512 | bytes 30000000 | tf_op jit(solution)/shard_map/ffn_backward/pallas_call | solution.py:318
  345.0 21.3 %ffn_weight.3 = (bf16[2,2,4,192,768]{4,3,2,1,0:T(8,128)(2,1)}, bf16[2,2,4,192,768]{4,3,2,1,0:T(8,128)(2,1)}) custom-call(s32[2]{0:T(128)} %pad_add_fusion.me_ref, bf16[1024,768]{1,0:T(8,128)(2,1)} %get-tuple-element.264.nffn_ref, f32[1024,768]{1,0:T(8,128)} %get-tuple-element.336.grad_ref, bf16[1024,3072]{1,0:T(8,128)(2,1)} %get-tuple-element.345.gupper_ref, ...), custom_call_target="tpu_custom_call" | custom-call | flops 15000000512 | bytes 30000000 | tf_op jit(solution)/shard_map/ffn_weight/pallas_call | solution.py:559
  372.4 9.3 %attention_backward.6 = (f32[1024,768]{1,0:T(8,128)}, bf16[1024,2304]{1,0:T(8,128)(2,1)}, f32[8,768]{1,0:T(8,128)}) custom-call(f32[1024,768]{1,0:T(8,128)} %get-tuple-element.368.gmiddle_ref, bf16[1024,768]{1,0:T(8,128)(2,1)} %stream_ref.4, bf16[1024,2304]{1,0:T(8,128)(2,1)} %get-tuple-element.356.proj_ref, ...), custom_call_target="tpu_custom_call" | custom-call | flops 15000000512 | bytes 20000000 | tf_op jit(solution)/shard_map/attention_backward/pallas_call | solution.py:442
  391.2 20.1 %attention_backward.7 = (f32[1024,768]{1,0:T(8,128)}, bf16[1024,2304]{1,0:T(8,128)(2,1)}, f32[8,768]{1,0:T(8,128)}) custom-call(f32[1024,768]{1,0:T(8,128)} %get-tuple-element.368.gmiddle_ref, bf16[1024,768]{1,0:T(8,128)(2,1)} %stream_ref.4, bf16[1024,2304]{1,0:T(8,128)(2,1)} %get-tuple-element.356.proj_ref, ...), custom_call_target="tpu_custom_call", output_to_operand_aliasing={{0}: (7, {}), {1}: (8, {})} | custom-call | flops 15000000512 | bytes 20000000 | tf_op jit(solution)/shard_map/attention_backward/pallas_call | solution.py:442
  412.5 6.1 %collective-permute-done.32 = bf16[2,4,192,768]{3,2,1,0:T(8,128)(2,1)} collective-permute-done((bf16[2,4,192,768]{3,2,1,0:T(8,128)(2,1)}, bf16[2,4,192,768]{3,2,1,0:T(8,128)(2,1)}, u32[]{:S(2)}, u32[]{:S(2)}) %collective-permute-start.32) | collective-permute-done | bytes 2359328 | tf_op jit(solution)/shard_map/ppermute | solution.py:696
  425.4 13.9 %attention_weight.3 = (bf16[2,2,4,112,768]{4,3,2,1,0:T(8,128)(2,1)}, bf16[2,2,4,112,768]{4,3,2,1,0:T(8,128)(2,1)}) custom-call(s32[2]{0:T(128)} %pad_add_fusion.me_ref, bf16[1024,768]{1,0:T(8,128)(2,1)} %get-tuple-element.381.normed_ref, bf16[1024,768]{1,0:T(8,128)(2,1)} %get-tuple-element.382.mixed_ref, bf16[1024,2304]{1,0:T(8,128)(2,1)} %get-tuple-element.383.gproj_ref, ...), custom_call_target="tpu_custom_call" | custom-call | flops 10000000000 | bytes 20000000 | tf_op jit(solution)/shard_map/attention_weight/pallas_call | solution.py:624
  452.1 15.2 %collective-permute-done.39 = bf16[192,768]{1,0:T(8,128)(2,1)S(1)} collective-permute-done((bf16[192,768]{1,0:T(8,128)(2,1)S(1)}, bf16[192,768]{1,0:T(8,128)(2,1)S(1)}, u32[]{:S(2)}, u32[]{:S(2)}) %collective-permute-start.39) | collective-permute-done | bytes 294944 | tf_op jit(solution)/shard_map/ppermute | solution.py:696
  480.3 7.2 %collective-permute-done.42 = bf16[192,768]{1,0:T(8,128)(2,1)S(1)} collective-permute-done((bf16[192,768]{1,0:T(8,128)(2,1)}, bf16[192,768]{1,0:T(8,128)(2,1)S(1)}, u32[]{:S(2)}, u32[]{:S(2)}) %collective-permute-start.42) | collective-permute-done | bytes 294944 | tf_op jit(solution)/shard_map/ppermute | solution.py:696
  (275 shorter events, 174.1 us)
Async XLA Ops:
  7.2 89.0 %all-gather.3.cloned.1.call-start = ((), (), s32[]{:S(2)}) async-start(), calls=%async_computation | async-start | bytes 2211840 | tf_op jit(solution)/shard_map/all_gather | solution.py:727
  31.4 16.9 %collective-permute-start.6 = (bf16[4,96,768]{2,1,0:T(8,128)(2,1)S(1)}, bf16[4,96,768]{2,1,0:T(8,128)(2,1)S(1)}, u32[]{:S(2)}, u32[]{:S(2)}) collective-permute-start(bf16[4,96,768]{2,1,0:T(8,128)(2,1)S(1)} %get-tuple-element.225), channel_id=1, source_target_pairs={{0,4},{1,3},{2,6},{3,1},{4,0},{5,7},{6,2},{7,5},{8,12},{9,11},{10,... | collective-permute-start | bytes 1769480 | tf_op jit(solution)/shard_map/ppermute | solution.py:696
  48.5 22.2 %collective-permute-start.8 = (bf16[2,4,96,768]{3,2,1,0:T(8,128)(2,1)S(1)}, bf16[2,4,96,768]{3,2,1,0:T(8,128)(2,1)}, u32[]{:S(2)}, u32[]{:S(2)}) collective-permute-start(bf16[2,4,96,768]{3,2,1,0:T(8,128)(2,1)S(1)} %pad_maximum_fusion.3.refs_0_), channel_id=1, source_target_pairs={{0,2},{1,5},{2,0},{3,7},{4,6},{5,1},{6,4},{7,3},{8,10},{9,13},{10,... | collective-permute-start | bytes 3538952 | tf_op jit(solution)/shard_map/ppermute | solution.py:696
  48.9 21.7 %collective-permute-start.9 = (bf16[2,4,96,768]{3,2,1,0:T(8,128)(2,1)S(1)}, bf16[2,4,96,768]{3,2,1,0:T(8,128)(2,1)}, u32[]{:S(2)}, u32[]{:S(2)}) collective-permute-start(bf16[2,4,96,768]{3,2,1,0:T(8,128)(2,1)S(1)} %pad_maximum_fusion.3.refs_0_), channel_id=1, source_target_pairs={{0,1},{1,0},{2,3},{3,2},{4,5},{5,4},{6,7},{7,6},{8,9},{9,8},{10,11... | collective-permute-start | bytes 3538952 | tf_op jit(solution)/shard_map/ppermute | solution.py:696
  50.7 19.9 %collective-permute-start.11 = (bf16[192,768]{1,0:T(8,128)(2,1)S(1)}, bf16[192,768]{1,0:T(8,128)(2,1)S(1)}, u32[]{:S(2)}, u32[]{:S(2)}) collective-permute-start(bf16[192,768]{1,0:T(8,128)(2,1)S(1)} %get-tuple-element.232), channel_id=1, source_target_pairs={{0,24},{1,25},{2,26},{3,27},{4,28},{5,29},{6,30},{7,31},{8,16},{9,... | collective-permute-start | bytes 884744 | tf_op jit(solution)/shard_map/ppermute | solution.py:696
  70.9 16.4 %collective-permute-start.13 = (bf16[4,192,768]{2,1,0:T(8,128)(2,1)S(1)}, bf16[4,192,768]{2,1,0:T(8,128)(2,1)}, u32[]{:S(2)}, u32[]{:S(2)}) collective-permute-start(bf16[4,192,768]{2,1,0:T(8,128)(2,1)S(1)} %get-tuple-element.237), channel_id=1, source_target_pairs={{0,4},{1,3},{2,6},{3,1},{4,0},{5,7},{6,2},{7,5},{8,12},{9,11},{10,... | collective-permute-start | bytes 3538952 | tf_op jit(solution)/shard_map/ppermute | solution.py:696
  88.9 29.7 %collective-permute-start.14 = (bf16[2,4,192,768]{3,2,1,0:T(8,128)(2,1)S(1)}, bf16[2,4,192,768]{3,2,1,0:T(8,128)(2,1)}, u32[]{:S(2)}, u32[]{:S(2)}) collective-permute-start(bf16[2,4,192,768]{3,2,1,0:T(8,128)(2,1)S(1)} %pad_maximum_fusion.1.refs_0_.refs_4_), channel_id=1, source_target_pairs={{0,2},{1,5},{2,0},{3,7},{4,6},{5,1},{6,4},{7,3},{8,10},{9,13},{10,... | collective-permute-start | bytes 7077896 | tf_op jit(solution)/shard_map/ppermute | solution.py:696
  89.3 29.3 %collective-permute-start.15 = (bf16[2,4,192,768]{3,2,1,0:T(8,128)(2,1)S(1)}, bf16[2,4,192,768]{3,2,1,0:T(8,128)(2,1)}, u32[]{:S(2)}, u32[]{:S(2)}) collective-permute-start(bf16[2,4,192,768]{3,2,1,0:T(8,128)(2,1)S(1)} %pad_maximum_fusion.1.refs_0_.refs_4_), channel_id=1, source_target_pairs={{0,1},{1,0},{2,3},{3,2},{4,5},{5,4},{6,7},{7,6},{8,9},{9,8},{10,11... | collective-permute-start | bytes 7077896 | tf_op jit(solution)/shard_map/ppermute | solution.py:696
  128.8 28.2 %collective-permute-start.18 = (bf16[2,4,96,768]{3,2,1,0:T(8,128)(2,1)S(1)}, bf16[2,4,96,768]{3,2,1,0:T(8,128)(2,1)}, u32[]{:S(2)}, u32[]{:S(2)}) collective-permute-start(bf16[2,4,96,768]{3,2,1,0:T(8,128)(2,1)S(1)} %pad_maximum_fusion.5.refs_0_), channel_id=1, source_target_pairs={{0,2},{1,5},{2,0},{3,7},{4,6},{5,1},{6,4},{7,3},{8,10},{9,13},{10,... | collective-permute-start | bytes 3538952 | tf_op jit(solution)/shard_map/ppermute | solution.py:696
  130.1 26.8 %collective-permute-start.19 = (bf16[2,4,96,768]{3,2,1,0:T(8,128)(2,1)S(1)}, bf16[2,4,96,768]{3,2,1,0:T(8,128)(2,1)S(1)}, u32[]{:S(2)}, u32[]{:S(2)}) collective-permute-start(bf16[2,4,96,768]{3,2,1,0:T(8,128)(2,1)S(1)} %pad_maximum_fusion.5.refs_0_), channel_id=1, source_target_pairs={{0,1},{1,0},{2,3},{3,2},{4,5},{5,4},{6,7},{7,6},{8,9},{9,8},{10,11... | collective-permute-start | bytes 3538952 | tf_op jit(solution)/shard_map/ppermute | solution.py:696
  130.2 26.8 %collective-permute-start.20 = (bf16[4,192,768]{2,1,0:T(8,128)(2,1)S(1)}, bf16[4,192,768]{2,1,0:T(8,128)(2,1)S(1)}, u32[]{:S(2)}, u32[]{:S(2)}) collective-permute-start(bf16[4,192,768]{2,1,0:T(8,128)(2,1)S(1)} %get-tuple-element.263), channel_id=1, source_target_pairs={{0,4},{1,3},{2,6},{3,1},{4,0},{5,7},{6,2},{7,5},{8,12},{9,11},{10,... | collective-permute-start | bytes 3538952 | tf_op jit(solution)/shard_map/ppermute | solution.py:696
  161.2 28.9 %collective-permute-start.22 = (bf16[2,4,192,768]{3,2,1,0:T(8,128)(2,1)S(1)}, bf16[2,4,192,768]{3,2,1,0:T(8,128)(2,1)}, u32[]{:S(2)}, u32[]{:S(2)}) collective-permute-start(bf16[2,4,192,768]{3,2,1,0:T(8,128)(2,1)S(1)} %pad_maximum_fusion.2.refs_0_.refs_4_), channel_id=1, source_target_pairs={{0,2},{1,5},{2,0},{3,7},{4,6},{5,1},{6,4},{7,3},{8,10},{9,13},{10,... | collective-permute-start | bytes 7077896 | tf_op jit(solution)/shard_map/ppermute | solution.py:696
  163.0 27.2 %collective-permute-start.23 = (bf16[2,4,192,768]{3,2,1,0:T(8,128)(2,1)S(1)}, bf16[2,4,192,768]{3,2,1,0:T(8,128)(2,1)}, u32[]{:S(2)}, u32[]{:S(2)}) collective-permute-start(bf16[2,4,192,768]{3,2,1,0:T(8,128)(2,1)S(1)} %pad_maximum_fusion.2.refs_0_.refs_4_), channel_id=1, source_target_pairs={{0,1},{1,0},{2,3},{3,2},{4,5},{5,4},{6,7},{7,6},{8,9},{9,8},{10,11... | collective-permute-start | bytes 7077896 | tf_op jit(solution)/shard_map/ppermute | solution.py:696
  272.2 29.0 %collective-permute-start.26 = (bf16[2,4,192,768]{3,2,1,0:T(8,128)(2,1)S(1)}, bf16[2,4,192,768]{3,2,1,0:T(8,128)(2,1)}, u32[]{:S(2)}, u32[]{:S(2)}) collective-permute-start(bf16[2,4,192,768]{3,2,1,0:T(8,128)(2,1)S(1)} %fusion.1), channel_id=1, source_target_pairs={{0,2},{1,5},{2,0},{3,7},{4,6},{5,1},{6,4},{7,3},{8,10},{9,13},{10,... | collective-permute-start | bytes 7077896 | tf_op jit(solution)/shard_map/ppermute | solution.py:696
  303.3 16.3 %collective-permute-start.27 = (bf16[4,192,768]{2,1,0:T(8,128)(2,1)S(1)}, bf16[4,192,768]{2,1,0:T(8,128)(2,1)S(1)}, u32[]{:S(2)}, u32[]{:S(2)}) collective-permute-start(bf16[4,192,768]{2,1,0:T(8,128)(2,1)S(1)} %fusion.6), channel_id=1, source_target_pairs={{0,4},{1,3},{2,6},{3,1},{4,0},{5,7},{6,2},{7,5},{8,12},{9,11},{10,... | collective-permute-start | bytes 3538952 | tf_op jit(solution)/shard_map/ppermute | solution.py:696
  319.6 21.0 %collective-permute-start.28 = (bf16[2,2,4,96,768]{4,3,2,1,0:T(8,128)(2,1)}, bf16[2,2,4,96,768]{4,3,2,1,0:T(8,128)(2,1)}, u32[]{:S(2)}, u32[]{:S(2)}) collective-permute-start(bf16[2,2,4,96,768]{4,3,2,1,0:T(8,128)(2,1)} %get-tuple-element.335), channel_id=1, source_target_pairs={{0,1},{1,0},{2,3},{3,2},{4,5},{5,4},{6,7},{7,6},{8,9},{9,8},{10,11... | collective-permute-start | bytes 7077896 | tf_op jit(solution)/shard_map/ppermute | solution.py:696
  343.2 23.1 %collective-permute-start.29 = (bf16[2,4,96,768]{3,2,1,0:T(8,128)(2,1)}, bf16[2,4,96,768]{3,2,1,0:T(8,128)(2,1)}, u32[]{:S(2)}, u32[]{:S(2)}) collective-permute-start(bf16[2,4,96,768]{3,2,1,0:T(8,128)(2,1)} %fusion.10), channel_id=1, source_target_pairs={{0,2},{1,5},{2,0},{3,7},{4,6},{5,1},{6,4},{7,3},{8,10},{9,13},{10,... | collective-permute-start | bytes 3538952 | tf_op jit(solution)/shard_map/ppermute | solution.py:696
  389.5 29.2 %collective-permute-start.32 = (bf16[2,4,192,768]{3,2,1,0:T(8,128)(2,1)}, bf16[2,4,192,768]{3,2,1,0:T(8,128)(2,1)}, u32[]{:S(2)}, u32[]{:S(2)}) collective-permute-start(bf16[2,4,192,768]{3,2,1,0:T(8,128)(2,1)} %fusion.2), channel_id=1, source_target_pairs={{0,2},{1,5},{2,0},{3,7},{4,6},{5,1},{6,4},{7,3},{8,10},{9,13},{10,... | collective-permute-start | bytes 7077896 | tf_op jit(solution)/shard_map/ppermute | solution.py:696
  390.5 22.0 %collective-permute-start.33 = (bf16[288,768]{1,0:T(8,128)(2,1)}, bf16[288,768]{1,0:T(8,128)(2,1)}, u32[]{:S(2)}, u32[]{:S(2)}) collective-permute-start(bf16[288,768]{1,0:T(8,128)(2,1)} %get-tuple-element.367), channel_id=1, source_target_pairs={{0,16},{1,17},{2,18},{3,19},{4,20},{5,21},{6,22},{7,23},{8,24},{9,... | collective-permute-start | bytes 1327112 | tf_op jit(solution)/shard_map/ppermute | solution.py:696
  421.8 22.3 %collective-permute-start.34 = (bf16[4,192,768]{2,1,0:T(8,128)(2,1)}, bf16[4,192,768]{2,1,0:T(8,128)(2,1)}, u32[]{:S(2)}, u32[]{:S(2)}) collective-permute-start(bf16[4,192,768]{2,1,0:T(8,128)(2,1)} %fusion.4), channel_id=1, source_target_pairs={{0,4},{1,3},{2,6},{3,1},{4,0},{5,7},{6,2},{7,5},{8,12},{9,11},{10,... | collective-permute-start | bytes 3538952 | tf_op jit(solution)/shard_map/ppermute | solution.py:696
  422.6 16.8 %collective-permute-start.35 = (bf16[288,768]{1,0:T(8,128)(2,1)}, bf16[288,768]{1,0:T(8,128)(2,1)}, u32[]{:S(2)}, u32[]{:S(2)}) collective-permute-start(bf16[288,768]{1,0:T(8,128)(2,1)} %get-tuple-element.379), channel_id=1, source_target_pairs={{0,8},{1,9},{2,10},{3,11},{4,12},{5,13},{6,14},{7,15},{8,0},{9,1},... | collective-permute-start | bytes 1327112 | tf_op jit(solution)/shard_map/ppermute | solution.py:696
  425.4 18.6 %collective-permute-start.36 = (bf16[288,768]{1,0:T(8,128)(2,1)}, bf16[288,768]{1,0:T(8,128)(2,1)}, u32[]{:S(2)}, u32[]{:S(2)}) collective-permute-start(bf16[288,768]{1,0:T(8,128)(2,1)} %get-tuple-element.380), channel_id=1, source_target_pairs={{0,24},{1,25},{2,26},{3,27},{4,28},{5,29},{6,30},{7,31},{8,16},{9,... | collective-permute-start | bytes 1327112 | tf_op jit(solution)/shard_map/ppermute | solution.py:696
  449.7 18.4 %collective-permute-start.38 = (bf16[2,4,112,768]{3,2,1,0:T(8,128)(2,1)S(1)}, bf16[2,4,112,768]{3,2,1,0:T(8,128)(2,1)S(1)}, u32[]{:S(2)}, u32[]{:S(2)}) collective-permute-start(bf16[2,4,112,768]{3,2,1,0:T(8,128)(2,1)S(1)} %fusion.7), channel_id=1, source_target_pairs={{0,2},{1,5},{2,0},{3,7},{4,6},{5,1},{6,4},{7,3},{8,10},{9,13},{10,... | collective-permute-start | bytes 4128776 | tf_op jit(solution)/shard_map/ppermute | solution.py:696
  469.5 18.1 %collective-permute-start.40 = (bf16[4,112,768]{2,1,0:T(8,128)(2,1)}, bf16[4,112,768]{2,1,0:T(8,128)(2,1)}, u32[]{:S(2)}, u32[]{:S(2)}) collective-permute-start(bf16[4,112,768]{2,1,0:T(8,128)(2,1)} %fusion.8), channel_id=1, source_target_pairs={{0,4},{1,3},{2,6},{3,1},{4,0},{5,7},{6,2},{7,5},{8,12},{9,11},{10,... | collective-permute-start | bytes 2064392 | tf_op jit(solution)/shard_map/ppermute | solution.py:696
  (73 other events, 950.2 us)
Sparse Core Ops, SparseCore 0:
  50.8 45.3 all-gather.2

commit v3 on v2

--- a/solution.py
+++ b/solution.py
@@ -70,17 +70,18 @@
 def weight_copies(plan, refs, me_ref, full, sems):
     copies = []
 
-    def add(source, target):
-        copies.append(pltpu.make_async_copy(source, target, sems.at[len(copies)]))
+    def add(source, part, rows):
+        copies.append(pltpu.make_async_copy(source, full.at[part, rows, :], sems.at[part]))
 
     parts, width, _ = full.shape
     if plan[0] == "whole":
-        add(refs[0], full)
+        for part in range(parts):
+            add(refs[0].at[part], part, pl.ds(0, width))
     elif plan[0] == "rows":
         high = width * parts // refs[0].shape[0]
         for index in range(refs[0].shape[0]):
             stripe, part = divmod(index, parts)
-            add(refs[0].at[index, pl.ds(plan[1], high), :], full.at[part, pl.ds(stripe * high, high), :])
+            add(refs[0].at[index, pl.ds(plan[1], high), :], part, pl.ds(stripe * high, high))
     else:
         for ref, positions in zip(refs, plan[2]):
             depth = ref.shape[1]
@@ -88,27 +89,31 @@
             for place, (first, second, core) in enumerate(positions):
                 x, y = plane(me_ref, first, second, core)
                 part = jnp.bitwise_xor(me_ref[1], 2 * y + core)
-                origin = jnp.bitwise_and(me_ref[0], 1) if plan[3] else me_ref[0]
+                if plan[3]:
+                    side = jnp.bitwise_xor(jnp.bitwise_and(me_ref[0], 1), x)
+                    stripes = full.reshape(parts, depth, 2, high, width).at[part, :, side]
+                    source = ref.at[place, :, pl.ds(plan[1], high), :]
+                    copies.append(pltpu.make_async_copy(source, stripes, sems.at[part]))
+                    continue
                 for z in range(depth):
-                    start = pl.multiple_of(jnp.bitwise_xor(origin, 2 * z + x) * high, 16)
-                    add(ref.at[place, z, pl.ds(plan[1], high), :], full.at[part, pl.ds(start, high), :])
+                    start = pl.multiple_of(jnp.bitwise_xor(me_ref[0], 2 * z + x) * high, 16)
+                    add(ref.at[place, z, pl.ds(plan[1], high), :], part, pl.ds(start, high))
     return copies
 
 
-def load_weights(groups):
-    copies = [copy for group in groups for copy in weight_copies(*group)]
-    for copy in copies:
+def start_weights(groups):
+    for copy in [copy for group in groups for copy in weight_copies(*group)]:
         copy.start()
-    for copy in copies:
-        copy.wait()
-
-
-def copy_count(plan, refs):
-    if plan[0] == "whole":
-        return 1
-    if plan[0] == "rows":
-        return refs[0].shape[0]
-    return sum(ref.shape[0] * ref.shape[1] for ref in refs)
+
+
+def wait_weight(full, sems, part):
+    pltpu.make_async_copy(full.at[part], full.at[part], sems.at[part]).wait()
+
+
+def part_order(me_ref, plan, parts):
+    if plan[0] != "near":
+        return list(range(parts))
+    return [jnp.bitwise_xor(me_ref[1], near) for near in (0, 2, 1, 3)]
 
 
 def split_attention(raw, qkv_s, out_s):
@@ -132,7 +137,9 @@
 
     @pl.when(pl.program_id(0) == 0)
     def _():
-        load_weights([(plan, weight_refs, me_ref, raw, sems)])
+        start_weights([(plan, weight_refs, me_ref, raw, sems)])
+        for part in range(raw.shape[0]):
+            wait_weight(raw, sems, part)
         split_attention(raw, qkv_s, out_s)
 
     width = stream_ref.shape[1]
@@ -210,7 +217,7 @@
         ],
         scratch_shapes=[
             pltpu.VMEM((parts, width, width), BF),
-            pltpu.SemaphoreType.DMA((copy_count(plan, arrays),)),
+            pltpu.SemaphoreType.DMA((parts,)),
         ],
         compiler_params=pltpu.CompilerParams(vmem_limit_bytes=VMEM_LIMIT),
         cost_estimate=pl.CostEstimate(flops=20 * 10**9, bytes_accessed=30 * 10**6, transcendentals=0),
@@ -219,31 +226,50 @@
 
 
 def ffn_forward_kernel(plans, me_ref, nffn_ref, middle_ref, vec_ref, hidden_ref, *refs):
-    result_ref, active_ref, slope_ref, up_s, down_s, up_sems, down_sems = refs[-7:]
-    up_refs = refs[: (len(refs) - 7) // 2]
-    down_refs = refs[len(up_refs) : -7]
-
-    @pl.when(pl.program_id(0) == 0)
+    result_ref, active_ref, slope_ref, up_ref, down_ref, up_s, down_s, up_sems, down_sems = refs[-9:]
+    up_refs = refs[: (len(refs) - 9) // 2]
+    down_refs = refs[len(up_refs) : -9]
+    kept = [pltpu.make_async_copy(up_s, up_ref, up_sems.at[0]), pltpu.make_async_copy(down_s, down_ref, down_sems.at[0])]
+
+    first = pl.program_id(0) == 0
+    parts, _, chunk = up_s.shape
+    curve = 0.7978845608028654
+
+    @pl.when(first)
     def _():
-        load_weights([(plans[0], up_refs, me_ref, up_s, up_sems), (plans[1], down_refs, me_ref, down_s, down_sems)])
-
-    nffn = nffn_ref[...]
-    parts, _, chunk = up_s.shape
-    total = middle_ref[...] + vec_ref[7:8, :]
-    curve = 0.7978845608028654
-    for part in range(parts):
-        cols = slice(part * chunk, (part + 1) * chunk)
-        upper = dot_nn(nffn, up_s[part]) + hidden_ref[:, cols]
-        square = upper * upper
-        angle = jnp.tanh(upper * (curve + (curve * 0.044715) * square))
-        half = 0.5 * upper
-        lift = 1.0 + angle
-        active = (half * lift).astype(BF)
-        slope = 0.5 * lift + half * (1.0 - angle * angle) * (curve + (3.0 * curve * 0.044715) * square)
-        active_ref[:, cols] = active
-        slope_ref[:, cols] = slope.astype(BF)
-        total = total + dot_nt(active, down_s[part])
-    result_ref[...] = total
+        start_weights([(plans[0], up_refs, me_ref, up_s, up_sems), (plans[1], down_refs, me_ref, down_s, down_sems)])
+
+    def body(wait):
+        nffn = nffn_ref[...]
+        total = middle_ref[...] + vec_ref[7:8, :]
+        for part in part_order(me_ref, plans[0], parts):
+            cols = pl.ds(pl.multiple_of(part * chunk, chunk), chunk)
+            if wait:
+                wait_weight(up_s, up_sems, part)
+            upper = dot_nn(nffn, up_s[part]) + hidden_ref[:, cols]
+            square = upper * upper
+            angle = jnp.tanh(upper * (curve + (curve * 0.044715) * square))
+            half = 0.5 * upper
+            lift = 1.0 + angle
+            active = (half * lift).astype(BF)
+            slope = 0.5 * lift + half * (1.0 - angle * angle) * (curve + (3.0 * curve * 0.044715) * square)
+            active_ref[:, cols] = active
+            slope_ref[:, cols] = slope.astype(BF)
+            if wait:
+                wait_weight(down_s, down_sems, part)
+            total = total + dot_nt(active, down_s[part])
+        result_ref[...] = total
+        if wait:
+            for copy in kept:
+                copy.start()
+
+    pl.when(first)(functools.partial(body, True))
+    pl.when(jnp.logical_not(first))(functools.partial(body, False))
+
+    @pl.when(pl.program_id(0) == pl.num_programs(0) - 1)
+    def _():
+        for copy in kept:
+            copy.wait()
 
 
 def ffn_forward(me, nffn, middle, vec, hidden, up_w, down_w, block, parts):
@@ -262,17 +288,18 @@
             pl.BlockSpec(hidden.shape, lambda i: (0, 0)),
         ]
         + [pl.BlockSpec(memory_space=pl.ANY)] * len(arrays),
-        out_specs=[row_spec(width), row_spec(ffn), row_spec(ffn)],
+        out_specs=[row_spec(width), row_spec(ffn), row_spec(ffn)] + [pl.BlockSpec(memory_space=pl.ANY)] * 2,
         out_shape=[
             jax.ShapeDtypeStruct((rows, width), F32),
             jax.ShapeDtypeStruct((rows, ffn), BF),
             jax.ShapeDtypeStruct((rows, ffn), BF),
-        ],
+        ]
+        + [jax.ShapeDtypeStruct((parts, width, ffn // parts), BF)] * 2,
         scratch_shapes=[
             pltpu.VMEM((parts, width, ffn // parts), BF),
             pltpu.VMEM((parts, width, ffn // parts), BF),
-            pltpu.SemaphoreType.DMA((copy_count(*up_w),)),
-            pltpu.SemaphoreType.DMA((copy_count(*down_w),)),
+            pltpu.SemaphoreType.DMA((parts,)),
+            pltpu.SemaphoreType.DMA((parts,)),
         ],
         compiler_params=pltpu.CompilerParams(vmem_limit_bytes=VMEM_LIMIT),
         cost_estimate=pl.CostEstimate(flops=15 * 10**9, bytes_accessed=30 * 10**6, transcendentals=0),
@@ -285,29 +312,39 @@
     up_refs = refs[: (len(refs) - 8) // 2]
     down_refs = refs[len(up_refs) : -8]
 
-    @pl.when(pl.program_id(0) == 0)
+    first = pl.program_id(0) == 0
+    parts, _, chunk = up_s.shape
+
+    @pl.when(first)
     def _():
+        start_weights([(plans[1], down_refs, me_ref, down_s, down_sems), (plans[0], up_refs, me_ref, up_s, up_sems)])
         small_ref[...] = jnp.zeros_like(small_ref)
         ghidden_ref[...] = jnp.zeros_like(ghidden_ref)
-        load_weights([(plans[0], up_refs, me_ref, up_s, up_sems), (plans[1], down_refs, me_ref, down_s, down_sems)])
-
-    grad = grad_ref[...].astype(F32)
-    lower = grad.astype(BF)
-    parts, _, chunk = up_s.shape
-    gnormed = jnp.zeros(grad.shape, F32)
-    for part in range(parts):
-        cols = slice(part * chunk, (part + 1) * chunk)
-        gupper = (dot_nn(lower, down_s[part]) * slope_ref[:, cols].astype(F32)).astype(BF)
-        gupper_ref[:, cols] = gupper
-        ghidden_ref[:, cols] += column_sum(gupper.astype(F32))
-        gnormed = gnormed + dot_nt(gupper, up_s[part])
-    unit, root = normalize(middle_ref[...])
-    gmiddle = grad + norm_backward(gnormed, unit, root, vec_ref[1:2, :])
-    gmiddle_ref[...] = gmiddle
-    small_ref[0:1, :] += column_sum(gnormed * unit)
-    small_ref[1:2, :] += column_sum(gnormed)
-    small_ref[2:3, :] += column_sum(lower.astype(F32))
-    small_ref[3:4, :] += column_sum(gmiddle.astype(BF).astype(F32))
+
+    def body(wait):
+        grad = grad_ref[...].astype(F32)
+        lower = grad.astype(BF)
+        gnormed = jnp.zeros(grad.shape, F32)
+        for part in part_order(me_ref, plans[0], parts):
+            cols = pl.ds(pl.multiple_of(part * chunk, chunk), chunk)
+            if wait:
+                wait_weight(down_s, down_sems, part)
+            gupper = (dot_nn(lower, down_s[part]) * slope_ref[:, cols].astype(F32)).astype(BF)
+            gupper_ref[:, cols] = gupper
+            ghidden_ref[:, cols] += column_sum(gupper.astype(F32))
+            if wait:
+                wait_weight(up_s, up_sems, part)
+            gnormed = gnormed + dot_nt(gupper, up_s[part])
+        unit, root = normalize(middle_ref[...])
+        gmiddle = grad + norm_backward(gnormed, unit, root, vec_ref[1:2, :])
+        gmiddle_ref[...] = gmiddle
+        small_ref[0:1, :] += column_sum(gnormed * unit)
+        small_ref[1:2, :] += column_sum(gnormed)
+        small_ref[2:3, :] += column_sum(lower.astype(F32))
+        small_ref[3:4, :] += column_sum(gmiddle.astype(BF).astype(F32))
+
+    pl.when(first)(functools.partial(body, True))
+    pl.when(jnp.logical_not(first))(functools.partial(body, False))
 
 
 def ffn_backward(me, grad, slope, middle, vec, up_w, down_w, block, parts):
@@ -341,8 +378,8 @@
         scratch_shapes=[
             pltpu.VMEM((parts, width, ffn // parts), BF),
             pltpu.VMEM((parts, width, ffn // parts), BF),
-            pltpu.SemaphoreType.DMA((copy_count(*up_w),)),
-            pltpu.SemaphoreType.DMA((copy_count(*down_w),)),
+            pltpu.SemaphoreType.DMA((parts,)),
+            pltpu.SemaphoreType.DMA((parts,)),
         ],
         compiler_params=pltpu.CompilerParams(vmem_limit_bytes=VMEM_LIMIT),
         cost_estimate=pl.CostEstimate(flops=15 * 10**9, bytes_accessed=30 * 10**6, transcendentals=0),
@@ -505,14 +542,33 @@
     for x in range(2):
         for z in range(depth):
             start = pl.multiple_of(jnp.bitwise_xor(me, 2 * z + x) * high, 16)
-            target[x, z * high : (z + 1) * high, :] = source[pl.ds(start, high), :]
+            at = (x * depth + z) * high
+            target[at : at + high, :] = source[pl.ds(start, high), :]
+
+
+def send_out(me_ref, core, y, staged, slot, own_ref, other_ref, sems):
+    for x in range(2):
+        first, second = plane(me_ref, x, y, core)
+
+        @pl.when(core == 0)
+        def _():
+            pltpu.make_async_copy(staged.at[slot, x], own_ref.at[second, first], sems.at[slot, x]).start()
+
+        @pl.when(core == 1)
+        def _():
+            pltpu.make_async_copy(staged.at[slot, x], other_ref.at[second, first], sems.at[slot, x]).start()
+
+
+def wait_out(staged, slot, own_ref, sems):
+    for x in range(2):
+        pltpu.make_async_copy(staged.at[slot, x], own_ref.at[0, 0], sems.at[slot, x]).wait()
 
 
 def ffn_weight_split_kernel(
-    me_ref, nffn_ref, grad_ref, gupper_ref, active_ref, other_ref, own_ref, turned, nffn_t, grad_t
+    me_ref, nffn_ref, grad_ref, gupper_ref, active_ref, other_ref, own_ref, turned, nffn_t, grad_t, staged, sems
 ):
     step = pl.program_id(0)
-    _, _, depth, high, width = own_ref.shape
+    _, _, depth, high, width = staged.shape
     high = high // 2
 
     @pl.when(step == 0)
@@ -522,19 +578,21 @@
         turned[...] = grad_ref[...].astype(BF).T
         relative_rows(turned, grad_t, me_ref[0], depth)
 
-    x, _ = plane(me_ref, step % 2, step // 2 % 2, 1 - step // 4)
-    gup = dot_nn(nffn_t[x], gupper_ref[...]).astype(BF).reshape(depth, high, width)
-    gdown = dot_nn(grad_t[x], active_ref[...]).astype(BF).reshape(depth, high, width)
-
-    @pl.when(step < 4)
+    slot = step % 2
+
+    @pl.when(step >= 2)
     def _():
-        other_ref[0, 0, :, :high, :] = gup
-        other_ref[0, 0, :, high:, :] = gdown
-
-    @pl.when(step >= 4)
+        wait_out(staged, slot, own_ref, sems)
+
+    shape = (2, depth, high, width)
+    staged[slot, :, :, :high, :] = dot_nn(nffn_t[...], gupper_ref[...]).astype(BF).reshape(shape)
+    staged[slot, :, :, high:, :] = dot_nn(grad_t[...], active_ref[...]).astype(BF).reshape(shape)
+    send_out(me_ref, 1 - step // 2, step % 2, staged, slot, own_ref, other_ref, sems)
+
+    @pl.when(step == 3)
     def _():
-        own_ref[0, 0, :, :high, :] = gup
-        own_ref[0, 0, :, high:, :] = gdown
+        wait_out(staged, 1 - slot, own_ref, sems)
+        wait_out(staged, slot, own_ref, sems)
 
 
 def ffn_weight_split(me, nffn, grad, gupper, active, depth):
@@ -543,27 +601,18 @@
     high = width // (2 * depth)
 
     def column(step, me):
-        core = 1 - step // 4
-        _, y = plane(me, step % 2, step // 2 % 2, core)
-        return (0, jnp.bitwise_xor(me[1], 2 * y + core))
-
-    def place(begin):
-        def at(step, me):
-            step = jnp.clip(step - begin, 0, 3)
-            return (step // 2, step % 2, 0, 0, 0)
-
-        return at
+        return (0, jnp.bitwise_xor(me[1], 2 * (step % 2) + 1 - step // 2))
 
     whole = pl.BlockSpec((rows, width), lambda i, me: (0, 0))
-    block = (1, 1, depth, 2 * high, piece)
     return pl.pallas_call(
         ffn_weight_split_kernel,
         grid_spec=pltpu.PrefetchScalarGridSpec(
             num_scalar_prefetch=1,
-            grid=(8,),
+            grid=(4,),
             in_specs=[whole, whole, pl.BlockSpec((rows, piece), column), pl.BlockSpec((rows, piece), column)],
-            out_specs=[pl.BlockSpec(block, place(0)), pl.BlockSpec(block, place(4))],
-            scratch_shapes=[pltpu.VMEM((width, rows), BF)] + [pltpu.VMEM((2, width // 2, rows), BF)] * 2,
+            out_specs=[pl.BlockSpec(memory_space=pl.ANY)] * 2,
+            scratch_shapes=[pltpu.VMEM((width, rows), BF)] * 3
+            + [pltpu.VMEM((2, 2, depth, 2 * high, piece), BF), pltpu.SemaphoreType.DMA((2, 2))],
         ),
         out_shape=[jax.ShapeDtypeStruct((2, 2, depth, 2 * high, piece), BF)] * 2,
         compiler_params=pltpu.CompilerParams(vmem_limit_bytes=VMEM_LIMIT),
@@ -573,20 +622,22 @@
 
 
 def attention_weight_split_kernel(me_ref, normed_ref, mixed_ref, gproj_ref, gmiddle_ref, *refs):
-    other_ref, own_ref, turned, normed_t, mixed_t, joined, extra_s = refs[-7:]
-    extra_refs = refs[:-7]
-    x = pl.program_id(0)
-    _, _, depth, rows, width = own_ref.shape
+    other_ref, own_ref, turned, normed_t, mixed_t, found, staged, extra_s, sems = refs[-9:]
+    extra_refs = refs[:-9]
+    step = pl.program_id(0)
+    _, _, depth, rows, width = staged.shape
     high = width // (2 * depth)
-
-    @pl.when(x == 0)
+    share = width // 4
+    shape = (2, depth, high, width)
+
+    @pl.when(step == 0)
     def _():
+        turned[...] = mixed_ref[...].T
+        relative_rows(turned, mixed_t, me_ref[0], depth)
+        found[:, 3 * width :] = dot_nn(mixed_t[...], gmiddle_ref[...].astype(BF)).astype(BF)
         turned[...] = normed_ref[...].T
         relative_rows(turned, normed_t, me_ref[0], depth)
-        turned[...] = mixed_ref[...].T
-        relative_rows(turned, mixed_t, me_ref[0], depth)
         if extra_refs:
-            share = width // 4
             extra_s[...] = jnp.zeros_like(extra_s)
             for index in range(2):
                 one_ref, more_ref, two_ref, hidden_ref = extra_refs[4 * index : 4 * index + 4]
@@ -595,23 +646,27 @@
                     at = index * (width // 3)
                     extra_s[part, :8, at : at + share] = sums[:, part * share : (part + 1) * share]
                     extra_s[part, 8 + index : 9 + index, :] = hidden_ref[:, part * width : (part + 1) * width]
-
-    gqkv = dot_nn(normed_t[x], gproj_ref[...])
-    gout = dot_nn(mixed_t[x], gmiddle_ref[...].astype(BF))
-    cut = gqkv.shape[1] // 4
-    rest = gout.shape[1] // 4
-    for part in range(4):
-        qkv_part = gqkv[:, part * cut : (part + 1) * cut].astype(BF)
-        out_part = gout[:, part * rest : (part + 1) * rest].astype(BF)
-        joined[jnp.bitwise_xor(me_ref[1], part)] = jnp.concatenate([qkv_part, out_part], axis=1)
-    for near in range(4):
-        y, core = divmod(near, 2)
-        first, second = plane(me_ref, x, y, core)
-        target = own_ref if core == 0 else other_ref
-        target[second, first, :, :high, :] = joined[near].reshape(depth, high, width)
-        if extra_refs:
-            extra = extra_s[jnp.bitwise_xor(me_ref[1], near)].astype(BF)
-            target[second, first, :, high:, :] = jnp.broadcast_to(extra[None], (depth,) + extra.shape)
+            for part in range(4):
+                extra = extra_s[part].astype(BF)
+                staged[part, :, :, high:, :] = jnp.broadcast_to(extra[None, None], (2, depth) + extra.shape)
+
+    def finish(part):
+        columns = slice(part * 3 * share, (part + 1) * 3 * share)
+        rest = slice(3 * width + part * share, 3 * width + (part + 1) * share)
+        staged[part, :, :, :high, :] = jnp.concatenate([found[:, columns], found[:, rest]], axis=1).reshape(shape)
+        near = jnp.bitwise_xor(me_ref[1], part)
+        send_out(me_ref, near % 2, near // 2, staged, part, own_ref, other_ref, sems)
+
+    for third in range(3):
+
+        @pl.when(step == third)
+        def _():
+            found[:, third * width : (third + 1) * width] = dot_nn(normed_t[...], gproj_ref[...]).astype(BF)
+            for part in ((0,), (1,), (2, 3))[third]:
+                finish(part)
+            if third == 2:
+                for part in range(4):
+                    wait_out(staged, part, own_ref, sems)
 
 
 def attention_weight_split(me, normed, mixed, gproj, gmiddle, depth, extra=None):
@@ -623,16 +678,18 @@
     operands = [normed, mixed, gproj, gmiddle] + extras
     return pl.pallas_call(
         attention_weight_split_kernel,
-        grid=(2,),
-        in_specs=[pl.BlockSpec(memory_space=pltpu.SMEM)] + [whole(operand) for operand in operands],
-        out_specs=[pl.BlockSpec(shape, lambda i: (0, 0, 0, 0, 0))] * 2,
+        grid=(3,),
+        in_specs=[pl.BlockSpec(memory_space=pltpu.SMEM), whole(normed), whole(mixed)]
+        + [pl.BlockSpec((rows, width), lambda i: (0, i))]
+        + [whole(operand) for operand in operands[3:]],
+        out_specs=[pl.BlockSpec(memory_space=pl.ANY)] * 2,
         out_shape=[jax.ShapeDtypeStruct(shape, BF)] * 2,
-        scratch_shapes=[
-            pltpu.VMEM((width, rows), BF),
-            pltpu.VMEM((2, width // 2, rows), BF),
-            pltpu.VMEM((2, width // 2, rows), BF),
-            pltpu.VMEM((4, width // 2, width), BF),
+        scratch_shapes=[pltpu.VMEM((width, rows), BF)] * 3
+        + [
+            pltpu.VMEM((width, 4 * width), BF),
+            pltpu.VMEM((4,) + shape[1:], BF),
             pltpu.VMEM((4, 16, width), F32),
+            pltpu.SemaphoreType.DMA((4, 2)),
         ],
         compiler_params=pltpu.CompilerParams(vmem_limit_bytes=VMEM_LIMIT),
         cost_estimate=pl.CostEstimate(flops=10 * 10**9, bytes_accessed=20 * 10**6, transcendentals=0),
@@ -879,21 +936,22 @@
             )
         return lambda gproj: (attention_weight(kept["normed"], kept["mixed"], gproj, gmiddle, stripes, parts),)
 
-    def keep(index, stream, attention, ffn, up_w, down_w):
+    def keep(index, stream, attention, ffn):
         middle, nffn, normed, proj, probs, mixed, qkv_w, out_w = attention
         saved[index] = dict(
             stream=stream, middle=middle, nffn=nffn, normed=normed, proj=proj, probs=probs, mixed=mixed,
-            weight=(qkv_w, out_w), active=ffn[1], slope=ffn[2], up_w=up_w, down_w=down_w,
+            weight=(qkv_w, out_w), active=ffn[1], slope=ffn[2], up_w=(("whole",), [ffn[3]]), down_w=(("whole",), [ffn[4]]),
         )
 
     if split:
         depth = exchange.depth
-        late = exchange.gather_z(jnp.concatenate([attn_pieces[1], up_pieces[1], down_pieces[1]], axis=0))
+        late = jnp.concatenate([attn_pieces[1], up_pieces[1], down_pieces[1]], axis=0)
         own_small = jnp.concatenate(
             [gain_weight, bias_weight, hidden_weight.reshape(2, -1, gain_weight.shape[2])], axis=1
         )
         own_small = lax.reduce_precision(own_small, 8, 7)
         small_sends = [(functools.partial(exchange.part, bits), own_small) for bits in range(1, 4)]
+        late = exchange.gather_z(late)
         came, _ = lane.step(exchange.z_sends([attn_pieces[0]] * depth) + small_sends)
         attn_zero = Spread(exchange, jnp.stack([attn_pieces[0]] + came[: depth - 1]), False)
         mine = lax.axis_index("tensor")
@@ -915,6 +973,7 @@
         came, _ = lane.step(attn_zero.go_core(came[:2]) + ffn_zero.go_first())
         attn_w = attn_zero.weight(came[:1])
         came, attention = lane.step(ffn_zero.go_second(came[1:]), attention_forward_of(0, attn_w), [tokens])
+        late = lane.after_last(late)
         attn_one = Spread(exchange, late[:, :high], True)
         ffn_one = Spread(exchange, late[:, high:], True)
         came, _ = lane.step(ffn_zero.go_core(came) + attn_one.go_first())
@@ -922,7 +981,7 @@
         came, ffn = lane.step(
             attn_one.go_second(came[1:]) + ffn_one.go_first(), ffn_forward_of(0, up_w, down_w), attention[1::-1]
         )
-        keep(0, tokens, attention, ffn, up_w, down_w)
+        keep(0, tokens, attention, ffn)
         stream = ffn[0]
         ffn_came = came[2:]
         came, _ = lane.step(attn_one.go_core(came[:2]))
@@ -931,7 +990,7 @@
         came, _ = lane.step(ffn_one.go_core(came))
         up_w, down_w = ffn_one.weight(came), ffn_one.weight(came, high)
         _, ffn = lane.step([], ffn_forward_of(1, up_w, down_w), attention[1::-1])
-        keep(1, stream, attention, ffn, up_w, down_w)
+        keep(1, stream, attention, ffn)
         block_output = ffn[0]
 
         _, (gupper, gmiddle, small_two, hidden_one) = lane.step([], ffn_backward_of(1), [out_grad])
@@ -1000,7 +1059,7 @@
             attn_w, up_w, down_w = gathered(index)
             attention = attention_forward_of(index, attn_w)(stream)
             ffn = ffn_forward_of(index, up_w, down_w)(*attention[1::-1])
-            keep(index, stream, attention, ffn, up_w, down_w)
+            keep(index, stream, attention, ffn)
             stream = ffn[0]
         block_output = stream
         grad = out_grad

time: 554 us -> 539 us (0.973)
  Pallas kernels: 256 us -> 242 us
  waiting for transfers between devices: 146 us -> 138 us
    pallas_call x2, Pallas kernels: 42.3 us -> 34.6 us  [ffn_weight_split(): pl.pallas_call(ffn_weight_split_kernel, grid_spec=pltpu.PrefetchScalarGri...]
  transfers between devices with their start and end apart: 52 -> 52, of which waited for: 31 -> 29; matrix products, arithmetic and copies ran while one was open for 5% -> 5% of each run, Pallas kernels for 35% -> 34%
where the time goes in v3:
time: 539 us; the launch traced here: 534 us
  Pallas kernels  242 us (45%)
  waiting for transfers between devices  138 us (26%)
  starting transfers between devices  58.4 us (11%)
  other arithmetic  52.4 us (10%)
  between operations  23 us (4%)
  local copies, waits for them, and re-layouts  20.8 us (4%)
    ppermute x51, waiting for transfers between devices, swap(): return lax.ppermute(value, ('dp', 'tensor'), pairs)  138 us
    pallas_call x4, Pallas kernels, attention_backward(): pl.pallas_call(attention_backward_kernel, grid=((end - begin) // block_pa...  58.8 us
    ppermute x51, starting transfers between devices, swap(): return lax.ppermute(value, ('dp', 'tensor'), pairs)  58.4 us
    pallas_call x2, Pallas kernels, ffn_forward(): pl.pallas_call(functools.partial(ffn_forward_kernel, (up_w[0], down_w[0])...  43.2 us
    pallas_call x2, Pallas kernels, attention_forward(): pl.pallas_call(functools.partial(attention_forward_kernel, plan), grid=(p...  41.3 us
    pallas_call x2, Pallas kernels, ffn_backward(): pl.pallas_call(functools.partial(ffn_backward_kernel, (up_w[0], down_w[0]...  40.1 us
    pallas_call x2, Pallas kernels, ffn_weight_split(): pl.pallas_call(ffn_weight_split_kernel, grid_spec=pltpu.PrefetchScalarGri...  34.6 us
    pallas_call x2, Pallas kernels, attention_weight_split(): pl.pallas_call(attention_weight_split_kernel, grid=(3,), in_specs=[pl.Blo...  24 us
  transfers between devices with their start and end apart: 52, of which 29 were waited for; matrix products, arithmetic and copies ran while one was open for 5% of the time, Pallas kernels for 34%

profile of v3, /device:TPU:0, one launch (start us, length us, event | category | flops | bytes accessed | tf_op | source)
XLA Modules:
  0.0 534.2 jit_solution(4705238373615944642)
XLA Ops:
  23.4 7.9 %collective-permute-done.1 = bf16[96,768]{1,0:T(8,128)(2,1)S(1)} collective-permute-done((bf16[96,768]{1,0:T(8,128)(2,1)S(1)}, bf16[96,768]{1,0:T(8,128)(2,1)S(1)}, u32[]{:S(2)}, u32[]{:S(2)}) %collective-permute-start.1) | collective-permute-done | bytes 147488 | tf_op jit(solution)/shard_map/ppermute | solution.py:753
  33.0 15.4 %collective-permute-done.7 = bf16[192,768]{1,0:T(8,128)(2,1)S(1)} collective-permute-done((bf16[192,768]{1,0:T(8,128)(2,1)S(1)}, bf16[192,768]{1,0:T(8,128)(2,1)S(1)}, u32[]{:S(2)}, u32[]{:S(2)}) %collective-permute-start.7) | collective-permute-done | bytes 294944 | tf_op jit(solution)/shard_map/ppermute | solution.py:753
  51.2 13.9 %collective-permute-done.10 = bf16[192,768]{1,0:T(8,128)(2,1)S(1)} collective-permute-done((bf16[192,768]{1,0:T(8,128)(2,1)S(1)}, bf16[192,768]{1,0:T(8,128)(2,1)S(1)}, u32[]{:S(2)}, u32[]{:S(2)}) %collective-permute-start.10) | collective-permute-done | bytes 294944 | tf_op jit(solution)/shard_map/ppermute | solution.py:753
  70.5 12.3 %collective-permute-done.13 = bf16[4,192,768]{2,1,0:T(8,128)(2,1)} collective-permute-done((bf16[4,192,768]{2,1,0:T(8,128)(2,1)S(1)}, bf16[4,192,768]{2,1,0:T(8,128)(2,1)}, u32[]{:S(2)}, u32[]{:S(2)}) %collective-permute-start.13) | collective-permute-done | bytes 1179680 | tf_op jit(solution)/shard_map/ppermute | solution.py:753
  91.5 20.6 %attention_forward.2 = (f32[1024,768]{1,0:T(8,128)}, bf16[1024,768]{1,0:T(8,128)(2,1)}, bf16[1024,768]{1,0:T(8,128)(2,1)}, bf16[1024,2304]{1,0:T(8,128)(2,1)}, b...) custom-call(s32[2]{0:T(128)} %pad_add_fusion.me_ref, ...), custom_call_target="tpu_custom_call" | custom-call | flops 20000000000 | bytes 30000000 | tf_op jit(solution)/shard_map/attention_forward/pallas_call | solution.py:188
  117.6 7.1 %collective-permute-done.17 = bf16[4,96,768]{2,1,0:T(8,128)(2,1)} collective-permute-done((bf16[4,96,768]{2,1,0:T(8,128)(2,1)S(1)}, bf16[4,96,768]{2,1,0:T(8,128)(2,1)}, u32[]{:S(2)}, u32[]{:S(2)}) %collective-permute-start.17) | collective-permute-done | bytes 589856 | tf_op jit(solution)/shard_map/ppermute | solution.py:753
  128.7 21.7 %ffn_forward.2 = (f32[1024,768]{1,0:T(8,128)}, bf16[1024,3072]{1,0:T(8,128)(2,1)}, bf16[1024,3072]{1,0:T(8,128)(2,1)}, bf16[4,768,768]{2,1,0:T(8,128)(2,1)}, bf16[4,768,768]{2,1,0:T(8,128)(2,1)}) custom-call(s32[2]{0:T(128)} %pad_add_fusion.me_ref, bf16[1024,768]{1,0:T(8,128)(2,1)} %get-tuple-element.272.nffn_ref, ...), custom_call_target="tpu_custom_call" | custom-call | flops 15000000512 | bytes 30000000 | tf_op jit(solution)/shard_map/ffn_forward/pallas_call | solution.py:280
  160.4 20.7 %attention_forward.3 = (f32[1024,768]{1,0:T(8,128)}, bf16[1024,768]{1,0:T(8,128)(2,1)}, bf16[1024,768]{1,0:T(8,128)(2,1)}, bf16[1024,2304]{1,0:T(8,128)(2,1)}, b...) custom-call(s32[2]{0:T(128)} %pad_add_fusion.me_ref, ...), custom_call_target="tpu_custom_call" | custom-call | flops 20000000000 | bytes 30000000 | tf_op jit(solution)/shard_map/attention_forward/pallas_call | solution.py:188
  181.1 6.0 %collective-permute-done.22.refs_1_.refs_5_ = bf16[2,4,192,768]{3,2,1,0:T(8,128)(2,1)} collective-permute-done((bf16[2,4,192,768]{3,2,1,0:T(8,128)(2,1)S(1)}, bf16[2,4,192,768]{3,2,1,0:T(8,128)(2,1)}, u32[]{:S(2)}, u32[]{:S(2)}) %collective-permute-start.22) | collective-permute-done | bytes 2359328 | tf_op jit(solution)/shard_map/ppermute | solution.py:753
  193.3 21.5 %ffn_forward.3 = (f32[1024,768]{1,0:T(8,128)}, bf16[1024,3072]{1,0:T(8,128)(2,1)}, bf16[1024,3072]{1,0:T(8,128)(2,1)}, bf16[4,768,768]{2,1,0:T(8,128)(2,1)}, bf16[4,768,768]{2,1,0:T(8,128)(2,1)}) custom-call(s32[2]{0:T(128)} %pad_add_fusion.me_ref, bf16[1024,768]{1,0:T(8,128)(2,1)} %get-tuple-element.303.nffn_ref, ...), custom_call_target="tpu_custom_call" | custom-call | flops 15000000512 | bytes 30000000 | tf_op jit(solution)/shard_map/ffn_forward/pallas_call | solution.py:280
  214.8 20.2 %ffn_backward.2 = (bf16[1024,3072]{1,0:T(8,128)(2,1)}, f32[1024,768]{1,0:T(8,128)}, f32[8,768]{1,0:T(8,128)}, f32[1,3072]{1,0:T(1,128)}) custom-call(s32[2]{0:T(128)} %pad_add_fusion.me_ref, bf16[1024,768]{1,0:T(8,128)(2,1)} %grad_ref.2, bf16[1024,3072]{1,0:T(8,128)(2,1)} %get-tuple-element.309.slope_ref, f32[1024,768]{1,0:T(8,128)} %get-tuple-element.304.middle_ref, ...), custom_call_target="tpu_custom_call" | custom-call | flops 15000000512 | bytes 30000000 | tf_op jit(solution)/shard_map/ffn_backward/pallas_call | solution.py:355
  234.9 16.9 %ffn_weight.2 = (bf16[2,2,4,192,768]{4,3,2,1,0:T(8,128)(2,1)}, bf16[2,2,4,192,768]{4,3,2,1,0:T(8,128)(2,1)}) custom-call(s32[2]{0:T(128)} %pad_add_fusion.me_ref, bf16[1024,768]{1,0:T(8,128)(2,1)} %get-tuple-element.303.nffn_ref, bf16[1024,768]{1,0:T(8,128)(2,1)} %grad_ref.2, bf16[1024,3072]{1,0:T(8,128)(2,1)} %get-tuple-element.313.gupper_ref, ...), custom_call_target="tpu_custom_call" | custom-call | flops 15000000512 | bytes 30000000 | tf_op jit(solution)/shard_map/ffn_weight/pallas_call | solution.py:607
  252.5 9.7 %attention_backward.4 = (f32[1024,768]{1,0:T(8,128)}, bf16[1024,2304]{1,0:T(8,128)(2,1)}, f32[8,768]{1,0:T(8,128)}) custom-call(f32[1024,768]{1,0:T(8,128)} %get-tuple-element.329.gmiddle_ref, f32[1024,768]{1,0:T(8,128)} %get-tuple-element.288.stream_ref, bf16[1024,2304]{1,0:T(8,128)(2,1)} %get-tuple-element.320.proj_ref, ...), custom_call_target="tpu_custom_call" | custom-call | flops 15000000512 | bytes 20000000 | tf_op jit(solution)/shard_map/attention_backward/pallas_call | solution.py:479
  266.1 19.9 %attention_backward.5 = (f32[1024,768]{1,0:T(8,128)}, bf16[1024,2304]{1,0:T(8,128)(2,1)}, f32[8,768]{1,0:T(8,128)}) custom-call(f32[1024,768]{1,0:T(8,128)} %get-tuple-element.329.gmiddle_ref, f32[1024,768]{1,0:T(8,128)} %get-tuple-element.288.stream_ref, ...), custom_call_target="tpu_custom_call", output_to_operand_aliasing={{0}: (7, {}), {1}: (8, {})} | custom-call | flops 15000000512 | bytes 20000000 | tf_op jit(solution)/shard_map/attention_backward/pallas_call | solution.py:479
  286.0 7.4 %collective-permute-done.26 = bf16[2,4,192,768]{3,2,1,0:T(8,128)(2,1)} collective-permute-done((bf16[2,4,192,768]{3,2,1,0:T(8,128)(2,1)S(1)}, bf16[2,4,192,768]{3,2,1,0:T(8,128)(2,1)}, u32[]{:S(2)}, u32[]{:S(2)}) %collective-permute-start.26) | collective-permute-done | bytes 2359328 | tf_op jit(solution)/shard_map/ppermute | solution.py:753
  296.9 11.8 %attention_weight.2 = (bf16[2,2,4,96,768]{4,3,2,1,0:T(8,128)(2,1)}, bf16[2,2,4,96,768]{4,3,2,1,0:T(8,128)(2,1)}) custom-call(s32[2]{0:T(128)} %pad_add_fusion.me_ref, bf16[1024,768]{1,0:T(8,128)(2,1)} %get-tuple-element.339.normed_ref, bf16[1024,768]{1,0:T(8,128)(2,1)} %get-tuple-element.340.mixed_ref, bf16[1024,2304]{1,0:T(8,128)(2,1)} %get-tuple-element.341.gproj_ref, ...), custom_call_target="tpu_custom_call" | custom-call | flops 10000000000 | bytes 20000000 | tf_op jit(solution)/shard_map/attention_weight/pallas_call | solution.py:679
  311.8 19.9 %ffn_backward.3 = (bf16[1024,3072]{1,0:T(8,128)(2,1)}, f32[1024,768]{1,0:T(8,128)}, f32[8,768]{1,0:T(8,128)}, f32[1,3072]{1,0:T(1,128)}) custom-call(s32[2]{0:T(128)} %pad_add_fusion.me_ref, f32[1024,768]{1,0:T(8,128)} %get-tuple-element.348.grad_ref, bf16[1024,3072]{1,0:T(8,128)(2,1)} %get-tuple-element.349.slope_ref, ...), custom_call_target="tpu_custom_call" | custom-call | flops 15000000512 | bytes 30000000 | tf_op jit(solution)/shard_map/ffn_backward/pallas_call | solution.py:355
  335.9 17.7 %ffn_weight.3 = (bf16[2,2,4,192,768]{4,3,2,1,0:T(8,128)(2,1)}, bf16[2,2,4,192,768]{4,3,2,1,0:T(8,128)(2,1)}) custom-call(s32[2]{0:T(128)} %pad_add_fusion.me_ref, bf16[1024,768]{1,0:T(8,128)(2,1)} %get-tuple-element.272.nffn_ref, f32[1024,768]{1,0:T(8,128)} %get-tuple-element.348.grad_ref, bf16[1024,3072]{1,0:T(8,128)(2,1)} %get-tuple-element.359.gupper_ref, ...), custom_call_target="tpu_custom_call" | custom-call | flops 15000000512 | bytes 30000000 | tf_op jit(solution)/shard_map/ffn_weight/pallas_call | solution.py:607
  359.8 9.3 %attention_backward.6 = (f32[1024,768]{1,0:T(8,128)}, bf16[1024,2304]{1,0:T(8,128)(2,1)}, f32[8,768]{1,0:T(8,128)}) custom-call(f32[1024,768]{1,0:T(8,128)} %get-tuple-element.382.gmiddle_ref, bf16[1024,768]{1,0:T(8,128)(2,1)} %stream_ref.4, bf16[1024,2304]{1,0:T(8,128)(2,1)} %get-tuple-element.370.proj_ref, ...), custom_call_target="tpu_custom_call" | custom-call | flops 15000000512 | bytes 20000000 | tf_op jit(solution)/shard_map/attention_backward/pallas_call | solution.py:479
  378.7 19.9 %attention_backward.7 = (f32[1024,768]{1,0:T(8,128)}, bf16[1024,2304]{1,0:T(8,128)(2,1)}, f32[8,768]{1,0:T(8,128)}) custom-call(f32[1024,768]{1,0:T(8,128)} %get-tuple-element.382.gmiddle_ref, bf16[1024,768]{1,0:T(8,128)(2,1)} %stream_ref.4, bf16[1024,2304]{1,0:T(8,128)(2,1)} %get-tuple-element.370.proj_ref, ...), custom_call_target="tpu_custom_call", output_to_operand_aliasing={{0}: (7, {}), {1}: (8, {})} | custom-call | flops 15000000512 | bytes 20000000 | tf_op jit(solution)/shard_map/attention_backward/pallas_call | solution.py:479
  399.1 6.1 %collective-permute-done.32 = bf16[2,4,192,768]{3,2,1,0:T(8,128)(2,1)} collective-permute-done((bf16[2,4,192,768]{3,2,1,0:T(8,128)(2,1)}, bf16[2,4,192,768]{3,2,1,0:T(8,128)(2,1)}, u32[]{:S(2)}, u32[]{:S(2)}) %collective-permute-start.32) | collective-permute-done | bytes 2359328 | tf_op jit(solution)/shard_map/ppermute | solution.py:753
  412.4 12.2 %attention_weight.3 = (bf16[2,2,4,112,768]{4,3,2,1,0:T(8,128)(2,1)}, bf16[2,2,4,112,768]{4,3,2,1,0:T(8,128)(2,1)}) custom-call(s32[2]{0:T(128)} %pad_add_fusion.me_ref, bf16[1024,768]{1,0:T(8,128)(2,1)} %get-tuple-element.395.normed_ref, bf16[1024,768]{1,0:T(8,128)(2,1)} %get-tuple-element.396.mixed_ref, bf16[1024,2304]{1,0:T(8,128)(2,1)} %get-tuple-element.397.gproj_ref, ...), custom_call_target="tpu_custom_call" | custom-call | flops 10000000000 | bytes 20000000 | tf_op jit(solution)/shard_map/attention_weight/pallas_call | solution.py:679
  424.6 6.3 %collective-permute-done.36 = bf16[288,768]{1,0:T(8,128)(2,1)} collective-permute-done((bf16[288,768]{1,0:T(8,128)(2,1)}, bf16[288,768]{1,0:T(8,128)(2,1)}, u32[]{:S(2)}, u32[]{:S(2)}) %collective-permute-start.36) | collective-permute-done | bytes 442400 | tf_op jit(solution)/shard_map/ppermute | solution.py:753
  437.8 16.5 %collective-permute-done.39 = bf16[192,768]{1,0:T(8,128)(2,1)S(1)} collective-permute-done((bf16[192,768]{1,0:T(8,128)(2,1)S(1)}, bf16[192,768]{1,0:T(8,128)(2,1)S(1)}, u32[]{:S(2)}, u32[]{:S(2)}) %collective-permute-start.39) | collective-permute-done | bytes 294944 | tf_op jit(solution)/shard_map/ppermute | solution.py:753
  (283 shorter events, 170.4 us)
Async XLA Ops:
  7.2 106.1 %all-gather.3.cloned.1.call-start = ((), (), s32[]{:S(2)}) async-start(), calls=%async_computation | async-start | bytes 2211840 | tf_op jit(solution)/shard_map/all_gather | solution.py:784
  31.4 16.9 %collective-permute-start.6 = (bf16[4,96,768]{2,1,0:T(8,128)(2,1)S(1)}, bf16[4,96,768]{2,1,0:T(8,128)(2,1)S(1)}, u32[]{:S(2)}, u32[]{:S(2)}) collective-permute-start(bf16[4,96,768]{2,1,0:T(8,128)(2,1)S(1)} %get-tuple-element.232), channel_id=1, source_target_pairs={{0,4},{1,3},{2,6},{3,1},{4,0},{5,7},{6,2},{7,5},{8,12},{9,11},{10,... | collective-permute-start | bytes 1769480 | tf_op jit(solution)/shard_map/ppermute | solution.py:753
  33.0 15.4 %collective-permute-start.7 = (bf16[192,768]{1,0:T(8,128)(2,1)S(1)}, bf16[192,768]{1,0:T(8,128)(2,1)S(1)}, u32[]{:S(2)}, u32[]{:S(2)}) collective-permute-start(bf16[192,768]{1,0:T(8,128)(2,1)S(1)} %get-tuple-element.239), channel_id=1, source_target_pairs={{0,16},{1,17},{2,18},{3,19},{4,20},{5,21},{6,22},{7,23},{8,24},{9,... | collective-permute-start | bytes 884744 | tf_op jit(solution)/shard_map/ppermute | solution.py:753
  48.5 16.6 %collective-permute-start.8 = (bf16[2,4,96,768]{3,2,1,0:T(8,128)(2,1)S(1)}, bf16[2,4,96,768]{3,2,1,0:T(8,128)(2,1)}, u32[]{:S(2)}, u32[]{:S(2)}) collective-permute-start(bf16[2,4,96,768]{3,2,1,0:T(8,128)(2,1)S(1)} %pad_maximum_fusion.3.refs_0_), channel_id=1, source_target_pairs={{0,2},{1,5},{2,0},{3,7},{4,6},{5,1},{6,4},{7,3},{8,10},{9,13},{10,... | collective-permute-start | bytes 3538952 | tf_op jit(solution)/shard_map/ppermute | solution.py:753
  48.9 16.1 %collective-permute-start.9 = (bf16[2,4,96,768]{3,2,1,0:T(8,128)(2,1)S(1)}, bf16[2,4,96,768]{3,2,1,0:T(8,128)(2,1)S(1)}, u32[]{:S(2)}, u32[]{:S(2)}) collective-permute-start(bf16[2,4,96,768]{3,2,1,0:T(8,128)(2,1)S(1)} %pad_maximum_fusion.3.refs_0_), channel_id=1, source_target_pairs={{0,1},{1,0},{2,3},{3,2},{4,5},{5,4},{6,7},{7,6},{8,9},{9,8},{10,11... | collective-permute-start | bytes 3538952 | tf_op jit(solution)/shard_map/ppermute | solution.py:753
  66.4 16.4 %collective-permute-start.13 = (bf16[4,192,768]{2,1,0:T(8,128)(2,1)S(1)}, bf16[4,192,768]{2,1,0:T(8,128)(2,1)}, u32[]{:S(2)}, u32[]{:S(2)}) collective-permute-start(bf16[4,192,768]{2,1,0:T(8,128)(2,1)S(1)} %get-tuple-element.244), channel_id=1, source_target_pairs={{0,4},{1,3},{2,6},{3,1},{4,0},{5,7},{6,2},{7,5},{8,12},{9,11},{10,... | collective-permute-start | bytes 3538952 | tf_op jit(solution)/shard_map/ppermute | solution.py:753
  84.3 29.0 %collective-permute-start.14 = (bf16[2,4,192,768]{3,2,1,0:T(8,128)(2,1)S(1)}, bf16[2,4,192,768]{3,2,1,0:T(8,128)(2,1)}, u32[]{:S(2)}, u32[]{:S(2)}) collective-permute-start(bf16[2,4,192,768]{3,2,1,0:T(8,128)(2,1)S(1)} %pad_maximum_fusion.1.refs_0_.refs_4_), channel_id=1, source_target_pairs={{0,2},{1,5},{2,0},{3,7},{4,6},{5,1},{6,4},{7,3},{8,10},{9,13},{10,... | collective-permute-start | bytes 7077896 | tf_op jit(solution)/shard_map/ppermute | solution.py:753
  85.6 27.7 %collective-permute-start.15 = (bf16[2,4,192,768]{3,2,1,0:T(8,128)(2,1)S(1)}, bf16[2,4,192,768]{3,2,1,0:T(8,128)(2,1)}, u32[]{:S(2)}, u32[]{:S(2)}) collective-permute-start(bf16[2,4,192,768]{3,2,1,0:T(8,128)(2,1)S(1)} %pad_maximum_fusion.1.refs_0_.refs_4_), channel_id=1, source_target_pairs={{0,1},{1,0},{2,3},{3,2},{4,5},{5,4},{6,7},{7,6},{8,9},{9,8},{10,11... | collective-permute-start | bytes 7077896 | tf_op jit(solution)/shard_map/ppermute | solution.py:753
  125.9 28.1 %collective-permute-start.18 = (bf16[2,4,96,768]{3,2,1,0:T(8,128)(2,1)S(1)}, bf16[2,4,96,768]{3,2,1,0:T(8,128)(2,1)S(1)}, u32[]{:S(2)}, u32[]{:S(2)}) collective-permute-start(bf16[2,4,96,768]{3,2,1,0:T(8,128)(2,1)S(1)} %pad_maximum_fusion.5.refs_0_), channel_id=1, source_target_pairs={{0,2},{1,5},{2,0},{3,7},{4,6},{5,1},{6,4},{7,3},{8,10},{9,13},{10,... | collective-permute-start | bytes 3538952 | tf_op jit(solution)/shard_map/ppermute | solution.py:753
  127.2 26.8 %collective-permute-start.19 = (bf16[2,4,96,768]{3,2,1,0:T(8,128)(2,1)S(1)}, bf16[2,4,96,768]{3,2,1,0:T(8,128)(2,1)S(1)}, u32[]{:S(2)}, u32[]{:S(2)}) collective-permute-start(bf16[2,4,96,768]{3,2,1,0:T(8,128)(2,1)S(1)} %pad_maximum_fusion.5.refs_0_), channel_id=1, source_target_pairs={{0,1},{1,0},{2,3},{3,2},{4,5},{5,4},{6,7},{7,6},{8,9},{9,8},{10,11... | collective-permute-start | bytes 3538952 | tf_op jit(solution)/shard_map/ppermute | solution.py:753
  127.2 26.8 %collective-permute-start.20 = (bf16[4,192,768]{2,1,0:T(8,128)(2,1)S(1)}, bf16[4,192,768]{2,1,0:T(8,128)(2,1)S(1)}, u32[]{:S(2)}, u32[]{:S(2)}) collective-permute-start(bf16[4,192,768]{2,1,0:T(8,128)(2,1)S(1)} %get-tuple-element.271), channel_id=1, source_target_pairs={{0,4},{1,3},{2,6},{3,1},{4,0},{5,7},{6,2},{7,5},{8,12},{9,11},{10,... | collective-permute-start | bytes 3538952 | tf_op jit(solution)/shard_map/ppermute | solution.py:753
  158.1 28.9 %collective-permute-start.22 = (bf16[2,4,192,768]{3,2,1,0:T(8,128)(2,1)S(1)}, bf16[2,4,192,768]{3,2,1,0:T(8,128)(2,1)}, u32[]{:S(2)}, u32[]{:S(2)}) collective-permute-start(bf16[2,4,192,768]{3,2,1,0:T(8,128)(2,1)S(1)} %pad_maximum_fusion.2.refs_0_.refs_4_), channel_id=1, source_target_pairs={{0,2},{1,5},{2,0},{3,7},{4,6},{5,1},{6,4},{7,3},{8,10},{9,13},{10,... | collective-permute-start | bytes 7077896 | tf_op jit(solution)/shard_map/ppermute | solution.py:753
  159.7 27.4 %collective-permute-start.23 = (bf16[2,4,192,768]{3,2,1,0:T(8,128)(2,1)S(1)}, bf16[2,4,192,768]{3,2,1,0:T(8,128)(2,1)}, u32[]{:S(2)}, u32[]{:S(2)}) collective-permute-start(bf16[2,4,192,768]{3,2,1,0:T(8,128)(2,1)S(1)} %pad_maximum_fusion.2.refs_0_.refs_4_), channel_id=1, source_target_pairs={{0,1},{1,0},{2,3},{3,2},{4,5},{5,4},{6,7},{7,6},{8,9},{9,8},{10,11... | collective-permute-start | bytes 7077896 | tf_op jit(solution)/shard_map/ppermute | solution.py:753
  264.4 29.0 %collective-permute-start.26 = (bf16[2,4,192,768]{3,2,1,0:T(8,128)(2,1)S(1)}, bf16[2,4,192,768]{3,2,1,0:T(8,128)(2,1)}, u32[]{:S(2)}, u32[]{:S(2)}) collective-permute-start(bf16[2,4,192,768]{3,2,1,0:T(8,128)(2,1)S(1)} %fusion.1), channel_id=1, source_target_pairs={{0,2},{1,5},{2,0},{3,7},{4,6},{5,1},{6,4},{7,3},{8,10},{9,13},{10,... | collective-permute-start | bytes 7077896 | tf_op jit(solution)/shard_map/ppermute | solution.py:753
  295.5 16.3 %collective-permute-start.27 = (bf16[4,192,768]{2,1,0:T(8,128)(2,1)S(1)}, bf16[4,192,768]{2,1,0:T(8,128)(2,1)S(1)}, u32[]{:S(2)}, u32[]{:S(2)}) collective-permute-start(bf16[4,192,768]{2,1,0:T(8,128)(2,1)S(1)} %fusion.6), channel_id=1, source_target_pairs={{0,4},{1,3},{2,6},{3,1},{4,0},{5,7},{6,2},{7,5},{8,12},{9,11},{10,... | collective-permute-start | bytes 3538952 | tf_op jit(solution)/shard_map/ppermute | solution.py:753
  311.8 19.9 %collective-permute-start.28 = (bf16[2,2,4,96,768]{4,3,2,1,0:T(8,128)(2,1)}, bf16[2,2,4,96,768]{4,3,2,1,0:T(8,128)(2,1)}, u32[]{:S(2)}, u32[]{:S(2)}) collective-permute-start(bf16[2,2,4,96,768]{4,3,2,1,0:T(8,128)(2,1)} %get-tuple-element.347), channel_id=1, source_target_pairs={{0,1},{1,0},{2,3},{3,2},{4,5},{5,4},{6,7},{7,6},{8,9},{9,8},{10,11... | collective-permute-start | bytes 7077896 | tf_op jit(solution)/shard_map/ppermute | solution.py:753
  334.3 19.3 %collective-permute-start.29 = (bf16[2,4,96,768]{3,2,1,0:T(8,128)(2,1)}, bf16[2,4,96,768]{3,2,1,0:T(8,128)(2,1)}, u32[]{:S(2)}, u32[]{:S(2)}) collective-permute-start(bf16[2,4,96,768]{3,2,1,0:T(8,128)(2,1)} %fusion.10), channel_id=1, source_target_pairs={{0,2},{1,5},{2,0},{3,7},{4,6},{5,1},{6,4},{7,3},{8,10},{9,13},{10,... | collective-permute-start | bytes 3538952 | tf_op jit(solution)/shard_map/ppermute | solution.py:753
  376.1 29.2 %collective-permute-start.32 = (bf16[2,4,192,768]{3,2,1,0:T(8,128)(2,1)}, bf16[2,4,192,768]{3,2,1,0:T(8,128)(2,1)}, u32[]{:S(2)}, u32[]{:S(2)}) collective-permute-start(bf16[2,4,192,768]{3,2,1,0:T(8,128)(2,1)} %fusion.2), channel_id=1, source_target_pairs={{0,2},{1,5},{2,0},{3,7},{4,6},{5,1},{6,4},{7,3},{8,10},{9,13},{10,... | collective-permute-start | bytes 7077896 | tf_op jit(solution)/shard_map/ppermute | solution.py:753
  377.1 22.1 %collective-permute-start.33 = (bf16[288,768]{1,0:T(8,128)(2,1)}, bf16[288,768]{1,0:T(8,128)(2,1)}, u32[]{:S(2)}, u32[]{:S(2)}) collective-permute-start(bf16[288,768]{1,0:T(8,128)(2,1)} %get-tuple-element.381), channel_id=1, source_target_pairs={{0,16},{1,17},{2,18},{3,19},{4,20},{5,21},{6,22},{7,23},{8,24},{9,... | collective-permute-start | bytes 1327112 | tf_op jit(solution)/shard_map/ppermute | solution.py:753
  408.4 22.5 %collective-permute-start.34 = (bf16[4,192,768]{2,1,0:T(8,128)(2,1)}, bf16[4,192,768]{2,1,0:T(8,128)(2,1)}, u32[]{:S(2)}, u32[]{:S(2)}) collective-permute-start(bf16[4,192,768]{2,1,0:T(8,128)(2,1)} %fusion.4), channel_id=1, source_target_pairs={{0,4},{1,3},{2,6},{3,1},{4,0},{5,7},{6,2},{7,5},{8,12},{9,11},{10,... | collective-permute-start | bytes 3538952 | tf_op jit(solution)/shard_map/ppermute | solution.py:753
  411.1 19.8 %collective-permute-start.36 = (bf16[288,768]{1,0:T(8,128)(2,1)}, bf16[288,768]{1,0:T(8,128)(2,1)}, u32[]{:S(2)}, u32[]{:S(2)}) collective-permute-start(bf16[288,768]{1,0:T(8,128)(2,1)} %get-tuple-element.394), channel_id=1, source_target_pairs={{0,24},{1,25},{2,26},{3,27},{4,28},{5,29},{6,30},{7,31},{8,16},{9,... | collective-permute-start | bytes 1327112 | tf_op jit(solution)/shard_map/ppermute | solution.py:753
  436.5 18.4 %collective-permute-start.38 = (bf16[2,4,112,768]{3,2,1,0:T(8,128)(2,1)S(1)}, bf16[2,4,112,768]{3,2,1,0:T(8,128)(2,1)S(1)}, u32[]{:S(2)}, u32[]{:S(2)}) collective-permute-start(bf16[2,4,112,768]{3,2,1,0:T(8,128)(2,1)S(1)} %fusion.7), channel_id=1, source_target_pairs={{0,2},{1,5},{2,0},{3,7},{4,6},{5,1},{6,4},{7,3},{8,10},{9,13},{10,... | collective-permute-start | bytes 4128776 | tf_op jit(solution)/shard_map/ppermute | solution.py:753
  437.8 16.5 %collective-permute-start.39 = (bf16[192,768]{1,0:T(8,128)(2,1)S(1)}, bf16[192,768]{1,0:T(8,128)(2,1)S(1)}, u32[]{:S(2)}, u32[]{:S(2)}) collective-permute-start(bf16[192,768]{1,0:T(8,128)(2,1)S(1)} %get-tuple-element.407), channel_id=1, source_target_pairs={{0,16},{1,17},{2,18},{3,19},{4,20},{5,21},{6,22},{7,23},{8,24},{9,... | collective-permute-start | bytes 884744 | tf_op jit(solution)/shard_map/ppermute | solution.py:753
  456.2 16.6 %collective-permute-start.40 = (bf16[4,112,768]{2,1,0:T(8,128)(2,1)}, bf16[4,112,768]{2,1,0:T(8,128)(2,1)}, u32[]{:S(2)}, u32[]{:S(2)}) collective-permute-start(bf16[4,112,768]{2,1,0:T(8,128)(2,1)} %fusion.8), channel_id=1, source_target_pairs={{0,4},{1,3},{2,6},{3,1},{4,0},{5,7},{6,2},{7,5},{8,12},{9,11},{10,... | collective-permute-start | bytes 2064392 | tf_op jit(solution)/shard_map/ppermute | solution.py:753
  (77 other events, 975.6 us)
Sparse Core Ops, SparseCore 0:
  68.7 39.1 all-gather.2

commit v4 on v3

--- a/solution.py
+++ b/solution.py
@@ -102,8 +102,9 @@
 
 
 def start_weights(groups):
-    for copy in [copy for group in groups for copy in weight_copies(*group)]:
-        copy.start()
+    for together in zip(*[weight_copies(*group) for group in groups]):
+        for copy in together:
+            copy.start()
 
 
 def wait_weight(full, sems, part):
@@ -564,59 +565,64 @@
         pltpu.make_async_copy(staged.at[slot, x], own_ref.at[0, 0], sems.at[slot, x]).wait()
 
 
-def ffn_weight_split_kernel(
-    me_ref, nffn_ref, grad_ref, gupper_ref, active_ref, other_ref, own_ref, turned, nffn_t, grad_t, staged, sems
-):
+def ffn_weight_split_kernel(core, me_ref, nffn_ref, grad_ref, gupper_ref, active_ref, out_ref, *refs):
     step = pl.program_id(0)
+    staged, sems = refs[-2:]
     _, _, depth, high, width = staged.shape
     high = high // 2
-
-    @pl.when(step == 0)
+    if core == 1:
+        nffn_out, grad_out, turned, nffn_t, grad_t = refs[:-2]
+        kept = [
+            pltpu.make_async_copy(nffn_t, nffn_out, sems.at[2, 0]),
+            pltpu.make_async_copy(grad_t, grad_out, sems.at[2, 1]),
+        ]
+
+        @pl.when(step == 0)
+        def _():
+            turned[...] = nffn_ref[...].T
+            relative_rows(turned, nffn_t, me_ref[0], depth)
+            turned[...] = grad_ref[...].astype(BF).T
+            relative_rows(turned, grad_t, me_ref[0], depth)
+            for copy in kept:
+                copy.start()
+    else:
+        nffn_t, grad_t, kept = nffn_ref, grad_ref, []
+
+    shape = (2, depth, high, width)
+    staged[step, :, :, :high, :] = dot_nn(nffn_t[...], gupper_ref[...]).astype(BF).reshape(shape)
+    staged[step, :, :, high:, :] = dot_nn(grad_t[...], active_ref[...]).astype(BF).reshape(shape)
+    for x in range(2):
+        first, second = plane(me_ref, x, step, core)
+        pltpu.make_async_copy(staged.at[step, x], out_ref.at[second, first], sems.at[step, x]).start()
+
+    @pl.when(step == 1)
     def _():
-        turned[...] = nffn_ref[...].T
-        relative_rows(turned, nffn_t, me_ref[0], depth)
-        turned[...] = grad_ref[...].astype(BF).T
-        relative_rows(turned, grad_t, me_ref[0], depth)
-
-    slot = step % 2
-
-    @pl.when(step >= 2)
-    def _():
-        wait_out(staged, slot, own_ref, sems)
-
-    shape = (2, depth, high, width)
-    staged[slot, :, :, :high, :] = dot_nn(nffn_t[...], gupper_ref[...]).astype(BF).reshape(shape)
-    staged[slot, :, :, high:, :] = dot_nn(grad_t[...], active_ref[...]).astype(BF).reshape(shape)
-    send_out(me_ref, 1 - step // 2, step % 2, staged, slot, own_ref, other_ref, sems)
-
-    @pl.when(step == 3)
-    def _():
-        wait_out(staged, 1 - slot, own_ref, sems)
-        wait_out(staged, slot, own_ref, sems)
-
-
-def ffn_weight_split(me, nffn, grad, gupper, active, depth):
-    rows, width = nffn.shape
-    piece = gupper.shape[1] // 4
+        wait_out(staged, 0, out_ref, sems)
+        wait_out(staged, 1, out_ref, sems)
+        for copy in kept:
+            copy.wait()
+
+
+def ffn_weight_split(me, nffn, grad, gupper, active, depth, core):
+    rows, piece = gupper.shape[0], gupper.shape[1] // 4
+    width = piece
     high = width // (2 * depth)
-
-    def column(step, me):
-        return (0, jnp.bitwise_xor(me[1], 2 * (step % 2) + 1 - step // 2))
-
-    whole = pl.BlockSpec((rows, width), lambda i, me: (0, 0))
+    whole = lambda array: pl.BlockSpec(array.shape, lambda i, me: (0, 0))
+    column = pl.BlockSpec((rows, piece), lambda i, me: (0, jnp.bitwise_xor(me[1], 2 * i + core)))
+    shape = (2, 2, depth, 2 * high, piece)
     return pl.pallas_call(
-        ffn_weight_split_kernel,
+        functools.partial(ffn_weight_split_kernel, core),
         grid_spec=pltpu.PrefetchScalarGridSpec(
             num_scalar_prefetch=1,
-            grid=(4,),
-            in_specs=[whole, whole, pl.BlockSpec((rows, piece), column), pl.BlockSpec((rows, piece), column)],
-            out_specs=[pl.BlockSpec(memory_space=pl.ANY)] * 2,
-            scratch_shapes=[pltpu.VMEM((width, rows), BF)] * 3
-            + [pltpu.VMEM((2, 2, depth, 2 * high, piece), BF), pltpu.SemaphoreType.DMA((2, 2))],
+            grid=(2,),
+            in_specs=[whole(nffn), whole(grad), column, column],
+            out_specs=[pl.BlockSpec(memory_space=pl.ANY)] * (1 + 2 * core),
+            scratch_shapes=[pltpu.VMEM((width, rows), BF)] * (3 * core)
+            + [pltpu.VMEM(shape, BF), pltpu.SemaphoreType.DMA((3, 2))],
         ),
-        out_shape=[jax.ShapeDtypeStruct((2, 2, depth, 2 * high, piece), BF)] * 2,
+        out_shape=[jax.ShapeDtypeStruct(shape, BF)] + [jax.ShapeDtypeStruct((width, rows), BF)] * (2 * core),
         compiler_params=pltpu.CompilerParams(vmem_limit_bytes=VMEM_LIMIT),
-        cost_estimate=pl.CostEstimate(flops=15 * 10**9, bytes_accessed=30 * 10**6, transcendentals=0),
+        cost_estimate=pl.CostEstimate(flops=8 * 10**9, bytes_accessed=15 * 10**6, transcendentals=0),
         name="ffn_weight",
     )(me, nffn, grad, gupper, active)
 
@@ -640,8 +646,8 @@
         if extra_refs:
             extra_s[...] = jnp.zeros_like(extra_s)
             for index in range(2):
-                one_ref, more_ref, two_ref, hidden_ref = extra_refs[4 * index : 4 * index + 4]
-                sums = jnp.concatenate([one_ref[:4, :] + more_ref[:4, :], two_ref[:4, :]], axis=0)
+                one_ref, two_ref, hidden_ref = extra_refs[3 * index : 3 * index + 3]
+                sums = jnp.concatenate([one_ref[:4, :], two_ref[:4, :]], axis=0)
                 for part in range(4):
                     at = index * (width // 3)
                     extra_s[part, :8, at : at + share] = sums[:, part * share : (part + 1) * share]
@@ -846,6 +852,11 @@
         )
 
 
+def mid_first(sends):
+    at = (len(sends) + 1) // 2 - 1
+    return sends[at : at + 1] + sends[:at] + sends[at + 1 :]
+
+
 class Lane:
     def __init__(self):
         self.last = None
@@ -888,7 +899,6 @@
     pages = slot_kind.shape[0]
     block_pages = 2 if pages % 2 == 0 else 1
     block = block_pages * slot_kind.shape[1]
-    middle_page = block_pages
     masks = [pair_bias(slot_kind, slot_valid, index == 0) for index in range(2)]
     lane = Lane()
     gathered = lambda index: gather_rows(
@@ -913,13 +923,13 @@
             me, grad, kept["slope"], kept["middle"], small[index], kept["up_w"], kept["down_w"], block, parts
         )
 
-    def ffn_weight_of(index, grad):
+    def ffn_weight_of(index, grad, turned=None):
         kept = saved[index]
-        if split:
-            return lambda gupper: ffn_weight_split(
-                me, kept["nffn"], grad, gupper, kept["active"], exchange.depth
-            )
-        return lambda gupper: (ffn_weight(kept["nffn"], grad, gupper, kept["active"], stripes, parts),)
+        if not split:
+            return lambda gupper: (ffn_weight(kept["nffn"], grad, gupper, kept["active"], stripes, parts),)
+        core = 1 if turned is None else 0
+        left, right = (kept["nffn"], grad) if turned is None else turned
+        return lambda gupper: ffn_weight_split(me, left, right, gupper, kept["active"], exchange.depth, core)
 
     def attention_backward_of(index, begin, end, before=None):
         kept = saved[index]
@@ -952,21 +962,25 @@
         own_small = lax.reduce_precision(own_small, 8, 7)
         small_sends = [(functools.partial(exchange.part, bits), own_small) for bits in range(1, 4)]
         late = exchange.gather_z(late)
-        came, _ = lane.step(exchange.z_sends([attn_pieces[0]] * depth) + small_sends)
-        attn_zero = Spread(exchange, jnp.stack([attn_pieces[0]] + came[: depth - 1]), False)
-        mine = lax.axis_index("tensor")
-        every = jnp.zeros((4,) + own_small.shape, F32)
-        for bits, value in enumerate([own_small] + came[depth - 1 :]):
-            every = lax.dynamic_update_slice_in_dim(every, value[None], jnp.bitwise_xor(mine, bits), 0)
-        small = jnp.moveaxis(every[:, :, :8], 0, 2).reshape(2, 8, width)
-        hidden = jnp.moveaxis(every[:, :, 8:], 0, 1).reshape(2, -1)
+        came, _ = lane.step(exchange.z_sends([attn_pieces[0]] * depth))
+        attn_zero = Spread(exchange, jnp.stack([attn_pieces[0]] + came), False)
         ffn_piece = jnp.concatenate([up_pieces[0], down_pieces[0]], axis=0)
         ffn_sends = exchange.z_sends([ffn_piece] * depth)
         middle_at = depth // 2 - 1
-        came, _ = lane.step(attn_zero.go_first() + ffn_sends[middle_at : middle_at + 1])
-        ffn_came = came[1:]
+        came, _ = lane.step(attn_zero.go_first() + ffn_sends[middle_at : middle_at + 1] + small_sends)
+        ffn_came = came[1:2]
+        mine = lax.axis_index("tensor")
+
+        def order_small(*values):
+            every = jnp.zeros((4,) + own_small.shape, F32)
+            for bits, value in enumerate(values):
+                every = lax.dynamic_update_slice_in_dim(every, value[None], jnp.bitwise_xor(mine, bits), 0)
+            small = jnp.moveaxis(every[:, :, :8], 0, 2).reshape(2, 8, width)
+            return small[0], small[1], jnp.moveaxis(every[:, :, 8:], 0, 1).reshape(2, -1)
+
         ffn_sends = ffn_sends[:middle_at] + ffn_sends[middle_at + 1 :]
-        came, _ = lane.step(attn_zero.go_second(came[:1]) + ffn_sends)
+        came, results = lane.step(attn_zero.go_second(came[:1]) + ffn_sends, order_small, [own_small] + came[2:])
+        small, hidden = results[:2], results[2]
         others = came[2:]
         others.insert(middle_at, ffn_came[0])
         ffn_zero = Spread(exchange, jnp.stack([ffn_piece] + others), False)
@@ -994,44 +1008,45 @@
         block_output = ffn[0]
 
         _, (gupper, gmiddle, small_two, hidden_one) = lane.step([], ffn_backward_of(1), [out_grad])
-        _, grads = lane.step([], ffn_weight_of(1, out_grad), [gupper])
-        ffn_one = Reduce(exchange, *grads)
-        came, before = lane.step(ffn_one.go_core(), attention_backward_of(1, 0, middle_page), [gmiddle])
-        came, after = lane.step(
-            ffn_one.go_second(came), attention_backward_of(1, middle_page, pages, before[:2]), [gmiddle]
-        )
-        grad, gproj = after[:2]
-        sums_one = (before[2], after[2], small_two, hidden_one)
+        _, (other, *turned) = lane.step([], ffn_weight_of(1, out_grad), [gupper])
+        came, (own,) = lane.step([(exchange.core, other)], ffn_weight_of(1, out_grad, turned), [gupper])
+        ffn_one = Reduce(exchange, other, own)
+        came, (grad, gproj, small_one) = lane.step(
+            ffn_one.go_second(came), attention_backward_of(1, 0, pages), [gmiddle]
+        )
+        sums_one = (small_one, small_two, hidden_one)
         came, grads = lane.step(ffn_one.go_first(came), attention_weight_of(1, gmiddle), [gproj])
-        layers = ffn_one.depths(came)
+        ffn_layers = ffn_one.depths(came)
+        ffn_sends = mid_first(exchange.z_sends([ffn_layers[z].astype(BF) for z in range(depth)]))
         attn_one = Reduce(exchange, *grads)
-        came, results = lane.step(attn_one.go_core(), ffn_backward_of(0), [grad])
+        came, results = lane.step(attn_one.go_core() + ffn_sends[:1], ffn_backward_of(0), [grad])
+        ffn_came = came[1:]
         gupper, gmiddle, small_two, hidden_zero = results
-        came, grads = lane.step(attn_one.go_second(came), ffn_weight_of(0, grad), [gupper])
-        ffn_zero = Reduce(exchange, *grads)
-        came, before = lane.step(
-            ffn_zero.go_core() + attn_one.go_first(came), attention_backward_of(0, 0, middle_page), [gmiddle]
-        )
-        layers = jnp.concatenate([attn_one.depths(came[1:]), layers], axis=1)
-        late_sends = exchange.z_sends([layers[z].astype(BF) for z in range(depth)])
-        late_sends = late_sends[middle_at : middle_at + 1] + late_sends[:middle_at] + late_sends[middle_at + 1 :]
-        came, after = lane.step(
-            ffn_zero.go_second(came[:1]) + late_sends[:1],
-            attention_backward_of(0, middle_page, pages, before[:2]),
-            [gmiddle],
-        )
-        late_came = came[1:]
-        input_grad, gproj = after[:2]
+        came, (other, *turned) = lane.step(
+            attn_one.go_second(came[:1]) + ffn_sends[1:], ffn_weight_of(0, grad), [gupper]
+        )
+        ffn_came = ffn_came + came[1:]
+        total = ffn_layers[0] + sum(value.astype(F32) for value in ffn_came)
+        grad_up, grad_down = [None, total[:high]], [None, total[high:]]
+        came, (own,) = lane.step(
+            [(exchange.core, other)] + attn_one.go_first(came[:1]), ffn_weight_of(0, grad, turned), [gupper]
+        )
+        ffn_zero = Reduce(exchange, other, own)
+        attn_layers = attn_one.depths(came[1:])
+        attn_sends = mid_first(exchange.z_sends([attn_layers[z].astype(BF) for z in range(depth)]))
+        came, (input_grad, gproj, small_one) = lane.step(
+            ffn_zero.go_second(came[:1]) + attn_sends[:1], attention_backward_of(0, 0, pages), [gmiddle]
+        )
+        attn_came = came[1:]
         came, grads = lane.step(
-            ffn_zero.go_first(came[:1]) + late_sends[1:],
-            attention_weight_of(0, gmiddle, (before[2], after[2], small_two, hidden_zero) + sums_one),
+            ffn_zero.go_first(came[:1]) + attn_sends[1:],
+            attention_weight_of(0, gmiddle, (small_one, small_two, hidden_zero) + sums_one),
             [gproj],
         )
-        total = layers[0] + sum(value.astype(F32) for value in late_came + came[1:])
-        grad_attn, grad_up, grad_down = ([None, total[at : at + high]] for at in (0, high, 2 * high))
+        grad_attn = [None, attn_layers[0] + sum(value.astype(F32) for value in attn_came + came[1:])]
         layers = ffn_zero.depths(came[:1])
         ffn_sends = exchange.z_sends([layers[z].astype(BF) for z in range(depth)])
-        ffn_sends = ffn_sends[middle_at : middle_at + 1] + ffn_sends[:middle_at] + ffn_sends[middle_at + 1 :]
+        ffn_sends = mid_first(ffn_sends)
         attn_zero = Reduce(exchange, *grads)
         came, _ = lane.step(attn_zero.go_core())
         came, _ = lane.step(attn_zero.go_second(came) + ffn_sends[:1])
@@ -1043,6 +1058,7 @@
         came, _ = lane.step(exchange.z_sends([layers[z].astype(BF) for z in range(depth)]))
         total = layers[0] + sum(value.astype(F32) for value in came)
         grad_attn[0] = total[:high]
+        shared_squares = jnp.sum(total[high:] * total[high:])
         share = width // parts
         vectors = []
         for at in (0, width // 3):
@@ -1078,12 +1094,11 @@
             whole, at * (whole.shape[-1] // parts), whole.shape[-1] // parts, whole.ndim - 1
         )
         vectors, grad_hidden = slice_of(vectors), slice_of(grad_hidden)
+        shared_squares = jnp.sum(vectors * vectors) + jnp.sum(grad_hidden * grad_hidden)
     grad_gain, grad_bias = vectors[:, :2], vectors[:, 2:]
+    local_squares = sum(jnp.sum(grad * grad) for pair in (grad_up, grad_down, grad_attn) for grad in pair[::-1])
     grad_attn, grad_up, grad_down = jnp.stack(grad_attn), jnp.stack(grad_up), jnp.stack(grad_down)
-    shared_squares = jnp.sum(vectors * vectors) + jnp.sum(grad_hidden * grad_hidden)
-    local_squares = (
-        jnp.sum(grad_attn * grad_attn) + jnp.sum(grad_up * grad_up) + jnp.sum(grad_down * grad_down)
-    ) + jnp.where(lax.axis_index("dp") == 0, shared_squares, 0.0)
+    local_squares = local_squares + jnp.where(lax.axis_index("dp") == 0, shared_squares, 0.0)
     grad_down = jnp.swapaxes(grad_down, 1, 2)
     if split:
         total_squares = exchange.total(local_squares.reshape(1, 1))[0, 0]

time: 539 us -> 526 us (0.976)
  waiting for transfers between devices: 138 us -> 119 us
  starting transfers between devices: 58.4 us -> 65.9 us
    ppermute x51 -> x54, waiting for transfers between devices: 138 us -> 119 us  [swap(): return lax.ppermute(value, ('dp', 'tensor'), pairs)]
    pallas_call x2 -> x4, Pallas kernels: 34.6 us -> 44.2 us  [ffn_weight_split(): pl.pallas_call(functools.partial(ffn_weight_split_kernel, core), grid_spe...]
    pallas_call x4 -> x2, Pallas kernels: 58.8 us -> 50.2 us  [attention_backward(): pl.pallas_call(attention_backward_kernel, grid=((end - begin) // block_pa...]
    ppermute x51 -> x54, starting transfers between devices: 58.4 us -> 65.8 us  [swap(): return lax.ppermute(value, ('dp', 'tensor'), pairs)]
    another operation x3 -> x6, other arithmetic: 6.16 us -> 13.1 us
    unnamed x103 -> x101, local copies, waits for them, and re-layouts: 8.19 us -> 11.1 us
  transfers between devices with their start and end apart: 52 -> 55, of which waited for: 29 -> 29; matrix products, arithmetic and copies ran while one was open for 5% -> 4% of each run, Pallas kernels for 34% -> 36%
where the time goes in v4:
time: 526 us; the launch traced here: 522 us
  Pallas kernels  243 us (46%)
  waiting for transfers between devices  119 us (23%)
  starting transfers between devices  65.9 us (13%)
  other arithmetic  50.5 us (10%)
  between operations  24 us (5%)
  local copies, waits for them, and re-layouts  19.6 us (4%)
    ppermute x54, waiting for transfers between devices, swap(): return lax.ppermute(value, ('dp', 'tensor'), pairs)  119 us
    ppermute x54, starting transfers between devices, swap(): return lax.ppermute(value, ('dp', 'tensor'), pairs)  65.8 us
    pallas_call x2, Pallas kernels, attention_backward(): pl.pallas_call(attention_backward_kernel, grid=((end - begin) // block_pa...  50.2 us
    pallas_call x4, Pallas kernels, ffn_weight_split(): pl.pallas_call(functools.partial(ffn_weight_split_kernel, core), grid_spe...  44.2 us
    pallas_call x2, Pallas kernels, ffn_forward(): pl.pallas_call(functools.partial(ffn_forward_kernel, (up_w[0], down_w[0])...  43.2 us
    pallas_call x2, Pallas kernels, attention_forward(): pl.pallas_call(functools.partial(attention_forward_kernel, plan), grid=(p...  41.5 us
    pallas_call x2, Pallas kernels, ffn_backward(): pl.pallas_call(functools.partial(ffn_backward_kernel, (up_w[0], down_w[0]...  40.2 us
    pallas_call x2, Pallas kernels, attention_weight_split(): pl.pallas_call(attention_weight_split_kernel, grid=(3,), in_specs=[pl.Blo...  23.9 us
  transfers between devices with their start and end apart: 55, of which 29 were waited for; matrix products, arithmetic and copies ran while one was open for 4% of the time, Pallas kernels for 36%

profile of v4, /device:TPU:0, one launch (start us, length us, event | category | flops | bytes accessed | tf_op | source)
XLA Modules:
  0.0 521.7 jit_solution(17181735347259958487)
XLA Ops:
  9.4 5.1 collective-permute-start.2
  19.3 7.7 %collective-permute-done.1 = bf16[96,768]{1,0:T(8,128)(2,1)S(1)} collective-permute-done((bf16[96,768]{1,0:T(8,128)(2,1)S(1)}, bf16[96,768]{1,0:T(8,128)(2,1)S(1)}, u32[]{:S(2)}, u32[]{:S(2)}) %collective-permute-start.1) | collective-permute-done | bytes 147488 | tf_op jit(solution)/shard_map/ppermute | solution.py:759
  36.3 7.1 %collective-permute-done.4 = bf16[192,768]{1,0:T(8,128)(2,1)S(1)} collective-permute-done((bf16[192,768]{1,0:T(8,128)(2,1)S(1)}, bf16[192,768]{1,0:T(8,128)(2,1)S(1)}, u32[]{:S(2)}, u32[]{:S(2)}) %collective-permute-start.4) | collective-permute-done | bytes 294944 | tf_op jit(solution)/shard_map/ppermute | solution.py:759
  48.8 11.7 %collective-permute-done.10 = bf16[192,768]{1,0:T(8,128)(2,1)S(1)} collective-permute-done((bf16[192,768]{1,0:T(8,128)(2,1)}, bf16[192,768]{1,0:T(8,128)(2,1)S(1)}, u32[]{:S(2)}, u32[]{:S(2)}) %collective-permute-start.10) | collective-permute-done | bytes 294944 | tf_op jit(solution)/shard_map/ppermute | solution.py:759
  65.8 13.2 %collective-permute-done.13 = bf16[4,192,768]{2,1,0:T(8,128)(2,1)} collective-permute-done((bf16[4,192,768]{2,1,0:T(8,128)(2,1)S(1)}, bf16[4,192,768]{2,1,0:T(8,128)(2,1)}, u32[]{:S(2)}, u32[]{:S(2)}) %collective-permute-start.13) | collective-permute-done | bytes 1179680 | tf_op jit(solution)/shard_map/ppermute | solution.py:759
  83.7 20.8 %attention_forward.2 = (f32[1024,768]{1,0:T(8,128)}, bf16[1024,768]{1,0:T(8,128)(2,1)}, bf16[1024,768]{1,0:T(8,128)(2,1)}, bf16[1024,2304]{1,0:T(8,128)(2,1)}, b...) custom-call(s32[2]{0:T(128)} %pad_add_fusion.me_ref, ...), custom_call_target="tpu_custom_call" | custom-call | flops 20000000000 | bytes 30000000 | tf_op jit(solution)/shard_map/attention_forward/pallas_call | solution.py:189
  114.3 7.8 %collective-permute-done.17 = bf16[4,96,768]{2,1,0:T(8,128)(2,1)S(1)} collective-permute-done((bf16[4,96,768]{2,1,0:T(8,128)(2,1)S(1)}, bf16[4,96,768]{2,1,0:T(8,128)(2,1)S(1)}, u32[]{:S(2)}, u32[]{:S(2)}) %collective-permute-start.17) | collective-permute-done | bytes 589856 | tf_op jit(solution)/shard_map/ppermute | solution.py:759
  126.5 21.7 %ffn_forward.2 = (f32[1024,768]{1,0:T(8,128)}, bf16[1024,3072]{1,0:T(8,128)(2,1)}, bf16[1024,3072]{1,0:T(8,128)(2,1)}, bf16[4,768,768]{2,1,0:T(8,128)(2,1)}, bf16[4,768,768]{2,1,0:T(8,128)(2,1)}) custom-call(s32[2]{0:T(128)} %pad_add_fusion.me_ref, bf16[1024,768]{1,0:T(8,128)(2,1)} %get-tuple-element.290.nffn_ref, ...), custom_call_target="tpu_custom_call" | custom-call | flops 15000000512 | bytes 30000000 | tf_op jit(solution)/shard_map/ffn_forward/pallas_call | solution.py:281
  156.7 20.7 %attention_forward.3 = (f32[1024,768]{1,0:T(8,128)}, bf16[1024,768]{1,0:T(8,128)(2,1)}, bf16[1024,768]{1,0:T(8,128)(2,1)}, bf16[1024,2304]{1,0:T(8,128)(2,1)}, b...) custom-call(s32[2]{0:T(128)} %pad_add_fusion.me_ref, ...), custom_call_target="tpu_custom_call" | custom-call | flops 20000000000 | bytes 30000000 | tf_op jit(solution)/shard_map/attention_forward/pallas_call | solution.py:189
  177.4 6.5 %collective-permute-done.22.refs_1_.refs_5_ = bf16[2,4,192,768]{3,2,1,0:T(8,128)(2,1)S(1)} collective-permute-done((bf16[2,4,192,768]{3,2,1,0:T(8,128)(2,1)S(1)}, bf16[2,4,192,768]{3,2,1,0:T(8,128)(2,1)S(1)}, u32[]{:S(2)}, u32[]{:S(2)}) %collective-permute-start.22) | collective-permute-done | bytes 2359328 | tf_op jit(solution)/shard_map/ppermute | solution.py:759
  189.9 21.5 %ffn_forward.3 = (f32[1024,768]{1,0:T(8,128)}, bf16[1024,3072]{1,0:T(8,128)(2,1)}, bf16[1024,3072]{1,0:T(8,128)(2,1)}, bf16[4,768,768]{2,1,0:T(8,128)(2,1)}, bf16[4,768,768]{2,1,0:T(8,128)(2,1)}) custom-call(s32[2]{0:T(128)} %pad_add_fusion.me_ref, bf16[1024,768]{1,0:T(8,128)(2,1)} %get-tuple-element.322.nffn_ref, ...), custom_call_target="tpu_custom_call" | custom-call | flops 15000000512 | bytes 30000000 | tf_op jit(solution)/shard_map/ffn_forward/pallas_call | solution.py:281
  211.4 20.2 %ffn_backward.2 = (bf16[1024,3072]{1,0:T(8,128)(2,1)}, f32[1024,768]{1,0:T(8,128)}, f32[8,768]{1,0:T(8,128)}, f32[1,3072]{1,0:T(1,128)}) custom-call(s32[2]{0:T(128)} %pad_add_fusion.me_ref, bf16[1024,768]{1,0:T(8,128)(2,1)} %grad_ref.2, bf16[1024,3072]{1,0:T(8,128)(2,1)} %get-tuple-element.328.slope_ref, f32[1024,768]{1,0:T(8,128)} %get-tuple-element.323.middle_ref, ...), custom_call_target="tpu_custom_call" | custom-call | flops 15000000512 | bytes 30000000 | tf_op jit(solution)/shard_map/ffn_backward/pallas_call | solution.py:356
  231.6 11.4 %ffn_weight.4 = (bf16[2,2,4,192,768]{4,3,2,1,0:T(8,128)(2,1)}, bf16[768,1024]{1,0:T(8,128)(2,1)}, bf16[768,1024]{1,0:T(8,128)(2,1)}) custom-call(s32[2]{0:T(128)} %pad_add_fusion.me_ref, bf16[1024,768]{1,0:T(8,128)(2,1)} %get-tuple-element.322.nffn_ref, bf16[1024,768]{1,0:T(8,128)(2,1)} %grad_ref.2, bf16[1024,3072]{1,0:T(8,128)(2,1)} %get-tuple-element.338.gupper_ref, ...), custom_call_target="tpu_custom_call" | custom-call | flops 8000000000 | bytes 15000000 | tf_op jit(solution)/shard_map/ffn_weight/pallas_call | solution.py:613
  243.5 10.2 %ffn_weight.5 = bf16[2,2,4,192,768]{4,3,2,1,0:T(8,128)(2,1)} custom-call(s32[2]{0:T(128)} %pad_add_fusion.me_ref, bf16[768,1024]{1,0:T(8,128)(2,1)} %get-tuple-element.337.nffn_ref, bf16[768,1024]{1,0:T(8,128)(2,1)} %get-tuple-element.335.grad_ref, bf16[1024,3072]{1,0:T(8,128)(2,1)} %get-tuple-element.338.gupper_ref, ...), custom_call_target="tpu_custom_call" | custom-call | flops 8000000000 | bytes 15000000 | tf_op jit(solution)/shard_map/ffn_weight/pallas_call | solution.py:613
  257.7 25.3 %attention_backward.2 = (f32[1024,768]{1,0:T(8,128)}, bf16[1024,2304]{1,0:T(8,128)(2,1)}, f32[8,768]{1,0:T(8,128)}) custom-call(f32[1024,768]{1,0:T(8,128)} %get-tuple-element.343.gmiddle_ref, f32[1024,768]{1,0:T(8,128)} %get-tuple-element.306.stream_ref, bf16[1024,2304]{1,0:T(8,128)(2,1)} %get-tuple-element.344.proj_ref, ...), custom_call_target="tpu_custom_call" | custom-call | flops 15000000512 | bytes 20000000 | tf_op jit(solution)/shard_map/attention_backward/pallas_call | solution.py:480
  288.4 11.7 %attention_weight.2 = (bf16[2,2,4,96,768]{4,3,2,1,0:T(8,128)(2,1)}, bf16[2,2,4,96,768]{4,3,2,1,0:T(8,128)(2,1)}) custom-call(s32[2]{0:T(128)} %pad_add_fusion.me_ref, bf16[1024,768]{1,0:T(8,128)(2,1)} %get-tuple-element.354.normed_ref, bf16[1024,768]{1,0:T(8,128)(2,1)} %get-tuple-element.355.mixed_ref, bf16[1024,2304]{1,0:T(8,128)(2,1)} %get-tuple-element.356.gproj_ref, ...), custom_call_target="tpu_custom_call" | custom-call | flops 10000000000 | bytes 20000000 | tf_op jit(solution)/shard_map/attention_weight/pallas_call | solution.py:685
  308.0 20.1 %ffn_backward.3 = (bf16[1024,3072]{1,0:T(8,128)(2,1)}, f32[1024,768]{1,0:T(8,128)}, f32[8,768]{1,0:T(8,128)}, f32[1,3072]{1,0:T(1,128)}) custom-call(s32[2]{0:T(128)} %pad_add_fusion.me_ref, f32[1024,768]{1,0:T(8,128)} %get-tuple-element.365.grad_ref, bf16[1024,3072]{1,0:T(8,128)(2,1)} %get-tuple-element.366.slope_ref, ...), custom_call_target="tpu_custom_call" | custom-call | flops 15000000512 | bytes 30000000 | tf_op jit(solution)/shard_map/ffn_backward/pallas_call | solution.py:356
  333.6 11.9 %ffn_weight.6 = (bf16[2,2,4,192,768]{4,3,2,1,0:T(8,128)(2,1)}, bf16[768,1024]{1,0:T(8,128)(2,1)}, bf16[768,1024]{1,0:T(8,128)(2,1)}) custom-call(s32[2]{0:T(128)} %pad_add_fusion.me_ref, bf16[1024,768]{1,0:T(8,128)(2,1)} %get-tuple-element.290.nffn_ref, f32[1024,768]{1,0:T(8,128)} %get-tuple-element.365.grad_ref, ...), custom_call_target="tpu_custom_call" | custom-call | flops 8000000000 | bytes 15000000 | tf_op jit(solution)/shard_map/ffn_weight/pallas_call | solution.py:613
  348.9 10.7 %ffn_weight.7 = bf16[2,2,4,192,768]{4,3,2,1,0:T(8,128)(2,1)} custom-call(s32[2]{0:T(128)} %pad_add_fusion.me_ref, bf16[768,1024]{1,0:T(8,128)(2,1)} %get-tuple-element.388.nffn_ref, bf16[768,1024]{1,0:T(8,128)(2,1)} %get-tuple-element.385.grad_ref, bf16[1024,3072]{1,0:T(8,128)(2,1)} %get-tuple-element.389.gupper_ref, ...), custom_call_target="tpu_custom_call" | custom-call | flops 8000000000 | bytes 15000000 | tf_op jit(solution)/shard_map/ffn_weight/pallas_call | solution.py:613
  369.2 24.9 %attention_backward.3 = (f32[1024,768]{1,0:T(8,128)}, bf16[1024,2304]{1,0:T(8,128)(2,1)}, f32[8,768]{1,0:T(8,128)}) custom-call(f32[1024,768]{1,0:T(8,128)} %get-tuple-element.396.gmiddle_ref, bf16[1024,768]{1,0:T(8,128)(2,1)} %stream_ref.2, bf16[1024,2304]{1,0:T(8,128)(2,1)} %get-tuple-element.397.proj_ref, ...), custom_call_target="tpu_custom_call" | custom-call | flops 15000000512 | bytes 20000000 | tf_op jit(solution)/shard_map/attention_backward/pallas_call | solution.py:480
  402.6 12.1 %attention_weight.3 = (bf16[2,2,4,112,768]{4,3,2,1,0:T(8,128)(2,1)}, bf16[2,2,4,112,768]{4,3,2,1,0:T(8,128)(2,1)}) custom-call(s32[2]{0:T(128)} %pad_add_fusion.me_ref, bf16[1024,768]{1,0:T(8,128)(2,1)} %get-tuple-element.413.normed_ref, bf16[1024,768]{1,0:T(8,128)(2,1)} %get-tuple-element.414.mixed_ref, bf16[1024,2304]{1,0:T(8,128)(2,1)} %get-tuple-element.415.gproj_ref, ...), custom_call_target="tpu_custom_call" | custom-call | flops 10000000000 | bytes 20000000 | tf_op jit(solution)/shard_map/attention_weight/pallas_call | solution.py:685
  423.7 13.9 %collective-permute-done.42 = bf16[192,768]{1,0:T(8,128)(2,1)S(1)} collective-permute-done((bf16[192,768]{1,0:T(8,128)(2,1)S(1)}, bf16[192,768]{1,0:T(8,128)(2,1)S(1)}, u32[]{:S(2)}, u32[]{:S(2)}) %collective-permute-start.42) | collective-permute-done | bytes 294944 | tf_op jit(solution)/shard_map/ppermute | solution.py:759
  452.9 6.0 %collective-permute-done.45 = bf16[192,768]{1,0:T(8,128)(2,1)S(1)} collective-permute-done((bf16[192,768]{1,0:T(8,128)(2,1)}, bf16[192,768]{1,0:T(8,128)(2,1)S(1)}, u32[]{:S(2)}, u32[]{:S(2)}) %collective-permute-start.45) | collective-permute-done | bytes 294944 | tf_op jit(solution)/shard_map/ppermute | solution.py:759
  471.4 5.4 %collective-permute-done.47 = bf16[112,768]{1,0:T(8,128)(2,1)} collective-permute-done((bf16[112,768]{1,0:T(8,128)(2,1)}, bf16[112,768]{1,0:T(8,128)(2,1)}, u32[]{:S(2)}, u32[]{:S(2)}) %collective-permute-start.47) | collective-permute-done | bytes 172064 | tf_op jit(solution)/shard_map/ppermute | solution.py:759
  (277 shorter events, 170.1 us)
Async XLA Ops:
  7.2 103.6 %all-gather.3.cloned.1.call-start = ((), (), s32[]{:S(2)}) async-start(), calls=%async_computation | async-start | bytes 2211840 | tf_op jit(solution)/shard_map/all_gather | solution.py:790
  27.1 16.3 %collective-permute-start.3 = (bf16[4,96,768]{2,1,0:T(8,128)(2,1)S(1)}, bf16[4,96,768]{2,1,0:T(8,128)(2,1)S(1)}, u32[]{:S(2)}, u32[]{:S(2)}) collective-permute-start(bf16[4,96,768]{2,1,0:T(8,128)(2,1)S(1)} %get-tuple-element.240), channel_id=1, source_target_pairs={{0,4},{1,3},{2,6},{3,1},{4,0},{5,7},{6,2},{7,5},{8,12},{9,11},{10,... | collective-permute-start | bytes 1769480 | tf_op jit(solution)/shard_map/ppermute | solution.py:759
  43.5 16.9 %collective-permute-start.8 = (bf16[2,4,96,768]{3,2,1,0:T(8,128)(2,1)S(1)}, bf16[2,4,96,768]{3,2,1,0:T(8,128)(2,1)}, u32[]{:S(2)}, u32[]{:S(2)}) collective-permute-start(bf16[2,4,96,768]{3,2,1,0:T(8,128)(2,1)S(1)} %pad_maximum_fusion.2.refs_0_), channel_id=1, source_target_pairs={{0,2},{1,5},{2,0},{3,7},{4,6},{5,1},{6,4},{7,3},{8,10},{9,13},{10,... | collective-permute-start | bytes 3538952 | tf_op jit(solution)/shard_map/ppermute | solution.py:759
  44.1 16.4 %collective-permute-start.9 = (bf16[2,4,96,768]{3,2,1,0:T(8,128)(2,1)S(1)}, bf16[2,4,96,768]{3,2,1,0:T(8,128)(2,1)}, u32[]{:S(2)}, u32[]{:S(2)}) collective-permute-start(bf16[2,4,96,768]{3,2,1,0:T(8,128)(2,1)S(1)} %pad_maximum_fusion.2.refs_0_), channel_id=1, source_target_pairs={{0,1},{1,0},{2,3},{3,2},{4,5},{5,4},{6,7},{7,6},{8,9},{9,8},{10,11... | collective-permute-start | bytes 3538952 | tf_op jit(solution)/shard_map/ppermute | solution.py:759
  45.0 15.5 %collective-permute-start.10 = (bf16[192,768]{1,0:T(8,128)(2,1)}, bf16[192,768]{1,0:T(8,128)(2,1)S(1)}, u32[]{:S(2)}, u32[]{:S(2)}) collective-permute-start(bf16[192,768]{1,0:T(8,128)(2,1)} %copy-done.26), channel_id=1, source_target_pairs={{0,8},{1,9},{2,10},{3,11},{4,12},{5,13},{6,14},{7,15},{8,0},{9,1},... | collective-permute-start | bytes 884744 | tf_op jit(solution)/shard_map/ppermute | solution.py:759
  45.0 15.4 %collective-permute-start.11 = (bf16[192,768]{1,0:T(8,128)(2,1)}, bf16[192,768]{1,0:T(8,128)(2,1)S(1)}, u32[]{:S(2)}, u32[]{:S(2)}) collective-permute-start(bf16[192,768]{1,0:T(8,128)(2,1)} %copy-done.26), channel_id=1, source_target_pairs={{0,24},{1,25},{2,26},{3,27},{4,28},{5,29},{6,30},{7,31},{8,16},{9,... | collective-permute-start | bytes 884744 | tf_op jit(solution)/shard_map/ppermute | solution.py:759
  62.6 16.4 %collective-permute-start.13 = (bf16[4,192,768]{2,1,0:T(8,128)(2,1)S(1)}, bf16[4,192,768]{2,1,0:T(8,128)(2,1)}, u32[]{:S(2)}, u32[]{:S(2)}) collective-permute-start(bf16[4,192,768]{2,1,0:T(8,128)(2,1)S(1)} %get-tuple-element.263), channel_id=1, source_target_pairs={{0,4},{1,3},{2,6},{3,1},{4,0},{5,7},{6,2},{7,5},{8,12},{9,11},{10,... | collective-permute-start | bytes 3538952 | tf_op jit(solution)/shard_map/ppermute | solution.py:759
  80.5 28.9 %collective-permute-start.14 = (bf16[2,4,192,768]{3,2,1,0:T(8,128)(2,1)S(1)}, bf16[2,4,192,768]{3,2,1,0:T(8,128)(2,1)S(1)}, u32[]{:S(2)}, u32[]{:S(2)}) collective-permute-start(bf16[2,4,192,768]{3,2,1,0:T(8,128)(2,1)S(1)} %pad_maximum_fusion.refs_0_.refs_4_), channel_id=1, source_target_pairs={{0,2},{1,5},{2,0},{3,7},{4,6},{5,1},{6,4},{7,3},{8,10},{9,13},{10,... | collective-permute-start | bytes 7077896 | tf_op jit(solution)/shard_map/ppermute | solution.py:759
  81.9 27.5 %collective-permute-start.15 = (bf16[2,4,192,768]{3,2,1,0:T(8,128)(2,1)S(1)}, bf16[2,4,192,768]{3,2,1,0:T(8,128)(2,1)}, u32[]{:S(2)}, u32[]{:S(2)}) collective-permute-start(bf16[2,4,192,768]{3,2,1,0:T(8,128)(2,1)S(1)} %pad_maximum_fusion.refs_0_.refs_4_), channel_id=1, source_target_pairs={{0,1},{1,0},{2,3},{3,2},{4,5},{5,4},{6,7},{7,6},{8,9},{9,8},{10,11... | collective-permute-start | bytes 7077896 | tf_op jit(solution)/shard_map/ppermute | solution.py:759
  123.7 28.1 %collective-permute-start.18 = (bf16[2,4,96,768]{3,2,1,0:T(8,128)(2,1)S(1)}, bf16[2,4,96,768]{3,2,1,0:T(8,128)(2,1)S(1)}, u32[]{:S(2)}, u32[]{:S(2)}) collective-permute-start(bf16[2,4,96,768]{3,2,1,0:T(8,128)(2,1)S(1)} %pad_maximum_fusion.4.refs_0_), channel_id=1, source_target_pairs={{0,2},{1,5},{2,0},{3,7},{4,6},{5,1},{6,4},{7,3},{8,10},{9,13},{10,... | collective-permute-start | bytes 3538952 | tf_op jit(solution)/shard_map/ppermute | solution.py:759
  125.1 26.7 %collective-permute-start.19 = (bf16[2,4,96,768]{3,2,1,0:T(8,128)(2,1)S(1)}, bf16[2,4,96,768]{3,2,1,0:T(8,128)(2,1)S(1)}, u32[]{:S(2)}, u32[]{:S(2)}) collective-permute-start(bf16[2,4,96,768]{3,2,1,0:T(8,128)(2,1)S(1)} %pad_maximum_fusion.4.refs_0_), channel_id=1, source_target_pairs={{0,1},{1,0},{2,3},{3,2},{4,5},{5,4},{6,7},{7,6},{8,9},{9,8},{10,11... | collective-permute-start | bytes 3538952 | tf_op jit(solution)/shard_map/ppermute | solution.py:759
  125.1 26.7 %collective-permute-start.20 = (bf16[4,192,768]{2,1,0:T(8,128)(2,1)S(1)}, bf16[4,192,768]{2,1,0:T(8,128)(2,1)S(1)}, u32[]{:S(2)}, u32[]{:S(2)}) collective-permute-start(bf16[4,192,768]{2,1,0:T(8,128)(2,1)S(1)} %get-tuple-element.289), channel_id=1, source_target_pairs={{0,4},{1,3},{2,6},{3,1},{4,0},{5,7},{6,2},{7,5},{8,12},{9,11},{10,... | collective-permute-start | bytes 3538952 | tf_op jit(solution)/shard_map/ppermute | solution.py:759
  155.0 28.8 %collective-permute-start.22 = (bf16[2,4,192,768]{3,2,1,0:T(8,128)(2,1)S(1)}, bf16[2,4,192,768]{3,2,1,0:T(8,128)(2,1)S(1)}, u32[]{:S(2)}, u32[]{:S(2)}) collective-permute-start(bf16[2,4,192,768]{3,2,1,0:T(8,128)(2,1)S(1)} %pad_maximum_fusion.1.refs_0_.refs_4_), channel_id=1, source_target_pairs={{0,2},{1,5},{2,0},{3,7},{4,6},{5,1},{6,4},{7,3},{8,10},{9,13},{10,... | collective-permute-start | bytes 7077896 | tf_op jit(solution)/shard_map/ppermute | solution.py:759
  156.7 27.2 %collective-permute-start.23 = (bf16[2,4,192,768]{3,2,1,0:T(8,128)(2,1)S(1)}, bf16[2,4,192,768]{3,2,1,0:T(8,128)(2,1)S(1)}, u32[]{:S(2)}, u32[]{:S(2)}) collective-permute-start(bf16[2,4,192,768]{3,2,1,0:T(8,128)(2,1)S(1)} %pad_maximum_fusion.1.refs_0_.refs_4_), channel_id=1, source_target_pairs={{0,1},{1,0},{2,3},{3,2},{4,5},{5,4},{6,7},{7,6},{8,9},{9,8},{10,11... | collective-permute-start | bytes 7077896 | tf_op jit(solution)/shard_map/ppermute | solution.py:759
  255.9 29.0 %collective-permute-start.26 = (bf16[2,4,192,768]{3,2,1,0:T(8,128)(2,1)S(1)}, bf16[2,4,192,768]{3,2,1,0:T(8,128)(2,1)}, u32[]{:S(2)}, u32[]{:S(2)}) collective-permute-start(bf16[2,4,192,768]{3,2,1,0:T(8,128)(2,1)S(1)} %fusion), channel_id=1, source_target_pairs={{0,2},{1,5},{2,0},{3,7},{4,6},{5,1},{6,4},{7,3},{8,10},{9,13},{10,... | collective-permute-start | bytes 7077896 | tf_op jit(solution)/shard_map/ppermute | solution.py:759
  287.0 16.3 %collective-permute-start.27 = (bf16[4,192,768]{2,1,0:T(8,128)(2,1)S(1)}, bf16[4,192,768]{2,1,0:T(8,128)(2,1)S(1)}, u32[]{:S(2)}, u32[]{:S(2)}) collective-permute-start(bf16[4,192,768]{2,1,0:T(8,128)(2,1)S(1)} %fusion.5), channel_id=1, source_target_pairs={{0,4},{1,3},{2,6},{3,1},{4,0},{5,7},{6,2},{7,5},{8,12},{9,11},{10,... | collective-permute-start | bytes 3538952 | tf_op jit(solution)/shard_map/ppermute | solution.py:759
  306.4 21.8 %collective-permute-start.28 = (bf16[2,2,4,96,768]{4,3,2,1,0:T(8,128)(2,1)}, bf16[2,2,4,96,768]{4,3,2,1,0:T(8,128)(2,1)S(1)}, u32[]{:S(2)}, u32[]{:S(2)}) collective-permute-start(bf16[2,2,4,96,768]{4,3,2,1,0:T(8,128)(2,1)} %get-tuple-element.363), channel_id=1, source_target_pairs={{0,1},{1,0},{2,3},{3,2},{4,5},{5,4},{6,7},{7,6},{8,9},{9,8},{10,11... | collective-permute-start | bytes 7077896 | tf_op jit(solution)/shard_map/ppermute | solution.py:759
  306.4 21.7 %collective-permute-start.29 = (bf16[192,768]{1,0:T(8,128)(2,1)S(1)}, bf16[192,768]{1,0:T(8,128)(2,1)S(1)}, u32[]{:S(2)}, u32[]{:S(2)}) collective-permute-start(bf16[192,768]{1,0:T(8,128)(2,1)S(1)} %get-tuple-element.364), channel_id=1, source_target_pairs={{0,16},{1,17},{2,18},{3,19},{4,20},{5,21},{6,22},{7,23},{8,24},{9,... | collective-permute-start | bytes 884744 | tf_op jit(solution)/shard_map/ppermute | solution.py:759
  329.1 17.7 %collective-permute-start.30 = (bf16[2,4,96,768]{3,2,1,0:T(8,128)(2,1)S(1)}, bf16[2,4,96,768]{3,2,1,0:T(8,128)(2,1)}, u32[]{:S(2)}, u32[]{:S(2)}) collective-permute-start(bf16[2,4,96,768]{3,2,1,0:T(8,128)(2,1)S(1)} %fusion.9), channel_id=1, source_target_pairs={{0,2},{1,5},{2,0},{3,7},{4,6},{5,1},{6,4},{7,3},{8,10},{9,13},{10,... | collective-permute-start | bytes 3538952 | tf_op jit(solution)/shard_map/ppermute | solution.py:759
  365.7 29.2 %collective-permute-start.35 = (bf16[2,4,192,768]{3,2,1,0:T(8,128)(2,1)}, bf16[2,4,192,768]{3,2,1,0:T(8,128)(2,1)}, u32[]{:S(2)}, u32[]{:S(2)}) collective-permute-start(bf16[2,4,192,768]{3,2,1,0:T(8,128)(2,1)} %fusion.1), channel_id=1, source_target_pairs={{0,2},{1,5},{2,0},{3,7},{4,6},{5,1},{6,4},{7,3},{8,10},{9,13},{10,... | collective-permute-start | bytes 7077896 | tf_op jit(solution)/shard_map/ppermute | solution.py:759
  367.4 26.7 %collective-permute-start.36 = (bf16[96,768]{1,0:T(8,128)(2,1)}, bf16[96,768]{1,0:T(8,128)(2,1)}, u32[]{:S(2)}, u32[]{:S(2)}) collective-permute-start(bf16[96,768]{1,0:T(8,128)(2,1)} %get-tuple-element.395), channel_id=1, source_target_pairs={{0,16},{1,17},{2,18},{3,19},{4,20},{5,21},{6,22},{7,23},{8,24},{9,... | collective-permute-start | bytes 442376 | tf_op jit(solution)/shard_map/ppermute | solution.py:759
  398.0 16.8 %collective-permute-start.37 = (bf16[4,192,768]{2,1,0:T(8,128)(2,1)}, bf16[4,192,768]{2,1,0:T(8,128)(2,1)}, u32[]{:S(2)}, u32[]{:S(2)}) collective-permute-start(bf16[4,192,768]{2,1,0:T(8,128)(2,1)} %fusion.2), channel_id=1, source_target_pairs={{0,4},{1,3},{2,6},{3,1},{4,0},{5,7},{6,2},{7,5},{8,12},{9,11},{10,... | collective-permute-start | bytes 3538952 | tf_op jit(solution)/shard_map/ppermute | solution.py:759
  420.5 18.4 %collective-permute-start.41 = (bf16[2,4,112,768]{3,2,1,0:T(8,128)(2,1)S(1)}, bf16[2,4,112,768]{3,2,1,0:T(8,128)(2,1)S(1)}, u32[]{:S(2)}, u32[]{:S(2)}) collective-permute-start(bf16[2,4,112,768]{3,2,1,0:T(8,128)(2,1)S(1)} %fusion.6), channel_id=1, source_target_pairs={{0,2},{1,5},{2,0},{3,7},{4,6},{5,1},{6,4},{7,3},{8,10},{9,13},{10,... | collective-permute-start | bytes 4128776 | tf_op jit(solution)/shard_map/ppermute | solution.py:759
  440.2 18.7 %collective-permute-start.43 = (bf16[4,112,768]{2,1,0:T(8,128)(2,1)}, bf16[4,112,768]{2,1,0:T(8,128)(2,1)}, u32[]{:S(2)}, u32[]{:S(2)}) collective-permute-start(bf16[4,112,768]{2,1,0:T(8,128)(2,1)} %fusion.8), channel_id=1, source_target_pairs={{0,4},{1,3},{2,6},{3,1},{4,0},{5,7},{6,2},{7,5},{8,12},{9,11},{10,... | collective-permute-start | bytes 2064392 | tf_op jit(solution)/shard_map/ppermute | solution.py:759
  (79 other events, 924.5 us)
Sparse Core Ops, SparseCore 0:
  64.9 39.1 all-gather.2

commit v5 on v4

--- a/solution.py
+++ b/solution.py
@@ -386,6 +386,104 @@
         cost_estimate=pl.CostEstimate(flops=15 * 10**9, bytes_accessed=30 * 10**6, transcendentals=0),
         name="ffn_backward",
     )(me, grad, slope, middle, vec, *arrays)
+
+
+def ffn_both_kernel(plans, me_ref, nffn_ref, middle_ref, grad_ref, vec_ref, hidden_ref, *refs):
+    result_ref, active_ref, gupper_ref, gmiddle_ref, small_ref, ghidden_ref, up_s, down_s, up_sems, down_sems = refs[-10:]
+    up_refs = refs[: (len(refs) - 10) // 2]
+    down_refs = refs[len(up_refs) : -10]
+    first = pl.program_id(0) == 0
+    parts, _, chunk = up_s.shape
+    curve = 0.7978845608028654
+
+    @pl.when(first)
+    def _():
+        start_weights([(plans[0], up_refs, me_ref, up_s, up_sems), (plans[1], down_refs, me_ref, down_s, down_sems)])
+        small_ref[...] = jnp.zeros_like(small_ref)
+        ghidden_ref[...] = jnp.zeros_like(ghidden_ref)
+
+    def body(wait):
+        nffn = nffn_ref[...]
+        middle = middle_ref[...]
+        grad = grad_ref[...].astype(F32)
+        lower = grad.astype(BF)
+        total = middle + vec_ref[7:8, :]
+        gnormed = jnp.zeros(grad.shape, F32)
+        for part in part_order(me_ref, plans[0], parts):
+            cols = pl.ds(pl.multiple_of(part * chunk, chunk), chunk)
+            if wait:
+                wait_weight(up_s, up_sems, part)
+                wait_weight(down_s, down_sems, part)
+            gactive = dot_nn(lower, down_s[part])
+            upper = dot_nn(nffn, up_s[part]) + hidden_ref[:, cols]
+            square = upper * upper
+            angle = jnp.tanh(upper * (curve + (curve * 0.044715) * square))
+            half = 0.5 * upper
+            lift = 1.0 + angle
+            active = (half * lift).astype(BF)
+            slope = 0.5 * lift + half * (1.0 - angle * angle) * (curve + (3.0 * curve * 0.044715) * square)
+            gupper = (gactive * slope).astype(BF)
+            active_ref[:, cols] = active
+            gupper_ref[:, cols] = gupper
+            ghidden_ref[:, cols] += column_sum(gupper.astype(F32))
+            total = total + dot_nt(active, down_s[part])
+            gnormed = gnormed + dot_nt(gupper, up_s[part])
+        result_ref[...] = total
+        unit, root = normalize(middle)
+        gmiddle = grad + norm_backward(gnormed, unit, root, vec_ref[1:2, :])
+        gmiddle_ref[...] = gmiddle
+        small_ref[0:1, :] += column_sum(gnormed * unit)
+        small_ref[1:2, :] += column_sum(gnormed)
+        small_ref[2:3, :] += column_sum(lower.astype(F32))
+        small_ref[3:4, :] += column_sum(gmiddle.astype(BF).astype(F32))
+
+    pl.when(first)(functools.partial(body, True))
+    pl.when(jnp.logical_not(first))(functools.partial(body, False))
+
+
+def ffn_both(me, nffn, middle, grad, vec, hidden, up_w, down_w, block, parts):
+    rows, width = nffn.shape
+    ffn = hidden.shape[1]
+    arrays = up_w[1] + down_w[1]
+    row_spec = lambda cols: pl.BlockSpec((block, cols), lambda i: (i, 0))
+    return pl.pallas_call(
+        functools.partial(ffn_both_kernel, (up_w[0], down_w[0])),
+        grid=(rows // block,),
+        in_specs=[
+            pl.BlockSpec(memory_space=pltpu.SMEM),
+            row_spec(width),
+            row_spec(width),
+            row_spec(width),
+            pl.BlockSpec(vec.shape, lambda i: (0, 0)),
+            pl.BlockSpec(hidden.shape, lambda i: (0, 0)),
+        ]
+        + [pl.BlockSpec(memory_space=pl.ANY)] * len(arrays),
+        out_specs=[
+            row_spec(width),
+            row_spec(ffn),
+            row_spec(ffn),
+            row_spec(width),
+            pl.BlockSpec((8, width), lambda i: (0, 0)),
+            pl.BlockSpec((1, ffn), lambda i: (0, 0)),
+        ],
+        out_shape=[
+            jax.ShapeDtypeStruct((rows, width), F32),
+            jax.ShapeDtypeStruct((rows, ffn), BF),
+            jax.ShapeDtypeStruct((rows, ffn), BF),
+            jax.ShapeDtypeStruct((rows, width), F32),
+            jax.ShapeDtypeStruct((8, width), F32),
+            jax.ShapeDtypeStruct((1, ffn), F32),
+        ],
+        scratch_shapes=[
+            pltpu.VMEM((parts, width, ffn // parts), BF),
+            pltpu.VMEM((parts, width, ffn // parts), BF),
+            pltpu.SemaphoreType.DMA((parts,)),
+            pltpu.SemaphoreType.DMA((parts,)),
+        ],
+        compiler_params=pltpu.CompilerParams(vmem_limit_bytes=VMEM_LIMIT),
+        cost_estimate=pl.CostEstimate(flops=25 * 10**9, bytes_accessed=40 * 10**6, transcendentals=0),
+        name="ffn_both",
+    )(me, nffn, middle, grad, vec, hidden, *arrays)
 
 
 def ffn_weight_kernel(nffn_ref, grad_ref, gupper_ref, active_ref, out_ref, nffn_t, grad_t):
@@ -950,8 +1048,10 @@
         middle, nffn, normed, proj, probs, mixed, qkv_w, out_w = attention
         saved[index] = dict(
             stream=stream, middle=middle, nffn=nffn, normed=normed, proj=proj, probs=probs, mixed=mixed,
-            weight=(qkv_w, out_w), active=ffn[1], slope=ffn[2], up_w=(("whole",), [ffn[3]]), down_w=(("whole",), [ffn[4]]),
-        )
+            weight=(qkv_w, out_w), active=ffn[1],
+        )
+        if len(ffn) > 2:
+            saved[index].update(slope=ffn[2], up_w=(("whole",), [ffn[3]]), down_w=(("whole",), [ffn[4]]))
 
     if split:
         depth = exchange.depth
@@ -1003,11 +1103,12 @@
         came, attention = lane.step(ffn_one.go_second(ffn_came), attention_forward_of(1, attn_w), [stream])
         came, _ = lane.step(ffn_one.go_core(came))
         up_w, down_w = ffn_one.weight(came), ffn_one.weight(came, high)
-        _, ffn = lane.step([], ffn_forward_of(1, up_w, down_w), attention[1::-1])
-        keep(1, stream, attention, ffn)
-        block_output = ffn[0]
-
-        _, (gupper, gmiddle, small_two, hidden_one) = lane.step([], ffn_backward_of(1), [out_grad])
+        both = lambda nffn, middle: ffn_both(
+            me, nffn, middle, out_grad, small[1], hidden[1:], up_w, down_w, block, parts
+        )
+        _, results = lane.step([], both, attention[1::-1])
+        block_output, active, gupper, gmiddle, small_two, hidden_one = results
+        keep(1, stream, attention, (None, active))
         _, (other, *turned) = lane.step([], ffn_weight_of(1, out_grad), [gupper])
         came, (own,) = lane.step([(exchange.core, other)], ffn_weight_of(1, out_grad, turned), [gupper])
         ffn_one = Reduce(exchange, other, own)
@@ -1048,11 +1149,13 @@
         ffn_sends = exchange.z_sends([layers[z].astype(BF) for z in range(depth)])
         ffn_sends = mid_first(ffn_sends)
         attn_zero = Reduce(exchange, *grads)
+        ((move, value),) = ffn_sends[:1]
+        ffn_came = [move(lane.after_last(value))]
         came, _ = lane.step(attn_zero.go_core())
-        came, _ = lane.step(attn_zero.go_second(came) + ffn_sends[:1])
-        ffn_came = came[1:]
-        came, _ = lane.step(attn_zero.go_first(came[:1]) + ffn_sends[1:])
-        total = layers[0] + sum(value.astype(F32) for value in ffn_came + came[1:])
+        came, _ = lane.step(attn_zero.go_second(came) + ffn_sends[1:])
+        ffn_came = ffn_came + came[1:]
+        came, _ = lane.step(attn_zero.go_first(came[:1]))
+        total = layers[0] + sum(value.astype(F32) for value in ffn_came)
         grad_up[0], grad_down[0] = total[:high], total[high:]
         layers = attn_zero.depths(came[:1])
         came, _ = lane.step(exchange.z_sends([layers[z].astype(BF) for z in range(depth)]))

time: 526 us -> 516 us (0.981)
  Pallas kernels: 243 us -> 234 us
  waiting for transfers between devices: 119 us -> 113 us
    pallas_call x0 -> x1, Pallas kernels: none -> 32.1 us  [ffn_both(): pl.pallas_call(functools.partial(ffn_both_kernel, (up_w[0], down_w[0])),...]
    pallas_call x2 -> x1, Pallas kernels: 43.2 us -> 21.9 us  [ffn_forward(): pl.pallas_call(functools.partial(ffn_forward_kernel, (up_w[0], down_w[0])...]
    pallas_call x2 -> x1, Pallas kernels: 40.2 us -> 20.1 us  [ffn_backward(): pl.pallas_call(functools.partial(ffn_backward_kernel, (up_w[0], down_w[0]...]
    ppermute x54, waiting for transfers between devices: 119 us -> 113 us  [swap(): return lax.ppermute(value, ('dp', 'tensor'), pairs)]
    unnamed x101 -> x107, local copies, waits for them, and re-layouts: 11.1 us -> 11.1 us
  transfers between devices with their start and end apart: 55 -> 55, of which waited for: 29 -> 30; matrix products, arithmetic and copies ran while one was open for 4% -> 5% of each run, Pallas kernels for 36% -> 38%
where the time goes in v5:
time: 516 us; the launch traced here: 508 us
  Pallas kernels  234 us (45%)
  waiting for transfers between devices  113 us (22%)
  starting transfers between devices  67.4 us (13%)
  other arithmetic  50.6 us (10%)
  between operations  23.7 us (5%)
  local copies, waits for them, and re-layouts  19.4 us (4%)
    ppermute x54, waiting for transfers between devices, swap(): return lax.ppermute(value, ('dp', 'tensor'), pairs)  113 us
    ppermute x54, starting transfers between devices, swap(): return lax.ppermute(value, ('dp', 'tensor'), pairs)  67.4 us
    pallas_call x2, Pallas kernels, attention_backward(): pl.pallas_call(attention_backward_kernel, grid=((end - begin) // block_pa...  50.1 us
    pallas_call x4, Pallas kernels, ffn_weight_split(): pl.pallas_call(functools.partial(ffn_weight_split_kernel, core), grid_spe...  44.1 us
    pallas_call x2, Pallas kernels, attention_forward(): pl.pallas_call(functools.partial(attention_forward_kernel, plan), grid=(p...  41.6 us
    pallas_call x1, Pallas kernels, ffn_both(): pl.pallas_call(functools.partial(ffn_both_kernel, (up_w[0], down_w[0])),...  32.1 us
    pallas_call x2, Pallas kernels, attention_weight_split(): pl.pallas_call(attention_weight_split_kernel, grid=(3,), in_specs=[pl.Blo...  24.1 us
    pallas_call x1, Pallas kernels, ffn_forward(): pl.pallas_call(functools.partial(ffn_forward_kernel, (up_w[0], down_w[0])...  21.9 us
  transfers between devices with their start and end apart: 55, of which 30 were waited for; matrix products, arithmetic and copies ran while one was open for 5% of the time, Pallas kernels for 38%

profile of v5, /device:TPU:0, one launch (start us, length us, event | category | flops | bytes accessed | tf_op | source)
XLA Modules:
  0.0 508.0 jit_solution(9295364843941231382)
XLA Ops:
  9.4 5.1 %collective-permute-start.2 = (bf16[96,768]{1,0:T(8,128)(2,1)S(1)}, bf16[96,768]{1,0:T(8,128)(2,1)S(1)}, u32[]{:S(2)}, u32[]{:S(2)}) collective-permute-start(bf16[96,768]{1,0:T(8,128)(2,1)S(1)} %bitcast.166), channel_id=1, source_target_pairs={{0,24},{1,25},{2,26},{3,27},{4,28},{5,29},{6,30},{7,31},{8,16},{9,... | collective-permute-start | bytes 442376 | tf_op jit(solution)/shard_map/ppermute | solution.py:857
  19.3 7.7 %collective-permute-done.1 = bf16[96,768]{1,0:T(8,128)(2,1)S(1)} collective-permute-done((bf16[96,768]{1,0:T(8,128)(2,1)S(1)}, bf16[96,768]{1,0:T(8,128)(2,1)S(1)}, u32[]{:S(2)}, u32[]{:S(2)}) %collective-permute-start.1) | collective-permute-done | bytes 147488 | tf_op jit(solution)/shard_map/ppermute | solution.py:857
  36.3 7.1 %collective-permute-done.4 = bf16[192,768]{1,0:T(8,128)(2,1)S(1)} collective-permute-done((bf16[192,768]{1,0:T(8,128)(2,1)S(1)}, bf16[192,768]{1,0:T(8,128)(2,1)S(1)}, u32[]{:S(2)}, u32[]{:S(2)}) %collective-permute-start.4) | collective-permute-done | bytes 294944 | tf_op jit(solution)/shard_map/ppermute | solution.py:857
  48.8 11.7 %collective-permute-done.10 = bf16[192,768]{1,0:T(8,128)(2,1)S(1)} collective-permute-done((bf16[192,768]{1,0:T(8,128)(2,1)}, bf16[192,768]{1,0:T(8,128)(2,1)S(1)}, u32[]{:S(2)}, u32[]{:S(2)}) %collective-permute-start.10) | collective-permute-done | bytes 294944 | tf_op jit(solution)/shard_map/ppermute | solution.py:857
  65.8 13.2 %collective-permute-done.13 = bf16[4,192,768]{2,1,0:T(8,128)(2,1)} collective-permute-done((bf16[4,192,768]{2,1,0:T(8,128)(2,1)S(1)}, bf16[4,192,768]{2,1,0:T(8,128)(2,1)}, u32[]{:S(2)}, u32[]{:S(2)}) %collective-permute-start.13) | collective-permute-done | bytes 1179680 | tf_op jit(solution)/shard_map/ppermute | solution.py:857
  83.7 20.9 %attention_forward.2 = (f32[1024,768]{1,0:T(8,128)}, bf16[1024,768]{1,0:T(8,128)(2,1)}, bf16[1024,768]{1,0:T(8,128)(2,1)}, bf16[1024,2304]{1,0:T(8,128)(2,1)}, b...) custom-call(s32[2]{0:T(128)} %pad_add_fusion.me_ref, ...), custom_call_target="tpu_custom_call" | custom-call | flops 20000000000 | bytes 30000000 | tf_op jit(solution)/shard_map/attention_forward/pallas_call | solution.py:189
  104.6 4.8 collective-permute-done.14.refs_1_.refs_5_
  114.3 7.8 %collective-permute-done.17 = bf16[4,96,768]{2,1,0:T(8,128)(2,1)S(1)} collective-permute-done((bf16[4,96,768]{2,1,0:T(8,128)(2,1)S(1)}, bf16[4,96,768]{2,1,0:T(8,128)(2,1)S(1)}, u32[]{:S(2)}, u32[]{:S(2)}) %collective-permute-start.17) | collective-permute-done | bytes 589856 | tf_op jit(solution)/shard_map/ppermute | solution.py:857
  126.5 21.9 %ffn_forward.1 = (f32[1024,768]{1,0:T(8,128)}, bf16[1024,3072]{1,0:T(8,128)(2,1)}, bf16[1024,3072]{1,0:T(8,128)(2,1)}, bf16[4,768,768]{2,1,0:T(8,128)(2,1)}, bf16[4,768,768]{2,1,0:T(8,128)(2,1)}) custom-call(s32[2]{0:T(128)} %pad_add_fusion.me_ref, bf16[1024,768]{1,0:T(8,128)(2,1)} %get-tuple-element.284.nffn_ref, ...), custom_call_target="tpu_custom_call" | custom-call | flops 15000000512 | bytes 30000000 | tf_op jit(solution)/shard_map/ffn_forward/pallas_call | solution.py:281
  156.7 20.7 %attention_forward.3 = (f32[1024,768]{1,0:T(8,128)}, bf16[1024,768]{1,0:T(8,128)(2,1)}, bf16[1024,768]{1,0:T(8,128)(2,1)}, bf16[1024,2304]{1,0:T(8,128)(2,1)}, b...) custom-call(s32[2]{0:T(128)} %pad_add_fusion.me_ref, ...), custom_call_target="tpu_custom_call" | custom-call | flops 20000000000 | bytes 30000000 | tf_op jit(solution)/shard_map/attention_forward/pallas_call | solution.py:189
  177.4 6.4 %collective-permute-done.22.refs_1_.refs_5_ = bf16[2,4,192,768]{3,2,1,0:T(8,128)(2,1)S(1)} collective-permute-done((bf16[2,4,192,768]{3,2,1,0:T(8,128)(2,1)S(1)}, bf16[2,4,192,768]{3,2,1,0:T(8,128)(2,1)S(1)}, u32[]{:S(2)}, u32[]{:S(2)}) %collective-permute-start.22) | collective-permute-done | bytes 2359328 | tf_op jit(solution)/shard_map/ppermute | solution.py:857
  189.9 32.1 %ffn_both.1 = (f32[1024,768]{1,0:T(8,128)}, bf16[1024,3072]{1,0:T(8,128)(2,1)}, bf16[1024,3072]{1,0:T(8,128)(2,1)}, f32[1024,768]{1,0:T(8,128)}, f32[8,768]{1,0:T(8,128)}, /*index=5*/f32[1,3072]{1,0:T(1,128)}) custom-call(s32[2]{0:T(128)} %pad_add_fusion.me_ref, bf16[1024,768]{1,0:T(8,128)(2,1)} %get-tuple-element.316.nffn_ref, ...), custom_call_target="tpu_custom_call" | custom-call | flops 24999999488 | bytes 40000000 | tf_op jit(solution)/shard_map/ffn_both/pallas_call | solution.py:449
  222.0 11.4 %ffn_weight.4 = (bf16[2,2,4,192,768]{4,3,2,1,0:T(8,128)(2,1)}, bf16[768,1024]{1,0:T(8,128)(2,1)}, bf16[768,1024]{1,0:T(8,128)(2,1)}) custom-call(s32[2]{0:T(128)} %pad_add_fusion.me_ref, bf16[1024,768]{1,0:T(8,128)(2,1)} %get-tuple-element.316.nffn_ref, bf16[1024,768]{1,0:T(8,128)(2,1)} %grad_ref.3, bf16[1024,3072]{1,0:T(8,128)(2,1)} %get-tuple-element.328.gupper_ref, ...), custom_call_target="tpu_custom_call" | custom-call | flops 8000000000 | bytes 15000000 | tf_op jit(solution)/shard_map/ffn_weight/pallas_call | solution.py:711
  234.0 10.3 %ffn_weight.5 = bf16[2,2,4,192,768]{4,3,2,1,0:T(8,128)(2,1)} custom-call(s32[2]{0:T(128)} %pad_add_fusion.me_ref, bf16[768,1024]{1,0:T(8,128)(2,1)} %get-tuple-element.327.nffn_ref, bf16[768,1024]{1,0:T(8,128)(2,1)} %get-tuple-element.325.grad_ref, bf16[1024,3072]{1,0:T(8,128)(2,1)} %get-tuple-element.328.gupper_ref, ...), custom_call_target="tpu_custom_call" | custom-call | flops 8000000000 | bytes 15000000 | tf_op jit(solution)/shard_map/ffn_weight/pallas_call | solution.py:711
  248.2 25.1 %attention_backward.2 = (f32[1024,768]{1,0:T(8,128)}, bf16[1024,2304]{1,0:T(8,128)(2,1)}, f32[8,768]{1,0:T(8,128)}) custom-call(f32[1024,768]{1,0:T(8,128)} %get-tuple-element.333.gmiddle_ref, f32[1024,768]{1,0:T(8,128)} %get-tuple-element.300.stream_ref, bf16[1024,2304]{1,0:T(8,128)(2,1)} %get-tuple-element.334.proj_ref, ...), custom_call_target="tpu_custom_call" | custom-call | flops 15000000512 | bytes 20000000 | tf_op jit(solution)/shard_map/attention_backward/pallas_call | solution.py:578
  279.0 11.9 %attention_weight.2 = (bf16[2,2,4,96,768]{4,3,2,1,0:T(8,128)(2,1)}, bf16[2,2,4,96,768]{4,3,2,1,0:T(8,128)(2,1)}) custom-call(s32[2]{0:T(128)} %pad_add_fusion.me_ref, bf16[1024,768]{1,0:T(8,128)(2,1)} %get-tuple-element.344.normed_ref, bf16[1024,768]{1,0:T(8,128)(2,1)} %get-tuple-element.345.mixed_ref, bf16[1024,2304]{1,0:T(8,128)(2,1)} %get-tuple-element.346.gproj_ref, ...), custom_call_target="tpu_custom_call" | custom-call | flops 10000000000 | bytes 20000000 | tf_op jit(solution)/shard_map/attention_weight/pallas_call | solution.py:783
  298.6 20.1 %ffn_backward.1 = (bf16[1024,3072]{1,0:T(8,128)(2,1)}, f32[1024,768]{1,0:T(8,128)}, f32[8,768]{1,0:T(8,128)}, f32[1,3072]{1,0:T(1,128)}) custom-call(s32[2]{0:T(128)} %pad_add_fusion.me_ref, f32[1024,768]{1,0:T(8,128)} %get-tuple-element.355.grad_ref, bf16[1024,3072]{1,0:T(8,128)(2,1)} %get-tuple-element.356.slope_ref, ...), custom_call_target="tpu_custom_call" | custom-call | flops 15000000512 | bytes 30000000 | tf_op jit(solution)/shard_map/ffn_backward/pallas_call | solution.py:356
  324.2 11.9 %ffn_weight.6 = (bf16[2,2,4,192,768]{4,3,2,1,0:T(8,128)(2,1)}, bf16[768,1024]{1,0:T(8,128)(2,1)}, bf16[768,1024]{1,0:T(8,128)(2,1)}) custom-call(s32[2]{0:T(128)} %pad_add_fusion.me_ref, bf16[1024,768]{1,0:T(8,128)(2,1)} %get-tuple-element.284.nffn_ref, f32[1024,768]{1,0:T(8,128)} %get-tuple-element.355.grad_ref, ...), custom_call_target="tpu_custom_call" | custom-call | flops 8000000000 | bytes 15000000 | tf_op jit(solution)/shard_map/ffn_weight/pallas_call | solution.py:711
  339.6 10.5 %ffn_weight.7 = bf16[2,2,4,192,768]{4,3,2,1,0:T(8,128)(2,1)} custom-call(s32[2]{0:T(128)} %pad_add_fusion.me_ref, bf16[768,1024]{1,0:T(8,128)(2,1)} %get-tuple-element.378.nffn_ref, bf16[768,1024]{1,0:T(8,128)(2,1)} %get-tuple-element.375.grad_ref, bf16[1024,3072]{1,0:T(8,128)(2,1)} %get-tuple-element.379.gupper_ref, ...), custom_call_target="tpu_custom_call" | custom-call | flops 8000000000 | bytes 15000000 | tf_op jit(solution)/shard_map/ffn_weight/pallas_call | solution.py:711
  359.5 25.0 %attention_backward.3 = (f32[1024,768]{1,0:T(8,128)}, bf16[1024,2304]{1,0:T(8,128)(2,1)}, f32[8,768]{1,0:T(8,128)}) custom-call(f32[1024,768]{1,0:T(8,128)} %get-tuple-element.386.gmiddle_ref, bf16[1024,768]{1,0:T(8,128)(2,1)} %stream_ref.2, bf16[1024,2304]{1,0:T(8,128)(2,1)} %get-tuple-element.387.proj_ref, ...), custom_call_target="tpu_custom_call" | custom-call | flops 15000000512 | bytes 20000000 | tf_op jit(solution)/shard_map/attention_backward/pallas_call | solution.py:578
  393.1 12.2 %attention_weight.3 = (bf16[2,2,4,112,768]{4,3,2,1,0:T(8,128)(2,1)}, bf16[2,2,4,112,768]{4,3,2,1,0:T(8,128)(2,1)}) custom-call(s32[2]{0:T(128)} %pad_add_fusion.me_ref, bf16[1024,768]{1,0:T(8,128)(2,1)} %get-tuple-element.403.normed_ref, bf16[1024,768]{1,0:T(8,128)(2,1)} %get-tuple-element.404.mixed_ref, bf16[1024,2304]{1,0:T(8,128)(2,1)} %get-tuple-element.405.gproj_ref, ...), custom_call_target="tpu_custom_call" | custom-call | flops 10000000000 | bytes 20000000 | tf_op jit(solution)/shard_map/attention_weight/pallas_call | solution.py:783
  415.5 5.3 %collective-permute-done.43 = bf16[192,768]{1,0:T(8,128)(2,1)S(1)} collective-permute-done((bf16[192,768]{1,0:T(8,128)(2,1)S(1)}, bf16[192,768]{1,0:T(8,128)(2,1)S(1)}, u32[]{:S(2)}, u32[]{:S(2)}) %collective-permute-start.43) | collective-permute-done | bytes 294944 | tf_op jit(solution)/shard_map/ppermute | solution.py:857
  420.8 7.6 %collective-permute-done.44 = bf16[192,768]{1,0:T(8,128)(2,1)S(1)} collective-permute-done((bf16[192,768]{1,0:T(8,128)(2,1)S(1)}, bf16[192,768]{1,0:T(8,128)(2,1)S(1)}, u32[]{:S(2)}, u32[]{:S(2)}) %collective-permute-start.44) | collective-permute-done | bytes 294944 | tf_op jit(solution)/shard_map/ppermute | solution.py:857
  471.5 5.3 %collective-permute-start.51 = (f32[1,1]{1,0:T(1,128)}, f32[1,1]{1,0:T(1,128)}, u32[]{:S(2)}, u32[]{:S(2)}) collective-permute-start(f32[1,1]{1,0:T(1,128)} %add.332), channel_id=1, source_target_pairs={{0,4},{1,5},{2,6},{3,7},{4,0},{5,1},{6,2},{7,3},{8,12},{9,13},{10,... | collective-permute-start | bytes 20 | tf_op jit(solution)/shard_map/ppermute | solution.py:857
  (282 shorter events, 168.1 us)
Async XLA Ops:
  7.2 103.6 %all-gather.3.cloned.1.call-start = ((), (), s32[]{:S(2)}) async-start(), calls=%async_computation | async-start | bytes 2211840 | tf_op jit(solution)/shard_map/all_gather | solution.py:888
  27.1 16.3 %collective-permute-start.3 = (bf16[4,96,768]{2,1,0:T(8,128)(2,1)S(1)}, bf16[4,96,768]{2,1,0:T(8,128)(2,1)S(1)}, u32[]{:S(2)}, u32[]{:S(2)}) collective-permute-start(bf16[4,96,768]{2,1,0:T(8,128)(2,1)S(1)} %get-tuple-element.234), channel_id=1, source_target_pairs={{0,4},{1,3},{2,6},{3,1},{4,0},{5,7},{6,2},{7,5},{8,12},{9,11},{10,... | collective-permute-start | bytes 1769480 | tf_op jit(solution)/shard_map/ppermute | solution.py:857
  43.5 16.9 %collective-permute-start.8 = (bf16[2,4,96,768]{3,2,1,0:T(8,128)(2,1)S(1)}, bf16[2,4,96,768]{3,2,1,0:T(8,128)(2,1)}, u32[]{:S(2)}, u32[]{:S(2)}) collective-permute-start(bf16[2,4,96,768]{3,2,1,0:T(8,128)(2,1)S(1)} %pad_maximum_fusion.2.refs_0_), channel_id=1, source_target_pairs={{0,2},{1,5},{2,0},{3,7},{4,6},{5,1},{6,4},{7,3},{8,10},{9,13},{10,... | collective-permute-start | bytes 3538952 | tf_op jit(solution)/shard_map/ppermute | solution.py:857
  44.1 16.4 %collective-permute-start.9 = (bf16[2,4,96,768]{3,2,1,0:T(8,128)(2,1)S(1)}, bf16[2,4,96,768]{3,2,1,0:T(8,128)(2,1)}, u32[]{:S(2)}, u32[]{:S(2)}) collective-permute-start(bf16[2,4,96,768]{3,2,1,0:T(8,128)(2,1)S(1)} %pad_maximum_fusion.2.refs_0_), channel_id=1, source_target_pairs={{0,1},{1,0},{2,3},{3,2},{4,5},{5,4},{6,7},{7,6},{8,9},{9,8},{10,11... | collective-permute-start | bytes 3538952 | tf_op jit(solution)/shard_map/ppermute | solution.py:857
  45.0 15.5 %collective-permute-start.10 = (bf16[192,768]{1,0:T(8,128)(2,1)}, bf16[192,768]{1,0:T(8,128)(2,1)S(1)}, u32[]{:S(2)}, u32[]{:S(2)}) collective-permute-start(bf16[192,768]{1,0:T(8,128)(2,1)} %copy-done.26), channel_id=1, source_target_pairs={{0,8},{1,9},{2,10},{3,11},{4,12},{5,13},{6,14},{7,15},{8,0},{9,1},... | collective-permute-start | bytes 884744 | tf_op jit(solution)/shard_map/ppermute | solution.py:857
  62.6 16.4 %collective-permute-start.13 = (bf16[4,192,768]{2,1,0:T(8,128)(2,1)S(1)}, bf16[4,192,768]{2,1,0:T(8,128)(2,1)}, u32[]{:S(2)}, u32[]{:S(2)}) collective-permute-start(bf16[4,192,768]{2,1,0:T(8,128)(2,1)S(1)} %get-tuple-element.257), channel_id=1, source_target_pairs={{0,4},{1,3},{2,6},{3,1},{4,0},{5,7},{6,2},{7,5},{8,12},{9,11},{10,... | collective-permute-start | bytes 3538952 | tf_op jit(solution)/shard_map/ppermute | solution.py:857
  80.5 28.9 %collective-permute-start.14 = (bf16[2,4,192,768]{3,2,1,0:T(8,128)(2,1)S(1)}, bf16[2,4,192,768]{3,2,1,0:T(8,128)(2,1)S(1)}, u32[]{:S(2)}, u32[]{:S(2)}) collective-permute-start(bf16[2,4,192,768]{3,2,1,0:T(8,128)(2,1)S(1)} %pad_maximum_fusion.refs_0_.refs_4_), channel_id=1, source_target_pairs={{0,2},{1,5},{2,0},{3,7},{4,6},{5,1},{6,4},{7,3},{8,10},{9,13},{10,... | collective-permute-start | bytes 7077896 | tf_op jit(solution)/shard_map/ppermute | solution.py:857
  81.9 27.5 %collective-permute-start.15 = (bf16[2,4,192,768]{3,2,1,0:T(8,128)(2,1)S(1)}, bf16[2,4,192,768]{3,2,1,0:T(8,128)(2,1)}, u32[]{:S(2)}, u32[]{:S(2)}) collective-permute-start(bf16[2,4,192,768]{3,2,1,0:T(8,128)(2,1)S(1)} %pad_maximum_fusion.refs_0_.refs_4_), channel_id=1, source_target_pairs={{0,1},{1,0},{2,3},{3,2},{4,5},{5,4},{6,7},{7,6},{8,9},{9,8},{10,11... | collective-permute-start | bytes 7077896 | tf_op jit(solution)/shard_map/ppermute | solution.py:857
  123.7 28.1 %collective-permute-start.18 = (bf16[2,4,96,768]{3,2,1,0:T(8,128)(2,1)S(1)}, bf16[2,4,96,768]{3,2,1,0:T(8,128)(2,1)S(1)}, u32[]{:S(2)}, u32[]{:S(2)}) collective-permute-start(bf16[2,4,96,768]{3,2,1,0:T(8,128)(2,1)S(1)} %pad_maximum_fusion.4.refs_0_), channel_id=1, source_target_pairs={{0,2},{1,5},{2,0},{3,7},{4,6},{5,1},{6,4},{7,3},{8,10},{9,13},{10,... | collective-permute-start | bytes 3538952 | tf_op jit(solution)/shard_map/ppermute | solution.py:857
  125.0 26.7 %collective-permute-start.19 = (bf16[2,4,96,768]{3,2,1,0:T(8,128)(2,1)S(1)}, bf16[2,4,96,768]{3,2,1,0:T(8,128)(2,1)S(1)}, u32[]{:S(2)}, u32[]{:S(2)}) collective-permute-start(bf16[2,4,96,768]{3,2,1,0:T(8,128)(2,1)S(1)} %pad_maximum_fusion.4.refs_0_), channel_id=1, source_target_pairs={{0,1},{1,0},{2,3},{3,2},{4,5},{5,4},{6,7},{7,6},{8,9},{9,8},{10,11... | collective-permute-start | bytes 3538952 | tf_op jit(solution)/shard_map/ppermute | solution.py:857
  125.1 26.7 %collective-permute-start.20 = (bf16[4,192,768]{2,1,0:T(8,128)(2,1)S(1)}, bf16[4,192,768]{2,1,0:T(8,128)(2,1)S(1)}, u32[]{:S(2)}, u32[]{:S(2)}) collective-permute-start(bf16[4,192,768]{2,1,0:T(8,128)(2,1)S(1)} %get-tuple-element.283), channel_id=1, source_target_pairs={{0,4},{1,3},{2,6},{3,1},{4,0},{5,7},{6,2},{7,5},{8,12},{9,11},{10,... | collective-permute-start | bytes 3538952 | tf_op jit(solution)/shard_map/ppermute | solution.py:857
  155.0 28.8 %collective-permute-start.22 = (bf16[2,4,192,768]{3,2,1,0:T(8,128)(2,1)S(1)}, bf16[2,4,192,768]{3,2,1,0:T(8,128)(2,1)S(1)}, u32[]{:S(2)}, u32[]{:S(2)}) collective-permute-start(bf16[2,4,192,768]{3,2,1,0:T(8,128)(2,1)S(1)} %pad_maximum_fusion.1.refs_0_.refs_4_), channel_id=1, source_target_pairs={{0,2},{1,5},{2,0},{3,7},{4,6},{5,1},{6,4},{7,3},{8,10},{9,13},{10,... | collective-permute-start | bytes 7077896 | tf_op jit(solution)/shard_map/ppermute | solution.py:857
  156.7 27.2 %collective-permute-start.23 = (bf16[2,4,192,768]{3,2,1,0:T(8,128)(2,1)S(1)}, bf16[2,4,192,768]{3,2,1,0:T(8,128)(2,1)S(1)}, u32[]{:S(2)}, u32[]{:S(2)}) collective-permute-start(bf16[2,4,192,768]{3,2,1,0:T(8,128)(2,1)S(1)} %pad_maximum_fusion.1.refs_0_.refs_4_), channel_id=1, source_target_pairs={{0,1},{1,0},{2,3},{3,2},{4,5},{5,4},{6,7},{7,6},{8,9},{9,8},{10,11... | collective-permute-start | bytes 7077896 | tf_op jit(solution)/shard_map/ppermute | solution.py:857
  246.5 29.0 %collective-permute-start.26 = (bf16[2,4,192,768]{3,2,1,0:T(8,128)(2,1)S(1)}, bf16[2,4,192,768]{3,2,1,0:T(8,128)(2,1)}, u32[]{:S(2)}, u32[]{:S(2)}) collective-permute-start(bf16[2,4,192,768]{3,2,1,0:T(8,128)(2,1)S(1)} %fusion), channel_id=1, source_target_pairs={{0,2},{1,5},{2,0},{3,7},{4,6},{5,1},{6,4},{7,3},{8,10},{9,13},{10,... | collective-permute-start | bytes 7077896 | tf_op jit(solution)/shard_map/ppermute | solution.py:857
  277.6 16.3 %collective-permute-start.27 = (bf16[4,192,768]{2,1,0:T(8,128)(2,1)S(1)}, bf16[4,192,768]{2,1,0:T(8,128)(2,1)S(1)}, u32[]{:S(2)}, u32[]{:S(2)}) collective-permute-start(bf16[4,192,768]{2,1,0:T(8,128)(2,1)S(1)} %fusion.5), channel_id=1, source_target_pairs={{0,4},{1,3},{2,6},{3,1},{4,0},{5,7},{6,2},{7,5},{8,12},{9,11},{10,... | collective-permute-start | bytes 3538952 | tf_op jit(solution)/shard_map/ppermute | solution.py:857
  296.9 21.8 %collective-permute-start.28 = (bf16[2,2,4,96,768]{4,3,2,1,0:T(8,128)(2,1)}, bf16[2,2,4,96,768]{4,3,2,1,0:T(8,128)(2,1)S(1)}, u32[]{:S(2)}, u32[]{:S(2)}) collective-permute-start(bf16[2,2,4,96,768]{4,3,2,1,0:T(8,128)(2,1)} %get-tuple-element.353), channel_id=1, source_target_pairs={{0,1},{1,0},{2,3},{3,2},{4,5},{5,4},{6,7},{7,6},{8,9},{9,8},{10,11... | collective-permute-start | bytes 7077896 | tf_op jit(solution)/shard_map/ppermute | solution.py:857
  296.9 21.8 %collective-permute-start.29 = (bf16[192,768]{1,0:T(8,128)(2,1)S(1)}, bf16[192,768]{1,0:T(8,128)(2,1)S(1)}, u32[]{:S(2)}, u32[]{:S(2)}) collective-permute-start(bf16[192,768]{1,0:T(8,128)(2,1)S(1)} %get-tuple-element.354), channel_id=1, source_target_pairs={{0,16},{1,17},{2,18},{3,19},{4,20},{5,21},{6,22},{7,23},{8,24},{9,... | collective-permute-start | bytes 884744 | tf_op jit(solution)/shard_map/ppermute | solution.py:857
  319.7 17.7 %collective-permute-start.30 = (bf16[2,4,96,768]{3,2,1,0:T(8,128)(2,1)S(1)}, bf16[2,4,96,768]{3,2,1,0:T(8,128)(2,1)}, u32[]{:S(2)}, u32[]{:S(2)}) collective-permute-start(bf16[2,4,96,768]{3,2,1,0:T(8,128)(2,1)S(1)} %fusion.9), channel_id=1, source_target_pairs={{0,2},{1,5},{2,0},{3,7},{4,6},{5,1},{6,4},{7,3},{8,10},{9,13},{10,... | collective-permute-start | bytes 3538952 | tf_op jit(solution)/shard_map/ppermute | solution.py:857
  356.2 29.2 %collective-permute-start.35 = (bf16[2,4,192,768]{3,2,1,0:T(8,128)(2,1)}, bf16[2,4,192,768]{3,2,1,0:T(8,128)(2,1)}, u32[]{:S(2)}, u32[]{:S(2)}) collective-permute-start(bf16[2,4,192,768]{3,2,1,0:T(8,128)(2,1)} %fusion.1), channel_id=1, source_target_pairs={{0,2},{1,5},{2,0},{3,7},{4,6},{5,1},{6,4},{7,3},{8,10},{9,13},{10,... | collective-permute-start | bytes 7077896 | tf_op jit(solution)/shard_map/ppermute | solution.py:857
  357.7 26.8 %collective-permute-start.36 = (bf16[96,768]{1,0:T(8,128)(2,1)}, bf16[96,768]{1,0:T(8,128)(2,1)}, u32[]{:S(2)}, u32[]{:S(2)}) collective-permute-start(bf16[96,768]{1,0:T(8,128)(2,1)} %get-tuple-element.385), channel_id=1, source_target_pairs={{0,16},{1,17},{2,18},{3,19},{4,20},{5,21},{6,22},{7,23},{8,24},{9,... | collective-permute-start | bytes 442376 | tf_op jit(solution)/shard_map/ppermute | solution.py:857
  388.5 16.9 %collective-permute-start.37 = (bf16[4,192,768]{2,1,0:T(8,128)(2,1)}, bf16[4,192,768]{2,1,0:T(8,128)(2,1)}, u32[]{:S(2)}, u32[]{:S(2)}) collective-permute-start(bf16[4,192,768]{2,1,0:T(8,128)(2,1)} %fusion.2), channel_id=1, source_target_pairs={{0,4},{1,3},{2,6},{3,1},{4,0},{5,7},{6,2},{7,5},{8,12},{9,11},{10,... | collective-permute-start | bytes 3538952 | tf_op jit(solution)/shard_map/ppermute | solution.py:857
  411.0 18.4 %collective-permute-start.42 = (bf16[2,4,112,768]{3,2,1,0:T(8,128)(2,1)S(1)}, bf16[2,4,112,768]{3,2,1,0:T(8,128)(2,1)S(1)}, u32[]{:S(2)}, u32[]{:S(2)}) collective-permute-start(bf16[2,4,112,768]{3,2,1,0:T(8,128)(2,1)S(1)} %fusion.6), channel_id=1, source_target_pairs={{0,2},{1,5},{2,0},{3,7},{4,6},{5,1},{6,4},{7,3},{8,10},{9,13},{10,... | collective-permute-start | bytes 4128776 | tf_op jit(solution)/shard_map/ppermute | solution.py:857
  434.6 18.5 %collective-permute-start.40 = (bf16[192,768]{1,0:T(8,128)(2,1)S(1)}, bf16[192,768]{1,0:T(8,128)(2,1)S(1)}, u32[]{:S(2)}, u32[]{:S(2)}) collective-permute-start(bf16[192,768]{1,0:T(8,128)(2,1)S(1)} %copy-done.27), channel_id=1, source_target_pairs={{0,16},{1,17},{2,18},{3,19},{4,20},{5,21},{6,22},{7,23},{8,24},{9,... | collective-permute-start | bytes 884744 | tf_op jit(solution)/shard_map/ppermute | solution.py:857
  445.3 16.4 %collective-permute-start.47 = (bf16[112,768]{1,0:T(8,128)(2,1)}, bf16[112,768]{1,0:T(8,128)(2,1)}, u32[]{:S(2)}, u32[]{:S(2)}) collective-permute-start(bf16[112,768]{1,0:T(8,128)(2,1)} %get-tuple-element.426), channel_id=1, source_target_pairs={{0,16},{1,17},{2,18},{3,19},{4,20},{5,21},{6,22},{7,23},{8,24},{9,... | collective-permute-start | bytes 516104 | tf_op jit(solution)/shard_map/ppermute | solution.py:857
  (82 other events, 935.7 us)
Sparse Core Ops, SparseCore 0:
  64.9 39.1 all-gather.2

commit v6 on v5

--- a/solution.py
+++ b/solution.py
@@ -1033,7 +1033,7 @@
         kept = saved[index]
         return lambda gmiddle: attention_backward(
             gmiddle, kept["stream"], kept["proj"], kept["probs"], small[index], kept["weight"],
-            block_pages, begin, end, before,
+            4 if pages % 4 == 0 else block_pages, begin, end, before,
         )
 
     def attention_weight_of(index, gmiddle, extra=None):

time: 516 us -> 512 us (level)
  transfers between devices with their start and end apart: 55 -> 55, of which waited for: 30 -> 30; matrix products, arithmetic and copies ran while one was open for 5% -> 5% of each run, Pallas kernels for 38% -> 37%
where the time goes in v6:
time: 512 us; the launch traced here: 508 us
  Pallas kernels  232 us (45%)
  waiting for transfers between devices  115 us (22%)
  starting transfers between devices  67.4 us (13%)
  other arithmetic  50.6 us (10%)
  between operations  23.7 us (5%)
  local copies, waits for them, and re-layouts  19.4 us (4%)
    ppermute x54, waiting for transfers between devices, swap(): return lax.ppermute(value, ('dp', 'tensor'), pairs)  115 us
    ppermute x54, starting transfers between devices, swap(): return lax.ppermute(value, ('dp', 'tensor'), pairs)  67.4 us
    pallas_call x2, Pallas kernels, attention_backward(): pl.pallas_call(attention_backward_kernel, grid=((end - begin) // block_pa...  48.2 us
    pallas_call x4, Pallas kernels, ffn_weight_split(): pl.pallas_call(functools.partial(ffn_weight_split_kernel, core), grid_spe...  44.3 us
    pallas_call x2, Pallas kernels, attention_forward(): pl.pallas_call(functools.partial(attention_forward_kernel, plan), grid=(p...  41.6 us
    pallas_call x1, Pallas kernels, ffn_both(): pl.pallas_call(functools.partial(ffn_both_kernel, (up_w[0], down_w[0])),...  32.2 us
    pallas_call x2, Pallas kernels, attention_weight_split(): pl.pallas_call(attention_weight_split_kernel, grid=(3,), in_specs=[pl.Blo...  23.9 us
    pallas_call x1, Pallas kernels, ffn_forward(): pl.pallas_call(functools.partial(ffn_forward_kernel, (up_w[0], down_w[0])...  21.9 us
  transfers between devices with their start and end apart: 55, of which 30 were waited for; matrix products, arithmetic and copies ran while one was open for 5% of the time, Pallas kernels for 37%

profile of v6, /device:TPU:0, one launch (start us, length us, event | category | flops | bytes accessed | tf_op | source)
XLA Modules:
  0.0 507.8 jit_solution(8351724060605694973)
XLA Ops:
  9.4 5.1 %collective-permute-start.2 = (bf16[96,768]{1,0:T(8,128)(2,1)S(1)}, bf16[96,768]{1,0:T(8,128)(2,1)S(1)}, u32[]{:S(2)}, u32[]{:S(2)}) collective-permute-start(bf16[96,768]{1,0:T(8,128)(2,1)S(1)} %bitcast.166), channel_id=1, source_target_pairs={{0,24},{1,25},{2,26},{3,27},{4,28},{5,29},{6,30},{7,31},{8,16},{9,... | collective-permute-start | bytes 442376 | tf_op jit(solution)/shard_map/ppermute | solution.py:857
  19.3 7.7 %collective-permute-done.1 = bf16[96,768]{1,0:T(8,128)(2,1)S(1)} collective-permute-done((bf16[96,768]{1,0:T(8,128)(2,1)S(1)}, bf16[96,768]{1,0:T(8,128)(2,1)S(1)}, u32[]{:S(2)}, u32[]{:S(2)}) %collective-permute-start.1) | collective-permute-done | bytes 147488 | tf_op jit(solution)/shard_map/ppermute | solution.py:857
  36.3 7.1 %collective-permute-done.4 = bf16[192,768]{1,0:T(8,128)(2,1)S(1)} collective-permute-done((bf16[192,768]{1,0:T(8,128)(2,1)S(1)}, bf16[192,768]{1,0:T(8,128)(2,1)S(1)}, u32[]{:S(2)}, u32[]{:S(2)}) %collective-permute-start.4) | collective-permute-done | bytes 294944 | tf_op jit(solution)/shard_map/ppermute | solution.py:857
  48.8 11.7 %collective-permute-done.10 = bf16[192,768]{1,0:T(8,128)(2,1)S(1)} collective-permute-done((bf16[192,768]{1,0:T(8,128)(2,1)}, bf16[192,768]{1,0:T(8,128)(2,1)S(1)}, u32[]{:S(2)}, u32[]{:S(2)}) %collective-permute-start.10) | collective-permute-done | bytes 294944 | tf_op jit(solution)/shard_map/ppermute | solution.py:857
  65.8 13.2 %collective-permute-done.13 = bf16[4,192,768]{2,1,0:T(8,128)(2,1)} collective-permute-done((bf16[4,192,768]{2,1,0:T(8,128)(2,1)S(1)}, bf16[4,192,768]{2,1,0:T(8,128)(2,1)}, u32[]{:S(2)}, u32[]{:S(2)}) %collective-permute-start.13) | collective-permute-done | bytes 1179680 | tf_op jit(solution)/shard_map/ppermute | solution.py:857
  83.7 20.8 %attention_forward.2 = (f32[1024,768]{1,0:T(8,128)}, bf16[1024,768]{1,0:T(8,128)(2,1)}, bf16[1024,768]{1,0:T(8,128)(2,1)}, bf16[1024,2304]{1,0:T(8,128)(2,1)}, b...) custom-call(s32[2]{0:T(128)} %pad_add_fusion.me_ref, ...), custom_call_target="tpu_custom_call" | custom-call | flops 20000000000 | bytes 30000000 | tf_op jit(solution)/shard_map/attention_forward/pallas_call | solution.py:189
  104.5 4.9 collective-permute-done.14.refs_1_.refs_5_
  114.3 7.8 %collective-permute-done.17 = bf16[4,96,768]{2,1,0:T(8,128)(2,1)S(1)} collective-permute-done((bf16[4,96,768]{2,1,0:T(8,128)(2,1)S(1)}, bf16[4,96,768]{2,1,0:T(8,128)(2,1)S(1)}, u32[]{:S(2)}, u32[]{:S(2)}) %collective-permute-start.17) | collective-permute-done | bytes 589856 | tf_op jit(solution)/shard_map/ppermute | solution.py:857
  126.5 21.9 %ffn_forward.1 = (f32[1024,768]{1,0:T(8,128)}, bf16[1024,3072]{1,0:T(8,128)(2,1)}, bf16[1024,3072]{1,0:T(8,128)(2,1)}, bf16[4,768,768]{2,1,0:T(8,128)(2,1)}, bf16[4,768,768]{2,1,0:T(8,128)(2,1)}) custom-call(s32[2]{0:T(128)} %pad_add_fusion.me_ref, bf16[1024,768]{1,0:T(8,128)(2,1)} %get-tuple-element.284.nffn_ref, ...), custom_call_target="tpu_custom_call" | custom-call | flops 15000000512 | bytes 30000000 | tf_op jit(solution)/shard_map/ffn_forward/pallas_call | solution.py:281
  156.7 20.7 %attention_forward.3 = (f32[1024,768]{1,0:T(8,128)}, bf16[1024,768]{1,0:T(8,128)(2,1)}, bf16[1024,768]{1,0:T(8,128)(2,1)}, bf16[1024,2304]{1,0:T(8,128)(2,1)}, b...) custom-call(s32[2]{0:T(128)} %pad_add_fusion.me_ref, ...), custom_call_target="tpu_custom_call" | custom-call | flops 20000000000 | bytes 30000000 | tf_op jit(solution)/shard_map/attention_forward/pallas_call | solution.py:189
  177.4 6.4 %collective-permute-done.22.refs_1_.refs_5_ = bf16[2,4,192,768]{3,2,1,0:T(8,128)(2,1)S(1)} collective-permute-done((bf16[2,4,192,768]{3,2,1,0:T(8,128)(2,1)S(1)}, bf16[2,4,192,768]{3,2,1,0:T(8,128)(2,1)S(1)}, u32[]{:S(2)}, u32[]{:S(2)}) %collective-permute-start.22) | collective-permute-done | bytes 2359328 | tf_op jit(solution)/shard_map/ppermute | solution.py:857
  189.9 32.2 %ffn_both.1 = (f32[1024,768]{1,0:T(8,128)}, bf16[1024,3072]{1,0:T(8,128)(2,1)}, bf16[1024,3072]{1,0:T(8,128)(2,1)}, f32[1024,768]{1,0:T(8,128)}, f32[8,768]{1,0:T(8,128)}, /*index=5*/f32[1,3072]{1,0:T(1,128)}) custom-call(s32[2]{0:T(128)} %pad_add_fusion.me_ref, bf16[1024,768]{1,0:T(8,128)(2,1)} %get-tuple-element.316.nffn_ref, ...), custom_call_target="tpu_custom_call" | custom-call | flops 24999999488 | bytes 40000000 | tf_op jit(solution)/shard_map/ffn_both/pallas_call | solution.py:449
  222.0 11.4 %ffn_weight.4 = (bf16[2,2,4,192,768]{4,3,2,1,0:T(8,128)(2,1)}, bf16[768,1024]{1,0:T(8,128)(2,1)}, bf16[768,1024]{1,0:T(8,128)(2,1)}) custom-call(s32[2]{0:T(128)} %pad_add_fusion.me_ref, bf16[1024,768]{1,0:T(8,128)(2,1)} %get-tuple-element.316.nffn_ref, bf16[1024,768]{1,0:T(8,128)(2,1)} %grad_ref.3, bf16[1024,3072]{1,0:T(8,128)(2,1)} %get-tuple-element.328.gupper_ref, ...), custom_call_target="tpu_custom_call" | custom-call | flops 8000000000 | bytes 15000000 | tf_op jit(solution)/shard_map/ffn_weight/pallas_call | solution.py:711
  234.0 10.3 %ffn_weight.5 = bf16[2,2,4,192,768]{4,3,2,1,0:T(8,128)(2,1)} custom-call(s32[2]{0:T(128)} %pad_add_fusion.me_ref, bf16[768,1024]{1,0:T(8,128)(2,1)} %get-tuple-element.327.nffn_ref, bf16[768,1024]{1,0:T(8,128)(2,1)} %get-tuple-element.325.grad_ref, bf16[1024,3072]{1,0:T(8,128)(2,1)} %get-tuple-element.328.gupper_ref, ...), custom_call_target="tpu_custom_call" | custom-call | flops 8000000000 | bytes 15000000 | tf_op jit(solution)/shard_map/ffn_weight/pallas_call | solution.py:711
  248.2 24.5 %attention_backward.2 = (f32[1024,768]{1,0:T(8,128)}, bf16[1024,2304]{1,0:T(8,128)(2,1)}, f32[8,768]{1,0:T(8,128)}) custom-call(f32[1024,768]{1,0:T(8,128)} %get-tuple-element.333.gmiddle_ref, f32[1024,768]{1,0:T(8,128)} %get-tuple-element.300.stream_ref, bf16[1024,2304]{1,0:T(8,128)(2,1)} %get-tuple-element.334.proj_ref, ...), custom_call_target="tpu_custom_call" | custom-call | flops 15000000512 | bytes 20000000 | tf_op jit(solution)/shard_map/attention_backward/pallas_call | solution.py:578
  279.0 11.7 %attention_weight.2 = (bf16[2,2,4,96,768]{4,3,2,1,0:T(8,128)(2,1)}, bf16[2,2,4,96,768]{4,3,2,1,0:T(8,128)(2,1)}) custom-call(s32[2]{0:T(128)} %pad_add_fusion.me_ref, bf16[1024,768]{1,0:T(8,128)(2,1)} %get-tuple-element.344.normed_ref, bf16[1024,768]{1,0:T(8,128)(2,1)} %get-tuple-element.345.mixed_ref, bf16[1024,2304]{1,0:T(8,128)(2,1)} %get-tuple-element.346.gproj_ref, ...), custom_call_target="tpu_custom_call" | custom-call | flops 10000000000 | bytes 20000000 | tf_op jit(solution)/shard_map/attention_weight/pallas_call | solution.py:783
  298.6 19.7 %ffn_backward.1 = (bf16[1024,3072]{1,0:T(8,128)(2,1)}, f32[1024,768]{1,0:T(8,128)}, f32[8,768]{1,0:T(8,128)}, f32[1,3072]{1,0:T(1,128)}) custom-call(s32[2]{0:T(128)} %pad_add_fusion.me_ref, f32[1024,768]{1,0:T(8,128)} %get-tuple-element.355.grad_ref, bf16[1024,3072]{1,0:T(8,128)(2,1)} %get-tuple-element.356.slope_ref, ...), custom_call_target="tpu_custom_call" | custom-call | flops 15000000512 | bytes 30000000 | tf_op jit(solution)/shard_map/ffn_backward/pallas_call | solution.py:356
  323.8 11.9 %ffn_weight.6 = (bf16[2,2,4,192,768]{4,3,2,1,0:T(8,128)(2,1)}, bf16[768,1024]{1,0:T(8,128)(2,1)}, bf16[768,1024]{1,0:T(8,128)(2,1)}) custom-call(s32[2]{0:T(128)} %pad_add_fusion.me_ref, bf16[1024,768]{1,0:T(8,128)(2,1)} %get-tuple-element.284.nffn_ref, f32[1024,768]{1,0:T(8,128)} %get-tuple-element.355.grad_ref, ...), custom_call_target="tpu_custom_call" | custom-call | flops 8000000000 | bytes 15000000 | tf_op jit(solution)/shard_map/ffn_weight/pallas_call | solution.py:711
  339.2 10.7 %ffn_weight.7 = bf16[2,2,4,192,768]{4,3,2,1,0:T(8,128)(2,1)} custom-call(s32[2]{0:T(128)} %pad_add_fusion.me_ref, bf16[768,1024]{1,0:T(8,128)(2,1)} %get-tuple-element.378.nffn_ref, bf16[768,1024]{1,0:T(8,128)(2,1)} %get-tuple-element.375.grad_ref, bf16[1024,3072]{1,0:T(8,128)(2,1)} %get-tuple-element.379.gupper_ref, ...), custom_call_target="tpu_custom_call" | custom-call | flops 8000000000 | bytes 15000000 | tf_op jit(solution)/shard_map/ffn_weight/pallas_call | solution.py:711
  359.3 23.7 %attention_backward.3 = (f32[1024,768]{1,0:T(8,128)}, bf16[1024,2304]{1,0:T(8,128)(2,1)}, f32[8,768]{1,0:T(8,128)}) custom-call(f32[1024,768]{1,0:T(8,128)} %get-tuple-element.386.gmiddle_ref, bf16[1024,768]{1,0:T(8,128)(2,1)} %stream_ref.2, bf16[1024,2304]{1,0:T(8,128)(2,1)} %get-tuple-element.387.proj_ref, ...), custom_call_target="tpu_custom_call" | custom-call | flops 15000000512 | bytes 20000000 | tf_op jit(solution)/shard_map/attention_backward/pallas_call | solution.py:578
  392.9 12.2 %attention_weight.3 = (bf16[2,2,4,112,768]{4,3,2,1,0:T(8,128)(2,1)}, bf16[2,2,4,112,768]{4,3,2,1,0:T(8,128)(2,1)}) custom-call(s32[2]{0:T(128)} %pad_add_fusion.me_ref, bf16[1024,768]{1,0:T(8,128)(2,1)} %get-tuple-element.403.normed_ref, bf16[1024,768]{1,0:T(8,128)(2,1)} %get-tuple-element.404.mixed_ref, bf16[1024,2304]{1,0:T(8,128)(2,1)} %get-tuple-element.405.gproj_ref, ...), custom_call_target="tpu_custom_call" | custom-call | flops 10000000000 | bytes 20000000 | tf_op jit(solution)/shard_map/attention_weight/pallas_call | solution.py:783
  415.3 5.4 %collective-permute-done.43 = bf16[192,768]{1,0:T(8,128)(2,1)S(1)} collective-permute-done((bf16[192,768]{1,0:T(8,128)(2,1)S(1)}, bf16[192,768]{1,0:T(8,128)(2,1)S(1)}, u32[]{:S(2)}, u32[]{:S(2)}) %collective-permute-start.43) | collective-permute-done | bytes 294944 | tf_op jit(solution)/shard_map/ppermute | solution.py:857
  420.6 7.5 %collective-permute-done.44 = bf16[192,768]{1,0:T(8,128)(2,1)S(1)} collective-permute-done((bf16[192,768]{1,0:T(8,128)(2,1)S(1)}, bf16[192,768]{1,0:T(8,128)(2,1)S(1)}, u32[]{:S(2)}, u32[]{:S(2)}) %collective-permute-start.44) | collective-permute-done | bytes 294944 | tf_op jit(solution)/shard_map/ppermute | solution.py:857
  471.3 5.3 %collective-permute-start.51 = (f32[1,1]{1,0:T(1,128)}, f32[1,1]{1,0:T(1,128)}, u32[]{:S(2)}, u32[]{:S(2)}) collective-permute-start(f32[1,1]{1,0:T(1,128)} %add.332), channel_id=1, source_target_pairs={{0,4},{1,5},{2,6},{3,7},{4,0},{5,1},{6,2},{7,3},{8,12},{9,13},{10,... | collective-permute-start | bytes 20 | tf_op jit(solution)/shard_map/ppermute | solution.py:857
  (282 shorter events, 170.2 us)
Async XLA Ops:
  7.2 103.6 %all-gather.3.cloned.1.call-start = ((), (), s32[]{:S(2)}) async-start(), calls=%async_computation | async-start | bytes 2211840 | tf_op jit(solution)/shard_map/all_gather | solution.py:888
  27.1 16.3 %collective-permute-start.3 = (bf16[4,96,768]{2,1,0:T(8,128)(2,1)S(1)}, bf16[4,96,768]{2,1,0:T(8,128)(2,1)S(1)}, u32[]{:S(2)}, u32[]{:S(2)}) collective-permute-start(bf16[4,96,768]{2,1,0:T(8,128)(2,1)S(1)} %get-tuple-element.234), channel_id=1, source_target_pairs={{0,4},{1,3},{2,6},{3,1},{4,0},{5,7},{6,2},{7,5},{8,12},{9,11},{10,... | collective-permute-start | bytes 1769480 | tf_op jit(solution)/shard_map/ppermute | solution.py:857
  43.5 16.9 %collective-permute-start.8 = (bf16[2,4,96,768]{3,2,1,0:T(8,128)(2,1)S(1)}, bf16[2,4,96,768]{3,2,1,0:T(8,128)(2,1)}, u32[]{:S(2)}, u32[]{:S(2)}) collective-permute-start(bf16[2,4,96,768]{3,2,1,0:T(8,128)(2,1)S(1)} %pad_maximum_fusion.2.refs_0_), channel_id=1, source_target_pairs={{0,2},{1,5},{2,0},{3,7},{4,6},{5,1},{6,4},{7,3},{8,10},{9,13},{10,... | collective-permute-start | bytes 3538952 | tf_op jit(solution)/shard_map/ppermute | solution.py:857
  44.1 16.4 %collective-permute-start.9 = (bf16[2,4,96,768]{3,2,1,0:T(8,128)(2,1)S(1)}, bf16[2,4,96,768]{3,2,1,0:T(8,128)(2,1)}, u32[]{:S(2)}, u32[]{:S(2)}) collective-permute-start(bf16[2,4,96,768]{3,2,1,0:T(8,128)(2,1)S(1)} %pad_maximum_fusion.2.refs_0_), channel_id=1, source_target_pairs={{0,1},{1,0},{2,3},{3,2},{4,5},{5,4},{6,7},{7,6},{8,9},{9,8},{10,11... | collective-permute-start | bytes 3538952 | tf_op jit(solution)/shard_map/ppermute | solution.py:857
  45.0 15.5 %collective-permute-start.10 = (bf16[192,768]{1,0:T(8,128)(2,1)}, bf16[192,768]{1,0:T(8,128)(2,1)S(1)}, u32[]{:S(2)}, u32[]{:S(2)}) collective-permute-start(bf16[192,768]{1,0:T(8,128)(2,1)} %copy-done.26), channel_id=1, source_target_pairs={{0,8},{1,9},{2,10},{3,11},{4,12},{5,13},{6,14},{7,15},{8,0},{9,1},... | collective-permute-start | bytes 884744 | tf_op jit(solution)/shard_map/ppermute | solution.py:857
  62.6 16.4 %collective-permute-start.13 = (bf16[4,192,768]{2,1,0:T(8,128)(2,1)S(1)}, bf16[4,192,768]{2,1,0:T(8,128)(2,1)}, u32[]{:S(2)}, u32[]{:S(2)}) collective-permute-start(bf16[4,192,768]{2,1,0:T(8,128)(2,1)S(1)} %get-tuple-element.257), channel_id=1, source_target_pairs={{0,4},{1,3},{2,6},{3,1},{4,0},{5,7},{6,2},{7,5},{8,12},{9,11},{10,... | collective-permute-start | bytes 3538952 | tf_op jit(solution)/shard_map/ppermute | solution.py:857
  80.5 28.9 %collective-permute-start.14 = (bf16[2,4,192,768]{3,2,1,0:T(8,128)(2,1)S(1)}, bf16[2,4,192,768]{3,2,1,0:T(8,128)(2,1)S(1)}, u32[]{:S(2)}, u32[]{:S(2)}) collective-permute-start(bf16[2,4,192,768]{3,2,1,0:T(8,128)(2,1)S(1)} %pad_maximum_fusion.refs_0_.refs_4_), channel_id=1, source_target_pairs={{0,2},{1,5},{2,0},{3,7},{4,6},{5,1},{6,4},{7,3},{8,10},{9,13},{10,... | collective-permute-start | bytes 7077896 | tf_op jit(solution)/shard_map/ppermute | solution.py:857
  81.9 27.5 %collective-permute-start.15 = (bf16[2,4,192,768]{3,2,1,0:T(8,128)(2,1)S(1)}, bf16[2,4,192,768]{3,2,1,0:T(8,128)(2,1)}, u32[]{:S(2)}, u32[]{:S(2)}) collective-permute-start(bf16[2,4,192,768]{3,2,1,0:T(8,128)(2,1)S(1)} %pad_maximum_fusion.refs_0_.refs_4_), channel_id=1, source_target_pairs={{0,1},{1,0},{2,3},{3,2},{4,5},{5,4},{6,7},{7,6},{8,9},{9,8},{10,11... | collective-permute-start | bytes 7077896 | tf_op jit(solution)/shard_map/ppermute | solution.py:857
  123.7 28.1 %collective-permute-start.18 = (bf16[2,4,96,768]{3,2,1,0:T(8,128)(2,1)S(1)}, bf16[2,4,96,768]{3,2,1,0:T(8,128)(2,1)S(1)}, u32[]{:S(2)}, u32[]{:S(2)}) collective-permute-start(bf16[2,4,96,768]{3,2,1,0:T(8,128)(2,1)S(1)} %pad_maximum_fusion.4.refs_0_), channel_id=1, source_target_pairs={{0,2},{1,5},{2,0},{3,7},{4,6},{5,1},{6,4},{7,3},{8,10},{9,13},{10,... | collective-permute-start | bytes 3538952 | tf_op jit(solution)/shard_map/ppermute | solution.py:857
  125.0 26.7 %collective-permute-start.19 = (bf16[2,4,96,768]{3,2,1,0:T(8,128)(2,1)S(1)}, bf16[2,4,96,768]{3,2,1,0:T(8,128)(2,1)S(1)}, u32[]{:S(2)}, u32[]{:S(2)}) collective-permute-start(bf16[2,4,96,768]{3,2,1,0:T(8,128)(2,1)S(1)} %pad_maximum_fusion.4.refs_0_), channel_id=1, source_target_pairs={{0,1},{1,0},{2,3},{3,2},{4,5},{5,4},{6,7},{7,6},{8,9},{9,8},{10,11... | collective-permute-start | bytes 3538952 | tf_op jit(solution)/shard_map/ppermute | solution.py:857
  125.1 26.7 %collective-permute-start.20 = (bf16[4,192,768]{2,1,0:T(8,128)(2,1)S(1)}, bf16[4,192,768]{2,1,0:T(8,128)(2,1)S(1)}, u32[]{:S(2)}, u32[]{:S(2)}) collective-permute-start(bf16[4,192,768]{2,1,0:T(8,128)(2,1)S(1)} %get-tuple-element.283), channel_id=1, source_target_pairs={{0,4},{1,3},{2,6},{3,1},{4,0},{5,7},{6,2},{7,5},{8,12},{9,11},{10,... | collective-permute-start | bytes 3538952 | tf_op jit(solution)/shard_map/ppermute | solution.py:857
  155.0 28.8 %collective-permute-start.22 = (bf16[2,4,192,768]{3,2,1,0:T(8,128)(2,1)S(1)}, bf16[2,4,192,768]{3,2,1,0:T(8,128)(2,1)S(1)}, u32[]{:S(2)}, u32[]{:S(2)}) collective-permute-start(bf16[2,4,192,768]{3,2,1,0:T(8,128)(2,1)S(1)} %pad_maximum_fusion.1.refs_0_.refs_4_), channel_id=1, source_target_pairs={{0,2},{1,5},{2,0},{3,7},{4,6},{5,1},{6,4},{7,3},{8,10},{9,13},{10,... | collective-permute-start | bytes 7077896 | tf_op jit(solution)/shard_map/ppermute | solution.py:857
  156.7 27.2 %collective-permute-start.23 = (bf16[2,4,192,768]{3,2,1,0:T(8,128)(2,1)S(1)}, bf16[2,4,192,768]{3,2,1,0:T(8,128)(2,1)S(1)}, u32[]{:S(2)}, u32[]{:S(2)}) collective-permute-start(bf16[2,4,192,768]{3,2,1,0:T(8,128)(2,1)S(1)} %pad_maximum_fusion.1.refs_0_.refs_4_), channel_id=1, source_target_pairs={{0,1},{1,0},{2,3},{3,2},{4,5},{5,4},{6,7},{7,6},{8,9},{9,8},{10,11... | collective-permute-start | bytes 7077896 | tf_op jit(solution)/shard_map/ppermute | solution.py:857
  246.5 29.0 %collective-permute-start.26 = (bf16[2,4,192,768]{3,2,1,0:T(8,128)(2,1)S(1)}, bf16[2,4,192,768]{3,2,1,0:T(8,128)(2,1)}, u32[]{:S(2)}, u32[]{:S(2)}) collective-permute-start(bf16[2,4,192,768]{3,2,1,0:T(8,128)(2,1)S(1)} %fusion), channel_id=1, source_target_pairs={{0,2},{1,5},{2,0},{3,7},{4,6},{5,1},{6,4},{7,3},{8,10},{9,13},{10,... | collective-permute-start | bytes 7077896 | tf_op jit(solution)/shard_map/ppermute | solution.py:857
  277.6 16.3 %collective-permute-start.27 = (bf16[4,192,768]{2,1,0:T(8,128)(2,1)S(1)}, bf16[4,192,768]{2,1,0:T(8,128)(2,1)S(1)}, u32[]{:S(2)}, u32[]{:S(2)}) collective-permute-start(bf16[4,192,768]{2,1,0:T(8,128)(2,1)S(1)} %fusion.5), channel_id=1, source_target_pairs={{0,4},{1,3},{2,6},{3,1},{4,0},{5,7},{6,2},{7,5},{8,12},{9,11},{10,... | collective-permute-start | bytes 3538952 | tf_op jit(solution)/shard_map/ppermute | solution.py:857
  296.9 21.4 %collective-permute-start.28 = (bf16[2,2,4,96,768]{4,3,2,1,0:T(8,128)(2,1)}, bf16[2,2,4,96,768]{4,3,2,1,0:T(8,128)(2,1)S(1)}, u32[]{:S(2)}, u32[]{:S(2)}) collective-permute-start(bf16[2,2,4,96,768]{4,3,2,1,0:T(8,128)(2,1)} %get-tuple-element.353), channel_id=1, source_target_pairs={{0,1},{1,0},{2,3},{3,2},{4,5},{5,4},{6,7},{7,6},{8,9},{9,8},{10,11... | collective-permute-start | bytes 7077896 | tf_op jit(solution)/shard_map/ppermute | solution.py:857
  296.9 21.4 %collective-permute-start.29 = (bf16[192,768]{1,0:T(8,128)(2,1)S(1)}, bf16[192,768]{1,0:T(8,128)(2,1)S(1)}, u32[]{:S(2)}, u32[]{:S(2)}) collective-permute-start(bf16[192,768]{1,0:T(8,128)(2,1)S(1)} %get-tuple-element.354), channel_id=1, source_target_pairs={{0,16},{1,17},{2,18},{3,19},{4,20},{5,21},{6,22},{7,23},{8,24},{9,... | collective-permute-start | bytes 884744 | tf_op jit(solution)/shard_map/ppermute | solution.py:857
  319.4 17.7 %collective-permute-start.30 = (bf16[2,4,96,768]{3,2,1,0:T(8,128)(2,1)S(1)}, bf16[2,4,96,768]{3,2,1,0:T(8,128)(2,1)}, u32[]{:S(2)}, u32[]{:S(2)}) collective-permute-start(bf16[2,4,96,768]{3,2,1,0:T(8,128)(2,1)S(1)} %fusion.9), channel_id=1, source_target_pairs={{0,2},{1,5},{2,0},{3,7},{4,6},{5,1},{6,4},{7,3},{8,10},{9,13},{10,... | collective-permute-start | bytes 3538952 | tf_op jit(solution)/shard_map/ppermute | solution.py:857
  356.0 29.2 %collective-permute-start.35 = (bf16[2,4,192,768]{3,2,1,0:T(8,128)(2,1)}, bf16[2,4,192,768]{3,2,1,0:T(8,128)(2,1)}, u32[]{:S(2)}, u32[]{:S(2)}) collective-permute-start(bf16[2,4,192,768]{3,2,1,0:T(8,128)(2,1)} %fusion.1), channel_id=1, source_target_pairs={{0,2},{1,5},{2,0},{3,7},{4,6},{5,1},{6,4},{7,3},{8,10},{9,13},{10,... | collective-permute-start | bytes 7077896 | tf_op jit(solution)/shard_map/ppermute | solution.py:857
  357.5 25.5 %collective-permute-start.36 = (bf16[96,768]{1,0:T(8,128)(2,1)}, bf16[96,768]{1,0:T(8,128)(2,1)}, u32[]{:S(2)}, u32[]{:S(2)}) collective-permute-start(bf16[96,768]{1,0:T(8,128)(2,1)} %get-tuple-element.385), channel_id=1, source_target_pairs={{0,16},{1,17},{2,18},{3,19},{4,20},{5,21},{6,22},{7,23},{8,24},{9,... | collective-permute-start | bytes 442376 | tf_op jit(solution)/shard_map/ppermute | solution.py:857
  388.3 16.9 %collective-permute-start.37 = (bf16[4,192,768]{2,1,0:T(8,128)(2,1)}, bf16[4,192,768]{2,1,0:T(8,128)(2,1)}, u32[]{:S(2)}, u32[]{:S(2)}) collective-permute-start(bf16[4,192,768]{2,1,0:T(8,128)(2,1)} %fusion.2), channel_id=1, source_target_pairs={{0,4},{1,3},{2,6},{3,1},{4,0},{5,7},{6,2},{7,5},{8,12},{9,11},{10,... | collective-permute-start | bytes 3538952 | tf_op jit(solution)/shard_map/ppermute | solution.py:857
  410.8 18.4 %collective-permute-start.42 = (bf16[2,4,112,768]{3,2,1,0:T(8,128)(2,1)S(1)}, bf16[2,4,112,768]{3,2,1,0:T(8,128)(2,1)S(1)}, u32[]{:S(2)}, u32[]{:S(2)}) collective-permute-start(bf16[2,4,112,768]{3,2,1,0:T(8,128)(2,1)S(1)} %fusion.6), channel_id=1, source_target_pairs={{0,2},{1,5},{2,0},{3,7},{4,6},{5,1},{6,4},{7,3},{8,10},{9,13},{10,... | collective-permute-start | bytes 4128776 | tf_op jit(solution)/shard_map/ppermute | solution.py:857
  434.4 18.5 %collective-permute-start.40 = (bf16[192,768]{1,0:T(8,128)(2,1)S(1)}, bf16[192,768]{1,0:T(8,128)(2,1)S(1)}, u32[]{:S(2)}, u32[]{:S(2)}) collective-permute-start(bf16[192,768]{1,0:T(8,128)(2,1)S(1)} %copy-done.27), channel_id=1, source_target_pairs={{0,16},{1,17},{2,18},{3,19},{4,20},{5,21},{6,22},{7,23},{8,24},{9,... | collective-permute-start | bytes 884744 | tf_op jit(solution)/shard_map/ppermute | solution.py:857
  445.1 16.4 %collective-permute-start.47 = (bf16[112,768]{1,0:T(8,128)(2,1)}, bf16[112,768]{1,0:T(8,128)(2,1)}, u32[]{:S(2)}, u32[]{:S(2)}) collective-permute-start(bf16[112,768]{1,0:T(8,128)(2,1)} %get-tuple-element.426), channel_id=1, source_target_pairs={{0,16},{1,17},{2,18},{3,19},{4,20},{5,21},{6,22},{7,23},{8,24},{9,... | collective-permute-start | bytes 516104 | tf_op jit(solution)/shard_map/ppermute | solution.py:857
  (82 other events, 935.7 us)
Sparse Core Ops, SparseCore 0:
  64.9 39.1 all-gather.2

commit v7 on v6

--- a/solution.py
+++ b/solution.py
@@ -1061,8 +1061,8 @@
         )
         own_small = lax.reduce_precision(own_small, 8, 7)
         small_sends = [(functools.partial(exchange.part, bits), own_small) for bits in range(1, 4)]
-        late = exchange.gather_z(late)
         came, _ = lane.step(exchange.z_sends([attn_pieces[0]] * depth))
+        late = exchange.gather_z(lane.after_last(late))
         attn_zero = Spread(exchange, jnp.stack([attn_pieces[0]] + came), False)
         ffn_piece = jnp.concatenate([up_pieces[0], down_pieces[0]], axis=0)
         ffn_sends = exchange.z_sends([ffn_piece] * depth)

time: 512 us -> 512 us (level)
  no operation moved by 1% of the time
where the time goes in v7:
time: 512 us; the launch traced here: 508 us
  Pallas kernels  232 us (45%)
  waiting for transfers between devices  115 us (22%)
  starting transfers between devices  67.4 us (13%)
  other arithmetic  50.6 us (10%)
  between operations  23.7 us (5%)
  local copies, waits for them, and re-layouts  19.4 us (4%)
    ppermute x54, waiting for transfers between devices, swap(): return lax.ppermute(value, ('dp', 'tensor'), pairs)  115 us
    ppermute x54, starting transfers between devices, swap(): return lax.ppermute(value, ('dp', 'tensor'), pairs)  67.4 us
    pallas_call x2, Pallas kernels, attention_backward(): pl.pallas_call(attention_backward_kernel, grid=((end - begin) // block_pa...  48.2 us
    pallas_call x4, Pallas kernels, ffn_weight_split(): pl.pallas_call(functools.partial(ffn_weight_split_kernel, core), grid_spe...  44.3 us
    pallas_call x2, Pallas kernels, attention_forward(): pl.pallas_call(functools.partial(attention_forward_kernel, plan), grid=(p...  41.6 us
    pallas_call x1, Pallas kernels, ffn_both(): pl.pallas_call(functools.partial(ffn_both_kernel, (up_w[0], down_w[0])),...  32.2 us
    pallas_call x2, Pallas kernels, attention_weight_split(): pl.pallas_call(attention_weight_split_kernel, grid=(3,), in_specs=[pl.Blo...  23.9 us
    pallas_call x1, Pallas kernels, ffn_forward(): pl.pallas_call(functools.partial(ffn_forward_kernel, (up_w[0], down_w[0])...  21.9 us
  transfers between devices with their start and end apart: 55, of which 30 were waited for; matrix products, arithmetic and copies ran while one was open for 5% of the time, Pallas kernels for 37%

profile of v7, /device:TPU:0, one launch (start us, length us, event | category | flops | bytes accessed | tf_op | source)
XLA Modules:
  0.0 507.8 jit_solution(8351724060605694973)
XLA Ops:
  9.4 5.1 %collective-permute-start.2 = (bf16[96,768]{1,0:T(8,128)(2,1)S(1)}, bf16[96,768]{1,0:T(8,128)(2,1)S(1)}, u32[]{:S(2)}, u32[]{:S(2)}) collective-permute-start(bf16[96,768]{1,0:T(8,128)(2,1)S(1)} %bitcast.166), channel_id=1, source_target_pairs={{0,24},{1,25},{2,26},{3,27},{4,28},{5,29},{6,30},{7,31},{8,16},{9,... | collective-permute-start | bytes 442376 | tf_op jit(solution)/shard_map/ppermute | solution.py:857
  19.3 7.7 %collective-permute-done.1 = bf16[96,768]{1,0:T(8,128)(2,1)S(1)} collective-permute-done((bf16[96,768]{1,0:T(8,128)(2,1)S(1)}, bf16[96,768]{1,0:T(8,128)(2,1)S(1)}, u32[]{:S(2)}, u32[]{:S(2)}) %collective-permute-start.1) | collective-permute-done | bytes 147488 | tf_op jit(solution)/shard_map/ppermute | solution.py:857
  36.3 7.1 %collective-permute-done.4 = bf16[192,768]{1,0:T(8,128)(2,1)S(1)} collective-permute-done((bf16[192,768]{1,0:T(8,128)(2,1)S(1)}, bf16[192,768]{1,0:T(8,128)(2,1)S(1)}, u32[]{:S(2)}, u32[]{:S(2)}) %collective-permute-start.4) | collective-permute-done | bytes 294944 | tf_op jit(solution)/shard_map/ppermute | solution.py:857
  48.8 11.7 %collective-permute-done.10 = bf16[192,768]{1,0:T(8,128)(2,1)S(1)} collective-permute-done((bf16[192,768]{1,0:T(8,128)(2,1)}, bf16[192,768]{1,0:T(8,128)(2,1)S(1)}, u32[]{:S(2)}, u32[]{:S(2)}) %collective-permute-start.10) | collective-permute-done | bytes 294944 | tf_op jit(solution)/shard_map/ppermute | solution.py:857
  65.8 13.2 %collective-permute-done.13 = bf16[4,192,768]{2,1,0:T(8,128)(2,1)} collective-permute-done((bf16[4,192,768]{2,1,0:T(8,128)(2,1)S(1)}, bf16[4,192,768]{2,1,0:T(8,128)(2,1)}, u32[]{:S(2)}, u32[]{:S(2)}) %collective-permute-start.13) | collective-permute-done | bytes 1179680 | tf_op jit(solution)/shard_map/ppermute | solution.py:857
  83.7 20.8 %attention_forward.2 = (f32[1024,768]{1,0:T(8,128)}, bf16[1024,768]{1,0:T(8,128)(2,1)}, bf16[1024,768]{1,0:T(8,128)(2,1)}, bf16[1024,2304]{1,0:T(8,128)(2,1)}, b...) custom-call(s32[2]{0:T(128)} %pad_add_fusion.me_ref, ...), custom_call_target="tpu_custom_call" | custom-call | flops 20000000000 | bytes 30000000 | tf_op jit(solution)/shard_map/attention_forward/pallas_call | solution.py:189
  104.5 4.9 collective-permute-done.14.refs_1_.refs_5_
  114.3 7.8 %collective-permute-done.17 = bf16[4,96,768]{2,1,0:T(8,128)(2,1)S(1)} collective-permute-done((bf16[4,96,768]{2,1,0:T(8,128)(2,1)S(1)}, bf16[4,96,768]{2,1,0:T(8,128)(2,1)S(1)}, u32[]{:S(2)}, u32[]{:S(2)}) %collective-permute-start.17) | collective-permute-done | bytes 589856 | tf_op jit(solution)/shard_map/ppermute | solution.py:857
  126.5 21.9 %ffn_forward.1 = (f32[1024,768]{1,0:T(8,128)}, bf16[1024,3072]{1,0:T(8,128)(2,1)}, bf16[1024,3072]{1,0:T(8,128)(2,1)}, bf16[4,768,768]{2,1,0:T(8,128)(2,1)}, bf16[4,768,768]{2,1,0:T(8,128)(2,1)}) custom-call(s32[2]{0:T(128)} %pad_add_fusion.me_ref, bf16[1024,768]{1,0:T(8,128)(2,1)} %get-tuple-element.286.nffn_ref, ...), custom_call_target="tpu_custom_call" | custom-call | flops 15000000512 | bytes 30000000 | tf_op jit(solution)/shard_map/ffn_forward/pallas_call | solution.py:281
  156.7 20.7 %attention_forward.3 = (f32[1024,768]{1,0:T(8,128)}, bf16[1024,768]{1,0:T(8,128)(2,1)}, bf16[1024,768]{1,0:T(8,128)(2,1)}, bf16[1024,2304]{1,0:T(8,128)(2,1)}, b...) custom-call(s32[2]{0:T(128)} %pad_add_fusion.me_ref, ...), custom_call_target="tpu_custom_call" | custom-call | flops 20000000000 | bytes 30000000 | tf_op jit(solution)/shard_map/attention_forward/pallas_call | solution.py:189
  177.4 6.4 %collective-permute-done.22.refs_1_.refs_5_ = bf16[2,4,192,768]{3,2,1,0:T(8,128)(2,1)S(1)} collective-permute-done((bf16[2,4,192,768]{3,2,1,0:T(8,128)(2,1)S(1)}, bf16[2,4,192,768]{3,2,1,0:T(8,128)(2,1)S(1)}, u32[]{:S(2)}, u32[]{:S(2)}) %collective-permute-start.22) | collective-permute-done | bytes 2359328 | tf_op jit(solution)/shard_map/ppermute | solution.py:857
  189.9 32.2 %ffn_both.1 = (f32[1024,768]{1,0:T(8,128)}, bf16[1024,3072]{1,0:T(8,128)(2,1)}, bf16[1024,3072]{1,0:T(8,128)(2,1)}, f32[1024,768]{1,0:T(8,128)}, f32[8,768]{1,0:T(8,128)}, /*index=5*/f32[1,3072]{1,0:T(1,128)}) custom-call(s32[2]{0:T(128)} %pad_add_fusion.me_ref, bf16[1024,768]{1,0:T(8,128)(2,1)} %get-tuple-element.318.nffn_ref, ...), custom_call_target="tpu_custom_call" | custom-call | flops 24999999488 | bytes 40000000 | tf_op jit(solution)/shard_map/ffn_both/pallas_call | solution.py:449
  222.0 11.4 %ffn_weight.4 = (bf16[2,2,4,192,768]{4,3,2,1,0:T(8,128)(2,1)}, bf16[768,1024]{1,0:T(8,128)(2,1)}, bf16[768,1024]{1,0:T(8,128)(2,1)}) custom-call(s32[2]{0:T(128)} %pad_add_fusion.me_ref, bf16[1024,768]{1,0:T(8,128)(2,1)} %get-tuple-element.318.nffn_ref, bf16[1024,768]{1,0:T(8,128)(2,1)} %grad_ref.3, bf16[1024,3072]{1,0:T(8,128)(2,1)} %get-tuple-element.330.gupper_ref, ...), custom_call_target="tpu_custom_call" | custom-call | flops 8000000000 | bytes 15000000 | tf_op jit(solution)/shard_map/ffn_weight/pallas_call | solution.py:711
  234.0 10.3 %ffn_weight.5 = bf16[2,2,4,192,768]{4,3,2,1,0:T(8,128)(2,1)} custom-call(s32[2]{0:T(128)} %pad_add_fusion.me_ref, bf16[768,1024]{1,0:T(8,128)(2,1)} %get-tuple-element.329.nffn_ref, bf16[768,1024]{1,0:T(8,128)(2,1)} %get-tuple-element.327.grad_ref, bf16[1024,3072]{1,0:T(8,128)(2,1)} %get-tuple-element.330.gupper_ref, ...), custom_call_target="tpu_custom_call" | custom-call | flops 8000000000 | bytes 15000000 | tf_op jit(solution)/shard_map/ffn_weight/pallas_call | solution.py:711
  248.2 24.5 %attention_backward.2 = (f32[1024,768]{1,0:T(8,128)}, bf16[1024,2304]{1,0:T(8,128)(2,1)}, f32[8,768]{1,0:T(8,128)}) custom-call(f32[1024,768]{1,0:T(8,128)} %get-tuple-element.335.gmiddle_ref, f32[1024,768]{1,0:T(8,128)} %get-tuple-element.302.stream_ref, bf16[1024,2304]{1,0:T(8,128)(2,1)} %get-tuple-element.336.proj_ref, ...), custom_call_target="tpu_custom_call" | custom-call | flops 15000000512 | bytes 20000000 | tf_op jit(solution)/shard_map/attention_backward/pallas_call | solution.py:578
  279.0 11.7 %attention_weight.2 = (bf16[2,2,4,96,768]{4,3,2,1,0:T(8,128)(2,1)}, bf16[2,2,4,96,768]{4,3,2,1,0:T(8,128)(2,1)}) custom-call(s32[2]{0:T(128)} %pad_add_fusion.me_ref, bf16[1024,768]{1,0:T(8,128)(2,1)} %get-tuple-element.346.normed_ref, bf16[1024,768]{1,0:T(8,128)(2,1)} %get-tuple-element.347.mixed_ref, bf16[1024,2304]{1,0:T(8,128)(2,1)} %get-tuple-element.348.gproj_ref, ...), custom_call_target="tpu_custom_call" | custom-call | flops 10000000000 | bytes 20000000 | tf_op jit(solution)/shard_map/attention_weight/pallas_call | solution.py:783
  298.6 19.7 %ffn_backward.1 = (bf16[1024,3072]{1,0:T(8,128)(2,1)}, f32[1024,768]{1,0:T(8,128)}, f32[8,768]{1,0:T(8,128)}, f32[1,3072]{1,0:T(1,128)}) custom-call(s32[2]{0:T(128)} %pad_add_fusion.me_ref, f32[1024,768]{1,0:T(8,128)} %get-tuple-element.357.grad_ref, bf16[1024,3072]{1,0:T(8,128)(2,1)} %get-tuple-element.358.slope_ref, ...), custom_call_target="tpu_custom_call" | custom-call | flops 15000000512 | bytes 30000000 | tf_op jit(solution)/shard_map/ffn_backward/pallas_call | solution.py:356
  323.8 11.9 %ffn_weight.6 = (bf16[2,2,4,192,768]{4,3,2,1,0:T(8,128)(2,1)}, bf16[768,1024]{1,0:T(8,128)(2,1)}, bf16[768,1024]{1,0:T(8,128)(2,1)}) custom-call(s32[2]{0:T(128)} %pad_add_fusion.me_ref, bf16[1024,768]{1,0:T(8,128)(2,1)} %get-tuple-element.286.nffn_ref, f32[1024,768]{1,0:T(8,128)} %get-tuple-element.357.grad_ref, ...), custom_call_target="tpu_custom_call" | custom-call | flops 8000000000 | bytes 15000000 | tf_op jit(solution)/shard_map/ffn_weight/pallas_call | solution.py:711
  339.2 10.7 %ffn_weight.7 = bf16[2,2,4,192,768]{4,3,2,1,0:T(8,128)(2,1)} custom-call(s32[2]{0:T(128)} %pad_add_fusion.me_ref, bf16[768,1024]{1,0:T(8,128)(2,1)} %get-tuple-element.380.nffn_ref, bf16[768,1024]{1,0:T(8,128)(2,1)} %get-tuple-element.377.grad_ref, bf16[1024,3072]{1,0:T(8,128)(2,1)} %get-tuple-element.381.gupper_ref, ...), custom_call_target="tpu_custom_call" | custom-call | flops 8000000000 | bytes 15000000 | tf_op jit(solution)/shard_map/ffn_weight/pallas_call | solution.py:711
  359.3 23.7 %attention_backward.3 = (f32[1024,768]{1,0:T(8,128)}, bf16[1024,2304]{1,0:T(8,128)(2,1)}, f32[8,768]{1,0:T(8,128)}) custom-call(f32[1024,768]{1,0:T(8,128)} %get-tuple-element.388.gmiddle_ref, bf16[1024,768]{1,0:T(8,128)(2,1)} %stream_ref.2, bf16[1024,2304]{1,0:T(8,128)(2,1)} %get-tuple-element.389.proj_ref, ...), custom_call_target="tpu_custom_call" | custom-call | flops 15000000512 | bytes 20000000 | tf_op jit(solution)/shard_map/attention_backward/pallas_call | solution.py:578
  392.9 12.2 %attention_weight.3 = (bf16[2,2,4,112,768]{4,3,2,1,0:T(8,128)(2,1)}, bf16[2,2,4,112,768]{4,3,2,1,0:T(8,128)(2,1)}) custom-call(s32[2]{0:T(128)} %pad_add_fusion.me_ref, bf16[1024,768]{1,0:T(8,128)(2,1)} %get-tuple-element.405.normed_ref, bf16[1024,768]{1,0:T(8,128)(2,1)} %get-tuple-element.406.mixed_ref, bf16[1024,2304]{1,0:T(8,128)(2,1)} %get-tuple-element.407.gproj_ref, ...), custom_call_target="tpu_custom_call" | custom-call | flops 10000000000 | bytes 20000000 | tf_op jit(solution)/shard_map/attention_weight/pallas_call | solution.py:783
  415.3 5.4 %collective-permute-done.43 = bf16[192,768]{1,0:T(8,128)(2,1)S(1)} collective-permute-done((bf16[192,768]{1,0:T(8,128)(2,1)S(1)}, bf16[192,768]{1,0:T(8,128)(2,1)S(1)}, u32[]{:S(2)}, u32[]{:S(2)}) %collective-permute-start.43) | collective-permute-done | bytes 294944 | tf_op jit(solution)/shard_map/ppermute | solution.py:857
  420.6 7.5 %collective-permute-done.44 = bf16[192,768]{1,0:T(8,128)(2,1)S(1)} collective-permute-done((bf16[192,768]{1,0:T(8,128)(2,1)S(1)}, bf16[192,768]{1,0:T(8,128)(2,1)S(1)}, u32[]{:S(2)}, u32[]{:S(2)}) %collective-permute-start.44) | collective-permute-done | bytes 294944 | tf_op jit(solution)/shard_map/ppermute | solution.py:857
  471.3 5.3 %collective-permute-start.51 = (f32[1,1]{1,0:T(1,128)}, f32[1,1]{1,0:T(1,128)}, u32[]{:S(2)}, u32[]{:S(2)}) collective-permute-start(f32[1,1]{1,0:T(1,128)} %add.332), channel_id=1, source_target_pairs={{0,4},{1,5},{2,6},{3,7},{4,0},{5,1},{6,2},{7,3},{8,12},{9,13},{10,... | collective-permute-start | bytes 20 | tf_op jit(solution)/shard_map/ppermute | solution.py:857
  (282 shorter events, 170.2 us)
Async XLA Ops:
  7.2 103.6 %all-gather.3.cloned.1.call-start = ((), (), s32[]{:S(2)}) async-start(), calls=%async_computation | async-start | bytes 2211840 | tf_op jit(solution)/shard_map/all_gather | solution.py:888
  27.1 16.3 %collective-permute-start.3 = (bf16[4,96,768]{2,1,0:T(8,128)(2,1)S(1)}, bf16[4,96,768]{2,1,0:T(8,128)(2,1)S(1)}, u32[]{:S(2)}, u32[]{:S(2)}) collective-permute-start(bf16[4,96,768]{2,1,0:T(8,128)(2,1)S(1)} %get-tuple-element.236), channel_id=1, source_target_pairs={{0,4},{1,3},{2,6},{3,1},{4,0},{5,7},{6,2},{7,5},{8,12},{9,11},{10,... | collective-permute-start | bytes 1769480 | tf_op jit(solution)/shard_map/ppermute | solution.py:857
  43.5 16.9 %collective-permute-start.8 = (bf16[2,4,96,768]{3,2,1,0:T(8,128)(2,1)S(1)}, bf16[2,4,96,768]{3,2,1,0:T(8,128)(2,1)}, u32[]{:S(2)}, u32[]{:S(2)}) collective-permute-start(bf16[2,4,96,768]{3,2,1,0:T(8,128)(2,1)S(1)} %pad_maximum_fusion.2.refs_0_), channel_id=1, source_target_pairs={{0,2},{1,5},{2,0},{3,7},{4,6},{5,1},{6,4},{7,3},{8,10},{9,13},{10,... | collective-permute-start | bytes 3538952 | tf_op jit(solution)/shard_map/ppermute | solution.py:857
  44.1 16.4 %collective-permute-start.9 = (bf16[2,4,96,768]{3,2,1,0:T(8,128)(2,1)S(1)}, bf16[2,4,96,768]{3,2,1,0:T(8,128)(2,1)}, u32[]{:S(2)}, u32[]{:S(2)}) collective-permute-start(bf16[2,4,96,768]{3,2,1,0:T(8,128)(2,1)S(1)} %pad_maximum_fusion.2.refs_0_), channel_id=1, source_target_pairs={{0,1},{1,0},{2,3},{3,2},{4,5},{5,4},{6,7},{7,6},{8,9},{9,8},{10,11... | collective-permute-start | bytes 3538952 | tf_op jit(solution)/shard_map/ppermute | solution.py:857
  45.0 15.5 %collective-permute-start.10 = (bf16[192,768]{1,0:T(8,128)(2,1)}, bf16[192,768]{1,0:T(8,128)(2,1)S(1)}, u32[]{:S(2)}, u32[]{:S(2)}) collective-permute-start(bf16[192,768]{1,0:T(8,128)(2,1)} %copy-done.26), channel_id=1, source_target_pairs={{0,8},{1,9},{2,10},{3,11},{4,12},{5,13},{6,14},{7,15},{8,0},{9,1},... | collective-permute-start | bytes 884744 | tf_op jit(solution)/shard_map/ppermute | solution.py:857
  62.6 16.4 %collective-permute-start.13 = (bf16[4,192,768]{2,1,0:T(8,128)(2,1)S(1)}, bf16[4,192,768]{2,1,0:T(8,128)(2,1)}, u32[]{:S(2)}, u32[]{:S(2)}) collective-permute-start(bf16[4,192,768]{2,1,0:T(8,128)(2,1)S(1)} %get-tuple-element.259), channel_id=1, source_target_pairs={{0,4},{1,3},{2,6},{3,1},{4,0},{5,7},{6,2},{7,5},{8,12},{9,11},{10,... | collective-permute-start | bytes 3538952 | tf_op jit(solution)/shard_map/ppermute | solution.py:857
  80.5 28.9 %collective-permute-start.14 = (bf16[2,4,192,768]{3,2,1,0:T(8,128)(2,1)S(1)}, bf16[2,4,192,768]{3,2,1,0:T(8,128)(2,1)S(1)}, u32[]{:S(2)}, u32[]{:S(2)}) collective-permute-start(bf16[2,4,192,768]{3,2,1,0:T(8,128)(2,1)S(1)} %pad_maximum_fusion.refs_0_.refs_4_), channel_id=1, source_target_pairs={{0,2},{1,5},{2,0},{3,7},{4,6},{5,1},{6,4},{7,3},{8,10},{9,13},{10,... | collective-permute-start | bytes 7077896 | tf_op jit(solution)/shard_map/ppermute | solution.py:857
  81.9 27.5 %collective-permute-start.15 = (bf16[2,4,192,768]{3,2,1,0:T(8,128)(2,1)S(1)}, bf16[2,4,192,768]{3,2,1,0:T(8,128)(2,1)}, u32[]{:S(2)}, u32[]{:S(2)}) collective-permute-start(bf16[2,4,192,768]{3,2,1,0:T(8,128)(2,1)S(1)} %pad_maximum_fusion.refs_0_.refs_4_), channel_id=1, source_target_pairs={{0,1},{1,0},{2,3},{3,2},{4,5},{5,4},{6,7},{7,6},{8,9},{9,8},{10,11... | collective-permute-start | bytes 7077896 | tf_op jit(solution)/shard_map/ppermute | solution.py:857
  123.7 28.1 %collective-permute-start.18 = (bf16[2,4,96,768]{3,2,1,0:T(8,128)(2,1)S(1)}, bf16[2,4,96,768]{3,2,1,0:T(8,128)(2,1)S(1)}, u32[]{:S(2)}, u32[]{:S(2)}) collective-permute-start(bf16[2,4,96,768]{3,2,1,0:T(8,128)(2,1)S(1)} %pad_maximum_fusion.4.refs_0_), channel_id=1, source_target_pairs={{0,2},{1,5},{2,0},{3,7},{4,6},{5,1},{6,4},{7,3},{8,10},{9,13},{10,... | collective-permute-start | bytes 3538952 | tf_op jit(solution)/shard_map/ppermute | solution.py:857
  125.0 26.7 %collective-permute-start.19 = (bf16[2,4,96,768]{3,2,1,0:T(8,128)(2,1)S(1)}, bf16[2,4,96,768]{3,2,1,0:T(8,128)(2,1)S(1)}, u32[]{:S(2)}, u32[]{:S(2)}) collective-permute-start(bf16[2,4,96,768]{3,2,1,0:T(8,128)(2,1)S(1)} %pad_maximum_fusion.4.refs_0_), channel_id=1, source_target_pairs={{0,1},{1,0},{2,3},{3,2},{4,5},{5,4},{6,7},{7,6},{8,9},{9,8},{10,11... | collective-permute-start | bytes 3538952 | tf_op jit(solution)/shard_map/ppermute | solution.py:857
  125.1 26.7 %collective-permute-start.20 = (bf16[4,192,768]{2,1,0:T(8,128)(2,1)S(1)}, bf16[4,192,768]{2,1,0:T(8,128)(2,1)S(1)}, u32[]{:S(2)}, u32[]{:S(2)}) collective-permute-start(bf16[4,192,768]{2,1,0:T(8,128)(2,1)S(1)} %get-tuple-element.285), channel_id=1, source_target_pairs={{0,4},{1,3},{2,6},{3,1},{4,0},{5,7},{6,2},{7,5},{8,12},{9,11},{10,... | collective-permute-start | bytes 3538952 | tf_op jit(solution)/shard_map/ppermute | solution.py:857
  155.0 28.8 %collective-permute-start.22 = (bf16[2,4,192,768]{3,2,1,0:T(8,128)(2,1)S(1)}, bf16[2,4,192,768]{3,2,1,0:T(8,128)(2,1)S(1)}, u32[]{:S(2)}, u32[]{:S(2)}) collective-permute-start(bf16[2,4,192,768]{3,2,1,0:T(8,128)(2,1)S(1)} %pad_maximum_fusion.1.refs_0_.refs_4_), channel_id=1, source_target_pairs={{0,2},{1,5},{2,0},{3,7},{4,6},{5,1},{6,4},{7,3},{8,10},{9,13},{10,... | collective-permute-start | bytes 7077896 | tf_op jit(solution)/shard_map/ppermute | solution.py:857
  156.7 27.2 %collective-permute-start.23 = (bf16[2,4,192,768]{3,2,1,0:T(8,128)(2,1)S(1)}, bf16[2,4,192,768]{3,2,1,0:T(8,128)(2,1)S(1)}, u32[]{:S(2)}, u32[]{:S(2)}) collective-permute-start(bf16[2,4,192,768]{3,2,1,0:T(8,128)(2,1)S(1)} %pad_maximum_fusion.1.refs_0_.refs_4_), channel_id=1, source_target_pairs={{0,1},{1,0},{2,3},{3,2},{4,5},{5,4},{6,7},{7,6},{8,9},{9,8},{10,11... | collective-permute-start | bytes 7077896 | tf_op jit(solution)/shard_map/ppermute | solution.py:857
  246.5 29.0 %collective-permute-start.26 = (bf16[2,4,192,768]{3,2,1,0:T(8,128)(2,1)S(1)}, bf16[2,4,192,768]{3,2,1,0:T(8,128)(2,1)}, u32[]{:S(2)}, u32[]{:S(2)}) collective-permute-start(bf16[2,4,192,768]{3,2,1,0:T(8,128)(2,1)S(1)} %fusion), channel_id=1, source_target_pairs={{0,2},{1,5},{2,0},{3,7},{4,6},{5,1},{6,4},{7,3},{8,10},{9,13},{10,... | collective-permute-start | bytes 7077896 | tf_op jit(solution)/shard_map/ppermute | solution.py:857
  277.6 16.3 %collective-permute-start.27 = (bf16[4,192,768]{2,1,0:T(8,128)(2,1)S(1)}, bf16[4,192,768]{2,1,0:T(8,128)(2,1)S(1)}, u32[]{:S(2)}, u32[]{:S(2)}) collective-permute-start(bf16[4,192,768]{2,1,0:T(8,128)(2,1)S(1)} %fusion.5), channel_id=1, source_target_pairs={{0,4},{1,3},{2,6},{3,1},{4,0},{5,7},{6,2},{7,5},{8,12},{9,11},{10,... | collective-permute-start | bytes 3538952 | tf_op jit(solution)/shard_map/ppermute | solution.py:857
  296.9 21.4 %collective-permute-start.28 = (bf16[2,2,4,96,768]{4,3,2,1,0:T(8,128)(2,1)}, bf16[2,2,4,96,768]{4,3,2,1,0:T(8,128)(2,1)S(1)}, u32[]{:S(2)}, u32[]{:S(2)}) collective-permute-start(bf16[2,2,4,96,768]{4,3,2,1,0:T(8,128)(2,1)} %get-tuple-element.355), channel_id=1, source_target_pairs={{0,1},{1,0},{2,3},{3,2},{4,5},{5,4},{6,7},{7,6},{8,9},{9,8},{10,11... | collective-permute-start | bytes 7077896 | tf_op jit(solution)/shard_map/ppermute | solution.py:857
  296.9 21.4 %collective-permute-start.29 = (bf16[192,768]{1,0:T(8,128)(2,1)S(1)}, bf16[192,768]{1,0:T(8,128)(2,1)S(1)}, u32[]{:S(2)}, u32[]{:S(2)}) collective-permute-start(bf16[192,768]{1,0:T(8,128)(2,1)S(1)} %get-tuple-element.356), channel_id=1, source_target_pairs={{0,16},{1,17},{2,18},{3,19},{4,20},{5,21},{6,22},{7,23},{8,24},{9,... | collective-permute-start | bytes 884744 | tf_op jit(solution)/shard_map/ppermute | solution.py:857
  319.4 17.7 %collective-permute-start.30 = (bf16[2,4,96,768]{3,2,1,0:T(8,128)(2,1)S(1)}, bf16[2,4,96,768]{3,2,1,0:T(8,128)(2,1)}, u32[]{:S(2)}, u32[]{:S(2)}) collective-permute-start(bf16[2,4,96,768]{3,2,1,0:T(8,128)(2,1)S(1)} %fusion.9), channel_id=1, source_target_pairs={{0,2},{1,5},{2,0},{3,7},{4,6},{5,1},{6,4},{7,3},{8,10},{9,13},{10,... | collective-permute-start | bytes 3538952 | tf_op jit(solution)/shard_map/ppermute | solution.py:857
  356.0 29.2 %collective-permute-start.35 = (bf16[2,4,192,768]{3,2,1,0:T(8,128)(2,1)}, bf16[2,4,192,768]{3,2,1,0:T(8,128)(2,1)}, u32[]{:S(2)}, u32[]{:S(2)}) collective-permute-start(bf16[2,4,192,768]{3,2,1,0:T(8,128)(2,1)} %fusion.1), channel_id=1, source_target_pairs={{0,2},{1,5},{2,0},{3,7},{4,6},{5,1},{6,4},{7,3},{8,10},{9,13},{10,... | collective-permute-start | bytes 7077896 | tf_op jit(solution)/shard_map/ppermute | solution.py:857
  357.5 25.5 %collective-permute-start.36 = (bf16[96,768]{1,0:T(8,128)(2,1)}, bf16[96,768]{1,0:T(8,128)(2,1)}, u32[]{:S(2)}, u32[]{:S(2)}) collective-permute-start(bf16[96,768]{1,0:T(8,128)(2,1)} %get-tuple-element.387), channel_id=1, source_target_pairs={{0,16},{1,17},{2,18},{3,19},{4,20},{5,21},{6,22},{7,23},{8,24},{9,... | collective-permute-start | bytes 442376 | tf_op jit(solution)/shard_map/ppermute | solution.py:857
  388.3 16.9 %collective-permute-start.37 = (bf16[4,192,768]{2,1,0:T(8,128)(2,1)}, bf16[4,192,768]{2,1,0:T(8,128)(2,1)}, u32[]{:S(2)}, u32[]{:S(2)}) collective-permute-start(bf16[4,192,768]{2,1,0:T(8,128)(2,1)} %fusion.2), channel_id=1, source_target_pairs={{0,4},{1,3},{2,6},{3,1},{4,0},{5,7},{6,2},{7,5},{8,12},{9,11},{10,... | collective-permute-start | bytes 3538952 | tf_op jit(solution)/shard_map/ppermute | solution.py:857
  410.8 18.4 %collective-permute-start.42 = (bf16[2,4,112,768]{3,2,1,0:T(8,128)(2,1)S(1)}, bf16[2,4,112,768]{3,2,1,0:T(8,128)(2,1)S(1)}, u32[]{:S(2)}, u32[]{:S(2)}) collective-permute-start(bf16[2,4,112,768]{3,2,1,0:T(8,128)(2,1)S(1)} %fusion.6), channel_id=1, source_target_pairs={{0,2},{1,5},{2,0},{3,7},{4,6},{5,1},{6,4},{7,3},{8,10},{9,13},{10,... | collective-permute-start | bytes 4128776 | tf_op jit(solution)/shard_map/ppermute | solution.py:857
  434.4 18.5 %collective-permute-start.40 = (bf16[192,768]{1,0:T(8,128)(2,1)S(1)}, bf16[192,768]{1,0:T(8,128)(2,1)S(1)}, u32[]{:S(2)}, u32[]{:S(2)}) collective-permute-start(bf16[192,768]{1,0:T(8,128)(2,1)S(1)} %copy-done.27), channel_id=1, source_target_pairs={{0,16},{1,17},{2,18},{3,19},{4,20},{5,21},{6,22},{7,23},{8,24},{9,... | collective-permute-start | bytes 884744 | tf_op jit(solution)/shard_map/ppermute | solution.py:857
  445.1 16.4 %collective-permute-start.47 = (bf16[112,768]{1,0:T(8,128)(2,1)}, bf16[112,768]{1,0:T(8,128)(2,1)}, u32[]{:S(2)}, u32[]{:S(2)}) collective-permute-start(bf16[112,768]{1,0:T(8,128)(2,1)} %get-tuple-element.428), channel_id=1, source_target_pairs={{0,16},{1,17},{2,18},{3,19},{4,20},{5,21},{6,22},{7,23},{8,24},{9,... | collective-permute-start | bytes 516104 | tf_op jit(solution)/shard_map/ppermute | solution.py:857
  (82 other events, 935.7 us)
Sparse Core Ops, SparseCore 0:
  64.9 39.1 all-gather.2
